TPU v7x, 256 devices: a whole 4x4x8 slice. The times are simulated.
256 devices in a mesh: face: 128 (over x, y_hi, z, core), sub: 2 (over y_lo).
Axes of the slice: x: 4, y: 4 (y_hi: 2, y_lo: 2; y = y_hi * 2 + y_lo), z: 8, core: 2. Of those that a mesh axis runs over, the one named last changes fastest.
Arguments:
- inputs: bfloat16 [128, 2, 64, 64, 128], P('face', 'sub'), may hold values from -6 to 6
- kernel_one: bfloat16 [3, 3, 128, 128], replicated, may hold values from -0.1875 to 0.1875
- kernel_two: bfloat16 [3, 3, 128, 128], replicated, may hold values from -0.1875 to 0.1875
- cotangent: bfloat16 [128, 2, 64, 64, 128], P('face', 'sub'), may hold values from -6 to 6
- edge_codes: int32 [128, 2, 4], replicated, may hold values from 0 to 7
- corner_codes: int32 [128, 2, 4], replicated, may hold values from 0 to 3
Outputs:
- outputs: bfloat16 [128, 2, 64, 64, 128], P('face', 'sub')
- grad_inputs: bfloat16 [128, 2, 64, 64, 128], P('face', 'sub')
- grad_kernel_one: float32 [3, 3, 128, 128], replicated
- grad_kernel_two: float32 [3, 3, 128, 128], replicated
All inputs are finite; a program needn't handle non-finite values.
Results may differ from a plain program's by a relative error of at most 0.005.
Values may be sent and summed in bfloat16 or wider, within the bound.
No kernel may reach another device: no remote copies, remote signals or barrier semaphores. Data moves between devices by JAX's collectives and lax.ppermute only.
A program may use at most 128 MiB of HBM per device.

v0:
```python
import math

import jax
import jax.numpy as jnp
from jax import lax
from jax.sharding import PartitionSpec as P

GRID_ROWS = 8


def shifted(x, axis, by):
    size = lax.axis_size(axis)
    return lax.ppermute(x, axis, [(i, (i + by) % size) for i in range(size)])


def neighbour_steps():
    row_width = lax.axis_size("face") // GRID_ROWS * lax.axis_size("sub")
    return (
        [-row_width, 1, row_width, -1],
        [-row_width - 1, -row_width + 1, row_width + 1, row_width - 1],
    )


def pull_sets(payload, offset):
    return shifted(payload, ("face", "sub"), offset)


def back_sets(payload, offset):
    return shifted(payload, ("face", "sub"), offset)


def fill_halo(fields, edge_codes, corner_codes):
    device_count = lax.axis_size(("face", "sub"))
    own_index = lax.axis_index(("face", "sub"))
    side_len = fields.shape[1]
    edge_table = edge_codes.reshape(device_count, 4)
    corner_table = corner_codes.reshape(device_count, 4)
    edge_steps, corner_steps = neighbour_steps()
    edge_sets = jnp.stack([fields[0, 0], fields[0, :, -1], fields[0, -1], fields[0, :, 0]])
    corner_sets = jnp.stack(
        [fields[0, 0, 0], fields[0, 0, -1], fields[0, -1, -1], fields[0, -1, 0]]
    )
    strips = []
    corner_vals = []
    for direction in range(4):
        arrived = pull_sets(edge_sets, -edge_steps[direction])
        edge_code = edge_table[own_index, direction]
        picked = lax.dynamic_index_in_dim(arrived, edge_code % 4, 0, keepdims=False)
        strips.append(jnp.where(edge_code >= 4, picked[::-1], picked))
    for corner in range(4):
        arrived = pull_sets(corner_sets, -corner_steps[corner])
        corner_vals.append(
            lax.dynamic_index_in_dim(arrived, corner_table[own_index, corner], 0, keepdims=False)
        )
    padded = jnp.pad(fields, ((0, 0), (1, 1), (1, 1), (0, 0)))
    last = side_len + 1
    padded = padded.at[0, 0, 1:last].set(strips[0]).at[0, 1:last, last].set(strips[1])
    padded = padded.at[0, last, 1:last].set(strips[2]).at[0, 1:last, 0].set(strips[3])
    padded = padded.at[0, 0, 0].set(corner_vals[0]).at[0, 0, last].set(corner_vals[1])
    padded = padded.at[0, last, last].set(corner_vals[2]).at[0, last, 0].set(corner_vals[3])
    return padded


def return_halo(grad_pad, edge_codes, corner_codes):
    device_count = lax.axis_size(("face", "sub"))
    own_index = lax.axis_index(("face", "sub"))
    edge_table = edge_codes.reshape(device_count, 4)
    corner_table = corner_codes.reshape(device_count, 4)
    edge_steps, corner_steps = neighbour_steps()
    interior = grad_pad[:, 1:-1, 1:-1]
    pad_strips = [
        grad_pad[0, 0, 1:-1],
        grad_pad[0, 1:-1, -1],
        grad_pad[0, -1, 1:-1],
        grad_pad[0, 1:-1, 0],
    ]
    pad_cells = [grad_pad[0, 0, 0], grad_pad[0, 0, -1], grad_pad[0, -1, -1], grad_pad[0, -1, 0]]
    slot_ids = jnp.arange(4, dtype=jnp.int32)
    edge_add = jnp.zeros((4,) + pad_strips[0].shape, jnp.float32)
    corner_add = jnp.zeros((4,) + pad_cells[0].shape, jnp.float32)
    for direction in range(4):
        edge_code = edge_table[own_index, direction]
        returned = jnp.where(edge_code >= 4, pad_strips[direction][::-1], pad_strips[direction])
        slots = (slot_ids == edge_code % 4).astype(jnp.float32)
        edge_add = edge_add + back_sets(
            slots[:, None, None] * returned[None], edge_steps[direction]
        )
    for corner in range(4):
        slots = (slot_ids == corner_table[own_index, corner]).astype(jnp.float32)
        corner_add = corner_add + back_sets(
            slots[:, None] * pad_cells[corner][None], corner_steps[corner]
        )
    interior = interior.at[0, 0, :].add(edge_add[0]).at[0, :, -1].add(edge_add[1])
    interior = interior.at[0, -1, :].add(edge_add[2]).at[0, :, 0].add(edge_add[3])
    interior = interior.at[0, 0, 0].add(corner_add[0]).at[0, 0, -1].add(corner_add[1])
    interior = interior.at[0, -1, -1].add(corner_add[2]).at[0, -1, 0].add(corner_add[3])
    return interior


def conv_forward(padded, kernel):
    return lax.conv_general_dilated(
        padded,
        kernel,
        (1, 1),
        "VALID",
        dimension_numbers=("NHWC", "HWIO", "NHWC"),
        preferred_element_type=jnp.float32,
    )


def conv_inputs(upstream, kernel):
    widened = jnp.pad(upstream, ((0, 0), (2, 2), (2, 2), (0, 0)))
    turned = jnp.transpose(jnp.flip(kernel, (0, 1)), (0, 1, 3, 2))
    return lax.conv_general_dilated(
        widened,
        turned,
        (1, 1),
        "VALID",
        dimension_numbers=("NHWC", "HWIO", "NHWC"),
        preferred_element_type=jnp.float32,
    )


def conv_kernel(padded, upstream):
    side_len = upstream.shape[1]
    chans = upstream.shape[-1]
    flat_up = upstream.reshape(-1, chans)
    rows_out = []
    for row_off in range(3):
        cols_out = []
        for col_off in range(3):
            window = padded[
                :, row_off : row_off + side_len, col_off : col_off + side_len, :
            ].reshape(-1, chans)
            cols_out.append(
                lax.dot_general(
                    window, flat_up, (((0,), (0,)), ((), ())), preferred_element_type=jnp.float32
                )
            )
        rows_out.append(jnp.stack(cols_out))
    return jnp.stack(rows_out)


def local(inputs, kernel_one, kernel_two, cotangent, edge_codes, corner_codes):
    fields = inputs[0]
    upstream = cotangent[0]
    side_len = fields.shape[1]
    norm_factor = 1.0 / math.sqrt(lax.axis_size(("face", "sub")) * side_len * side_len)
    padded_one = fill_halo(fields, edge_codes, corner_codes)
    preact = conv_forward(padded_one, kernel_one)
    hidden = jax.nn.silu(preact).astype(jnp.bfloat16)
    padded_two = fill_halo(hidden, edge_codes, corner_codes)
    outputs = conv_forward(padded_two, kernel_two).astype(jnp.bfloat16)
    grad_two = conv_kernel(padded_two, upstream)
    grad_hidden = return_halo(conv_inputs(upstream, kernel_two), edge_codes, corner_codes)
    sigmoid_vals = jax.nn.sigmoid(preact)
    grad_pre = (grad_hidden * sigmoid_vals * (1.0 + preact * (1.0 - sigmoid_vals))).astype(
        jnp.bfloat16
    )
    grad_one = conv_kernel(padded_one, grad_pre)
    grad_fields = return_halo(conv_inputs(grad_pre, kernel_one), edge_codes, corner_codes).astype(
        jnp.bfloat16
    )
    grad_one, grad_two = lax.psum((grad_one, grad_two), ("face", "sub"))
    return (outputs[None], grad_fields[None], grad_one * norm_factor, grad_two * norm_factor)


def solution(mesh):
    in_specs = (
        P("face", "sub", None, None, None),
        P(),
        P(),
        P("face", "sub", None, None, None),
        P(),
        P(),
    )
    out_specs = (P("face", "sub", None, None, None), P("face", "sub", None, None, None), P(), P())
    return jax.shard_map(local, mesh=mesh, in_specs=in_specs, out_specs=out_specs, check_vma=False)
```

profile of v0, /device:TPU:1, one launch (start us, length us, event | category | flops | bytes accessed | tf_op | source)
XLA Modules:
  0.0 515.2 jit_solution(1585408178761811315)
XLA Ops:
  8.0 5.8 %collective-permute-start.7 = (bf16[4,128]{1,0:T(4,128)(2,1)S(1)}, bf16[4,128]{1,0:T(4,128)(2,1)S(1)}, u32[]{:S(2)}, u32[]{:S(2)}) collective-permute-start(bf16[4,128]{1,0:T(4,128)(2,1)S(1)} %pad_maximum_fusion.4), channel_id=1, source_target_pairs={{0,225},{1,226},{2,227},{3,228},{4,229},{5,230},{6,231},{7,232},{8... | collective-permute-start | bytes 3080 | tf_op jit(solution)/shard_map/ppermute | solution.py:13
  14.5 3.1 collective-permute-start.5
  35.8 3.1 convolution_select_fusion.1
  57.3 5.0 collective-permute-start.20
  63.3 5.2 %collective-permute-start.21 = (f32[4,128]{1,0:T(4,128)S(1)}, f32[4,128]{1,0:T(4,128)S(1)}, u32[]{:S(2)}, u32[]{:S(2)}) collective-permute-start(f32[4,128]{1,0:T(4,128)S(1)} %broadcast_multiply_fusion.16), channel_id=1, source_target_pairs={{0,225},{1,226},{2,227},{3,228},{4,229},{5,230},{6,231},{7,232},{8... | collective-permute-start | bytes 6152 | tf_op jit(solution)/shard_map/ppermute | solution.py:13
  68.7 3.9 collective-permute-start.1
  72.9 4.6 collective-permute-start.19
  80.8 3.8 collective-permute-start.16
  99.4 5.0 add_divide_fusion
  111.4 9.5 %collective-permute-start.14 = (bf16[4,128]{1,0:T(4,128)(2,1)}, bf16[4,128]{1,0:T(4,128)(2,1)S(1)}, u32[]{:S(2)}, u32[]{:S(2)}) collective-permute-start(bf16[4,128]{1,0:T(4,128)(2,1)} %pad_maximum_fusion.5), channel_id=1, source_target_pairs={{0,223},{1,224},{2,225},{3,226},{4,227},{5,228},{6,229},{7,230},{8... | collective-permute-start | bytes 3080 | tf_op jit(solution)/shard_map/ppermute | solution.py:13
  124.5 3.2 collective-permute-done.13
  129.4 5.2 %collective-permute-done.12 = bf16[4,128]{1,0:T(4,128)(2,1)S(1)} collective-permute-done((bf16[4,128]{1,0:T(4,128)(2,1)}, bf16[4,128]{1,0:T(4,128)(2,1)S(1)}, u32[]{:S(2)}, u32[]{:S(2)}) %collective-permute-start.12) | collective-permute-done | bytes 1056 | tf_op jit(solution)/shard_map/ppermute | solution.py:13
  134.8 3.4 collective-permute-start.9
  159.1 3.7 fusion.5
  181.6 3.1 convolution_select_fusion
  188.0 3.3 slice.1289
  192.9 3.9 fusion.71
  197.9 2.9 select_convert_fusion
  203.1 4.1 collective-permute-start.31
  207.2 10.5 %collective-permute-start.28 = (f32[4,128]{1,0:T(4,128)S(1)}, f32[4,128]{1,0:T(4,128)S(1)}, u32[]{:S(2)}, u32[]{:S(2)}) collective-permute-start(f32[4,128]{1,0:T(4,128)S(1)} %broadcast_multiply_fusion.13), channel_id=1, source_target_pairs={{0,223},{1,224},{2,225},{3,226},{4,227},{5,228},{6,229},{7,230},{8... | collective-permute-start | bytes 6152 | tf_op jit(solution)/shard_map/ppermute | solution.py:13
  219.3 2.9 copy.152
  241.9 5.1 collective-permute-start.24
  251.3 5.7 %collective-permute-done.25 = f32[4,64,128]{2,1,0:T(8,128)S(1)} collective-permute-done((f32[4,64,128]{2,1,0:T(8,128)S(1)}, f32[4,64,128]{2,1,0:T(8,128)S(1)}, u32[]{:S(2)}, u32[]{:S(2)}) %collective-permute-start.25) | collective-permute-done | bytes 131104 | tf_op jit(solution)/shard_map/ppermute | solution.py:13
  263.6 240.7 %all-reduce.5.cloned.1.call-done = (f32[3,3,128,128]{3,2,1,0:T(8,128)}, f32[3,3,128,128]{3,2,1,0:T(8,128)}) async-done(((f32[3,3,128,128]{3,2,1,0:T(8,128)}, f32[3,3,128,128]{3,2,1,0:T(8,128)}), (f32[3,3,128,128]{3,2,1,0:T(8,128)}, f32[3,3,128,128]{3,2,1,0:T(8,128)})) %all-reduce.5.cloned.1.call-update) | async-done | bytes 1179664 | tf_op jit(solution)/shard_map/psum | solution.py:164
  (370 shorter events, 135.1 us)
Async XLA Ops:
  7.2 497.1 %all-reduce.5.cloned.1.call-start = ((), (), s32[]{:S(2)}) async-start(), calls=%async_computation | async-start | bytes 2359296 | tf_op jit(solution)/shard_map/psum | solution.py:164
  8.0 49.3 %collective-permute-start.7 = (bf16[4,128]{1,0:T(4,128)(2,1)S(1)}, bf16[4,128]{1,0:T(4,128)(2,1)S(1)}, u32[]{:S(2)}, u32[]{:S(2)}) collective-permute-start(bf16[4,128]{1,0:T(4,128)(2,1)S(1)} %pad_maximum_fusion.4), channel_id=1, source_target_pairs={{0,225},{1,226},{2,227},{3,228},{4,229},{5,230},{6,231},{7,232},{8... | collective-permute-start | bytes 3080 | tf_op jit(solution)/shard_map/ppermute | solution.py:13
  13.9 48.5 %collective-permute-start.6 = (bf16[4,128]{1,0:T(4,128)(2,1)S(1)}, bf16[4,128]{1,0:T(4,128)(2,1)S(1)}, u32[]{:S(2)}, u32[]{:S(2)}) collective-permute-start(bf16[4,128]{1,0:T(4,128)(2,1)S(1)} %pad_maximum_fusion.4), channel_id=1, source_target_pairs={{0,223},{1,224},{2,225},{3,226},{4,227},{5,228},{6,229},{7,230},{8... | collective-permute-start | bytes 3080 | tf_op jit(solution)/shard_map/ppermute | solution.py:13
  14.5 47.9 %collective-permute-start.5 = (bf16[4,128]{1,0:T(4,128)(2,1)S(1)}, bf16[4,128]{1,0:T(4,128)(2,1)S(1)}, u32[]{:S(2)}, u32[]{:S(2)}) collective-permute-start(bf16[4,128]{1,0:T(4,128)(2,1)S(1)} %pad_maximum_fusion.4), channel_id=1, source_target_pairs={{0,31},{1,32},{2,33},{3,34},{4,35},{5,36},{6,37},{7,38},{8,39},{9,... | collective-permute-start | bytes 3080 | tf_op jit(solution)/shard_map/ppermute | solution.py:13
  17.7 45.6 %collective-permute-start.4 = (bf16[4,128]{1,0:T(4,128)(2,1)S(1)}, bf16[4,128]{1,0:T(4,128)(2,1)S(1)}, u32[]{:S(2)}, u32[]{:S(2)}) collective-permute-start(bf16[4,128]{1,0:T(4,128)(2,1)S(1)} %pad_maximum_fusion.4), channel_id=1, source_target_pairs={{0,33},{1,34},{2,35},{3,36},{4,37},{5,38},{6,39},{7,40},{8,41},{9,... | collective-permute-start | bytes 3080 | tf_op jit(solution)/shard_map/ppermute | solution.py:13
  19.5 65.1 %collective-permute-start.3 = (bf16[4,64,128]{2,1,0:T(8,128)(2,1)S(1)}, bf16[4,64,128]{2,1,0:T(8,128)(2,1)}, u32[]{:S(2)}, u32[]{:S(2)}) collective-permute-start(bf16[4,64,128]{2,1,0:T(8,128)(2,1)S(1)} %pad_maximum_fusion.2), channel_id=1, source_target_pairs={{0,1},{1,2},{2,3},{3,4},{4,5},{5,6},{6,7},{7,8},{8,9},{9,10},{10,1... | collective-permute-start | bytes 196616 | tf_op jit(solution)/shard_map/ppermute | solution.py:13
  57.3 11.1 %collective-permute-start.20 = (f32[4,128]{1,0:T(4,128)S(1)}, f32[4,128]{1,0:T(4,128)S(1)}, u32[]{:S(2)}, u32[]{:S(2)}) collective-permute-start(f32[4,128]{1,0:T(4,128)S(1)} %broadcast_multiply_fusion.17), channel_id=1, source_target_pairs={{0,223},{1,224},{2,225},{3,226},{4,227},{5,228},{6,229},{7,230},{8... | collective-permute-start | bytes 6152 | tf_op jit(solution)/shard_map/ppermute | solution.py:13
  62.4 10.1 %collective-permute-start.23 = (f32[4,128]{1,0:T(4,128)S(1)}, f32[4,128]{1,0:T(4,128)S(1)}, u32[]{:S(2)}, u32[]{:S(2)}) collective-permute-start(f32[4,128]{1,0:T(4,128)S(1)} %broadcast_multiply_fusion.14), channel_id=1, source_target_pairs={{0,31},{1,32},{2,33},{3,34},{4,35},{5,36},{6,37},{7,38},{8,39},{9,... | collective-permute-start | bytes 6152 | tf_op jit(solution)/shard_map/ppermute | solution.py:13
  68.4 12.4 %collective-permute-start.2 = (bf16[4,64,128]{2,1,0:T(8,128)(2,1)S(1)}, bf16[4,64,128]{2,1,0:T(8,128)(2,1)S(1)}, u32[]{:S(2)}, u32[]{:S(2)}) collective-permute-start(bf16[4,64,128]{2,1,0:T(8,128)(2,1)S(1)} %pad_maximum_fusion.2), channel_id=1, source_target_pairs={{0,224},{1,225},{2,226},{3,227},{4,228},{5,229},{6,230},{7,231},{8... | collective-permute-start | bytes 196616 | tf_op jit(solution)/shard_map/ppermute | solution.py:13
  72.9 61.8 %collective-permute-start.19 = (f32[4,64,128]{2,1,0:T(8,128)}, f32[4,64,128]{2,1,0:T(8,128)S(1)}, u32[]{:S(2)}, u32[]{:S(2)}) collective-permute-start(f32[4,64,128]{2,1,0:T(8,128)} %broadcast_multiply_fusion.6), channel_id=1, source_target_pairs={{0,255},{1,0},{2,1},{3,2},{4,3},{5,4},{6,5},{7,6},{8,7},{9,8},{10,... | collective-permute-start | bytes 393224 | tf_op jit(solution)/shard_map/ppermute | solution.py:13
  78.0 56.7 %collective-permute-start.17 = (f32[4,64,128]{2,1,0:T(8,128)S(1)}, f32[4,64,128]{2,1,0:T(8,128)S(1)}, u32[]{:S(2)}, u32[]{:S(2)}) collective-permute-start(f32[4,64,128]{2,1,0:T(8,128)S(1)} %broadcast_multiply_fusion.8), channel_id=1, source_target_pairs={{0,1},{1,2},{2,3},{3,4},{4,5},{5,6},{6,7},{7,8},{8,9},{9,10},{10,1... | collective-permute-start | bytes 393224 | tf_op jit(solution)/shard_map/ppermute | solution.py:13
  79.3 58.8 %collective-permute-start.18 = (f32[4,64,128]{2,1,0:T(8,128)S(1)}, f32[4,64,128]{2,1,0:T(8,128)S(1)}, u32[]{:S(2)}, u32[]{:S(2)}) collective-permute-start(f32[4,64,128]{2,1,0:T(8,128)S(1)} %broadcast_multiply_fusion.7), channel_id=1, source_target_pairs={{0,32},{1,33},{2,34},{3,35},{4,36},{5,37},{6,38},{7,39},{8,40},{9,... | collective-permute-start | bytes 393224 | tf_op jit(solution)/shard_map/ppermute | solution.py:13
  80.8 59.7 %collective-permute-start.16 = (f32[4,64,128]{2,1,0:T(8,128)S(1)}, f32[4,64,128]{2,1,0:T(8,128)S(1)}, u32[]{:S(2)}, u32[]{:S(2)}) collective-permute-start(f32[4,64,128]{2,1,0:T(8,128)S(1)} %broadcast_multiply_fusion.9), channel_id=1, source_target_pairs={{0,224},{1,225},{2,226},{3,227},{4,228},{5,229},{6,230},{7,231},{8... | collective-permute-start | bytes 393224 | tf_op jit(solution)/shard_map/ppermute | solution.py:13
  111.4 10.4 %collective-permute-start.14 = (bf16[4,128]{1,0:T(4,128)(2,1)}, bf16[4,128]{1,0:T(4,128)(2,1)S(1)}, u32[]{:S(2)}, u32[]{:S(2)}) collective-permute-start(bf16[4,128]{1,0:T(4,128)(2,1)} %pad_maximum_fusion.5), channel_id=1, source_target_pairs={{0,223},{1,224},{2,225},{3,226},{4,227},{5,228},{6,229},{7,230},{8... | collective-permute-start | bytes 3080 | tf_op jit(solution)/shard_map/ppermute | solution.py:13
  134.7 56.7 %collective-permute-start.11 = (bf16[4,64,128]{2,1,0:T(8,128)(2,1)S(1)}, bf16[4,64,128]{2,1,0:T(8,128)(2,1)S(1)}, u32[]{:S(2)}, u32[]{:S(2)}) collective-permute-start(bf16[4,64,128]{2,1,0:T(8,128)(2,1)S(1)} %pad_maximum_fusion.3), channel_id=1, source_target_pairs={{0,1},{1,2},{2,3},{3,4},{4,5},{5,6},{6,7},{7,8},{8,9},{9,10},{10,1... | collective-permute-start | bytes 196616 | tf_op jit(solution)/shard_map/ppermute | solution.py:13
  134.7 52.6 %collective-permute-start.10 = (bf16[4,64,128]{2,1,0:T(8,128)(2,1)S(1)}, bf16[4,64,128]{2,1,0:T(8,128)(2,1)S(1)}, u32[]{:S(2)}, u32[]{:S(2)}) collective-permute-start(bf16[4,64,128]{2,1,0:T(8,128)(2,1)S(1)} %pad_maximum_fusion.3), channel_id=1, source_target_pairs={{0,224},{1,225},{2,226},{3,227},{4,228},{5,229},{6,230},{7,231},{8... | collective-permute-start | bytes 196616 | tf_op jit(solution)/shard_map/ppermute | solution.py:13
  134.8 56.6 %collective-permute-start.9 = (bf16[4,64,128]{2,1,0:T(8,128)(2,1)S(1)}, bf16[4,64,128]{2,1,0:T(8,128)(2,1)S(1)}, u32[]{:S(2)}, u32[]{:S(2)}) collective-permute-start(bf16[4,64,128]{2,1,0:T(8,128)(2,1)S(1)} %pad_maximum_fusion.3), channel_id=1, source_target_pairs={{0,255},{1,0},{2,1},{3,2},{4,3},{5,4},{6,5},{7,6},{8,7},{9,8},{10,... | collective-permute-start | bytes 196616 | tf_op jit(solution)/shard_map/ppermute | solution.py:13
  138.1 53.3 %collective-permute-start.8 = (bf16[4,64,128]{2,1,0:T(8,128)(2,1)S(1)}, bf16[4,64,128]{2,1,0:T(8,128)(2,1)S(1)}, u32[]{:S(2)}, u32[]{:S(2)}) collective-permute-start(bf16[4,64,128]{2,1,0:T(8,128)(2,1)S(1)} %pad_maximum_fusion.3), channel_id=1, source_target_pairs={{0,32},{1,33},{2,34},{3,35},{4,36},{5,37},{6,38},{7,39},{8,40},{9,... | collective-permute-start | bytes 196616 | tf_op jit(solution)/shard_map/ppermute | solution.py:13
  203.1 38.7 %collective-permute-start.31 = (f32[4,128]{1,0:T(4,128)S(1)}, f32[4,128]{1,0:T(4,128)S(1)}, u32[]{:S(2)}, u32[]{:S(2)}) collective-permute-start(f32[4,128]{1,0:T(4,128)S(1)} %broadcast_multiply_fusion.10), channel_id=1, source_target_pairs={{0,31},{1,32},{2,33},{3,34},{4,35},{5,36},{6,37},{7,38},{8,39},{9,... | collective-permute-start | bytes 6152 | tf_op jit(solution)/shard_map/ppermute | solution.py:13
  207.2 39.8 %collective-permute-start.30 = (f32[4,128]{1,0:T(4,128)S(1)}, f32[4,128]{1,0:T(4,128)S(1)}, u32[]{:S(2)}, u32[]{:S(2)}) collective-permute-start(f32[4,128]{1,0:T(4,128)S(1)} %broadcast_multiply_fusion.11), channel_id=1, source_target_pairs={{0,33},{1,34},{2,35},{3,36},{4,37},{5,38},{6,39},{7,40},{8,41},{9,... | collective-permute-start | bytes 6152 | tf_op jit(solution)/shard_map/ppermute | solution.py:13
  207.2 40.0 %collective-permute-start.28 = (f32[4,128]{1,0:T(4,128)S(1)}, f32[4,128]{1,0:T(4,128)S(1)}, u32[]{:S(2)}, u32[]{:S(2)}) collective-permute-start(f32[4,128]{1,0:T(4,128)S(1)} %broadcast_multiply_fusion.13), channel_id=1, source_target_pairs={{0,223},{1,224},{2,225},{3,226},{4,227},{5,228},{6,229},{7,230},{8... | collective-permute-start | bytes 6152 | tf_op jit(solution)/shard_map/ppermute | solution.py:13
  217.7 30.9 %collective-permute-start.29 = (f32[4,128]{1,0:T(4,128)S(1)}, f32[4,128]{1,0:T(4,128)S(1)}, u32[]{:S(2)}, u32[]{:S(2)}) collective-permute-start(f32[4,128]{1,0:T(4,128)S(1)} %broadcast_multiply_fusion.12), channel_id=1, source_target_pairs={{0,225},{1,226},{2,227},{3,228},{4,229},{5,230},{6,231},{7,232},{8... | collective-permute-start | bytes 6152 | tf_op jit(solution)/shard_map/ppermute | solution.py:13
  224.6 24.1 %collective-permute-start.26 = (f32[4,64,128]{2,1,0:T(8,128)}, f32[4,64,128]{2,1,0:T(8,128)}, u32[]{:S(2)}, u32[]{:S(2)}) collective-permute-start(f32[4,64,128]{2,1,0:T(8,128)} %broadcast_multiply_fusion.3), channel_id=1, source_target_pairs={{0,32},{1,33},{2,34},{3,35},{4,36},{5,37},{6,38},{7,39},{8,40},{9,... | collective-permute-start | bytes 393224 | tf_op jit(solution)/shard_map/ppermute | solution.py:13
  247.2 9.8 %collective-permute-start.25 = (f32[4,64,128]{2,1,0:T(8,128)S(1)}, f32[4,64,128]{2,1,0:T(8,128)S(1)}, u32[]{:S(2)}, u32[]{:S(2)}) collective-permute-start(f32[4,64,128]{2,1,0:T(8,128)S(1)} %copy-done.17), channel_id=1, source_target_pairs={{0,1},{1,2},{2,3},{3,4},{4,5},{5,6},{6,7},{7,8},{8,9},{9,10},{10,1... | collective-permute-start | bytes 393224 | tf_op jit(solution)/shard_map/ppermute | solution.py:13
  (57 other events, 566.1 us)
Sparse Core Ops, SparseCore 0:
  242.0 262.2 all-reduce.4
where the time goes:
time: 523 us; the launch traced here: 515 us
  waiting for transfers between devices  259 us (50%)
  starting transfers between devices  76.8 us (15%)
  local copies, waits for them, and re-layouts  75.8 us (14%)
  matrix products  36.3 us (7%)
  other arithmetic  33.6 us (6%)
  between operations  33.4 us (6%)
    psum x1, waiting for transfers between devices, local(): grad_one, grad_two = lax.psum((grad_one, grad_two), ('face', 'sub'))  241 us
    ppermute x32, starting transfers between devices, shifted(): return lax.ppermute(x, axis, [(i, (i + by) % size) for i in range(size)])  76.8 us
    dot_general x18, matrix products, conv_kernel(): lax.dot_general(window, flat_up, (((0,), (0,)), ((), ())), preferred_elem...  22.1 us
    unnamed x104, local copies, waits for them, and re-layouts  20.4 us
    ppermute x32, waiting for transfers between devices, shifted(): return lax.ppermute(x, axis, [(i, (i + by) % size) for i in range(size)])  18.6 us
  transfers between devices with their start and end apart: 33, of which 9 were waited for; matrix products, arithmetic and copies ran while one was open for 24% of the time, Pallas kernels for 0%

commit v1 on v0

v1 whole, which is shorter than its diff:
```python
import math

import jax
import jax.numpy as jnp
from jax import lax
from jax.experimental import pallas as pl
from jax.experimental.pallas import tpu as pltpu
from jax.sharding import PartitionSpec as P

AXES = ("face", "sub")
GRID_ROWS = 8
SIDE = 64
CH = 128
HALF = SIDE // 2
STRIPS = 2 * SIDE
VROWS = STRIPS + 32
BF16 = jnp.bfloat16
F32 = jnp.float32
N, E, S, W = 0, 1, 2, 3
NW, NE, SE, SW = 0, 1, 2, 3
VMEM = pl.BlockSpec(memory_space=pltpu.VMEM)
SMEM = pl.BlockSpec(memory_space=pltpu.SMEM)
PARAMS = pltpu.CompilerParams(vmem_limit_bytes=50 * 1024 * 1024)


def iota(shape, dim):
    return lax.broadcasted_iota(jnp.int32, shape, dim)


def side_strips(block, dst):
    dst[N] = block[0, 0].astype(F32)
    dst[S] = block[HALF - 1, 1].astype(F32)
    low = block[:, :, 0:16, :].reshape(SIDE, 16, CH).astype(F32)
    dst[W] = jnp.sum(jnp.where(iota(low.shape, 1) == 0, low, 0.0), axis=1)
    high = block[:, :, SIDE - 16 : SIDE, :].reshape(SIDE, 16, CH).astype(F32)
    dst[E] = jnp.sum(jnp.where(iota(high.shape, 1) == 15, high, 0.0), axis=1)


def corner_rows(strips):
    north = strips[N]
    south = strips[S]
    last = SIDE - 1
    return [north[0:1], north[last : last + 1], south[last : last + 1], south[0:1]]


def turned(strip, flip):
    row = iota((SIDE, SIDE), 0)
    col = iota((SIDE, SIDE), 1)
    target = jnp.where(flip, SIDE - 1 - row, row)
    matrix = jnp.where(col == target, 1.0, 0.0).astype(BF16)
    return jnp.dot(matrix, strip.astype(BF16), preferred_element_type=F32).astype(BF16)


def corner_block(code, own, other):
    picked = jnp.where(code == 0, own[0], jnp.where(code == 1, own[1], jnp.where(code == 2, own[2], own[3])))
    row = iota((16, CH), 0)
    return (jnp.where(row == 0, picked, 0.0) + jnp.where(row == 1, other, 0.0)).astype(BF16)


def pack(me, edge, corner, count, width, fore, back, vp, vm, hp, hm):
    fore_corners = corner_rows(fore)
    back_corners = corner_rows(back)

    def block(offset):
        return lax.rem(me + offset + 2 * count, count)

    def strips(dst, offset, read_side, own_side):
        code = edge[block(offset) * 4 + read_side]
        dst[0:SIDE] = turned(fore[lax.rem(code, 4)], code >= 4)
        dst[SIDE:STRIPS] = turned(back[own_side], edge[me * 4 + own_side] >= 4)

    def relayed(offset, read_corner, own_corner):
        return corner_block(
            corner[block(offset) * 4 + read_corner], fore_corners, back_corners[own_corner]
        )

    strips(vp, width, N, S)
    vp[STRIPS : STRIPS + 16] = relayed(width + 1, NW, SE)
    vp[STRIPS + 16 : VROWS] = relayed(width - 1, NE, SW)
    strips(vm, -width, S, N)
    vm[STRIPS : STRIPS + 16] = relayed(-width + 1, SW, NE)
    vm[STRIPS + 16 : VROWS] = relayed(-width - 1, SE, NW)
    strips(hp, 1, W, E)
    strips(hm, -1, E, W)


def put_row(dst, pair, part, row, west, east):
    col = iota((SIDE, CH), 0)
    wide = row.astype(F32)
    dst[1, pair, part] = row.astype(BF16)
    dst[0, pair, part] = jnp.where(col == 0, west, pltpu.roll(wide, 1, 0)).astype(BF16)
    dst[2, pair, part] = jnp.where(col == SIDE - 1, east, pltpu.roll(wide, SIDE - 1, 0)).astype(BF16)


def shift_copies(dst, src, west=None, east=None):
    def step(k, _):
        for part in range(2):
            i = 2 * k + part
            w = 0.0 if west is None else west[pl.ds(i, 1), :]
            e = 0.0 if east is None else east[pl.ds(i, 1), :]
            put_row(dst, k + part, 1 - part, src[k, part], w, e)
        return 0

    lax.fori_loop(0, HALF, step, 0, unroll=4)


def halo_copies(dst, src, west, east, vp, vm, hp, hm):
    west[...] = hp[0:SIDE].astype(F32)
    east[...] = hm[0:SIDE].astype(F32)
    shift_copies(dst, src, west, east)
    hp1 = hp[STRIPS : STRIPS + 16].astype(F32)
    hp2 = hp[STRIPS + 16 : VROWS].astype(F32)
    hm1 = hm[STRIPS : STRIPS + 16].astype(F32)
    hm2 = hm[STRIPS + 16 : VROWS].astype(F32)
    put_row(dst, 0, 0, vp[0:SIDE], hp1[0:1], hm1[0:1])
    put_row(dst, HALF, 1, vm[0:SIDE], hp2[0:1], hm2[0:1])


def zero_copies(dst, src):
    zero = jnp.zeros((SIDE, CH), BF16)
    for b in range(3):
        dst[b, 0, 0] = zero
        dst[b, HALF, 1] = zero
    shift_copies(dst, src)


def window(copies, m, mb):
    parts = [
        copies[b, pl.ds(m + a // 2, mb), a % 2].reshape(mb * SIDE, CH)
        for a in range(4)
        for b in range(3)
    ]
    return jnp.concatenate(parts, axis=1)


def conv_pairs(copies, weights, m, mb):
    return jnp.dot(window(copies, m, mb), weights[...], preferred_element_type=F32)


def edge_tap(side, k):
    return {N: (0, k), S: (2, k), W: (k, 0), E: (k, 2)}[side]


CORNER_TAP = {NW: (0, 0), NE: (0, 2), SE: (2, 2), SW: (2, 0)}


def tap_transposed(turned_weights, a, b):
    at = ((2 - a) * 3 + 2 - b) * CH
    return turned_weights[at : at + CH, 0:CH]


def returned(me, edge, corner, count, width, turned_weights, vp, vm, hp, hm, adds, pieces=None, corners=None):
    def block(offset):
        return lax.rem(me + offset + 2 * count, count)

    adds[...] = jnp.zeros_like(adds)
    row = iota((SIDE, CH), 0)
    for side, offset, message in ((N, width, vm), (E, -1, hp), (S, -width, vp), (W, 1, hm)):
        code = edge[block(offset) * 4 + side]
        flip = code >= 4
        strip = message[SIDE:STRIPS].astype(F32)
        up = jnp.where(row == SIDE - 1, 0.0, pltpu.roll(strip, SIDE - 1, 0))
        down = jnp.where(row == 0, 0.0, pltpu.roll(strip, 1, 0))
        joined = jnp.concatenate(
            [jnp.where(flip, down, up), strip, jnp.where(flip, up, down)], axis=1
        ).astype(BF16)
        if pieces is not None:
            pieces[side] = joined
        taps = jnp.concatenate(
            [tap_transposed(turned_weights, *edge_tap(side, k)) for k in range(3)], axis=0
        )
        at = lax.rem(code, 4)
        adds[at] = adds[at] + jnp.dot(joined, taps, preferred_element_type=F32)
    for q, offset, message, start in (
        (NW, width + 1, hm, STRIPS + 16),
        (NE, width - 1, hp, STRIPS + 16),
        (SE, -width - 1, hp, STRIPS),
        (SW, -width + 1, hm, STRIPS),
    ):
        code = corner[block(offset) * 4 + q]
        cells = message[start : start + 16]
        if corners is not None:
            corners[q] = cells
        given = jnp.dot(
            cells, tap_transposed(turned_weights, *CORNER_TAP[q]), preferred_element_type=F32
        )[1:2]
        first = jnp.where(row == 0, given, 0.0)
        last = jnp.where(row == SIDE - 1, given, 0.0)
        adds[N] = adds[N] + jnp.where(code == NW, first, 0.0) + jnp.where(code == NE, last, 0.0)
        adds[S] = adds[S] + jnp.where(code == SW, first, 0.0) + jnp.where(code == SE, last, 0.0)


def with_adds(rows, i, adds, at_first, at_last):
    col = iota((SIDE, CH), 0)
    rows = rows + jnp.where(col == SIDE - 1, adds[E, pl.ds(i, 1), :], 0.0)
    rows = rows + jnp.where(col == 0, adds[W, pl.ds(i, 1), :], 0.0)
    if at_first is not None:
        rows = rows + jnp.where(at_first, adds[N], 0.0)
    if at_last is not None:
        rows = rows + jnp.where(at_last, adds[S], 0.0)
    return rows


def pack_kernel(count, width, me, edge, corner, fields, upstream, vp, vm, hp, hm, fore, back):
    side_strips(fields, fore)
    side_strips(upstream, back)
    pack(me[0], edge, corner, count, width, fore, back, vp, vm, hp, hm)


def prepare_kernel(kernel_one, kernel_two, upstream, fwd_one, fwd_two, in_one, in_two, up_copies):
    zero = jnp.zeros((CH, CH), BF16)
    for source, plain, back in ((kernel_one, fwd_one, in_one), (kernel_two, fwd_two, in_two)):
        for b in range(3):
            for a in range(4):
                at = (a * 3 + b) * CH
                if a < 3:
                    block = source[a, b]
                    plain[at : at + CH, 0:CH] = block
                    plain[at + 3 * CH : at + 4 * CH, CH : 2 * CH] = block
                    swapped = source[2 - a, 2 - b].astype(F32).T.astype(BF16)
                    back[at : at + CH, 0:CH] = swapped
                    back[at + 3 * CH : at + 4 * CH, CH : 2 * CH] = swapped
                else:
                    plain[at : at + CH, 0:CH] = zero
                    back[at : at + CH, 0:CH] = zero
            plain[b * CH : (b + 1) * CH, CH : 2 * CH] = zero
            back[b * CH : (b + 1) * CH, CH : 2 * CH] = zero
    zero_copies(up_copies, upstream)


def middle_kernel(
    count, width, scale, me, edge, corner, fields, vp, vm, hp, hm, fwd_one, in_two, up_copies,
    hidden, grad_pre, vp2, vm2, hp2, hm2, sums,
    copies, west, east, adds, pieces, corners, fore, back, acc,
):
    where_am_i = me[0]
    returned(where_am_i, edge, corner, count, width, in_two, vp, vm, hp, hm, adds, pieces, corners)
    halo_copies(copies, fields, west, east, vp, vm, hp, hm)
    mb = 4
    steps = HALF // mb

    def step(n, _):
        m = n * mb
        pre = conv_pairs(copies, fwd_one, m, mb)
        grad = conv_pairs(up_copies, in_two, m, mb)
        for k in range(mb):
            for part in range(2):
                rows = slice(k * SIDE, (k + 1) * SIDE)
                lanes = slice(part * CH, (part + 1) * CH)
                p = pre[rows, lanes]
                g = with_adds(
                    grad[rows, lanes], 2 * (m + k) + part, adds,
                    n == 0 if k == 0 and part == 0 else None,
                    n == steps - 1 if k == mb - 1 and part == 1 else None,
                )
                s = 1.0 / (1.0 + jnp.exp(-p))
                hidden[m + k, part] = (p * s).astype(BF16)
                grad_pre[m + k, part] = (g * s * (1.0 + p * (1.0 - s))).astype(BF16)
        return 0

    lax.fori_loop(0, steps, step, 0)
    side_strips(hidden, fore)
    side_strips(grad_pre, back)
    pack(where_am_i, edge, corner, count, width, fore, back, vp2, vm2, hp2, hm2)

    gb = 8
    first = (((0,), (0,)), ((), ()))

    def gather(values, shifted):
        def grad_step(n, _):
            m = n * gb
            left = jnp.concatenate(
                [values[pl.ds(m, gb), part].reshape(gb * SIDE, CH) for part in range(2)], axis=1
            )
            acc[...] += lax.dot_general(left, window(shifted, m, gb), first, preferred_element_type=F32)
            return 0

        acc[...] = jnp.zeros_like(acc)
        lax.fori_loop(0, HALF // gb, grad_step, 0)

    def from_acc(a, b):
        low = (a * 3 + b) * CH
        high = low + 3 * CH
        return acc[0:CH, low : low + CH] + acc[CH : 2 * CH, high : high + CH]

    gather(grad_pre, copies)
    for a in range(3):
        for b in range(3):
            at = (a * 3 + b) * CH
            sums[at : at + CH] = from_acc(a, b).T * scale
    gather(hidden, up_copies)
    for a in range(3):
        for b in range(3):
            at = (9 + a * 3 + b) * CH
            sums[at : at + CH] = from_acc(2 - a, 2 - b) * scale

    def block(offset):
        return lax.rem(where_am_i + offset + 2 * count, count)

    for side, offset in ((N, width), (E, -1), (S, -width), (W, 1)):
        code = lax.rem(edge[block(offset) * 4 + side], 4)
        term = lax.dot_general(fore[code].astype(BF16), pieces[side], first, preferred_element_type=F32)
        for k in range(3):
            a, b = edge_tap(side, k)
            at = (9 + a * 3 + b) * CH
            sums[at : at + CH] = sums[at : at + CH] + term[:, k * CH : (k + 1) * CH] * scale
    own = corner_rows(fore)
    row = iota((16, CH), 0)
    for q, offset in ((NW, width + 1), (NE, width - 1), (SE, -width - 1), (SW, -width + 1)):
        code = corner[block(offset) * 4 + q]
        cell = jnp.where(code == 0, own[0], jnp.where(code == 1, own[1], jnp.where(code == 2, own[2], own[3])))
        left = jnp.where(row == 1, cell, 0.0).astype(BF16)
        a, b = CORNER_TAP[q]
        at = (9 + a * 3 + b) * CH
        term = lax.dot_general(left, corners[q], first, preferred_element_type=F32)
        sums[at : at + CH] = sums[at : at + CH] + term * scale


def last_kernel(
    count, width, me, edge, corner, hidden, grad_pre, vp, vm, hp, hm, fwd_two, in_one,
    outputs, grad_fields, copies, west, east, adds,
):
    mb = 4
    steps = HALF // mb
    halo_copies(copies, hidden, west, east, vp, vm, hp, hm)

    def out_step(n, _):
        m = n * mb
        got = conv_pairs(copies, fwd_two, m, mb)
        for part in range(2):
            lanes = slice(part * CH, (part + 1) * CH)
            outputs[pl.ds(m, mb), part] = got[:, lanes].reshape(mb, SIDE, CH).astype(BF16)
        return 0

    lax.fori_loop(0, steps, out_step, 0)
    returned(me[0], edge, corner, count, width, in_one, vp, vm, hp, hm, adds)
    zero_copies(copies, grad_pre)

    def grad_step(n, _):
        m = n * mb
        got = conv_pairs(copies, in_one, m, mb)
        for k in range(mb):
            for part in range(2):
                g = with_adds(
                    got[k * SIDE : (k + 1) * SIDE, part * CH : (part + 1) * CH],
                    2 * (m + k) + part, adds,
                    n == 0 if k == 0 and part == 0 else None,
                    n == steps - 1 if k == mb - 1 and part == 1 else None,
                )
                grad_fields[m + k, part] = g.astype(BF16)
        return 0

    lax.fori_loop(0, steps, grad_step, 0)


def struct(shape, dtype=BF16):
    return jax.ShapeDtypeStruct(shape, dtype)


BLOCK = (HALF, 2, SIDE, CH)
COPIES = (3, HALF + 1, 2, SIDE, CH)
WEIGHTS = (12 * CH, 2 * CH)


def call(body, tables, arrays, outs, scratch, flops=0, moved=4 << 20):
    return pl.pallas_call(
        body,
        out_shape=outs,
        in_specs=[SMEM] * tables + [VMEM] * arrays,
        out_specs=tuple(VMEM for _ in outs),
        scratch_shapes=scratch,
        compiler_params=PARAMS,
        cost_estimate=pl.CostEstimate(flops=flops, bytes_accessed=moved, transcendentals=0),
    )


def shifted(x, by):
    size = lax.axis_size(AXES)
    return lax.ppermute(x, AXES, [(i, (i + by) % size) for i in range(size)])


def swap(x, bit):
    size = lax.axis_size(AXES)
    return lax.ppermute(x, AXES, [(i, i ^ bit) for i in range(size)])


def exchange(vp, vm, hp, hm, width):
    vp = shifted(vp, width)
    vm = shifted(vm, -width)
    hp = jnp.concatenate([hp, vp[STRIPS : STRIPS + 16], vm[STRIPS : STRIPS + 16]])
    hm = jnp.concatenate([hm, vp[STRIPS + 16 : VROWS], vm[STRIPS + 16 : VROWS]])
    return vp, vm, shifted(hp, 1), shifted(hm, -1)


HALVED = (2, 1, 4, 64)
WHOLE = (32, 128, 8, 16)


def total(x):
    me = lax.axis_index(AXES)
    rows = x.shape[0]
    for bit in HALVED:
        rows //= 2
        high = (me // bit) % 2
        send = lax.dynamic_slice_in_dim(x, (1 - high) * rows, rows, 0)
        keep = lax.dynamic_slice_in_dim(x, high * rows, rows, 0)
        x = keep + swap(send, bit)
    for bit in WHOLE:
        x = x + swap(x, bit)
    for bit in reversed(HALVED):
        high = (me // bit) % 2
        other = swap(x, bit)
        x = jnp.where(high == 1, jnp.concatenate([other, x]), jnp.concatenate([x, other]))
    return x


def local(inputs, kernel_one, kernel_two, cotangent, edge_codes, corner_codes):
    count = lax.axis_size(AXES)
    width = lax.axis_size("face") // GRID_ROWS * lax.axis_size("sub")
    scale = 1.0 / math.sqrt(count * SIDE * SIDE)
    me = lax.axis_index(AXES).astype(jnp.int32).reshape(1)
    edge = edge_codes.reshape(-1)
    corner = corner_codes.reshape(-1)
    tables = (me, edge, corner)
    fields = inputs.reshape(BLOCK)
    upstream = cotangent.reshape(BLOCK)
    message = struct((VROWS, CH))
    own = struct((STRIPS, CH))
    strips = pltpu.VMEM((4, SIDE, CH), F32)
    column = pltpu.VMEM((SIDE, CH), F32)
    conv_flops = 2 * SIDE * SIDE * 9 * CH * CH

    sent = call(
        lambda *refs: pack_kernel(count, width, *refs), 3, 2, (message, message, own, own), [strips, strips],
    )(*tables, fields, upstream)
    weights = struct(WEIGHTS)
    fwd_one, fwd_two, in_one, in_two, up_copies = call(
        prepare_kernel, 0, 3, (weights, weights, weights, weights, struct(COPIES)), [], conv_flops,
    )(kernel_one, kernel_two, upstream)
    arrived = exchange(*sent, width)
    hidden, grad_pre, vp2, vm2, hp2, hm2, sums = call(
        lambda *refs: middle_kernel(count, width, scale, *refs), 3, 8,
        (struct(BLOCK), struct(BLOCK), message, message, own, own, struct((18 * CH, CH), F32)),
        [
            pltpu.VMEM(COPIES, BF16), column, column, strips,
            pltpu.VMEM((4, SIDE, 3 * CH), BF16), pltpu.VMEM((4, 16, CH), BF16), strips, strips,
            pltpu.VMEM((2 * CH, 12 * CH), F32),
        ],
        4 * conv_flops,
    )(*tables, fields, *arrived, fwd_one, in_two, up_copies)
    arrived = exchange(vp2, vm2, hp2, hm2, width)
    outputs, grad_fields = call(
        lambda *refs: last_kernel(count, width, *refs), 3, 8, (struct(BLOCK), struct(BLOCK)),
        [pltpu.VMEM(COPIES, BF16), column, column, strips],
        2 * conv_flops,
    )(*tables, hidden, grad_pre, *arrived, fwd_two, in_one)
    sums = total(sums)
    shape = (1, 1, SIDE, SIDE, CH)
    grads = sums.reshape(2, 3, 3, CH, CH)
    return outputs.reshape(shape), grad_fields.reshape(shape), grads[0], grads[1]


def solution(mesh):
    block = P("face", "sub", None, None, None)
    return jax.shard_map(
        local,
        mesh=mesh,
        in_specs=(block, P(), P(), block, P(), P()),
        out_specs=(block, block, P(), P()),
        check_vma=False,
    )
```

time: 523 us -> 140 us (0.27); the launches traced: 515 us -> 138 us
  waiting for transfers between devices: 259 us -> 54.2 us
  local copies, waits for them, and re-layouts: 75.8 us -> 12.1 us
  starting transfers between devices: 76.8 us -> 37.7 us
  matrix products: 36.3 us -> 0 us
  between operations: 33.4 us -> 0.95 us
  other arithmetic: 33.6 us -> 3.61 us
  Pallas kernels: 0 us -> 29.1 us
    psum x1 -> x0, waiting for transfers between devices: 241 us -> none  [local(): grad_one, grad_two = lax.psum((grad_one, grad_two), ('face', 'sub'))]
    ppermute x32 -> x20, starting transfers between devices: 76.8 us -> 37.7 us  [the longest x12 24.2 us: swap(): return lax.ppermute(x, AXES, [(i, i ^ bit) for i in range(size)])]
    ppermute x32 -> x20, waiting for transfers between devices: 18.6 us -> 54.2 us  [the longest x12 44.2 us: swap(): return lax.ppermute(x, AXES, [(i, i ^ bit) for i in range(size)])]
    pallas_call x0 -> x4, Pallas kernels: none -> 29.1 us  [the longest x1 15.1 us: local(): call(lambda *refs: middle_kernel(count, width, scale, *refs), 3, 8, (stru...]
    dot_general x18 -> x0, matrix products: 22.1 us -> none  [conv_kernel(): lax.dot_general(window, flat_up, (((0,), (0,)), ((), ())), preferred_elem...]
    slice x17 -> x5, local copies, waits for them, and re-layouts: 16.2 us -> 1.09 us  [the longest x1 1.08 us: local(): grads[1]]
    conv_general_dilated x4 -> x0, matrix products: 14.2 us -> none  [the longest x2 7.9 us: conv_forward(): lax.conv_general_dilated(padded, kernel, (1, 1), 'VALID', dimension_numbe...]
    scatter x18 -> x0, local copies, waits for them, and re-layouts: 12.5 us -> none  [the longest x4 3.44 us: fill_halo(): padded.at[0, 0, 1:last].set(strips[0]).at[0, 1:last, last].set(strips[1])]
  transfers between devices with their start and end apart: 33 -> 20, of which waited for: 9 -> 15; matrix products, arithmetic and copies ran while one was open for 24% -> 1% of each run, Pallas kernels for 0% -> 9%
where the time goes in v1:
time: 140 us; the launch traced here: 138 us
  waiting for transfers between devices  54.2 us (39%)
  starting transfers between devices  37.7 us (27%)
  Pallas kernels  29.1 us (21%)
  local copies, waits for them, and re-layouts  12.1 us (9%)
  other arithmetic  3.61 us (3%)
    ppermute x12, waiting for transfers between devices, swap(): return lax.ppermute(x, AXES, [(i, i ^ bit) for i in range(size)])  44.2 us
    ppermute x12, starting transfers between devices, swap(): return lax.ppermute(x, AXES, [(i, i ^ bit) for i in range(size)])  24.2 us
    pallas_call x1, Pallas kernels, local(): call(lambda *refs: middle_kernel(count, width, scale, *refs), 3, 8, (stru...  15.1 us
    ppermute x8, starting transfers between devices, shifted(): return lax.ppermute(x, AXES, [(i, (i + by) % size) for i in range(size)])  13.5 us
    ppermute x8, waiting for transfers between devices, shifted(): return lax.ppermute(x, AXES, [(i, (i + by) % size) for i in range(size)])  9.94 us
    unnamed x24, local copies, waits for them, and re-layouts  9.32 us
    pallas_call x1, Pallas kernels, local(): call(lambda *refs: last_kernel(count, width, *refs), 3, 8, (struct(BLOCK)...  8.93 us
    pallas_call x1, Pallas kernels, local(): call(prepare_kernel, 0, 3, (weights, weights, weights, weights, struct(CO...  3.93 us
  transfers between devices with their start and end apart: 20, of which 15 were waited for; matrix products, arithmetic and copies ran while one was open for 1% of the time, Pallas kernels for 9%

profile of v1, /device:TPU:1, one launch (start us, length us, event | category | flops | bytes accessed | tf_op | source)
XLA Modules:
  0.0 137.6 jit_solution(16078363160725112043)
XLA Ops:
  2.7 1.2 copy-done
  6.3 6.0 %collective-permute-start.1 = (bf16[160,128]{1,0:T(8,128)(2,1)S(1)}, bf16[160,128]{1,0:T(8,128)(2,1)S(1)}, u32[]{:S(2)}, u32[]{:S(2)}) collective-permute-start(bf16[160,128]{1,0:T(8,128)(2,1)S(1)} %get-tuple-element.23), channel_id=1, source_target_pairs={{0,224},{1,225},{2,226},{3,227},{4,228},{5,229},{6,230},{7,231},{8... | collective-permute-start | bytes 122888 | tf_op jit(solution)/shard_map/ppermute | solution.py:379
  13.5 5.4 %collective-permute-done.refs_4_ = bf16[160,128]{1,0:T(8,128)(2,1)S(1)} collective-permute-done((bf16[160,128]{1,0:T(8,128)(2,1)S(1)}, bf16[160,128]{1,0:T(8,128)(2,1)S(1)}, u32[]{:S(2)}, u32[]{:S(2)}) %collective-permute-start) | collective-permute-done | bytes 40992 | tf_op jit(solution)/shard_map/ppermute | solution.py:379
  19.2 2.2 %collective-permute-start.3 = (bf16[160,128]{1,0:T(8,128)(2,1)S(1)}, bf16[160,128]{1,0:T(8,128)(2,1)S(1)}, u32[]{:S(2)}, u32[]{:S(2)}) collective-permute-start(bf16[160,128]{1,0:T(8,128)(2,1)S(1)} %pad_maximum_fusion.1), channel_id=1, source_target_pairs={{0,255},{1,0},{2,1},{3,2},{4,3},{5,4},{6,5},{7,6},{8,7},{9,8},{10,... | collective-permute-start | bytes 122888 | tf_op jit(solution)/shard_map/ppermute | solution.py:379
  21.4 3.9 %shard_map.94 = (bf16[1536,256]{1,0:T(8,128)(2,1)S(1)}, bf16[1536,256]{1,0:T(8,128)(2,1)S(1)}, bf16[1536,256]{1,0:T(8,128)(2,1)S(1)}, bf16[1536,256]{1,0:T(8,128)(2,1)S(1)}, bf16[3,33,2,64,128]{4,3,2,1,0:T(8,128)(2,1)}) custom-call(bf16[3,3,128,128]{3,2,1,0:T(8,128)(2,1)S(1)} %copy-done.2, bf16[3,3,128,128]{3,2,1,0:T(8,128)(2,1)S(1)} %copy-done.3, ...), custom_call_target="tpu_custom_call" | custom-call | flops 1207959552 | bytes 4194304 | tf_op jit(solution)/shard_map/pallas_call | solution.py:437
  27.4 15.1 %shard_map.95 = (bf16[32,2,64,128]{3,2,1,0:T(8,128)(2,1)S(1)}, bf16[32,2,64,128]{3,2,1,0:T(8,128)(2,1)S(1)}, bf16[160,128]{1,0:T(8,128)(2,1)S(1)}, bf16[160,128]...) custom-call(s32[1]{0:T(128)} %bitcast.refs_0_, ...), custom_call_target="tpu_custom_call" | custom-call | flops 4831838208 | bytes 4194304 | tf_op jit(solution)/shard_map/pallas_call | solution.py:441
  45.6 6.8 %collective-permute-start.8 = (f32[1152,128]{1,0:T(8,128)S(1)}, f32[1152,128]{1,0:T(8,128)}, u32[]{:S(2)}, u32[]{:S(2)}) collective-permute-start(f32[1152,128]{1,0:T(8,128)S(1)} %constant_dynamic-slice_fusion.3), channel_id=1, source_target_pairs={{0,2},{1,3},{2,0},{3,1},{4,6},{5,7},{6,4},{7,5},{8,10},{9,11},{10,... | collective-permute-start | bytes 1769480 | tf_op jit(solution)/shard_map/ppermute | solution.py:384
  52.4 1.8 %collective-permute-done.8 = f32[1152,128]{1,0:T(8,128)} collective-permute-done((f32[1152,128]{1,0:T(8,128)S(1)}, f32[1152,128]{1,0:T(8,128)}, u32[]{:S(2)}, u32[]{:S(2)}) %collective-permute-start.8) | collective-permute-done | bytes 589856 | tf_op jit(solution)/shard_map/ppermute | solution.py:384
  55.5 8.2 %collective-permute-done.9 = f32[576,128]{1,0:T(8,128)S(1)} collective-permute-done((f32[576,128]{1,0:T(8,128)S(1)}, f32[576,128]{1,0:T(8,128)S(1)}, u32[]{:S(2)}, u32[]{:S(2)}) %collective-permute-start.9) | collective-permute-done | bytes 294944 | tf_op jit(solution)/shard_map/ppermute | solution.py:384
  63.9 3.9 %collective-permute-done.10 = f32[288,128]{1,0:T(8,128)S(1)} collective-permute-done((f32[288,128]{1,0:T(8,128)S(1)}, f32[288,128]{1,0:T(8,128)S(1)}, u32[]{:S(2)}, u32[]{:S(2)}) %collective-permute-start.10) | collective-permute-done | bytes 147488 | tf_op jit(solution)/shard_map/ppermute | solution.py:384
  68.0 3.2 %collective-permute-done.11 = f32[144,128]{1,0:T(8,128)S(1)} collective-permute-done((f32[144,128]{1,0:T(8,128)S(1)}, f32[144,128]{1,0:T(8,128)S(1)}, u32[]{:S(2)}, u32[]{:S(2)}) %collective-permute-start.11) | collective-permute-done | bytes 73760 | tf_op jit(solution)/shard_map/ppermute | solution.py:384
  71.3 4.7 %collective-permute-done.12 = f32[144,128]{1,0:T(8,128)S(1)} collective-permute-done((f32[144,128]{1,0:T(8,128)S(1)}, f32[144,128]{1,0:T(8,128)S(1)}, u32[]{:S(2)}, u32[]{:S(2)}) %collective-permute-start.12) | collective-permute-done | bytes 73760 | tf_op jit(solution)/shard_map/ppermute | solution.py:384
  76.1 4.7 %collective-permute-done.13 = f32[144,128]{1,0:T(8,128)S(1)} collective-permute-done((f32[144,128]{1,0:T(8,128)S(1)}, f32[144,128]{1,0:T(8,128)S(1)}, u32[]{:S(2)}, u32[]{:S(2)}) %collective-permute-start.13) | collective-permute-done | bytes 73760 | tf_op jit(solution)/shard_map/ppermute | solution.py:384
  81.9 4.2 %collective-permute-done.14 = f32[144,128]{1,0:T(8,128)S(1)} collective-permute-done((f32[144,128]{1,0:T(8,128)S(1)}, f32[144,128]{1,0:T(8,128)S(1)}, u32[]{:S(2)}, u32[]{:S(2)}) %collective-permute-start.14) | collective-permute-done | bytes 73760 | tf_op jit(solution)/shard_map/ppermute | solution.py:384
  86.1 3.9 %collective-permute-start.15 = (f32[144,128]{1,0:T(8,128)S(1)}, f32[144,128]{1,0:T(8,128)S(1)}, u32[]{:S(2)}, u32[]{:S(2)}) collective-permute-start(f32[144,128]{1,0:T(8,128)S(1)} %add.92), channel_id=1, source_target_pairs={{0,16},{1,17},{2,18},{3,19},{4,20},{5,21},{6,22},{7,23},{8,24},{9,... | collective-permute-start | bytes 221192 | tf_op jit(solution)/shard_map/ppermute | solution.py:384
  89.9 4.3 %collective-permute-done.15 = f32[144,128]{1,0:T(8,128)S(1)} collective-permute-done((f32[144,128]{1,0:T(8,128)S(1)}, f32[144,128]{1,0:T(8,128)S(1)}, u32[]{:S(2)}, u32[]{:S(2)}) %collective-permute-start.15) | collective-permute-done | bytes 73760 | tf_op jit(solution)/shard_map/ppermute | solution.py:384
  94.4 3.2 %collective-permute-done.16 = f32[144,128]{1,0:T(8,128)S(1)} collective-permute-done((f32[144,128]{1,0:T(8,128)S(1)}, f32[144,128]{1,0:T(8,128)S(1)}, u32[]{:S(2)}, u32[]{:S(2)}) %collective-permute-start.16) | collective-permute-done | bytes 73760 | tf_op jit(solution)/shard_map/ppermute | solution.py:384
  97.7 5.0 %collective-permute-done.17 = f32[288,128]{1,0:T(8,128)S(1)} collective-permute-done((f32[288,128]{1,0:T(8,128)S(1)}, f32[288,128]{1,0:T(8,128)S(1)}, u32[]{:S(2)}, u32[]{:S(2)}) %collective-permute-start.17) | collective-permute-done | bytes 147488 | tf_op jit(solution)/shard_map/ppermute | solution.py:384
  102.9 3.0 %collective-permute-start.4 = (bf16[160,128]{1,0:T(8,128)(2,1)S(1)}, bf16[160,128]{1,0:T(8,128)(2,1)S(1)}, u32[]{:S(2)}, u32[]{:S(2)}) collective-permute-start(bf16[160,128]{1,0:T(8,128)(2,1)S(1)} %get-tuple-element.31), channel_id=1, source_target_pairs={{0,32},{1,33},{2,34},{3,35},{4,36},{5,37},{6,38},{7,39},{8,40},{9,... | collective-permute-start | bytes 122888 | tf_op jit(solution)/shard_map/ppermute | solution.py:379
  105.9 1.4 %collective-permute-done.5.refs_6_ = bf16[160,128]{1,0:T(8,128)(2,1)S(1)} collective-permute-done((bf16[160,128]{1,0:T(8,128)(2,1)S(1)}, bf16[160,128]{1,0:T(8,128)(2,1)S(1)}, u32[]{:S(2)}, u32[]{:S(2)}) %collective-permute-start.5) | collective-permute-done | bytes 40992 | tf_op jit(solution)/shard_map/ppermute | solution.py:379
  109.3 11.8 %collective-permute-start.19 = (f32[1152,128]{1,0:T(8,128)}, f32[1152,128]{1,0:T(8,128)S(1)}, u32[]{:S(2)}, u32[]{:S(2)}) collective-permute-start(f32[1152,128]{1,0:T(8,128)} %maximum_select_fusion.1), channel_id=1, source_target_pairs={{0,2},{1,3},{2,0},{3,1},{4,6},{5,7},{6,4},{7,5},{8,10},{9,11},{10,... | collective-permute-start | bytes 1769480 | tf_op jit(solution)/shard_map/ppermute | solution.py:384
  122.9 2.1 %collective-permute-done.6.refs_7_ = bf16[160,128]{1,0:T(8,128)(2,1)S(1)} collective-permute-done((bf16[160,128]{1,0:T(8,128)(2,1)S(1)}, bf16[160,128]{1,0:T(8,128)(2,1)S(1)}, u32[]{:S(2)}, u32[]{:S(2)}) %collective-permute-start.6) | collective-permute-done | bytes 40992 | tf_op jit(solution)/shard_map/ppermute | solution.py:379
  126.2 8.9 %shard_map.96 = (bf16[32,2,64,128]{3,2,1,0:T(8,128)(2,1)}, bf16[32,2,64,128]{3,2,1,0:T(8,128)(2,1)}) custom-call(s32[1]{0:T(128)} %bitcast.refs_0_, s32[1024]{0:T(1024)S(1)} %reshape.35.refs_1_, s32[1024]{0:T(1024)S(1)} %reshape.36.refs_2_, bf16[32,2,64,128]{3,2,1,0:T(8,128)(2,1)S(1)} %copy-done.7, bf16[32,2,64,128]{3,2,1,0:T(8,128)(2,1)S(1)} %copy-done.9, ...), custom_call_target="tpu_custom_call" | custom-call | flops 2415919104 | bytes 4194304 | tf_op jit(solution)/shard_map/pallas_call | solution.py:452
  135.1 1.4 %maximum_select_fusion = f32[2304,128]{1,0:T(8,128)S(1)} fusion(f32[1152,128]{1,0:T(8,128)} %maximum_select_fusion.1, f32[1152,128]{1,0:T(8,128)S(1)} %collective-permute-done.19, pred[]{:T(512)S(6)} %eq.21), kind=kLoop, calls=%fused_computation | loop fusion | flops 884736 | bytes 2359297 | tf_op jit(solution)/shard_map/jit(_where)/select_n | solution.py:413
  (71 shorter events, 20.5 us)
Async XLA Ops:
  1.5 20.0 %copy-start.2 = (bf16[3,3,128,128]{3,2,1,0:T(8,128)(2,1)S(1)}, bf16[3,3,128,128]{3,2,1,0:T(8,128)(2,1)}, u32[]{:S(2)}) copy-start(bf16[3,3,128,128]{3,2,1,0:T(8,128)(2,1)} %kernel_one.1) | copy-start | bytes 884740
  5.2 16.2 %copy-start.3 = (bf16[3,3,128,128]{3,2,1,0:T(8,128)(2,1)S(1)}, bf16[3,3,128,128]{3,2,1,0:T(8,128)(2,1)}, u32[]{:S(2)}) copy-start(bf16[3,3,128,128]{3,2,1,0:T(8,128)(2,1)} %kernel_two.1) | copy-start | bytes 884740
  6.3 7.1 %collective-permute-start.1 = (bf16[160,128]{1,0:T(8,128)(2,1)S(1)}, bf16[160,128]{1,0:T(8,128)(2,1)S(1)}, u32[]{:S(2)}, u32[]{:S(2)}) collective-permute-start(bf16[160,128]{1,0:T(8,128)(2,1)S(1)} %get-tuple-element.23), channel_id=1, source_target_pairs={{0,224},{1,225},{2,226},{3,227},{4,228},{5,229},{6,230},{7,231},{8... | collective-permute-start | bytes 122888 | tf_op jit(solution)/shard_map/ppermute | solution.py:379
  12.4 6.5 %collective-permute-start = (bf16[160,128]{1,0:T(8,128)(2,1)S(1)}, bf16[160,128]{1,0:T(8,128)(2,1)S(1)}, u32[]{:S(2)}, u32[]{:S(2)}) collective-permute-start(bf16[160,128]{1,0:T(8,128)(2,1)S(1)} %get-tuple-element.22), channel_id=1, source_target_pairs={{0,32},{1,33},{2,34},{3,35},{4,36},{5,37},{6,38},{7,39},{8,40},{9,... | collective-permute-start | bytes 122888 | tf_op jit(solution)/shard_map/ppermute | solution.py:379
  18.8 7.4 %collective-permute-start.2 = (bf16[160,128]{1,0:T(8,128)(2,1)S(1)}, bf16[160,128]{1,0:T(8,128)(2,1)S(1)}, u32[]{:S(2)}, u32[]{:S(2)}) collective-permute-start(bf16[160,128]{1,0:T(8,128)(2,1)S(1)} %pad_maximum_fusion), channel_id=1, source_target_pairs={{0,1},{1,2},{2,3},{3,4},{4,5},{5,6},{6,7},{7,8},{8,9},{9,10},{10,1... | collective-permute-start | bytes 122888 | tf_op jit(solution)/shard_map/ppermute | solution.py:379
  19.2 7.0 %collective-permute-start.3 = (bf16[160,128]{1,0:T(8,128)(2,1)S(1)}, bf16[160,128]{1,0:T(8,128)(2,1)S(1)}, u32[]{:S(2)}, u32[]{:S(2)}) collective-permute-start(bf16[160,128]{1,0:T(8,128)(2,1)S(1)} %pad_maximum_fusion.1), channel_id=1, source_target_pairs={{0,255},{1,0},{2,1},{3,2},{4,3},{5,4},{6,5},{7,6},{8,7},{9,8},{10,... | collective-permute-start | bytes 122888 | tf_op jit(solution)/shard_map/ppermute | solution.py:379
  44.4 9.7 %copy-start.10 = (f32[2304,128]{1,0:T(8,128)S(1)}, f32[2304,128]{1,0:T(8,128)}, u32[]{:S(2)}) copy-start(f32[2304,128]{1,0:T(8,128)} %get-tuple-element.39) | copy-start | bytes 3538948
  45.6 8.5 %collective-permute-start.8 = (f32[1152,128]{1,0:T(8,128)S(1)}, f32[1152,128]{1,0:T(8,128)}, u32[]{:S(2)}, u32[]{:S(2)}) collective-permute-start(f32[1152,128]{1,0:T(8,128)S(1)} %constant_dynamic-slice_fusion.3), channel_id=1, source_target_pairs={{0,2},{1,3},{2,0},{3,1},{4,6},{5,7},{6,4},{7,5},{8,10},{9,11},{10,... | collective-permute-start | bytes 1769480 | tf_op jit(solution)/shard_map/ppermute | solution.py:384
  55.4 8.3 %collective-permute-start.9 = (f32[576,128]{1,0:T(8,128)S(1)}, f32[576,128]{1,0:T(8,128)S(1)}, u32[]{:S(2)}, u32[]{:S(2)}) collective-permute-start(f32[576,128]{1,0:T(8,128)S(1)} %constant_dynamic-slice_fusion.2), channel_id=1, source_target_pairs={{0,1},{1,0},{2,3},{3,2},{4,5},{5,4},{6,7},{7,6},{8,9},{9,8},{10,11... | collective-permute-start | bytes 884744 | tf_op jit(solution)/shard_map/ppermute | solution.py:384
  63.7 4.1 %collective-permute-start.10 = (f32[288,128]{1,0:T(8,128)S(1)}, f32[288,128]{1,0:T(8,128)S(1)}, u32[]{:S(2)}, u32[]{:S(2)}) collective-permute-start(f32[288,128]{1,0:T(8,128)S(1)} %constant_dynamic-slice_fusion.1), channel_id=1, source_target_pairs={{0,4},{1,5},{2,6},{3,7},{4,0},{5,1},{6,2},{7,3},{8,12},{9,13},{10,... | collective-permute-start | bytes 442376 | tf_op jit(solution)/shard_map/ppermute | solution.py:384
  67.9 3.3 %collective-permute-start.11 = (f32[144,128]{1,0:T(8,128)S(1)}, f32[144,128]{1,0:T(8,128)S(1)}, u32[]{:S(2)}, u32[]{:S(2)}) collective-permute-start(f32[144,128]{1,0:T(8,128)S(1)} %constant_dynamic-slice_fusion), channel_id=1, source_target_pairs={{0,64},{1,65},{2,66},{3,67},{4,68},{5,69},{6,70},{7,71},{8,72},{9,... | collective-permute-start | bytes 221192 | tf_op jit(solution)/shard_map/ppermute | solution.py:384
  71.2 4.8 %collective-permute-start.12 = (f32[144,128]{1,0:T(8,128)S(1)}, f32[144,128]{1,0:T(8,128)S(1)}, u32[]{:S(2)}, u32[]{:S(2)}) collective-permute-start(f32[144,128]{1,0:T(8,128)S(1)} %dynamic-slice_add_fusion.3), channel_id=1, source_target_pairs={{0,32},{1,33},{2,34},{3,35},{4,36},{5,37},{6,38},{7,39},{8,40},{9,... | collective-permute-start | bytes 221192 | tf_op jit(solution)/shard_map/ppermute | solution.py:384
  76.0 4.8 %collective-permute-start.13 = (f32[144,128]{1,0:T(8,128)S(1)}, f32[144,128]{1,0:T(8,128)S(1)}, u32[]{:S(2)}, u32[]{:S(2)}) collective-permute-start(f32[144,128]{1,0:T(8,128)S(1)} %add.90), channel_id=1, source_target_pairs={{0,128},{1,129},{2,130},{3,131},{4,132},{5,133},{6,134},{7,135},{8... | collective-permute-start | bytes 221192 | tf_op jit(solution)/shard_map/ppermute | solution.py:384
  80.8 5.3 %collective-permute-start.14 = (f32[144,128]{1,0:T(8,128)S(1)}, f32[144,128]{1,0:T(8,128)S(1)}, u32[]{:S(2)}, u32[]{:S(2)}) collective-permute-start(f32[144,128]{1,0:T(8,128)S(1)} %add.91), channel_id=1, source_target_pairs={{0,8},{1,9},{2,10},{3,11},{4,12},{5,13},{6,14},{7,15},{8,0},{9,1},... | collective-permute-start | bytes 221192 | tf_op jit(solution)/shard_map/ppermute | solution.py:384
  86.1 8.2 %collective-permute-start.15 = (f32[144,128]{1,0:T(8,128)S(1)}, f32[144,128]{1,0:T(8,128)S(1)}, u32[]{:S(2)}, u32[]{:S(2)}) collective-permute-start(f32[144,128]{1,0:T(8,128)S(1)} %add.92), channel_id=1, source_target_pairs={{0,16},{1,17},{2,18},{3,19},{4,20},{5,21},{6,22},{7,23},{8,24},{9,... | collective-permute-start | bytes 221192 | tf_op jit(solution)/shard_map/ppermute | solution.py:384
  94.3 30.7 %copy-start.7 = (bf16[32,2,64,128]{3,2,1,0:T(8,128)(2,1)S(1)}, bf16[32,2,64,128]{3,2,1,0:T(8,128)(2,1)}, u32[]{:S(2)}) copy-start(bf16[32,2,64,128]{3,2,1,0:T(8,128)(2,1)} %copy-done.6) | copy-start | bytes 3145732
  94.3 3.3 %collective-permute-start.16 = (f32[144,128]{1,0:T(8,128)S(1)}, f32[144,128]{1,0:T(8,128)S(1)}, u32[]{:S(2)}, u32[]{:S(2)}) collective-permute-start(f32[144,128]{1,0:T(8,128)S(1)} %add.93), channel_id=1, source_target_pairs={{0,64},{1,65},{2,66},{3,67},{4,68},{5,69},{6,70},{7,71},{8,72},{9,... | collective-permute-start | bytes 221192 | tf_op jit(solution)/shard_map/ppermute | solution.py:384
  97.6 5.1 %collective-permute-start.17 = (f32[288,128]{1,0:T(8,128)S(1)}, f32[288,128]{1,0:T(8,128)S(1)}, u32[]{:S(2)}, u32[]{:S(2)}) collective-permute-start(f32[288,128]{1,0:T(8,128)S(1)} %maximum_select_fusion.3), channel_id=1, source_target_pairs={{0,4},{1,5},{2,6},{3,7},{4,0},{5,1},{6,2},{7,3},{8,12},{9,13},{10,... | collective-permute-start | bytes 442376 | tf_op jit(solution)/shard_map/ppermute | solution.py:384
  102.7 5.7 %collective-permute-start.18 = (f32[576,128]{1,0:T(8,128)S(1)}, f32[576,128]{1,0:T(8,128)S(1)}, u32[]{:S(2)}, u32[]{:S(2)}) collective-permute-start(f32[576,128]{1,0:T(8,128)S(1)} %maximum_select_fusion.2), channel_id=1, source_target_pairs={{0,1},{1,0},{2,3},{3,2},{4,5},{5,4},{6,7},{7,6},{8,9},{9,8},{10,11... | collective-permute-start | bytes 884744 | tf_op jit(solution)/shard_map/ppermute | solution.py:384
  102.8 4.4 %collective-permute-start.5 = (bf16[160,128]{1,0:T(8,128)(2,1)S(1)}, bf16[160,128]{1,0:T(8,128)(2,1)S(1)}, u32[]{:S(2)}, u32[]{:S(2)}) collective-permute-start(bf16[160,128]{1,0:T(8,128)(2,1)S(1)} %get-tuple-element.32), channel_id=1, source_target_pairs={{0,224},{1,225},{2,226},{3,227},{4,228},{5,229},{6,230},{7,231},{8... | collective-permute-start | bytes 122888 | tf_op jit(solution)/shard_map/ppermute | solution.py:379
  102.9 18.1 %collective-permute-start.4 = (bf16[160,128]{1,0:T(8,128)(2,1)S(1)}, bf16[160,128]{1,0:T(8,128)(2,1)S(1)}, u32[]{:S(2)}, u32[]{:S(2)}) collective-permute-start(bf16[160,128]{1,0:T(8,128)(2,1)S(1)} %get-tuple-element.31), channel_id=1, source_target_pairs={{0,32},{1,33},{2,34},{3,35},{4,36},{5,37},{6,38},{7,39},{8,40},{9,... | collective-permute-start | bytes 122888 | tf_op jit(solution)/shard_map/ppermute | solution.py:379
  109.3 25.9 %collective-permute-start.19 = (f32[1152,128]{1,0:T(8,128)}, f32[1152,128]{1,0:T(8,128)S(1)}, u32[]{:S(2)}, u32[]{:S(2)}) collective-permute-start(f32[1152,128]{1,0:T(8,128)} %maximum_select_fusion.1), channel_id=1, source_target_pairs={{0,2},{1,3},{2,0},{3,1},{4,6},{5,7},{6,4},{7,5},{8,10},{9,11},{10,... | collective-permute-start | bytes 1769480 | tf_op jit(solution)/shard_map/ppermute | solution.py:384
  121.0 3.9 %collective-permute-start.6 = (bf16[160,128]{1,0:T(8,128)(2,1)S(1)}, bf16[160,128]{1,0:T(8,128)(2,1)S(1)}, u32[]{:S(2)}, u32[]{:S(2)}) collective-permute-start(bf16[160,128]{1,0:T(8,128)(2,1)S(1)} %pad_maximum_fusion.2), channel_id=1, source_target_pairs={{0,1},{1,2},{2,3},{3,4},{4,5},{5,6},{6,7},{7,8},{8,9},{9,10},{10,1... | collective-permute-start | bytes 122888 | tf_op jit(solution)/shard_map/ppermute | solution.py:379
  121.7 3.3 %collective-permute-start.7 = (bf16[160,128]{1,0:T(8,128)(2,1)S(1)}, bf16[160,128]{1,0:T(8,128)(2,1)S(1)}, u32[]{:S(2)}, u32[]{:S(2)}) collective-permute-start(bf16[160,128]{1,0:T(8,128)(2,1)S(1)} %pad_maximum_fusion.3), channel_id=1, source_target_pairs={{0,255},{1,0},{2,1},{3,2},{4,3},{5,4},{6,5},{7,6},{8,7},{9,8},{10,... | collective-permute-start | bytes 122888 | tf_op jit(solution)/shard_map/ppermute | solution.py:379
  (7 other events, 7.6 us)

commit v2 on v1

v2 whole, which is shorter than its diff:
```python
import math

import jax
import jax.numpy as jnp
from jax import lax
from jax.experimental import pallas as pl
from jax.experimental.pallas import tpu as pltpu
from jax.sharding import PartitionSpec as P

AXES = ("face", "sub")
GRID_ROWS = 8
SIDE = 64
CH = 128
HALF = SIDE // 2
STRIPS = 2 * SIDE
VROWS = STRIPS + 32
BF16 = jnp.bfloat16
F32 = jnp.float32
N, E, S, W = 0, 1, 2, 3
NW, NE, SE, SW = 0, 1, 2, 3
VMEM = pl.BlockSpec(memory_space=pltpu.VMEM)
SMEM = pl.BlockSpec(memory_space=pltpu.SMEM)
HBM = pl.BlockSpec(memory_space=pltpu.HBM)
PARAMS = pltpu.CompilerParams(vmem_limit_bytes=24 * 1024 * 1024)


def code_at(table, block, which):
    return table[block // 2, block % 2, which]


def iota(shape, dim):
    return lax.broadcasted_iota(jnp.int32, shape, dim)


def strips_from(north, south, low, high, dst):
    dst[N] = north.astype(F32)
    dst[S] = south.astype(F32)
    low = low.reshape(SIDE, 16, CH).astype(F32)
    dst[W] = jnp.sum(jnp.where(iota(low.shape, 1) == 0, low, 0.0), axis=1)
    high = high.reshape(SIDE, 16, CH).astype(F32)
    dst[E] = jnp.sum(jnp.where(iota(high.shape, 1) == 15, high, 0.0), axis=1)


def side_strips(block, dst):
    strips_from(
        block[0, 0], block[HALF - 1, 1], block[:, :, 0:16, :], block[:, :, SIDE - 16 : SIDE, :], dst
    )


def corner_rows(strips):
    north = strips[N]
    south = strips[S]
    last = SIDE - 1
    return [north[0:1], north[last : last + 1], south[last : last + 1], south[0:1]]


def turned(strip, flip):
    row = iota((SIDE, SIDE), 0)
    col = iota((SIDE, SIDE), 1)
    target = jnp.where(flip, SIDE - 1 - row, row)
    matrix = jnp.where(col == target, 1.0, 0.0).astype(BF16)
    return jnp.dot(matrix, strip.astype(BF16), preferred_element_type=F32).astype(BF16)


def corner_block(code, own, other):
    picked = jnp.where(code == 0, own[0], jnp.where(code == 1, own[1], jnp.where(code == 2, own[2], own[3])))
    row = iota((16, CH), 0)
    return (jnp.where(row == 0, picked, 0.0) + jnp.where(row == 1, other, 0.0)).astype(BF16)


def pack(me, edge, corner, count, width, fore, back, vp, vm, hp, hm):
    fore_corners = corner_rows(fore)
    back_corners = corner_rows(back)

    def block(offset):
        return lax.rem(me + offset + 2 * count, count)

    def strips(dst, offset, read_side, own_side):
        code = code_at(edge, block(offset), read_side)
        dst[0:SIDE] = turned(fore[lax.rem(code, 4)], code >= 4)
        dst[SIDE:STRIPS] = turned(back[own_side], code_at(edge, me, own_side) >= 4)

    def relayed(offset, read_corner, own_corner):
        return corner_block(
            code_at(corner, block(offset), read_corner), fore_corners, back_corners[own_corner]
        )

    strips(vp, width, N, S)
    vp[STRIPS : STRIPS + 16] = relayed(width + 1, NW, SE)
    vp[STRIPS + 16 : VROWS] = relayed(width - 1, NE, SW)
    strips(vm, -width, S, N)
    vm[STRIPS : STRIPS + 16] = relayed(-width + 1, SW, NE)
    vm[STRIPS + 16 : VROWS] = relayed(-width - 1, SE, NW)
    strips(hp, 1, W, E)
    strips(hm, -1, E, W)


def put_row(dst, pair, part, row, west, east):
    col = iota((SIDE, CH), 0)
    wide = row.astype(F32)
    dst[1, pair, part] = row.astype(BF16)
    dst[0, pair, part] = jnp.where(col == 0, west, pltpu.roll(wide, 1, 0)).astype(BF16)
    dst[2, pair, part] = jnp.where(col == SIDE - 1, east, pltpu.roll(wide, SIDE - 1, 0)).astype(BF16)


def shift_copies(dst, src, west=None, east=None):
    def step(k, _):
        for part in range(2):
            i = 2 * k + part
            w = 0.0 if west is None else west[pl.ds(i, 1), :]
            e = 0.0 if east is None else east[pl.ds(i, 1), :]
            put_row(dst, k + part, 1 - part, src[k, part], w, e)
        return 0

    lax.fori_loop(0, HALF, step, 0, unroll=4)


def halo_copies(dst, src, west, east, vp, vm, hp, hm):
    west[...] = hp[0:SIDE].astype(F32)
    east[...] = hm[0:SIDE].astype(F32)
    shift_copies(dst, src, west, east)
    hp1 = hp[STRIPS : STRIPS + 16].astype(F32)
    hp2 = hp[STRIPS + 16 : VROWS].astype(F32)
    hm1 = hm[STRIPS : STRIPS + 16].astype(F32)
    hm2 = hm[STRIPS + 16 : VROWS].astype(F32)
    put_row(dst, 0, 0, vp[0:SIDE], hp1[0:1], hm1[0:1])
    put_row(dst, HALF, 1, vm[0:SIDE], hp2[0:1], hm2[0:1])


def zero_copies(dst, src):
    zero = jnp.zeros((SIDE, CH), BF16)
    for b in range(3):
        dst[b, 0, 0] = zero
        dst[b, HALF, 1] = zero
    shift_copies(dst, src)


def window(copies, m, mb):
    parts = [
        copies[b, pl.ds(m + a // 2, mb), a % 2].reshape(mb * SIDE, CH)
        for a in range(4)
        for b in range(3)
    ]
    return jnp.concatenate(parts, axis=1)


def conv_pairs(copies, weights, m, mb):
    return jnp.dot(window(copies, m, mb), weights[...], preferred_element_type=F32)


def edge_tap(side, k):
    return {N: (0, k), S: (2, k), W: (k, 0), E: (k, 2)}[side]


CORNER_TAP = {NW: (0, 0), NE: (0, 2), SE: (2, 2), SW: (2, 0)}


def neighbours(strip):
    row = iota((SIDE, CH), 0)
    up = jnp.where(row == SIDE - 1, 0.0, pltpu.roll(strip, SIDE - 1, 0))
    down = jnp.where(row == 0, 0.0, pltpu.roll(strip, 1, 0))
    return up, down


def tap_plain(weights, a, b):
    at = (a * 3 + b) * CH
    return weights[at : at + CH, 0:CH]


def tap_transposed(turned_weights, a, b):
    at = ((2 - a) * 3 + 2 - b) * CH
    return turned_weights[at : at + CH, 0:CH]


def returned(me, edge, corner, count, width, turned_weights, vp, vm, hp, hm, adds, pieces=None, corners=None):
    def block(offset):
        return lax.rem(me + offset + 2 * count, count)

    adds[...] = jnp.zeros_like(adds)
    row = iota((SIDE, CH), 0)
    for side, offset, message in ((N, width, vm), (E, -1, hp), (S, -width, vp), (W, 1, hm)):
        code = code_at(edge, block(offset), side)
        flip = code >= 4
        strip = message[SIDE:STRIPS].astype(F32)
        up, down = neighbours(strip)
        joined = jnp.concatenate(
            [jnp.where(flip, down, up), strip, jnp.where(flip, up, down)], axis=1
        ).astype(BF16)
        if pieces is not None:
            pieces[side] = joined
        taps = jnp.concatenate(
            [tap_transposed(turned_weights, *edge_tap(side, k)) for k in range(3)], axis=0
        )
        at = lax.rem(code, 4)
        adds[at] = adds[at] + jnp.dot(joined, taps, preferred_element_type=F32)
    for q, offset, message, start in (
        (NW, width + 1, hm, STRIPS + 16),
        (NE, width - 1, hp, STRIPS + 16),
        (SE, -width - 1, hp, STRIPS),
        (SW, -width + 1, hm, STRIPS),
    ):
        code = code_at(corner, block(offset), q)
        cells = message[start : start + 16]
        if corners is not None:
            corners[q] = cells
        given = jnp.dot(
            cells, tap_transposed(turned_weights, *CORNER_TAP[q]), preferred_element_type=F32
        )[1:2]
        first = jnp.where(row == 0, given, 0.0)
        last = jnp.where(row == SIDE - 1, given, 0.0)
        adds[N] = adds[N] + jnp.where(code == NW, first, 0.0) + jnp.where(code == NE, last, 0.0)
        adds[S] = adds[S] + jnp.where(code == SW, first, 0.0) + jnp.where(code == SE, last, 0.0)


def with_adds(rows, i, adds, first=False, last=False):
    col = iota((8, CH), 0)
    rows = jnp.concatenate(
        [
            rows[0:8] + jnp.where(col == 0, adds[W, pl.ds(i, 1), :], 0.0),
            rows[8 : SIDE - 8],
            rows[SIDE - 8 :] + jnp.where(col == 7, adds[E, pl.ds(i, 1), :], 0.0),
        ],
        axis=0,
    )
    if first:
        rows = rows + adds[N]
    if last:
        rows = rows + adds[S]
    return rows


def pad_sides(vp, vm, hp, hm):
    return ((N, vp), (S, vm), (W, hp), (E, hm))


def pad_corners(hp, hm):
    return ((NW, hp, STRIPS), (NE, hm, STRIPS), (SE, hm, STRIPS + 16), (SW, hp, STRIPS + 16))


def received(weights, vp, vm, hp, hm, adds):
    row = iota((SIDE, CH), 0)
    for side, message in pad_sides(vp, vm, hp, hm):
        strip = message[0:SIDE].astype(F32)
        up, down = neighbours(strip)
        joined = jnp.concatenate([down, strip, up], axis=1).astype(BF16)
        taps = jnp.concatenate([tap_plain(weights, *edge_tap(side, k)) for k in range(3)], axis=0)
        adds[side] = jnp.dot(joined, taps, preferred_element_type=F32)
    for q, message, start in pad_corners(hp, hm):
        cells = message[start : start + 16]
        given = jnp.dot(cells, tap_plain(weights, *CORNER_TAP[q]), preferred_element_type=F32)[0:1]
        side = N if q in (NW, NE) else S
        place = 0 if q in (NW, SW) else SIDE - 1
        adds[side] = adds[side] + jnp.where(row == place, given, 0.0)


def pack_kernel(
    count, width, me, edge, corner, fields, upstream, vp, vm, hp, hm, fore, back, rows, columns, sems
):
    copies = []
    for k, source in enumerate((fields, upstream)):
        for j, (part, dst) in enumerate((
            (source.at[0, 0], rows.at[k, 0]),
            (source.at[HALF - 1, 1], rows.at[k, 1]),
            (source.at[:, :, pl.ds(0, 16), :], columns.at[k, 0]),
            (source.at[:, :, pl.ds(SIDE - 16, 16), :], columns.at[k, 1]),
        )):
            copies.append(pltpu.make_async_copy(part, dst, sems.at[k, j]))
    for copy in copies:
        copy.start()
    for copy in copies:
        copy.wait()
    for k, dst in enumerate((fore, back)):
        strips_from(rows[k, 0], rows[k, 1], columns[k, 0], columns[k, 1], dst)
    pack(me[0], edge, corner, count, width, fore, back, vp, vm, hp, hm)


def plain_weights(source, dst):
    zero = jnp.zeros((CH, CH), BF16)
    for b in range(3):
        for a in range(3):
            at = (a * 3 + b) * CH
            dst[at : at + CH, 0:CH] = source[a, b]
            dst[at + 3 * CH : at + 4 * CH, CH : 2 * CH] = source[a, b]
        dst[(9 + b) * CH : (10 + b) * CH, 0:CH] = zero
        dst[b * CH : (b + 1) * CH, CH : 2 * CH] = zero


def turned_weights(source, dst):
    zero = jnp.zeros((CH, CH), BF16)
    for b in range(3):
        for a in range(3):
            at = (a * 3 + b) * CH
            swapped = source[2 - a, 2 - b].astype(F32).T.astype(BF16)
            dst[at : at + CH, 0:CH] = swapped
            dst[at + 3 * CH : at + 4 * CH, CH : 2 * CH] = swapped
        dst[(9 + b) * CH : (10 + b) * CH, 0:CH] = zero
        dst[b * CH : (b + 1) * CH, CH : 2 * CH] = zero


def conv_all(copies, weights, dst):
    mb = 4

    def step(n, _):
        m = n * mb
        got = conv_pairs(copies, weights, m, mb)
        for part in range(2):
            lanes = slice(part * CH, (part + 1) * CH)
            dst[pl.ds(m, mb), part] = got[:, lanes].reshape(mb, SIDE, CH).astype(dst.dtype)
        return 0

    lax.fori_loop(0, HALF // mb, step, 0)


def back_kernel(kernel_two, upstream, in_two, up_copies, grad):
    turned_weights(kernel_two, in_two)
    zero_copies(up_copies, upstream)
    conv_all(up_copies, in_two, grad)


def fore_kernel(kernel_one, fields, fwd_one, copies, pre):
    plain_weights(kernel_one, fwd_one)
    zero_copies(copies, fields)
    conv_all(copies, fwd_one, pre)


def middle_kernel(
    count, width, me, edge, corner, vp, vm, hp, hm, fwd_one, in_two, pre, grad,
    hidden, grad_pre, vp2, vm2, hp2, hm2, fore, back, pieces, corners, grad_adds, pre_adds,
):
    returned(me[0], edge, corner, count, width, in_two, vp, vm, hp, hm, grad_adds, pieces, corners)
    received(fwd_one, vp, vm, hp, hm, pre_adds)

    def one(m, part, first=False, last=False):
        i = 2 * m + part
        p = with_adds(pre[m, part], i, pre_adds, first, last)
        g = with_adds(grad[m, part], i, grad_adds, first, last)
        s = 1.0 / (1.0 + jnp.exp(-p))
        hidden[m, part] = (p * s).astype(BF16)
        grad_pre[m, part] = (g * s * (1.0 + p * (1.0 - s))).astype(BF16)

    def step(m, _):
        one(m, 0)
        one(m, 1)
        return 0

    one(0, 0, first=True)
    one(0, 1)
    lax.fori_loop(1, HALF - 1, step, 0, unroll=2)
    one(HALF - 1, 0)
    one(HALF - 1, 1, last=True)
    side_strips(hidden, fore)
    side_strips(grad_pre, back)
    pack(me[0], edge, corner, count, width, fore, back, vp2, vm2, hp2, hm2)


def sums_kernel(
    count, width, scale, me, edge, corner, vp, vm, hp, hm, hidden, grad_pre, field_copies, up_copies,
    fore, back, pieces, corners, keep, send, acc, sums,
):
    gb = 8
    first = (((0,), (0,)), ((), ()))

    def gather(values, shifted):
        def grad_step(n, _):
            m = n * gb
            left = jnp.concatenate(
                [values[pl.ds(m, gb), part].reshape(gb * SIDE, CH) for part in range(2)], axis=1
            )
            acc[...] += lax.dot_general(left, window(shifted, m, gb), first, preferred_element_type=F32)
            return 0

        acc[...] = jnp.zeros_like(acc)
        lax.fori_loop(0, HALF // gb, grad_step, 0)

    def from_acc(a, b):
        low = (a * 3 + b) * CH
        high = low + 3 * CH
        return acc[0:CH, low : low + CH] + acc[CH : 2 * CH, high : high + CH]

    def add(half, tap, term):
        at = (tap[0] * 3 + tap[1]) * CH
        sums[half, at : at + CH] = sums[half, at : at + CH] + term * scale

    def block(offset):
        return lax.rem(me[0] + offset + 2 * count, count)

    row = iota((16, CH), 0)
    gather(grad_pre, field_copies)
    for a in range(3):
        for b in range(3):
            at = (a * 3 + b) * CH
            sums[0, at : at + CH] = from_acc(a, b).T * scale
    for side, message in pad_sides(vp, vm, hp, hm):
        strip = back[side]
        up, down = neighbours(strip)
        joined = jnp.concatenate([up, strip, down], axis=1).astype(BF16)
        term = lax.dot_general(message[0:SIDE], joined, first, preferred_element_type=F32)
        for k in range(3):
            add(0, edge_tap(side, k), term[:, k * CH : (k + 1) * CH])
    own = corner_rows(back)
    for q, message, start in pad_corners(hp, hm):
        right = jnp.where(row == 0, own[q], 0.0).astype(BF16)
        add(0, CORNER_TAP[q], lax.dot_general(message[start : start + 16], right, first, preferred_element_type=F32))

    gather(hidden, up_copies)
    for a in range(3):
        for b in range(3):
            at = (a * 3 + b) * CH
            sums[1, at : at + CH] = from_acc(2 - a, 2 - b) * scale
    for side, offset in ((N, width), (E, -1), (S, -width), (W, 1)):
        code = lax.rem(code_at(edge, block(offset), side), 4)
        term = lax.dot_general(fore[code].astype(BF16), pieces[side], first, preferred_element_type=F32)
        for k in range(3):
            add(1, edge_tap(side, k), term[:, k * CH : (k + 1) * CH])
    own = corner_rows(fore)
    for q, offset in ((NW, width + 1), (NE, width - 1), (SE, -width - 1), (SW, -width + 1)):
        code = code_at(corner, block(offset), q)
        cell = jnp.where(code == 0, own[0], jnp.where(code == 1, own[1], jnp.where(code == 2, own[2], own[3])))
        left = jnp.where(row == 1, cell, 0.0).astype(BF16)
        add(1, CORNER_TAP[q], lax.dot_general(left, corners[q], first, preferred_element_type=F32))

    high = (me[0] // 2) % 2
    keep[...] = sums[high]
    send[...] = sums[1 - high]


def weights_kernel(kernel_one, kernel_two, in_one, fwd_two):
    turned_weights(kernel_one, in_one)
    plain_weights(kernel_two, fwd_two)


def outputs_kernel(hidden, vp, vm, hp, hm, fwd_two, outputs, copies, west, east):
    halo_copies(copies, hidden, west, east, vp, vm, hp, hm)
    conv_all(copies, fwd_two, outputs)


def grads_kernel(
    count, width, me, edge, corner, vp, vm, hp, hm, grad_pre, in_one, grad_fields, copies, adds
):
    mb = 4
    returned(me[0], edge, corner, count, width, in_one, vp, vm, hp, hm, adds)
    zero_copies(copies, grad_pre)

    def rows(n, first=False, last=False):
        m = n * mb
        got = conv_pairs(copies, in_one, m, mb)
        for k in range(mb):
            for part in range(2):
                g = with_adds(
                    got[k * SIDE : (k + 1) * SIDE, part * CH : (part + 1) * CH],
                    2 * (m + k) + part, adds,
                    first and k == 0 and part == 0, last and k == mb - 1 and part == 1,
                )
                grad_fields[m + k, part] = g.astype(BF16)

    def step(n, _):
        rows(n)
        return 0

    rows(0, first=True)
    lax.fori_loop(1, HALF // mb - 1, step, 0)
    rows(HALF // mb - 1, last=True)


def struct(shape, dtype=BF16):
    return jax.ShapeDtypeStruct(shape, dtype)


BLOCK = (HALF, 2, SIDE, CH)
COPIES = (3, HALF + 1, 2, SIDE, CH)
WEIGHTS = (12 * CH, 2 * CH)


def call(body, tables, arrays, outs, scratch=(), flops=0, moved=4 << 20, space=VMEM):
    return pl.pallas_call(
        body,
        out_shape=outs,
        in_specs=[SMEM] * tables + [space] * arrays,
        out_specs=tuple(VMEM for _ in outs),
        scratch_shapes=list(scratch),
        compiler_params=PARAMS,
        cost_estimate=pl.CostEstimate(flops=flops, bytes_accessed=moved, transcendentals=0),
    )


def shifted(x, by):
    size = lax.axis_size(AXES)
    return lax.ppermute(x, AXES, [(i, (i + by) % size) for i in range(size)])


def swap(x, bit):
    size = lax.axis_size(AXES)
    return lax.ppermute(x, AXES, [(i, i ^ bit) for i in range(size)])


def vertical(vp, vm, width):
    return shifted(vp, width), shifted(vm, -width)


def horizontal(vp, vm, hp, hm):
    hp = jnp.concatenate([hp, vp[STRIPS : STRIPS + 16], vm[STRIPS : STRIPS + 16]])
    hm = jnp.concatenate([hm, vp[STRIPS + 16 : VROWS], vm[STRIPS + 16 : VROWS]])
    return shifted(hp, 1), shifted(hm, -1)


FIRST = 2
HALVED = (1, 4, 64)
NARROW = (1, 4)
WHOLE = (32, 128, 8, 16)


def total(keep, send, works):
    me = lax.axis_index(AXES)
    done = {}
    steps = [0]

    def beside(sent, bit):
        work = works.get(steps[0])
        steps[0] += 1
        if work is None:
            return swap(sent, bit)
        sent, held = lax.optimization_barrier((sent, done.copy()))
        done.update(held)
        got = swap(sent, bit)
        gave = work(done)
        got, gave = lax.optimization_barrier((got, gave))
        done.update(gave)
        return got

    x = keep + beside(send, FIRST)
    rows = x.shape[0]
    for bit in HALVED:
        rows //= 2
        high = (me // bit) % 2
        send = lax.dynamic_slice_in_dim(x, (1 - high) * rows, rows, 0)
        keep = lax.dynamic_slice_in_dim(x, high * rows, rows, 0)
        if bit in NARROW:
            x = keep + beside(send.astype(BF16), bit).astype(F32)
        else:
            x = keep + beside(send, bit)
    for bit in WHOLE:
        x = x + beside(x, bit)
    x = x.astype(BF16)
    for bit in reversed(HALVED):
        high = (me // bit) % 2
        other = beside(x, bit)
        x = jnp.where(high == 1, jnp.concatenate([other, x]), jnp.concatenate([x, other]))
    other = beside(x, FIRST)
    high = (me // FIRST) % 2
    grads = jnp.where(high == 0, x, other), jnp.where(high == 0, other, x)
    return [grad.astype(F32) for grad in grads], done


def local(inputs, kernel_one, kernel_two, cotangent, edge_codes, corner_codes):
    count = lax.axis_size(AXES)
    width = lax.axis_size("face") // GRID_ROWS * lax.axis_size("sub")
    scale = 1.0 / math.sqrt(count * SIDE * SIDE)
    me = lax.axis_index(AXES).astype(jnp.int32).reshape(1)
    tables = (me, edge_codes, corner_codes)
    fields = inputs.reshape(BLOCK)
    upstream = cotangent.reshape(BLOCK)
    message = struct((VROWS, CH))
    own = struct((STRIPS, CH))
    weights = struct(WEIGHTS)
    block = struct(BLOCK)
    copies = struct(COPIES)
    wide = struct(BLOCK, F32)
    sides = (4, SIDE, CH)
    strips = pltpu.VMEM(sides, F32)
    column = pltpu.VMEM((SIDE, CH), F32)
    conv_flops = 2 * SIDE * SIDE * 9 * CH * CH

    vp, vm, hp, hm = call(
        lambda *refs: pack_kernel(count, width, *refs), 3, 2, (message, message, own, own),
        [
            strips, strips, pltpu.VMEM((2, 2, SIDE, CH), BF16),
            pltpu.VMEM((2, 2, HALF, 2, 16, CH), BF16), pltpu.SemaphoreType.DMA((2, 4)),
        ],
        space=HBM,
    )(*tables, fields, upstream)
    vp, vm, kernel_two, upstream = lax.optimization_barrier((vp, vm, kernel_two, upstream))
    vp, vm = vertical(vp, vm, width)
    in_two, up_copies, grad = call(back_kernel, 0, 2, (weights, copies, wide), (), conv_flops)(
        kernel_two, upstream
    )
    vp, vm, in_two, up_copies, grad, kernel_one, fields = lax.optimization_barrier(
        (vp, vm, in_two, up_copies, grad, kernel_one, fields)
    )
    hp, hm = horizontal(vp, vm, hp, hm)
    fwd_one, field_copies, pre = call(fore_kernel, 0, 2, (weights, copies, wide), (), conv_flops)(
        kernel_one, fields
    )
    hidden, grad_pre, vp2, vm2, hp2, hm2, fore, back, pieces, corners = call(
        lambda *refs: middle_kernel(count, width, *refs), 3, 8,
        (
            block, block, message, message, own, own, struct(sides, F32), struct(sides, F32),
            struct((4, SIDE, 3 * CH)), struct((4, 16, CH)),
        ),
        [strips, strips], conv_flops,
    )(*tables, vp, vm, hp, hm, fwd_one, in_two, pre, grad)
    keep, send = call(
        lambda *refs: sums_kernel(count, width, scale, *refs), 3, 12,
        (struct((9 * CH, CH), F32), struct((9 * CH, CH), F32)),
        [pltpu.VMEM((2 * CH, 12 * CH), F32), pltpu.VMEM((2, 9 * CH, CH), F32)],
        2 * conv_flops,
    )(*tables, vp, vm, hp, hm, hidden, grad_pre, field_copies, up_copies, fore, back, pieces, corners)

    def first_permutes(done):
        vp, vm = vertical(vp2, vm2, width)
        return dict(vp=vp, vm=vm)

    def second_permutes(done):
        hp, hm = horizontal(done["vp"], done["vm"], hp2, hm2)
        return dict(hp=hp, hm=hm)

    def make_weights(done):
        in_one, fwd_two = call(weights_kernel, 0, 2, (weights, weights))(
            done["kernel_one"], done["kernel_two"]
        )
        return dict(in_one=in_one, fwd_two=fwd_two)

    def messages(done):
        return done["vp"], done["vm"], done["hp"], done["hm"]

    def make_outputs(done):
        outputs, = call(
            outputs_kernel, 0, 6, (block,), [pltpu.VMEM(COPIES, BF16), column, column], conv_flops
        )(hidden, *messages(done), done["fwd_two"])
        return dict(outputs=outputs)

    def make_grads(done):
        grad_fields, = call(
            lambda *refs: grads_kernel(count, width, *refs), 3, 6, (block,),
            [pltpu.VMEM(COPIES, BF16), strips], conv_flops,
        )(*tables, *messages(done), grad_pre, done["in_one"])
        return dict(grad_fields=grad_fields)

    def given(work, **arrays):
        return lambda done: work({**arrays, **done})

    grads, done = total(
        keep, send,
        {
            1: first_permutes,
            2: second_permutes,
            4: given(make_weights, kernel_one=kernel_one, kernel_two=kernel_two),
            5: make_outputs,
            6: make_grads,
        },
    )
    shape = (1, 1, SIDE, SIDE, CH)
    taps = (3, 3, CH, CH)
    return (
        done["outputs"].reshape(shape), done["grad_fields"].reshape(shape),
        grads[0].reshape(taps), grads[1].reshape(taps),
    )


def solution(mesh):
    block = P("face", "sub", None, None, None)
    return jax.shard_map(
        local,
        mesh=mesh,
        in_specs=(block, P(), P(), block, P(), P()),
        out_specs=(block, block, P(), P()),
        check_vma=False,
    )
```

time: 140 us -> 138 us (0.986); the launches traced: 138 us -> 137 us
  waiting for transfers between devices: 54.2 us -> 25.6 us
  Pallas kernels: 29.1 us -> 45.5 us
  starting transfers between devices: 37.7 us -> 49.9 us
  local copies, waits for them, and re-layouts: 12.1 us -> 8.2 us
  other arithmetic: 3.61 us -> 7.13 us
    ppermute x12, waiting for transfers between devices: 44.2 us -> 19.2 us  [swap(): return lax.ppermute(x, AXES, [(i, i ^ bit) for i in range(size)])]
    ppermute x12, starting transfers between devices: 24.2 us -> 36.4 us  [swap(): return lax.ppermute(x, AXES, [(i, i ^ bit) for i in range(size)])]
    pallas_call x3 -> x7, Pallas kernels: 28 us -> 39.9 us  [the longest x1 11.5 us: local(): call(lambda *refs: sums_kernel(count, width, scale, *refs), 3, 12, (struc...]
    pallas_call x1, Pallas kernels: 1.14 us -> 5.63 us  [local(): call(lambda *refs: pack_kernel(count, width, *refs), 3, 2, (message, mess...]
    ppermute x8, waiting for transfers between devices: 9.94 us -> 6.36 us  [shifted(): return lax.ppermute(x, AXES, [(i, (i + by) % size) for i in range(size)])]
    select_n x4 -> x3, other arithmetic: 2.33 us -> 0.15 us  [total(): jnp.where(high == 1, jnp.concatenate([other, x]), jnp.concatenate([x, oth...]
    concatenate x4, other arithmetic: 0.02 us -> 2.15 us  [the longest x2 1.38 us: horizontal(): hm = jnp.concatenate([hm, vp[STRIPS + 16:VROWS], vm[STRIPS + 16:VROWS]])]
    add x8 -> x7, other arithmetic: 1.27 us -> 3.05 us  [the longest x2 1.89 us: total(): x = keep + beside(send.astype(BF16), bit).astype(F32)]
  transfers between devices with their start and end apart: 20 -> 20, of which waited for: 15 -> 14; matrix products, arithmetic and copies ran while one was open for 1% -> 1% of each run, Pallas kernels for 9% -> 16%
where the time goes in v2:
time: 138 us; the launch traced here: 137 us
  starting transfers between devices  49.9 us (36%)
  Pallas kernels  45.5 us (33%)
  waiting for transfers between devices  25.6 us (19%)
  local copies, waits for them, and re-layouts  8.2 us (6%)
  other arithmetic  7.13 us (5%)
    ppermute x12, starting transfers between devices, swap(): return lax.ppermute(x, AXES, [(i, i ^ bit) for i in range(size)])  36.4 us
    ppermute x12, waiting for transfers between devices, swap(): return lax.ppermute(x, AXES, [(i, i ^ bit) for i in range(size)])  19.2 us
    ppermute x8, starting transfers between devices, shifted(): return lax.ppermute(x, AXES, [(i, (i + by) % size) for i in range(size)])  13.4 us
    pallas_call x1, Pallas kernels, local(): call(lambda *refs: sums_kernel(count, width, scale, *refs), 3, 12, (struc...  11.5 us
    pallas_call x1, Pallas kernels, make_grads(): call(lambda *refs: grads_kernel(count, width, *refs), 3, 6, (block,), [pl...  9.56 us
    unnamed x26, local copies, waits for them, and re-layouts  8.13 us
    pallas_call x1, Pallas kernels, local(): call(lambda *refs: middle_kernel(count, width, *refs), 3, 8, (block, bloc...  6.75 us
    ppermute x8, waiting for transfers between devices, shifted(): return lax.ppermute(x, AXES, [(i, (i + by) % size) for i in range(size)])  6.36 us
  transfers between devices with their start and end apart: 20, of which 14 were waited for; matrix products, arithmetic and copies ran while one was open for 1% of the time, Pallas kernels for 16%

profile of v2, /device:TPU:1, one launch (start us, length us, event | category | flops | bytes accessed | tf_op | source)
XLA Modules:
  0.0 137.2 jit_solution(17410134037835186458)
XLA Ops:
  4.8 5.6 %shard_map.93 = (bf16[160,128]{1,0:T(8,128)(2,1)S(1)}, bf16[160,128]{1,0:T(8,128)(2,1)S(1)}, bf16[128,128]{1,0:T(8,128)(2,1)S(1)}, bf16[128,128]{1,0:T(8,128)(2,1)S(1)}) custom-call(s32[1]{0:T(128)} %bitcast.refs_0_, s32[128,2,4]{2,1,0:T(2,128)S(1)} %copy.14.refs_1_, s32[128,2,4]{2,1,0:T(2,128)S(1)} %copy.15.refs_2_, bf16[32,2,64,128]{3,2,1,0:T(8,128)(2,1)S(1)} %bitcast.11, ...), custom_call_target="tpu_custom_call" | custom-call | bytes 4194304 | tf_op jit(solution)/shard_map/pallas_call | solution.py:573
  10.4 3.8 %collective-permute-start = (bf16[160,128]{1,0:T(8,128)(2,1)S(1)}, bf16[160,128]{1,0:T(8,128)(2,1)S(1)}, u32[]{:S(2)}, u32[]{:S(2)}) collective-permute-start(bf16[160,128]{1,0:T(8,128)(2,1)S(1)} %get-tuple-element.76), channel_id=1, source_target_pairs={{0,32},{1,33},{2,34},{3,35},{4,36},{5,37},{6,38},{7,39},{8,40},{9,... | collective-permute-start | bytes 122888 | tf_op jit(solution)/shard_map/ppermute | solution.py:488
  14.2 2.3 %collective-permute-start.1 = (bf16[160,128]{1,0:T(8,128)(2,1)S(1)}, bf16[160,128]{1,0:T(8,128)(2,1)S(1)}, u32[]{:S(2)}, u32[]{:S(2)}) collective-permute-start(bf16[160,128]{1,0:T(8,128)(2,1)S(1)} %get-tuple-element.77), channel_id=1, source_target_pairs={{0,224},{1,225},{2,226},{3,227},{4,228},{5,229},{6,230},{7,231},{8... | collective-permute-start | bytes 122888 | tf_op jit(solution)/shard_map/ppermute | solution.py:488
  18.7 3.7 %shard_map.94 = (bf16[1536,256]{1,0:T(8,128)(2,1)S(1)}, bf16[3,33,2,64,128]{4,3,2,1,0:T(8,128)(2,1)S(1)}, f32[32,2,64,128]{3,2,1,0:T(8,128)S(1)}) custom-call(bf16[3,3,128,128]{3,2,1,0:T(8,128)(2,1)S(1)} %copy-done.5, bf16[32,2,64,128]{3,2,1,0:T(8,128)(2,1)S(1)} %bitcast.10), custom_call_target="tpu_custom_call" | custom-call | flops 1207959552 | bytes 4194304 | tf_op jit(solution)/shard_map/pallas_call | solution.py:583
  22.5 2.4 %collective-permute-start.3 = (bf16[160,128]{1,0:T(8,128)(2,1)S(1)}, bf16[160,128]{1,0:T(8,128)(2,1)S(1)}, u32[]{:S(2)}, u32[]{:S(2)}) collective-permute-start(bf16[160,128]{1,0:T(8,128)(2,1)S(1)} %pad_maximum_fusion.1), channel_id=1, source_target_pairs={{0,255},{1,0},{2,1},{3,2},{4,3},{5,4},{6,5},{7,6},{8,7},{9,8},{10,... | collective-permute-start | bytes 122888 | tf_op jit(solution)/shard_map/ppermute | solution.py:488
  24.9 3.6 %shard_map.95 = (bf16[1536,256]{1,0:T(8,128)(2,1)S(1)}, bf16[3,33,2,64,128]{4,3,2,1,0:T(8,128)(2,1)S(1)}, f32[32,2,64,128]{3,2,1,0:T(8,128)S(1)}) custom-call(bf16[3,3,128,128]{3,2,1,0:T(8,128)(2,1)S(1)} %copy-done.4, bf16[32,2,64,128]{3,2,1,0:T(8,128)(2,1)S(1)} %bitcast.12), custom_call_target="tpu_custom_call" | custom-call | flops 1207959552 | bytes 4194304 | tf_op jit(solution)/shard_map/pallas_call | solution.py:590
  29.2 6.7 %shard_map.96 = (bf16[32,2,64,128]{3,2,1,0:T(8,128)(2,1)S(1)}, bf16[32,2,64,128]{3,2,1,0:T(8,128)(2,1)S(1)}, bf16[160,128]{1,0:T(8,128)(2,1)S(1)}, bf16[160,128]...) custom-call(s32[1]{0:T(128)} %bitcast.refs_0_, ...), custom_call_target="tpu_custom_call" | custom-call | flops 1207959552 | bytes 4194304 | tf_op jit(solution)/shard_map/pallas_call | solution.py:593
  37.2 11.5 %shard_map.97 = (f32[1152,128]{1,0:T(8,128)S(1)}, f32[1152,128]{1,0:T(8,128)}) custom-call(s32[1]{0:T(128)} %bitcast.refs_0_, s32[128,2,4]{2,1,0:T(2,128)S(1)} %copy.14.refs_1_, s32[128,2,4]{2,1,0:T(2,128)S(1)} %copy.15.refs_2_, bf16[160,128]{1,0:T(8,128)(2,1)S(1)} %collective-permute-done.refs_3_, bf16[160,128]{1,0:T(8,128)(2,1)S(1)} %collective-permute-done.1.refs_4_, ...), custom_call_target="tpu_custom_call" | custom-call | flops 2415919104 | bytes 4194304 | tf_op jit(solution)/shard_map/pallas_call | solution.py:601
  48.6 10.7 %collective-permute-start.4 = (f32[1152,128]{1,0:T(8,128)}, f32[1152,128]{1,0:T(8,128)}, u32[]{:S(2)}, u32[]{:S(2)}) collective-permute-start(f32[1152,128]{1,0:T(8,128)} %get-tuple-element.102), channel_id=1, source_target_pairs={{0,2},{1,3},{2,0},{3,1},{4,6},{5,7},{6,4},{7,5},{8,10},{9,11},{10,... | collective-permute-start | bytes 1769480 | tf_op jit(solution)/shard_map/ppermute | solution.py:493
  59.4 2.0 %collective-permute-done.4 = f32[1152,128]{1,0:T(8,128)} collective-permute-done((f32[1152,128]{1,0:T(8,128)}, f32[1152,128]{1,0:T(8,128)}, u32[]{:S(2)}, u32[]{:S(2)}) %collective-permute-start.4) | collective-permute-done | bytes 589856 | tf_op jit(solution)/shard_map/ppermute | solution.py:493
  63.3 2.4 %collective-permute-start.7 = (bf16[160,128]{1,0:T(8,128)(2,1)}, bf16[160,128]{1,0:T(8,128)(2,1)S(1)}, u32[]{:S(2)}, u32[]{:S(2)}) collective-permute-start(bf16[160,128]{1,0:T(8,128)(2,1)} %copy-done.9), channel_id=1, source_target_pairs={{0,32},{1,33},{2,34},{3,35},{4,36},{5,37},{6,38},{7,39},{8,40},{9,... | collective-permute-start | bytes 122888 | tf_op jit(solution)/shard_map/ppermute | solution.py:488
  67.3 2.7 %collective-permute-done.7.vp.refs_3_ = bf16[160,128]{1,0:T(8,128)(2,1)S(1)} collective-permute-done((bf16[160,128]{1,0:T(8,128)(2,1)}, bf16[160,128]{1,0:T(8,128)(2,1)S(1)}, u32[]{:S(2)}, u32[]{:S(2)}) %collective-permute-start.7) | collective-permute-done | bytes 40992 | tf_op jit(solution)/shard_map/ppermute | solution.py:488
  74.0 1.7 %collective-permute-start.9 = (bf16[160,128]{1,0:T(8,128)(2,1)}, bf16[160,128]{1,0:T(8,128)(2,1)S(1)}, u32[]{:S(2)}, u32[]{:S(2)}) collective-permute-start(bf16[160,128]{1,0:T(8,128)(2,1)} %pad_maximum_fusion.2), channel_id=1, source_target_pairs={{0,255},{1,0},{2,1},{3,2},{4,3},{5,4},{6,5},{7,6},{8,7},{9,8},{10,... | collective-permute-start | bytes 122888 | tf_op jit(solution)/shard_map/ppermute | solution.py:488
  78.1 3.5 %collective-permute-done.11 = f32[144,128]{1,0:T(8,128)S(1)} collective-permute-done((f32[144,128]{1,0:T(8,128)S(1)}, f32[144,128]{1,0:T(8,128)S(1)}, u32[]{:S(2)}, u32[]{:S(2)}) %collective-permute-start.11) | collective-permute-done | bytes 73760 | tf_op jit(solution)/shard_map/ppermute | solution.py:493
  83.4 3.0 %collective-permute-done.12 = f32[144,128]{1,0:T(8,128)S(1)} collective-permute-done((f32[144,128]{1,0:T(8,128)S(1)}, f32[144,128]{1,0:T(8,128)S(1)}, u32[]{:S(2)}, u32[]{:S(2)}) %collective-permute-start.12) | collective-permute-done | bytes 73760 | tf_op jit(solution)/shard_map/ppermute | solution.py:493
  86.5 4.5 %shard_map.99 = bf16[32,2,64,128]{3,2,1,0:T(8,128)(2,1)} custom-call(bf16[32,2,64,128]{3,2,1,0:T(8,128)(2,1)S(1)} %get-tuple-element.93.refs_7_.hidden, bf16[160,128]{1,0:T(8,128)(2,1)S(1)} %collective-permute-done.7.vp.refs_3_, bf16[160,128]{1,0:T(8,128)(2,1)S(1)} %collective-permute-done.6.vm.refs_4_, ...), custom_call_target="tpu_custom_call" | custom-call | flops 1207959552 | bytes 4194304 | tf_op jit(solution)/shard_map/pallas_call | solution.py:626
  92.1 9.6 %shard_map.100 = bf16[32,2,64,128]{3,2,1,0:T(8,128)(2,1)} custom-call(s32[1]{0:T(128)} %bitcast.refs_0_, s32[128,2,4]{2,1,0:T(2,128)S(1)} %copy.14.refs_1_, s32[128,2,4]{2,1,0:T(2,128)S(1)} %copy.15.refs_2_, bf16[160,128]{1,0:T(8,128)(2,1)S(1)} %collective-permute-done.7.vp.refs_3_, bf16[160,128]{1,0:T(8,128)(2,1)S(1)} %collective-permute-done.6.vm.refs_4_, ...), custom_call_target="tpu_custom_call" | custom-call | flops 1207959552 | bytes 4194304 | tf_op jit(solution)/shard_map/pallas_call | solution.py:632
  101.7 7.3 %collective-permute-start.15 = (f32[144,128]{1,0:T(8,128)S(1)}, f32[144,128]{1,0:T(8,128)S(1)}, u32[]{:S(2)}, u32[]{:S(2)}) collective-permute-start(f32[144,128]{1,0:T(8,128)S(1)} %add.83), channel_id=1, source_target_pairs={{0,16},{1,17},{2,18},{3,19},{4,20},{5,21},{6,22},{7,23},{8,24},{9,... | collective-permute-start | bytes 221192 | tf_op jit(solution)/shard_map/ppermute | solution.py:493
  109.0 1.7 %collective-permute-done.15 = f32[144,128]{1,0:T(8,128)S(1)} collective-permute-done((f32[144,128]{1,0:T(8,128)S(1)}, f32[144,128]{1,0:T(8,128)S(1)}, u32[]{:S(2)}, u32[]{:S(2)}) %collective-permute-start.15) | collective-permute-done | bytes 73760 | tf_op jit(solution)/shard_map/ppermute | solution.py:493
  111.7 1.9 %collective-permute-done.16 = bf16[144,128]{1,0:T(8,128)(2,1)S(1)} collective-permute-done((bf16[144,128]{1,0:T(8,128)(2,1)S(1)}, bf16[144,128]{1,0:T(8,128)(2,1)S(1)}, u32[]{:S(2)}, u32[]{:S(2)}) %collective-permute-start.16) | collective-permute-done | bytes 36896 | tf_op jit(solution)/shard_map/ppermute | solution.py:493
  113.8 3.2 %collective-permute-done.17 = bf16[288,128]{1,0:T(8,128)(2,1)S(1)} collective-permute-done((bf16[288,128]{1,0:T(8,128)(2,1)S(1)}, bf16[288,128]{1,0:T(8,128)(2,1)S(1)}, u32[]{:S(2)}, u32[]{:S(2)}) %collective-permute-start.17) | collective-permute-done | bytes 73760 | tf_op jit(solution)/shard_map/ppermute | solution.py:493
  117.0 7.5 %collective-permute-start.18 = (bf16[576,128]{1,0:T(8,128)(2,1)S(1)}, bf16[576,128]{1,0:T(8,128)(2,1)S(1)}, u32[]{:S(2)}, u32[]{:S(2)}) collective-permute-start(bf16[576,128]{1,0:T(8,128)(2,1)S(1)} %maximum_select_fusion.1), channel_id=1, source_target_pairs={{0,1},{1,0},{2,3},{3,2},{4,5},{5,4},{6,7},{7,6},{8,9},{9,8},{10,11... | collective-permute-start | bytes 442376 | tf_op jit(solution)/shard_map/ppermute | solution.py:493
  124.5 2.5 %collective-permute-done.18 = bf16[576,128]{1,0:T(8,128)(2,1)S(1)} collective-permute-done((bf16[576,128]{1,0:T(8,128)(2,1)S(1)}, bf16[576,128]{1,0:T(8,128)(2,1)S(1)}, u32[]{:S(2)}, u32[]{:S(2)}) %collective-permute-start.18) | collective-permute-done | bytes 147488 | tf_op jit(solution)/shard_map/ppermute | solution.py:493
  127.1 7.1 %collective-permute-start.19 = (bf16[1152,128]{1,0:T(8,128)(2,1)S(1)}, bf16[1152,128]{1,0:T(8,128)(2,1)S(1)}, u32[]{:S(2)}, u32[]{:S(2)}) collective-permute-start(bf16[1152,128]{1,0:T(8,128)(2,1)S(1)} %maximum_select_fusion), channel_id=1, source_target_pairs={{0,2},{1,3},{2,0},{3,1},{4,6},{5,7},{6,4},{7,5},{8,10},{9,11},{10,... | collective-permute-start | bytes 884744 | tf_op jit(solution)/shard_map/ppermute | solution.py:493
  (74 shorter events, 25.3 us)
Async XLA Ops:
  4.8 20.1 %copy-start.3 = (bf16[1,1,64,64,128]{4,3,2,1,0:T(8,128)(2,1)S(1)}, bf16[1,1,64,64,128]{4,3,2,1,0:T(8,128)(2,1)}, u32[]{:S(2)}) copy-start(bf16[1,1,64,64,128]{4,3,2,1,0:T(8,128)(2,1)} %param.6) | copy-start | bytes 3145732
  4.8 20.1 %copy-start.4 = (bf16[3,3,128,128]{3,2,1,0:T(8,128)(2,1)S(1)}, bf16[3,3,128,128]{3,2,1,0:T(8,128)(2,1)}, u32[]{:S(2)}) copy-start(bf16[3,3,128,128]{3,2,1,0:T(8,128)(2,1)} %kernel_one.1) | copy-start | bytes 884740
  10.4 12.0 %collective-permute-start = (bf16[160,128]{1,0:T(8,128)(2,1)S(1)}, bf16[160,128]{1,0:T(8,128)(2,1)S(1)}, u32[]{:S(2)}, u32[]{:S(2)}) collective-permute-start(bf16[160,128]{1,0:T(8,128)(2,1)S(1)} %get-tuple-element.76), channel_id=1, source_target_pairs={{0,32},{1,33},{2,34},{3,35},{4,36},{5,37},{6,38},{7,39},{8,40},{9,... | collective-permute-start | bytes 122888 | tf_op jit(solution)/shard_map/ppermute | solution.py:488
  14.2 8.2 %collective-permute-start.1 = (bf16[160,128]{1,0:T(8,128)(2,1)S(1)}, bf16[160,128]{1,0:T(8,128)(2,1)S(1)}, u32[]{:S(2)}, u32[]{:S(2)}) collective-permute-start(bf16[160,128]{1,0:T(8,128)(2,1)S(1)} %get-tuple-element.77), channel_id=1, source_target_pairs={{0,224},{1,225},{2,226},{3,227},{4,228},{5,229},{6,230},{7,231},{8... | collective-permute-start | bytes 122888 | tf_op jit(solution)/shard_map/ppermute | solution.py:488
  22.5 6.0 %collective-permute-start.3 = (bf16[160,128]{1,0:T(8,128)(2,1)S(1)}, bf16[160,128]{1,0:T(8,128)(2,1)S(1)}, u32[]{:S(2)}, u32[]{:S(2)}) collective-permute-start(bf16[160,128]{1,0:T(8,128)(2,1)S(1)} %pad_maximum_fusion.1), channel_id=1, source_target_pairs={{0,255},{1,0},{2,1},{3,2},{4,3},{5,4},{6,5},{7,6},{8,7},{9,8},{10,... | collective-permute-start | bytes 122888 | tf_op jit(solution)/shard_map/ppermute | solution.py:488
  24.9 4.3 %collective-permute-start.2 = (bf16[160,128]{1,0:T(8,128)(2,1)S(1)}, bf16[160,128]{1,0:T(8,128)(2,1)S(1)}, u32[]{:S(2)}, u32[]{:S(2)}) collective-permute-start(bf16[160,128]{1,0:T(8,128)(2,1)S(1)} %pad_maximum_fusion), channel_id=1, source_target_pairs={{0,1},{1,2},{2,3},{3,4},{4,5},{5,6},{6,7},{7,8},{8,9},{9,10},{10,1... | collective-permute-start | bytes 122888 | tf_op jit(solution)/shard_map/ppermute | solution.py:488
  37.2 11.5 %copy-start.8 = (bf16[128,128]{1,0:T(8,128)(2,1)}, bf16[128,128]{1,0:T(8,128)(2,1)S(1)}, u32[]{:S(2)}) copy-start(bf16[128,128]{1,0:T(8,128)(2,1)S(1)} %get-tuple-element.112) | copy-start | bytes 98308
  48.6 34.5 %copy-start.6 = (bf16[3,3,128,128]{3,2,1,0:T(8,128)(2,1)S(1)}, bf16[3,3,128,128]{3,2,1,0:T(8,128)(2,1)}, u32[]{:S(2)}) copy-start(bf16[3,3,128,128]{3,2,1,0:T(8,128)(2,1)} %kernel_two.1) | copy-start | bytes 884740
  48.6 12.7 %collective-permute-start.4 = (f32[1152,128]{1,0:T(8,128)}, f32[1152,128]{1,0:T(8,128)}, u32[]{:S(2)}, u32[]{:S(2)}) collective-permute-start(f32[1152,128]{1,0:T(8,128)} %get-tuple-element.102), channel_id=1, source_target_pairs={{0,2},{1,3},{2,0},{3,1},{4,6},{5,7},{6,4},{7,5},{8,10},{9,11},{10,... | collective-permute-start | bytes 1769480 | tf_op jit(solution)/shard_map/ppermute | solution.py:493
  62.5 7.5 %collective-permute-start.5 = (bf16[576,128]{1,0:T(8,128)(2,1)S(1)}, bf16[576,128]{1,0:T(8,128)(2,1)S(1)}, u32[]{:S(2)}, u32[]{:S(2)}) collective-permute-start(bf16[576,128]{1,0:T(8,128)(2,1)S(1)} %dynamic-slice_convert_fusion), channel_id=1, source_target_pairs={{0,1},{1,0},{2,3},{3,2},{4,5},{5,4},{6,7},{7,6},{8,9},{9,8},{10,11... | collective-permute-start | bytes 442376 | tf_op jit(solution)/shard_map/ppermute | solution.py:493
  62.6 4.6 %collective-permute-start.6 = (bf16[160,128]{1,0:T(8,128)(2,1)}, bf16[160,128]{1,0:T(8,128)(2,1)S(1)}, u32[]{:S(2)}, u32[]{:S(2)}) collective-permute-start(bf16[160,128]{1,0:T(8,128)(2,1)} %copy-done.10), channel_id=1, source_target_pairs={{0,224},{1,225},{2,226},{3,227},{4,228},{5,229},{6,230},{7,231},{8... | collective-permute-start | bytes 122888 | tf_op jit(solution)/shard_map/ppermute | solution.py:488
  63.3 6.7 %collective-permute-start.7 = (bf16[160,128]{1,0:T(8,128)(2,1)}, bf16[160,128]{1,0:T(8,128)(2,1)S(1)}, u32[]{:S(2)}, u32[]{:S(2)}) collective-permute-start(bf16[160,128]{1,0:T(8,128)(2,1)} %copy-done.9), channel_id=1, source_target_pairs={{0,32},{1,33},{2,34},{3,35},{4,36},{5,37},{6,38},{7,39},{8,40},{9,... | collective-permute-start | bytes 122888 | tf_op jit(solution)/shard_map/ppermute | solution.py:488
  71.8 4.2 %collective-permute-start.10 = (bf16[160,128]{1,0:T(8,128)(2,1)S(1)}, bf16[160,128]{1,0:T(8,128)(2,1)S(1)}, u32[]{:S(2)}, u32[]{:S(2)}) collective-permute-start(bf16[160,128]{1,0:T(8,128)(2,1)S(1)} %pad_maximum_fusion.3), channel_id=1, source_target_pairs={{0,1},{1,2},{2,3},{3,4},{4,5},{5,6},{6,7},{7,8},{8,9},{9,10},{10,1... | collective-permute-start | bytes 122888 | tf_op jit(solution)/shard_map/ppermute | solution.py:488
  72.6 4.5 %collective-permute-start.8 = (bf16[288,128]{1,0:T(8,128)(2,1)S(1)}, bf16[288,128]{1,0:T(8,128)(2,1)}, u32[]{:S(2)}, u32[]{:S(2)}) collective-permute-start(bf16[288,128]{1,0:T(8,128)(2,1)S(1)} %dynamic-slice_convert_fusion.1), channel_id=1, source_target_pairs={{0,4},{1,5},{2,6},{3,7},{4,0},{5,1},{6,2},{7,3},{8,12},{9,13},{10,... | collective-permute-start | bytes 221192 | tf_op jit(solution)/shard_map/ppermute | solution.py:493
  74.0 3.1 %collective-permute-start.9 = (bf16[160,128]{1,0:T(8,128)(2,1)}, bf16[160,128]{1,0:T(8,128)(2,1)S(1)}, u32[]{:S(2)}, u32[]{:S(2)}) collective-permute-start(bf16[160,128]{1,0:T(8,128)(2,1)} %pad_maximum_fusion.2), channel_id=1, source_target_pairs={{0,255},{1,0},{2,1},{3,2},{4,3},{5,4},{6,5},{7,6},{8,7},{9,8},{10,... | collective-permute-start | bytes 122888 | tf_op jit(solution)/shard_map/ppermute | solution.py:488
  78.0 3.6 %collective-permute-start.11 = (f32[144,128]{1,0:T(8,128)S(1)}, f32[144,128]{1,0:T(8,128)S(1)}, u32[]{:S(2)}, u32[]{:S(2)}) collective-permute-start(f32[144,128]{1,0:T(8,128)S(1)} %constant_dynamic-slice_fusion), channel_id=1, source_target_pairs={{0,64},{1,65},{2,66},{3,67},{4,68},{5,69},{6,70},{7,71},{8,72},{9,... | collective-permute-start | bytes 221192 | tf_op jit(solution)/shard_map/ppermute | solution.py:493
  81.6 4.8 %collective-permute-start.12 = (f32[144,128]{1,0:T(8,128)S(1)}, f32[144,128]{1,0:T(8,128)S(1)}, u32[]{:S(2)}, u32[]{:S(2)}) collective-permute-start(f32[144,128]{1,0:T(8,128)S(1)} %dynamic-slice_add_fusion), channel_id=1, source_target_pairs={{0,32},{1,33},{2,34},{3,35},{4,36},{5,37},{6,38},{7,39},{8,40},{9,... | collective-permute-start | bytes 221192 | tf_op jit(solution)/shard_map/ppermute | solution.py:493
  86.4 4.8 %collective-permute-start.13 = (f32[144,128]{1,0:T(8,128)S(1)}, f32[144,128]{1,0:T(8,128)S(1)}, u32[]{:S(2)}, u32[]{:S(2)}) collective-permute-start(f32[144,128]{1,0:T(8,128)S(1)} %add.80), channel_id=1, source_target_pairs={{0,128},{1,129},{2,130},{3,131},{4,132},{5,133},{6,134},{7,135},{8... | collective-permute-start | bytes 221192 | tf_op jit(solution)/shard_map/ppermute | solution.py:493
  91.2 10.5 %collective-permute-start.14 = (f32[144,128]{1,0:T(8,128)S(1)}, f32[144,128]{1,0:T(8,128)S(1)}, u32[]{:S(2)}, u32[]{:S(2)}) collective-permute-start(f32[144,128]{1,0:T(8,128)S(1)} %add.81), channel_id=1, source_target_pairs={{0,8},{1,9},{2,10},{3,11},{4,12},{5,13},{6,14},{7,15},{8,0},{9,1},... | collective-permute-start | bytes 221192 | tf_op jit(solution)/shard_map/ppermute | solution.py:493
  101.7 9.0 %collective-permute-start.15 = (f32[144,128]{1,0:T(8,128)S(1)}, f32[144,128]{1,0:T(8,128)S(1)}, u32[]{:S(2)}, u32[]{:S(2)}) collective-permute-start(f32[144,128]{1,0:T(8,128)S(1)} %add.83), channel_id=1, source_target_pairs={{0,16},{1,17},{2,18},{3,19},{4,20},{5,21},{6,22},{7,23},{8,24},{9,... | collective-permute-start | bytes 221192 | tf_op jit(solution)/shard_map/ppermute | solution.py:493
  110.7 2.9 %collective-permute-start.16 = (bf16[144,128]{1,0:T(8,128)(2,1)S(1)}, bf16[144,128]{1,0:T(8,128)(2,1)S(1)}, u32[]{:S(2)}, u32[]{:S(2)}) collective-permute-start(bf16[144,128]{1,0:T(8,128)(2,1)S(1)} %add_convert_fusion), channel_id=1, source_target_pairs={{0,64},{1,65},{2,66},{3,67},{4,68},{5,69},{6,70},{7,71},{8,72},{9,... | collective-permute-start | bytes 110600 | tf_op jit(solution)/shard_map/ppermute | solution.py:493
  113.7 3.3 %collective-permute-start.17 = (bf16[288,128]{1,0:T(8,128)(2,1)S(1)}, bf16[288,128]{1,0:T(8,128)(2,1)S(1)}, u32[]{:S(2)}, u32[]{:S(2)}) collective-permute-start(bf16[288,128]{1,0:T(8,128)(2,1)S(1)} %maximum_select_fusion.2), channel_id=1, source_target_pairs={{0,4},{1,5},{2,6},{3,7},{4,0},{5,1},{6,2},{7,3},{8,12},{9,13},{10,... | collective-permute-start | bytes 221192 | tf_op jit(solution)/shard_map/ppermute | solution.py:493
  117.0 10.1 %collective-permute-start.18 = (bf16[576,128]{1,0:T(8,128)(2,1)S(1)}, bf16[576,128]{1,0:T(8,128)(2,1)S(1)}, u32[]{:S(2)}, u32[]{:S(2)}) collective-permute-start(bf16[576,128]{1,0:T(8,128)(2,1)S(1)} %maximum_select_fusion.1), channel_id=1, source_target_pairs={{0,1},{1,0},{2,3},{3,2},{4,5},{5,4},{6,7},{7,6},{8,9},{9,8},{10,11... | collective-permute-start | bytes 442376 | tf_op jit(solution)/shard_map/ppermute | solution.py:493
  127.1 8.3 %collective-permute-start.19 = (bf16[1152,128]{1,0:T(8,128)(2,1)S(1)}, bf16[1152,128]{1,0:T(8,128)(2,1)S(1)}, u32[]{:S(2)}, u32[]{:S(2)}) collective-permute-start(bf16[1152,128]{1,0:T(8,128)(2,1)S(1)} %maximum_select_fusion), channel_id=1, source_target_pairs={{0,2},{1,3},{2,0},{3,1},{4,6},{5,7},{6,4},{7,5},{8,10},{9,11},{10,... | collective-permute-start | bytes 884744 | tf_op jit(solution)/shard_map/ppermute | solution.py:493
  (8 other events, 18.2 us)

commit v3 on v2

--- a/solution.py
+++ b/solution.py
@@ -20,12 +20,12 @@
 NW, NE, SE, SW = 0, 1, 2, 3
 VMEM = pl.BlockSpec(memory_space=pltpu.VMEM)
 SMEM = pl.BlockSpec(memory_space=pltpu.SMEM)
-HBM = pl.BlockSpec(memory_space=pltpu.HBM)
-PARAMS = pltpu.CompilerParams(vmem_limit_bytes=24 * 1024 * 1024)
+ANY = pl.BlockSpec(memory_space=pl.ANY)
+ROOM = 20 << 20
 
 
 def code_at(table, block, which):
-    return table[block // 2, block % 2, which]
+    return table[block % 2, which, block // 2]
 
 
 def iota(shape, dim):
@@ -298,7 +298,7 @@
 
 
 def conv_all(copies, weights, dst):
-    mb = 4
+    mb = 16
 
     def step(n, _):
         m = n * mb
@@ -311,13 +311,13 @@
     lax.fori_loop(0, HALF // mb, step, 0)
 
 
-def back_kernel(kernel_two, upstream, in_two, up_copies, grad):
+def back_kernel(token, kernel_two, upstream, in_two, up_copies, grad):
     turned_weights(kernel_two, in_two)
     zero_copies(up_copies, upstream)
     conv_all(up_copies, in_two, grad)
 
 
-def fore_kernel(kernel_one, fields, fwd_one, copies, pre):
+def fore_kernel(token, kernel_one, fields, fwd_one, copies, pre):
     plain_weights(kernel_one, fwd_one)
     zero_copies(copies, fields)
     conv_all(copies, fwd_one, pre)
@@ -424,7 +424,7 @@
     send[...] = sums[1 - high]
 
 
-def weights_kernel(kernel_one, kernel_two, in_one, fwd_two):
+def weights_kernel(token, kernel_one, kernel_two, in_one, fwd_two):
     turned_weights(kernel_one, in_one)
     plain_weights(kernel_two, fwd_two)
 
@@ -437,7 +437,7 @@
 def grads_kernel(
     count, width, me, edge, corner, vp, vm, hp, hm, grad_pre, in_one, grad_fields, copies, adds
 ):
-    mb = 4
+    mb = 8
     returned(me[0], edge, corner, count, width, in_one, vp, vm, hp, hm, adds)
     zero_copies(copies, grad_pre)
 
@@ -462,6 +462,20 @@
     rows(HALF // mb - 1, last=True)
 
 
+def finish_kernel(me, mine, other, first, second):
+    high = (me[0] // FIRST) % 2
+
+    @pl.when(high == 0)
+    def _():
+        first[...] = mine[...].astype(F32)
+        second[...] = other[...].astype(F32)
+
+    @pl.when(high == 1)
+    def _():
+        first[...] = other[...].astype(F32)
+        second[...] = mine[...].astype(F32)
+
+
 def struct(shape, dtype=BF16):
     return jax.ShapeDtypeStruct(shape, dtype)
 
@@ -471,14 +485,14 @@
 WEIGHTS = (12 * CH, 2 * CH)
 
 
-def call(body, tables, arrays, outs, scratch=(), flops=0, moved=4 << 20, space=VMEM):
+def call(body, tables, arrays, outs, scratch=(), flops=0, moved=4 << 20, space=VMEM, room=ROOM):
     return pl.pallas_call(
         body,
         out_shape=outs,
         in_specs=[SMEM] * tables + [space] * arrays,
         out_specs=tuple(VMEM for _ in outs),
         scratch_shapes=list(scratch),
-        compiler_params=PARAMS,
+        compiler_params=pltpu.CompilerParams(vmem_limit_bytes=room),
         cost_estimate=pl.CostEstimate(flops=flops, bytes_accessed=moved, transcendentals=0),
     )
 
@@ -509,9 +523,8 @@
 WHOLE = (32, 128, 8, 16)
 
 
-def total(keep, send, works):
-    me = lax.axis_index(AXES)
-    done = {}
+def total(keep, send, done, works):
+    me = lax.axis_index(AXES).astype(jnp.int32)
     steps = [0]
 
     def beside(sent, bit):
@@ -545,10 +558,9 @@
         high = (me // bit) % 2
         other = beside(x, bit)
         x = jnp.where(high == 1, jnp.concatenate([other, x]), jnp.concatenate([x, other]))
-    other = beside(x, FIRST)
-    high = (me // FIRST) % 2
-    grads = jnp.where(high == 0, x, other), jnp.where(high == 0, other, x)
-    return [grad.astype(F32) for grad in grads], done
+    out = struct(x.shape, F32)
+    grads = call(finish_kernel, 1, 2, (out, out))(me.reshape(1), x, beside(x, FIRST))
+    return grads, done
 
 
 def local(inputs, kernel_one, kernel_two, cotangent, edge_codes, corner_codes):
@@ -556,7 +568,7 @@
     width = lax.axis_size("face") // GRID_ROWS * lax.axis_size("sub")
     scale = 1.0 / math.sqrt(count * SIDE * SIDE)
     me = lax.axis_index(AXES).astype(jnp.int32).reshape(1)
-    tables = (me, edge_codes, corner_codes)
+    tables = (me, jnp.transpose(edge_codes, (1, 2, 0)), jnp.transpose(corner_codes, (1, 2, 0)))
     fields = inputs.reshape(BLOCK)
     upstream = cotangent.reshape(BLOCK)
     message = struct((VROWS, CH))
@@ -576,19 +588,19 @@
             strips, strips, pltpu.VMEM((2, 2, SIDE, CH), BF16),
             pltpu.VMEM((2, 2, HALF, 2, 16, CH), BF16), pltpu.SemaphoreType.DMA((2, 4)),
         ],
-        space=HBM,
+        space=ANY, room=56 << 20,
     )(*tables, fields, upstream)
-    vp, vm, kernel_two, upstream = lax.optimization_barrier((vp, vm, kernel_two, upstream))
+    vp, vm, token = lax.optimization_barrier((vp, vm, me))
     vp, vm = vertical(vp, vm, width)
-    in_two, up_copies, grad = call(back_kernel, 0, 2, (weights, copies, wide), (), conv_flops)(
-        kernel_two, upstream
-    )
-    vp, vm, in_two, up_copies, grad, kernel_one, fields = lax.optimization_barrier(
-        (vp, vm, in_two, up_copies, grad, kernel_one, fields)
+    in_two, up_copies, grad = call(back_kernel, 1, 2, (weights, copies, wide), (), conv_flops)(
+        token, kernel_two, upstream
+    )
+    vp, vm, in_two, up_copies, grad, token = lax.optimization_barrier(
+        (vp, vm, in_two, up_copies, grad, token)
     )
     hp, hm = horizontal(vp, vm, hp, hm)
-    fwd_one, field_copies, pre = call(fore_kernel, 0, 2, (weights, copies, wide), (), conv_flops)(
-        kernel_one, fields
+    fwd_one, field_copies, pre = call(fore_kernel, 1, 2, (weights, copies, wide), (), conv_flops)(
+        token, kernel_one, fields
     )
     hidden, grad_pre, vp2, vm2, hp2, hm2, fore, back, pieces, corners = call(
         lambda *refs: middle_kernel(count, width, *refs), 3, 8,
@@ -598,6 +610,8 @@
         ),
         [strips, strips], conv_flops,
     )(*tables, vp, vm, hp, hm, fwd_one, in_two, pre, grad)
+    hidden, grad_pre, vp2, vm2 = lax.optimization_barrier((hidden, grad_pre, vp2, vm2))
+    vp2, vm2 = vertical(vp2, vm2, width)
     keep, send = call(
         lambda *refs: sums_kernel(count, width, scale, *refs), 3, 12,
         (struct((9 * CH, CH), F32), struct((9 * CH, CH), F32)),
@@ -605,17 +619,15 @@
         2 * conv_flops,
     )(*tables, vp, vm, hp, hm, hidden, grad_pre, field_copies, up_copies, fore, back, pieces, corners)
 
-    def first_permutes(done):
-        vp, vm = vertical(vp2, vm2, width)
-        return dict(vp=vp, vm=vm)
+    keep, send, vp2, vm2 = lax.optimization_barrier((keep, send, vp2, vm2))
 
     def second_permutes(done):
         hp, hm = horizontal(done["vp"], done["vm"], hp2, hm2)
         return dict(hp=hp, hm=hm)
 
     def make_weights(done):
-        in_one, fwd_two = call(weights_kernel, 0, 2, (weights, weights))(
-            done["kernel_one"], done["kernel_two"]
+        in_one, fwd_two = call(weights_kernel, 1, 2, (weights, weights))(
+            done["token"], kernel_one, kernel_two
         )
         return dict(in_one=in_one, fwd_two=fwd_two)
 
@@ -635,18 +647,9 @@
         )(*tables, *messages(done), grad_pre, done["in_one"])
         return dict(grad_fields=grad_fields)
 
-    def given(work, **arrays):
-        return lambda done: work({**arrays, **done})
-
     grads, done = total(
-        keep, send,
-        {
-            1: first_permutes,
-            2: second_permutes,
-            4: given(make_weights, kernel_one=kernel_one, kernel_two=kernel_two),
-            5: make_outputs,
-            6: make_grads,
-        },
+        keep, send, dict(token=token, vp=vp2, vm=vm2),
+        {1: second_permutes, 3: make_weights, 4: make_outputs, 6: make_grads},
     )
     shape = (1, 1, SIDE, SIDE, CH)
     taps = (3, 3, CH, CH)

time: 138 us -> 115 us (0.83)
  Pallas kernels: 45.5 us -> 28.2 us
  waiting for transfers between devices: 25.6 us -> 34.8 us
  local copies, waits for them, and re-layouts: 8.2 us -> 2.81 us
  other arithmetic: 7.13 us -> 2.36 us
  starting transfers between devices: 49.9 us -> 45.8 us
    ppermute x12, waiting for transfers between devices: 19.2 us -> 28.9 us  [swap(): return lax.ppermute(x, AXES, [(i, i ^ bit) for i in range(size)])]
    ppermute x12, starting transfers between devices: 36.4 us -> 30.5 us  [swap(): return lax.ppermute(x, AXES, [(i, i ^ bit) for i in range(size)])]
    unnamed x26 -> x20, local copies, waits for them, and re-layouts: 8.13 us -> 2.74 us
    pallas_call x1, Pallas kernels: 9.56 us -> 4.72 us  [make_grads(): call(lambda *refs: grads_kernel(count, width, *refs), 3, 6, (block,), [pl...]
    pallas_call x1, Pallas kernels: 6.75 us -> 2.58 us  [local(): call(lambda *refs: middle_kernel(count, width, *refs), 3, 8, (block, bloc...]
    pallas_call x1, Pallas kernels: 11.5 us -> 7.39 us  [local(): call(lambda *refs: sums_kernel(count, width, scale, *refs), 3, 12, (struc...]
    pallas_call x1, Pallas kernels: 5.63 us -> 3.36 us  [local(): call(lambda *refs: pack_kernel(count, width, *refs), 3, 2, (message, mess...]
    ppermute x8, starting transfers between devices: 13.4 us -> 15.3 us  [shifted(): return lax.ppermute(x, AXES, [(i, (i + by) % size) for i in range(size)])]
  transfers between devices with their start and end apart: 20 -> 20, of which waited for: 14 -> 13; matrix products, arithmetic and copies ran while one was open for 1% -> 0% of each run, Pallas kernels for 16% -> 18%
where the time goes in v3:
time: 115 us
  starting transfers between devices  45.8 us (40%)
  waiting for transfers between devices  34.8 us (30%)
  Pallas kernels  28.2 us (25%)
  local copies, waits for them, and re-layouts  2.81 us (2%)
  other arithmetic  2.36 us (2%)
    ppermute x12, starting transfers between devices, swap(): return lax.ppermute(x, AXES, [(i, i ^ bit) for i in range(size)])  30.5 us
    ppermute x12, waiting for transfers between devices, swap(): return lax.ppermute(x, AXES, [(i, i ^ bit) for i in range(size)])  28.9 us
    ppermute x8, starting transfers between devices, shifted(): return lax.ppermute(x, AXES, [(i, (i + by) % size) for i in range(size)])  15.3 us
    pallas_call x1, Pallas kernels, local(): call(lambda *refs: sums_kernel(count, width, scale, *refs), 3, 12, (struc...  7.39 us
    ppermute x8, waiting for transfers between devices, shifted(): return lax.ppermute(x, AXES, [(i, (i + by) % size) for i in range(size)])  5.92 us
    pallas_call x1, Pallas kernels, make_grads(): call(lambda *refs: grads_kernel(count, width, *refs), 3, 6, (block,), [pl...  4.72 us
    pallas_call x1, Pallas kernels, make_outputs(): call(outputs_kernel, 0, 6, (block,), [pltpu.VMEM(COPIES, BF16), column, c...  3.48 us
    pallas_call x1, Pallas kernels, local(): call(lambda *refs: pack_kernel(count, width, *refs), 3, 2, (message, mess...  3.36 us
  transfers between devices with their start and end apart: 20, of which 13 were waited for; matrix products, arithmetic and copies ran while one was open for 0% of the time, Pallas kernels for 18%

profile of v3, /device:TPU:1, one launch (start us, length us, event | category | flops | bytes accessed | tf_op | source)
XLA Modules:
  0.0 115.1 jit_solution(13694222003496863071)
XLA Ops:
  0.7 3.4 %shard_map.93 = (bf16[160,128]{1,0:T(8,128)(2,1)}, bf16[160,128]{1,0:T(8,128)(2,1)}, bf16[128,128]{1,0:T(8,128)(2,1)}, bf16[128,128]{1,0:T(8,128)(2,1)}) custom-call(s32[1]{0:T(128)} %bitcast.refs_0_.token.me, s32[2,4,128]{2,1,0:T(4,128)} %bitcast.13, s32[2,4,128]{2,1,0:T(4,128)} %bitcast.17, bf16[32,2,64,128]{3,2,1,0:T(8,128)(2,1)} %bitcast.11, ...), custom_call_target="tpu_custom_call" | custom-call | bytes 4194304 | tf_op jit(solution)/shard_map/pallas_call | solution.py:585
  4.0 3.8 %collective-permute-start = (bf16[160,128]{1,0:T(8,128)(2,1)}, bf16[160,128]{1,0:T(8,128)(2,1)S(1)}, u32[]{:S(2)}, u32[]{:S(2)}) collective-permute-start(bf16[160,128]{1,0:T(8,128)(2,1)} %get-tuple-element.83), channel_id=1, source_target_pairs={{0,32},{1,33},{2,34},{3,35},{4,36},{5,37},{6,38},{7,39},{8,40},{9,... | collective-permute-start | bytes 122888 | tf_op jit(solution)/shard_map/ppermute | solution.py:502
  7.8 2.3 %collective-permute-start.1 = (bf16[160,128]{1,0:T(8,128)(2,1)}, bf16[160,128]{1,0:T(8,128)(2,1)S(1)}, u32[]{:S(2)}, u32[]{:S(2)}) collective-permute-start(bf16[160,128]{1,0:T(8,128)(2,1)} %get-tuple-element.84), channel_id=1, source_target_pairs={{0,224},{1,225},{2,226},{3,227},{4,228},{5,229},{6,230},{7,231},{8... | collective-permute-start | bytes 122888 | tf_op jit(solution)/shard_map/ppermute | solution.py:502
  12.3 2.7 %shard_map.94 = (bf16[1536,256]{1,0:T(8,128)(2,1)S(1)}, bf16[3,33,2,64,128]{4,3,2,1,0:T(8,128)(2,1)S(1)}, f32[32,2,64,128]{3,2,1,0:T(8,128)S(1)}) custom-call(s32[1]{0:T(128)} %bitcast.refs_0_.token.me, bf16[3,3,128,128]{3,2,1,0:T(8,128)(2,1)S(1)} %copy-done.3, bf16[32,2,64,128]{3,2,1,0:T(8,128)(2,1)S(1)} %bitcast.10), custom_call_target="tpu_custom_call" | custom-call | flops 1207959552 | bytes 4194304 | tf_op jit(solution)/shard_map/pallas_call | solution.py:595
  15.1 2.4 %collective-permute-start.3 = (bf16[160,128]{1,0:T(8,128)(2,1)S(1)}, bf16[160,128]{1,0:T(8,128)(2,1)S(1)}, u32[]{:S(2)}, u32[]{:S(2)}) collective-permute-start(bf16[160,128]{1,0:T(8,128)(2,1)S(1)} %pad_maximum_fusion.1), channel_id=1, source_target_pairs={{0,255},{1,0},{2,1},{3,2},{4,3},{5,4},{6,5},{7,6},{8,7},{9,8},{10,... | collective-permute-start | bytes 122888 | tf_op jit(solution)/shard_map/ppermute | solution.py:502
  17.5 2.6 %shard_map.95 = (bf16[1536,256]{1,0:T(8,128)(2,1)S(1)}, bf16[3,33,2,64,128]{4,3,2,1,0:T(8,128)(2,1)S(1)}, f32[32,2,64,128]{3,2,1,0:T(8,128)S(1)}) custom-call(s32[1]{0:T(128)} %bitcast.refs_0_.token.me, bf16[3,3,128,128]{3,2,1,0:T(8,128)(2,1)S(1)} %copy-done.2, bf16[32,2,64,128]{3,2,1,0:T(8,128)(2,1)S(1)} %bitcast.12), custom_call_target="tpu_custom_call" | custom-call | flops 1207959552 | bytes 4194304 | tf_op jit(solution)/shard_map/pallas_call | solution.py:602
  21.8 2.6 %shard_map.96 = (bf16[32,2,64,128]{3,2,1,0:T(8,128)(2,1)S(1)}, bf16[32,2,64,128]{3,2,1,0:T(8,128)(2,1)S(1)}, bf16[160,128]{1,0:T(8,128)(2,1)S(1)}, bf16[160,128]...) custom-call(s32[1]{0:T(128)} %bitcast.refs_0_.token.me, ...), custom_call_target="tpu_custom_call" | custom-call | flops 1207959552 | bytes 4194304 | tf_op jit(solution)/shard_map/pallas_call | solution.py:605
  24.5 5.1 %collective-permute-start.5 = (bf16[160,128]{1,0:T(8,128)(2,1)S(1)}, bf16[160,128]{1,0:T(8,128)(2,1)S(1)}, u32[]{:S(2)}, u32[]{:S(2)}) collective-permute-start(bf16[160,128]{1,0:T(8,128)(2,1)S(1)} %get-tuple-element.113), channel_id=1, source_target_pairs={{0,224},{1,225},{2,226},{3,227},{4,228},{5,229},{6,230},{7,231},{8... | collective-permute-start | bytes 122888 | tf_op jit(solution)/shard_map/ppermute | solution.py:502
  29.5 7.4 %shard_map.97 = (f32[1152,128]{1,0:T(8,128)S(1)}, f32[1152,128]{1,0:T(8,128)}) custom-call(s32[1]{0:T(128)} %bitcast.refs_0_.token.me, s32[2,4,128]{2,1,0:T(4,128)S(1)} %bitcast.15, s32[2,4,128]{2,1,0:T(4,128)S(1)} %bitcast.19, bf16[160,128]{1,0:T(8,128)(2,1)S(1)} %collective-permute-done.refs_3_, bf16[160,128]{1,0:T(8,128)(2,1)S(1)} %collective-permute-done.1.refs_4_, ...), custom_call_target="tpu_custom_call" | custom-call | flops 2415919104 | bytes 4194304 | tf_op jit(solution)/shard_map/pallas_call | solution.py:615
  36.9 11.3 %collective-permute-start.6 = (f32[1152,128]{1,0:T(8,128)}, f32[1152,128]{1,0:T(8,128)}, u32[]{:S(2)}, u32[]{:S(2)}) collective-permute-start(f32[1152,128]{1,0:T(8,128)} %get-tuple-element.115), channel_id=1, source_target_pairs={{0,2},{1,3},{2,0},{3,1},{4,6},{5,7},{6,4},{7,5},{8,10},{9,11},{10,... | collective-permute-start | bytes 1769480 | tf_op jit(solution)/shard_map/ppermute | solution.py:507
  48.2 2.0 %collective-permute-done.6 = f32[1152,128]{1,0:T(8,128)} collective-permute-done((f32[1152,128]{1,0:T(8,128)}, f32[1152,128]{1,0:T(8,128)}, u32[]{:S(2)}, u32[]{:S(2)}) %collective-permute-start.6) | collective-permute-done | bytes 589856 | tf_op jit(solution)/shard_map/ppermute | solution.py:507
  55.3 2.7 %collective-permute-done.8.hm.refs_6_ = bf16[160,128]{1,0:T(8,128)(2,1)S(1)} collective-permute-done((bf16[160,128]{1,0:T(8,128)(2,1)S(1)}, bf16[160,128]{1,0:T(8,128)(2,1)S(1)}, u32[]{:S(2)}, u32[]{:S(2)}) %collective-permute-start.8) | collective-permute-done | bytes 40992 | tf_op jit(solution)/shard_map/ppermute | solution.py:502
  59.1 3.1 %collective-permute-done.10 = bf16[288,128]{1,0:T(8,128)(2,1)S(1)} collective-permute-done((bf16[288,128]{1,0:T(8,128)(2,1)S(1)}, bf16[288,128]{1,0:T(8,128)(2,1)S(1)}, u32[]{:S(2)}, u32[]{:S(2)}) %collective-permute-start.10) | collective-permute-done | bytes 73760 | tf_op jit(solution)/shard_map/ppermute | solution.py:507
  62.7 3.2 %collective-permute-done.11 = f32[144,128]{1,0:T(8,128)S(1)} collective-permute-done((f32[144,128]{1,0:T(8,128)S(1)}, f32[144,128]{1,0:T(8,128)S(1)}, u32[]{:S(2)}, u32[]{:S(2)}) %collective-permute-start.11) | collective-permute-done | bytes 73760 | tf_op jit(solution)/shard_map/ppermute | solution.py:507
  66.0 3.5 %shard_map.99 = bf16[32,2,64,128]{3,2,1,0:T(8,128)(2,1)} custom-call(bf16[32,2,64,128]{3,2,1,0:T(8,128)(2,1)S(1)} %get-tuple-element.102.refs_7_.hidden, bf16[160,128]{1,0:T(8,128)(2,1)S(1)} %collective-permute-done.4.vp.refs_3_, bf16[160,128]{1,0:T(8,128)(2,1)S(1)} %collective-permute-done.5.vm.refs_4_, ...), custom_call_target="tpu_custom_call" | custom-call | flops 1207959552 | bytes 4194304 | tf_op jit(solution)/shard_map/pallas_call | solution.py:638
  70.8 5.0 %collective-permute-done.13 = f32[144,128]{1,0:T(8,128)S(1)} collective-permute-done((f32[144,128]{1,0:T(8,128)S(1)}, f32[144,128]{1,0:T(8,128)S(1)}, u32[]{:S(2)}, u32[]{:S(2)}) %collective-permute-start.13) | collective-permute-done | bytes 73760 | tf_op jit(solution)/shard_map/ppermute | solution.py:507
  75.9 4.7 %shard_map.100 = bf16[32,2,64,128]{3,2,1,0:T(8,128)(2,1)} custom-call(s32[1]{0:T(128)} %bitcast.refs_0_.token.me, s32[2,4,128]{2,1,0:T(4,128)S(1)} %bitcast.16, s32[2,4,128]{2,1,0:T(4,128)S(1)} %bitcast.20, bf16[160,128]{1,0:T(8,128)(2,1)S(1)} %collective-permute-done.4.vp.refs_3_, bf16[160,128]{1,0:T(8,128)(2,1)S(1)} %collective-permute-done.5.vm.refs_4_, ...), custom_call_target="tpu_custom_call" | custom-call | flops 1207959552 | bytes 4194304 | tf_op jit(solution)/shard_map/pallas_call | solution.py:644
  80.7 2.9 %collective-permute-start.15 = (f32[144,128]{1,0:T(8,128)S(1)}, f32[144,128]{1,0:T(8,128)S(1)}, u32[]{:S(2)}, u32[]{:S(2)}) collective-permute-start(f32[144,128]{1,0:T(8,128)S(1)} %add.78), channel_id=1, source_target_pairs={{0,16},{1,17},{2,18},{3,19},{4,20},{5,21},{6,22},{7,23},{8,24},{9,... | collective-permute-start | bytes 221192 | tf_op jit(solution)/shard_map/ppermute | solution.py:507
  83.5 4.7 %collective-permute-done.15 = f32[144,128]{1,0:T(8,128)S(1)} collective-permute-done((f32[144,128]{1,0:T(8,128)S(1)}, f32[144,128]{1,0:T(8,128)S(1)}, u32[]{:S(2)}, u32[]{:S(2)}) %collective-permute-start.15) | collective-permute-done | bytes 73760 | tf_op jit(solution)/shard_map/ppermute | solution.py:507
  88.3 2.8 %collective-permute-done.16 = bf16[144,128]{1,0:T(8,128)(2,1)S(1)} collective-permute-done((bf16[144,128]{1,0:T(8,128)(2,1)S(1)}, bf16[144,128]{1,0:T(8,128)(2,1)S(1)}, u32[]{:S(2)}, u32[]{:S(2)}) %collective-permute-start.16) | collective-permute-done | bytes 36896 | tf_op jit(solution)/shard_map/ppermute | solution.py:507
  91.2 3.2 %collective-permute-done.17 = bf16[288,128]{1,0:T(8,128)(2,1)S(1)} collective-permute-done((bf16[288,128]{1,0:T(8,128)(2,1)S(1)}, bf16[288,128]{1,0:T(8,128)(2,1)S(1)}, u32[]{:S(2)}, u32[]{:S(2)}) %collective-permute-start.17) | collective-permute-done | bytes 73760 | tf_op jit(solution)/shard_map/ppermute | solution.py:507
  94.5 4.0 %collective-permute-start.18 = (bf16[576,128]{1,0:T(8,128)(2,1)S(1)}, bf16[576,128]{1,0:T(8,128)(2,1)S(1)}, u32[]{:S(2)}, u32[]{:S(2)}) collective-permute-start(bf16[576,128]{1,0:T(8,128)(2,1)S(1)} %maximum_select_fusion.1), channel_id=1, source_target_pairs={{0,1},{1,0},{2,3},{3,2},{4,5},{5,4},{6,7},{7,6},{8,9},{9,8},{10,11... | collective-permute-start | bytes 442376 | tf_op jit(solution)/shard_map/ppermute | solution.py:507
  98.4 2.5 %collective-permute-done.18 = bf16[576,128]{1,0:T(8,128)(2,1)S(1)} collective-permute-done((bf16[576,128]{1,0:T(8,128)(2,1)S(1)}, bf16[576,128]{1,0:T(8,128)(2,1)S(1)}, u32[]{:S(2)}, u32[]{:S(2)}) %collective-permute-start.18) | collective-permute-done | bytes 147488 | tf_op jit(solution)/shard_map/ppermute | solution.py:507
  101.1 11.7 %collective-permute-start.19 = (bf16[1152,128]{1,0:T(8,128)(2,1)S(1)}, bf16[1152,128]{1,0:T(8,128)(2,1)S(1)}, u32[]{:S(2)}, u32[]{:S(2)}) collective-permute-start(bf16[1152,128]{1,0:T(8,128)(2,1)S(1)} %maximum_select_fusion.mine), channel_id=1, source_target_pairs={{0,2},{1,3},{2,0},{3,1},{4,6},{5,7},{6,4},{7,5},{8,10},{9,11},{10,... | collective-permute-start | bytes 884744 | tf_op jit(solution)/shard_map/ppermute | solution.py:507
  (66 shorter events, 14.7 us)
Async XLA Ops:
  0.6 16.9 %copy-start.1 = (bf16[1,1,64,64,128]{4,3,2,1,0:T(8,128)(2,1)S(1)}, bf16[1,1,64,64,128]{4,3,2,1,0:T(8,128)(2,1)}, u32[]{:S(2)}) copy-start(bf16[1,1,64,64,128]{4,3,2,1,0:T(8,128)(2,1)} %param.6) | copy-start | bytes 3145732
  0.6 16.9 %copy-start.2 = (bf16[3,3,128,128]{3,2,1,0:T(8,128)(2,1)S(1)}, bf16[3,3,128,128]{3,2,1,0:T(8,128)(2,1)}, u32[]{:S(2)}) copy-start(bf16[3,3,128,128]{3,2,1,0:T(8,128)(2,1)} %kernel_one.3) | copy-start | bytes 884740
  4.0 11.0 %collective-permute-start = (bf16[160,128]{1,0:T(8,128)(2,1)}, bf16[160,128]{1,0:T(8,128)(2,1)S(1)}, u32[]{:S(2)}, u32[]{:S(2)}) collective-permute-start(bf16[160,128]{1,0:T(8,128)(2,1)} %get-tuple-element.83), channel_id=1, source_target_pairs={{0,32},{1,33},{2,34},{3,35},{4,36},{5,37},{6,38},{7,39},{8,40},{9,... | collective-permute-start | bytes 122888 | tf_op jit(solution)/shard_map/ppermute | solution.py:502
  7.8 7.2 %collective-permute-start.1 = (bf16[160,128]{1,0:T(8,128)(2,1)}, bf16[160,128]{1,0:T(8,128)(2,1)S(1)}, u32[]{:S(2)}, u32[]{:S(2)}) collective-permute-start(bf16[160,128]{1,0:T(8,128)(2,1)} %get-tuple-element.84), channel_id=1, source_target_pairs={{0,224},{1,225},{2,226},{3,227},{4,228},{5,229},{6,230},{7,231},{8... | collective-permute-start | bytes 122888 | tf_op jit(solution)/shard_map/ppermute | solution.py:502
  15.0 6.8 %copy-start.5 = (s32[128,2,4]{0,2,1:T(4,128)S(1)}, s32[128,2,4]{0,2,1:T(4,128)}, u32[]{:S(2)}) copy-start(s32[128,2,4]{0,2,1:T(4,128)} %param.10) | copy-start | bytes 12292
  15.1 5.0 %collective-permute-start.3 = (bf16[160,128]{1,0:T(8,128)(2,1)S(1)}, bf16[160,128]{1,0:T(8,128)(2,1)S(1)}, u32[]{:S(2)}, u32[]{:S(2)}) collective-permute-start(bf16[160,128]{1,0:T(8,128)(2,1)S(1)} %pad_maximum_fusion.1), channel_id=1, source_target_pairs={{0,255},{1,0},{2,1},{3,2},{4,3},{5,4},{6,5},{7,6},{8,7},{9,8},{10,... | collective-permute-start | bytes 122888 | tf_op jit(solution)/shard_map/ppermute | solution.py:502
  17.5 4.3 %collective-permute-start.2 = (bf16[160,128]{1,0:T(8,128)(2,1)S(1)}, bf16[160,128]{1,0:T(8,128)(2,1)S(1)}, u32[]{:S(2)}, u32[]{:S(2)}) collective-permute-start(bf16[160,128]{1,0:T(8,128)(2,1)S(1)} %pad_maximum_fusion), channel_id=1, source_target_pairs={{0,1},{1,2},{2,3},{3,4},{4,5},{5,6},{6,7},{7,8},{8,9},{9,10},{10,1... | collective-permute-start | bytes 122888 | tf_op jit(solution)/shard_map/ppermute | solution.py:502
  24.4 12.6 %collective-permute-start.4 = (bf16[160,128]{1,0:T(8,128)(2,1)S(1)}, bf16[160,128]{1,0:T(8,128)(2,1)S(1)}, u32[]{:S(2)}, u32[]{:S(2)}) collective-permute-start(bf16[160,128]{1,0:T(8,128)(2,1)S(1)} %get-tuple-element.112), channel_id=1, source_target_pairs={{0,32},{1,33},{2,34},{3,35},{4,36},{5,37},{6,38},{7,39},{8,40},{9,... | collective-permute-start | bytes 122888 | tf_op jit(solution)/shard_map/ppermute | solution.py:502
  24.5 12.5 %collective-permute-start.5 = (bf16[160,128]{1,0:T(8,128)(2,1)S(1)}, bf16[160,128]{1,0:T(8,128)(2,1)S(1)}, u32[]{:S(2)}, u32[]{:S(2)}) collective-permute-start(bf16[160,128]{1,0:T(8,128)(2,1)S(1)} %get-tuple-element.113), channel_id=1, source_target_pairs={{0,224},{1,225},{2,226},{3,227},{4,228},{5,229},{6,230},{7,231},{8... | collective-permute-start | bytes 122888 | tf_op jit(solution)/shard_map/ppermute | solution.py:502
  36.9 25.5 %copy-start.4 = (bf16[3,3,128,128]{3,2,1,0:T(8,128)(2,1)S(1)}, bf16[3,3,128,128]{3,2,1,0:T(8,128)(2,1)}, u32[]{:S(2)}) copy-start(bf16[3,3,128,128]{3,2,1,0:T(8,128)(2,1)} %kernel_two.3) | copy-start | bytes 884740
  36.9 13.3 %collective-permute-start.6 = (f32[1152,128]{1,0:T(8,128)}, f32[1152,128]{1,0:T(8,128)}, u32[]{:S(2)}, u32[]{:S(2)}) collective-permute-start(f32[1152,128]{1,0:T(8,128)} %get-tuple-element.115), channel_id=1, source_target_pairs={{0,2},{1,3},{2,0},{3,1},{4,6},{5,7},{6,4},{7,5},{8,10},{9,11},{10,... | collective-permute-start | bytes 1769480 | tf_op jit(solution)/shard_map/ppermute | solution.py:507
  51.4 3.9 %collective-permute-start.9 = (bf16[160,128]{1,0:T(8,128)(2,1)S(1)}, bf16[160,128]{1,0:T(8,128)(2,1)S(1)}, u32[]{:S(2)}, u32[]{:S(2)}) collective-permute-start(bf16[160,128]{1,0:T(8,128)(2,1)S(1)} %pad_maximum_fusion.3), channel_id=1, source_target_pairs={{0,1},{1,2},{2,3},{3,4},{4,5},{5,6},{6,7},{7,8},{8,9},{9,10},{10,1... | collective-permute-start | bytes 122888 | tf_op jit(solution)/shard_map/ppermute | solution.py:502
  51.5 6.4 %collective-permute-start.7 = (bf16[576,128]{1,0:T(8,128)(2,1)S(1)}, bf16[576,128]{1,0:T(8,128)(2,1)S(1)}, u32[]{:S(2)}, u32[]{:S(2)}) collective-permute-start(bf16[576,128]{1,0:T(8,128)(2,1)S(1)} %dynamic-slice_convert_fusion), channel_id=1, source_target_pairs={{0,1},{1,0},{2,3},{3,2},{4,5},{5,4},{6,7},{7,6},{8,9},{9,8},{10,11... | collective-permute-start | bytes 442376 | tf_op jit(solution)/shard_map/ppermute | solution.py:507
  52.1 5.8 %collective-permute-start.8 = (bf16[160,128]{1,0:T(8,128)(2,1)S(1)}, bf16[160,128]{1,0:T(8,128)(2,1)S(1)}, u32[]{:S(2)}, u32[]{:S(2)}) collective-permute-start(bf16[160,128]{1,0:T(8,128)(2,1)S(1)} %pad_maximum_fusion.2), channel_id=1, source_target_pairs={{0,255},{1,0},{2,1},{3,2},{4,3},{5,4},{6,5},{7,6},{8,7},{9,8},{10,... | collective-permute-start | bytes 122888 | tf_op jit(solution)/shard_map/ppermute | solution.py:502
  59.0 3.3 %collective-permute-start.10 = (bf16[288,128]{1,0:T(8,128)(2,1)S(1)}, bf16[288,128]{1,0:T(8,128)(2,1)S(1)}, u32[]{:S(2)}, u32[]{:S(2)}) collective-permute-start(bf16[288,128]{1,0:T(8,128)(2,1)S(1)} %dynamic-slice_convert_fusion.1), channel_id=1, source_target_pairs={{0,4},{1,5},{2,6},{3,7},{4,0},{5,1},{6,2},{7,3},{8,12},{9,13},{10,... | collective-permute-start | bytes 221192 | tf_op jit(solution)/shard_map/ppermute | solution.py:507
  62.3 3.6 %collective-permute-start.11 = (f32[144,128]{1,0:T(8,128)S(1)}, f32[144,128]{1,0:T(8,128)S(1)}, u32[]{:S(2)}, u32[]{:S(2)}) collective-permute-start(f32[144,128]{1,0:T(8,128)S(1)} %constant_dynamic-slice_fusion), channel_id=1, source_target_pairs={{0,64},{1,65},{2,66},{3,67},{4,68},{5,69},{6,70},{7,71},{8,72},{9,... | collective-permute-start | bytes 221192 | tf_op jit(solution)/shard_map/ppermute | solution.py:507
  65.9 4.8 %collective-permute-start.12 = (f32[144,128]{1,0:T(8,128)S(1)}, f32[144,128]{1,0:T(8,128)S(1)}, u32[]{:S(2)}, u32[]{:S(2)}) collective-permute-start(f32[144,128]{1,0:T(8,128)S(1)} %dynamic-slice_add_fusion), channel_id=1, source_target_pairs={{0,32},{1,33},{2,34},{3,35},{4,36},{5,37},{6,38},{7,39},{8,40},{9,... | collective-permute-start | bytes 221192 | tf_op jit(solution)/shard_map/ppermute | solution.py:507
  70.7 5.1 %collective-permute-start.13 = (f32[144,128]{1,0:T(8,128)S(1)}, f32[144,128]{1,0:T(8,128)S(1)}, u32[]{:S(2)}, u32[]{:S(2)}) collective-permute-start(f32[144,128]{1,0:T(8,128)S(1)} %add.76), channel_id=1, source_target_pairs={{0,128},{1,129},{2,130},{3,131},{4,132},{5,133},{6,134},{7,135},{8... | collective-permute-start | bytes 221192 | tf_op jit(solution)/shard_map/ppermute | solution.py:507
  75.8 4.8 %collective-permute-start.14 = (f32[144,128]{1,0:T(8,128)S(1)}, f32[144,128]{1,0:T(8,128)S(1)}, u32[]{:S(2)}, u32[]{:S(2)}) collective-permute-start(f32[144,128]{1,0:T(8,128)S(1)} %add.77), channel_id=1, source_target_pairs={{0,8},{1,9},{2,10},{3,11},{4,12},{5,13},{6,14},{7,15},{8,0},{9,1},... | collective-permute-start | bytes 221192 | tf_op jit(solution)/shard_map/ppermute | solution.py:507
  80.7 7.5 %collective-permute-start.15 = (f32[144,128]{1,0:T(8,128)S(1)}, f32[144,128]{1,0:T(8,128)S(1)}, u32[]{:S(2)}, u32[]{:S(2)}) collective-permute-start(f32[144,128]{1,0:T(8,128)S(1)} %add.78), channel_id=1, source_target_pairs={{0,16},{1,17},{2,18},{3,19},{4,20},{5,21},{6,22},{7,23},{8,24},{9,... | collective-permute-start | bytes 221192 | tf_op jit(solution)/shard_map/ppermute | solution.py:507
  88.2 2.9 %collective-permute-start.16 = (bf16[144,128]{1,0:T(8,128)(2,1)S(1)}, bf16[144,128]{1,0:T(8,128)(2,1)S(1)}, u32[]{:S(2)}, u32[]{:S(2)}) collective-permute-start(bf16[144,128]{1,0:T(8,128)(2,1)S(1)} %add_convert_fusion), channel_id=1, source_target_pairs={{0,64},{1,65},{2,66},{3,67},{4,68},{5,69},{6,70},{7,71},{8,72},{9,... | collective-permute-start | bytes 110600 | tf_op jit(solution)/shard_map/ppermute | solution.py:507
  91.1 3.3 %collective-permute-start.17 = (bf16[288,128]{1,0:T(8,128)(2,1)S(1)}, bf16[288,128]{1,0:T(8,128)(2,1)S(1)}, u32[]{:S(2)}, u32[]{:S(2)}) collective-permute-start(bf16[288,128]{1,0:T(8,128)(2,1)S(1)} %maximum_select_fusion.2), channel_id=1, source_target_pairs={{0,4},{1,5},{2,6},{3,7},{4,0},{5,1},{6,2},{7,3},{8,12},{9,13},{10,... | collective-permute-start | bytes 221192 | tf_op jit(solution)/shard_map/ppermute | solution.py:507
  94.5 6.5 %collective-permute-start.18 = (bf16[576,128]{1,0:T(8,128)(2,1)S(1)}, bf16[576,128]{1,0:T(8,128)(2,1)S(1)}, u32[]{:S(2)}, u32[]{:S(2)}) collective-permute-start(bf16[576,128]{1,0:T(8,128)(2,1)S(1)} %maximum_select_fusion.1), channel_id=1, source_target_pairs={{0,1},{1,0},{2,3},{3,2},{4,5},{5,4},{6,7},{7,6},{8,9},{9,8},{10,11... | collective-permute-start | bytes 442376 | tf_op jit(solution)/shard_map/ppermute | solution.py:507
  101.1 12.9 %collective-permute-start.19 = (bf16[1152,128]{1,0:T(8,128)(2,1)S(1)}, bf16[1152,128]{1,0:T(8,128)(2,1)S(1)}, u32[]{:S(2)}, u32[]{:S(2)}) collective-permute-start(bf16[1152,128]{1,0:T(8,128)(2,1)S(1)} %maximum_select_fusion.mine), channel_id=1, source_target_pairs={{0,2},{1,3},{2,0},{3,1},{4,6},{5,7},{6,4},{7,5},{8,10},{9,11},{10,... | collective-permute-start | bytes 884744 | tf_op jit(solution)/shard_map/ppermute | solution.py:507
  (6 other events, 17.7 us)

commit v4 on v3

--- a/solution.py
+++ b/solution.py
@@ -497,67 +497,75 @@
     )
 
 
-def shifted(x, by):
-    size = lax.axis_size(AXES)
-    return lax.ppermute(x, AXES, [(i, (i + by) % size) for i in range(size)])
-
-
 def swap(x, bit):
     size = lax.axis_size(AXES)
     return lax.ppermute(x, AXES, [(i, i ^ bit) for i in range(size)])
 
 
+def both_ways(ahead, behind, step):
+    size = lax.axis_size(AXES)
+    even = (lax.axis_index(AXES) // step) % 2 == 0
+
+    def pairs(turn):
+        return [(i, (i + (step if (i // step + turn) % 2 == 0 else -step)) % size) for i in range(size)]
+
+    one = lax.ppermute(jnp.where(even, ahead, behind), AXES, pairs(0))
+    two = lax.ppermute(jnp.where(even, behind, ahead), AXES, pairs(1))
+    return jnp.where(even, two, one), jnp.where(even, one, two)
+
+
 def vertical(vp, vm, width):
-    return shifted(vp, width), shifted(vm, -width)
+    return both_ways(vp, vm, width)
 
 
 def horizontal(vp, vm, hp, hm):
     hp = jnp.concatenate([hp, vp[STRIPS : STRIPS + 16], vm[STRIPS : STRIPS + 16]])
     hm = jnp.concatenate([hm, vp[STRIPS + 16 : VROWS], vm[STRIPS + 16 : VROWS]])
-    return shifted(hp, 1), shifted(hm, -1)
+    return both_ways(hp, hm, 1)
 
 
 FIRST = 2
-HALVED = (1, 4, 64)
-NARROW = (1, 4)
-WHOLE = (32, 128, 8, 16)
+PLANE = (128, 64, 32, 1)
+WHOLE = (4, 8, 16)
+
+
+def plane_groups(size):
+    mask = sum(PLANE)
+    rest = [i for i in range(size) if i & mask == 0]
+    members = [sum(bit for k, bit in enumerate(PLANE) if n >> k & 1) for n in range(1 << len(PLANE))]
+    return [[base + member for member in members] for base in rest]
 
 
 def total(keep, send, done, works):
     me = lax.axis_index(AXES).astype(jnp.int32)
+    groups = plane_groups(lax.axis_size(AXES))
     steps = [0]
 
+    def scatter(sent):
+        return lax.all_to_all(sent, AXES, 0, 0, axis_index_groups=groups, tiled=True)
+
     def beside(sent, bit):
+        move = scatter if bit is None else lambda sent: swap(sent, bit)
         work = works.get(steps[0])
         steps[0] += 1
         if work is None:
-            return swap(sent, bit)
+            return move(sent)
         sent, held = lax.optimization_barrier((sent, done.copy()))
         done.update(held)
-        got = swap(sent, bit)
+        got = move(sent)
         gave = work(done)
         got, gave = lax.optimization_barrier((got, gave))
         done.update(gave)
         return got
 
     x = keep + beside(send, FIRST)
-    rows = x.shape[0]
-    for bit in HALVED:
-        rows //= 2
-        high = (me // bit) % 2
-        send = lax.dynamic_slice_in_dim(x, (1 - high) * rows, rows, 0)
-        keep = lax.dynamic_slice_in_dim(x, high * rows, rows, 0)
-        if bit in NARROW:
-            x = keep + beside(send.astype(BF16), bit).astype(F32)
-        else:
-            x = keep + beside(send, bit)
+    parts = (len(groups[0]), x.shape[0] // len(groups[0]), CH)
+    spread = beside(x.astype(BF16).reshape(parts), None)
+    x = jnp.sum(spread.astype(F32), axis=0)
     for bit in WHOLE:
         x = x + beside(x, bit)
-    x = x.astype(BF16)
-    for bit in reversed(HALVED):
-        high = (me // bit) % 2
-        other = beside(x, bit)
-        x = jnp.where(high == 1, jnp.concatenate([other, x]), jnp.concatenate([x, other]))
+    spread = jnp.broadcast_to(x.astype(BF16)[None], parts)
+    x = beside(spread, None).reshape(-1, CH)
     out = struct(x.shape, F32)
     grads = call(finish_kernel, 1, 2, (out, out))(me.reshape(1), x, beside(x, FIRST))
     return grads, done
@@ -610,8 +618,8 @@
         ),
         [strips, strips], conv_flops,
     )(*tables, vp, vm, hp, hm, fwd_one, in_two, pre, grad)
-    hidden, grad_pre, vp2, vm2 = lax.optimization_barrier((hidden, grad_pre, vp2, vm2))
-    vp2, vm2 = vertical(vp2, vm2, width)
+    hidden, grad_pre, vp2, vm2, token = lax.optimization_barrier((hidden, grad_pre, vp2, vm2, token))
+    in_one, fwd_two = call(weights_kernel, 1, 2, (weights, weights))(token, kernel_one, kernel_two)
     keep, send = call(
         lambda *refs: sums_kernel(count, width, scale, *refs), 3, 12,
         (struct((9 * CH, CH), F32), struct((9 * CH, CH), F32)),
@@ -619,17 +627,10 @@
         2 * conv_flops,
     )(*tables, vp, vm, hp, hm, hidden, grad_pre, field_copies, up_copies, fore, back, pieces, corners)
 
-    keep, send, vp2, vm2 = lax.optimization_barrier((keep, send, vp2, vm2))
-
-    def second_permutes(done):
-        hp, hm = horizontal(done["vp"], done["vm"], hp2, hm2)
-        return dict(hp=hp, hm=hm)
-
-    def make_weights(done):
-        in_one, fwd_two = call(weights_kernel, 1, 2, (weights, weights))(
-            done["token"], kernel_one, kernel_two
-        )
-        return dict(in_one=in_one, fwd_two=fwd_two)
+    def second_round(done):
+        vp, vm = vertical(done["vp"], done["vm"], width)
+        hp, hm = horizontal(vp, vm, hp2, hm2)
+        return dict(vp=vp, vm=vm, hp=hp, hm=hm)
 
     def messages(done):
         return done["vp"], done["vm"], done["hp"], done["hm"]
@@ -637,19 +638,19 @@
     def make_outputs(done):
         outputs, = call(
             outputs_kernel, 0, 6, (block,), [pltpu.VMEM(COPIES, BF16), column, column], conv_flops
-        )(hidden, *messages(done), done["fwd_two"])
+        )(hidden, *messages(done), fwd_two)
         return dict(outputs=outputs)
 
     def make_grads(done):
         grad_fields, = call(
             lambda *refs: grads_kernel(count, width, *refs), 3, 6, (block,),
             [pltpu.VMEM(COPIES, BF16), strips], conv_flops,
-        )(*tables, *messages(done), grad_pre, done["in_one"])
+        )(*tables, *messages(done), grad_pre, in_one)
         return dict(grad_fields=grad_fields)
 
     grads, done = total(
-        keep, send, dict(token=token, vp=vp2, vm=vm2),
-        {1: second_permutes, 3: make_weights, 4: make_outputs, 6: make_grads},
+        keep, send, dict(vp=vp2, vm=vm2),
+        {1: second_round, 2: make_outputs, 3: make_grads},
     )
     shape = (1, 1, SIDE, SIDE, CH)
     taps = (3, 3, CH, CH)

time: 115 us -> 100 us (0.87)
  waiting for transfers between devices: 34.8 us -> 8.92 us
  blocking collectives: 0 us -> 12.7 us
  starting transfers between devices: 45.8 us -> 35.3 us
  local copies, waits for them, and re-layouts: 2.81 us -> 8.68 us
  other arithmetic: 2.36 us -> 5.85 us
    ppermute x12 -> x5, waiting for transfers between devices: 28.9 us -> 6.55 us  [swap(): return lax.ppermute(x, AXES, [(i, i ^ bit) for i in range(size)])]
    ppermute x12 -> x5, starting transfers between devices: 30.5 us -> 16.7 us  [swap(): return lax.ppermute(x, AXES, [(i, i ^ bit) for i in range(size)])]
    all_to_all x0 -> x1, blocking collectives: none -> 12.7 us  [scatter(): lax.all_to_all(sent, AXES, 0, 0, axis_index_groups=groups, tiled=True)]
    unnamed x20 -> x38, local copies, waits for them, and re-layouts: 2.74 us -> 8.63 us
    all_to_all x0 -> x1, starting transfers between devices: none -> 4.19 us  [scatter(): lax.all_to_all(sent, AXES, 0, 0, axis_index_groups=groups, tiled=True)]
    select_n x3 -> x8, other arithmetic: 0.15 us -> 4.05 us  [the longest x2 2.24 us: both_ways(): one = lax.ppermute(jnp.where(even, ahead, behind), AXES, pairs(0))]
    ppermute x8, waiting for transfers between devices: 5.92 us -> 2.29 us  [the longest x4 1.62 us: both_ways(): two = lax.ppermute(jnp.where(even, behind, ahead), AXES, pairs(1))]
    add x4 -> x0, other arithmetic: 2.15 us -> none  [the longest x1 1.12 us: total(): x = keep + beside(send, FIRST)]
  transfers between devices with their start and end apart: 20 -> 14, of which waited for: 13 -> 6; matrix products, arithmetic and copies ran while one was open for 0% -> 1% of each run, Pallas kernels for 18% -> 14%
where the time goes in v4:
time: 100 us; the launch traced here: 99.8 us
  starting transfers between devices  35.3 us (35%)
  Pallas kernels  27.4 us (27%)
  blocking collectives  12.7 us (13%)
  waiting for transfers between devices  8.92 us (9%)
  local copies, waits for them, and re-layouts  8.68 us (9%)
  other arithmetic  5.85 us (6%)
  between operations  1.01 us (1%)
    ppermute x5, starting transfers between devices, swap(): return lax.ppermute(x, AXES, [(i, i ^ bit) for i in range(size)])  16.7 us
    all_to_all x1, blocking collectives, scatter(): lax.all_to_all(sent, AXES, 0, 0, axis_index_groups=groups, tiled=True)  12.7 us
    unnamed x38, local copies, waits for them, and re-layouts  8.63 us
    ppermute x4, starting transfers between devices, both_ways(): one = lax.ppermute(jnp.where(even, ahead, behind), AXES, pairs(0))  7.4 us
    ppermute x4, starting transfers between devices, both_ways(): two = lax.ppermute(jnp.where(even, behind, ahead), AXES, pairs(1))  7.02 us
    ppermute x5, waiting for transfers between devices, swap(): return lax.ppermute(x, AXES, [(i, i ^ bit) for i in range(size)])  6.55 us
    pallas_call x1, Pallas kernels, local(): call(lambda *refs: sums_kernel(count, width, scale, *refs), 3, 12, (struc...  6.55 us
    pallas_call x1, Pallas kernels, make_grads(): call(lambda *refs: grads_kernel(count, width, *refs), 3, 6, (block,), [pl...  4.73 us
  transfers between devices with their start and end apart: 14, of which 6 were waited for; matrix products, arithmetic and copies ran while one was open for 1% of the time, Pallas kernels for 14%

profile of v4, /device:TPU:1, one launch (start us, length us, event | category | flops | bytes accessed | tf_op | source)
XLA Modules:
  0.0 99.8 jit_solution(659944994017618980)
XLA Ops:
  0.7 3.3 %shard_map.93 = (bf16[160,128]{1,0:T(8,128)(2,1)}, bf16[160,128]{1,0:T(8,128)(2,1)}, bf16[128,128]{1,0:T(8,128)(2,1)}, bf16[128,128]{1,0:T(8,128)(2,1)}) custom-call(s32[1]{0:T(128)} %bitcast.refs_0_.token.me, s32[2,4,128]{2,1,0:T(4,128)} %bitcast.17, s32[2,4,128]{2,1,0:T(4,128)} %bitcast.21, bf16[32,2,64,128]{3,2,1,0:T(8,128)(2,1)} %bitcast.15, ...), custom_call_target="tpu_custom_call" | custom-call | bytes 4194304 | tf_op jit(solution)/shard_map/pallas_call | solution.py:593
  4.0 1.4 %broadcast_select_fusion.14 = (bf16[160,128]{1,0:T(8,128)(2,1)}, bf16[160,128]{1,0:T(8,128)(2,1)}) fusion(bf16[160,128]{1,0:T(8,128)(2,1)} %get-tuple-element.70, bf16[160,128]{1,0:T(8,128)(2,1)} %get-tuple-element.69, pred[]{:T(512)S(6)} %eq.13), kind=kLoop, calls=%fused_computation.20 | loop fusion | flops 40960 | bytes 163841 | tf_op jit(solution)/shard_map/jit(_where)/select_n | solution.py:512
  5.5 3.7 %collective-permute-start.1 = (bf16[160,128]{1,0:T(8,128)(2,1)}, bf16[160,128]{1,0:T(8,128)(2,1)}, u32[]{:S(2)}, u32[]{:S(2)}) collective-permute-start(bf16[160,128]{1,0:T(8,128)(2,1)} %get-tuple-element.144), channel_id=1, source_target_pairs={{0,32},{1,33},{2,34},{3,35},{4,36},{5,37},{6,38},{7,39},{8,40},{9,... | collective-permute-start | bytes 122888 | tf_op jit(solution)/shard_map/ppermute | solution.py:512
  9.2 2.3 %collective-permute-start = (bf16[160,128]{1,0:T(8,128)(2,1)}, bf16[160,128]{1,0:T(8,128)(2,1)}, u32[]{:S(2)}, u32[]{:S(2)}) collective-permute-start(bf16[160,128]{1,0:T(8,128)(2,1)} %get-tuple-element.145), channel_id=1, source_target_pairs={{0,224},{1,225},{2,226},{3,227},{4,228},{5,229},{6,230},{7,231},{8... | collective-permute-start | bytes 122888 | tf_op jit(solution)/shard_map/ppermute | solution.py:513
  13.7 2.7 %shard_map.94 = (bf16[1536,256]{1,0:T(8,128)(2,1)S(1)}, bf16[3,33,2,64,128]{4,3,2,1,0:T(8,128)(2,1)S(1)}, f32[32,2,64,128]{3,2,1,0:T(8,128)S(1)}) custom-call(s32[1]{0:T(128)} %bitcast.refs_0_.token.me, bf16[3,3,128,128]{3,2,1,0:T(8,128)(2,1)S(1)} %copy-done.11, bf16[32,2,64,128]{3,2,1,0:T(8,128)(2,1)S(1)} %bitcast.14), custom_call_target="tpu_custom_call" | custom-call | flops 1207959552 | bytes 4194304 | tf_op jit(solution)/shard_map/pallas_call | solution.py:603
  16.4 1.3 %copy-done = f32[32,2,64,128]{3,2,1,0:T(8,128)} copy-done((f32[32,2,64,128]{3,2,1,0:T(8,128)}, f32[32,2,64,128]{3,2,1,0:T(8,128)S(1)}, u32[]{:S(2)}) %copy-start) | copy-done | bytes 2097176
  20.4 1.4 %collective-permute-start.3 = (bf16[160,128]{1,0:T(8,128)(2,1)S(1)}, bf16[160,128]{1,0:T(8,128)(2,1)S(1)}, u32[]{:S(2)}, u32[]{:S(2)}) collective-permute-start(bf16[160,128]{1,0:T(8,128)(2,1)S(1)} %get-tuple-element.140), channel_id=1, source_target_pairs={{0,1},{1,0},{2,3},{3,2},{4,5},{5,4},{6,7},{7,6},{8,9},{9,8},{10,11... | collective-permute-start | bytes 122888 | tf_op jit(solution)/shard_map/ppermute | solution.py:512
  21.8 1.6 %collective-permute-start.2 = (bf16[160,128]{1,0:T(8,128)(2,1)S(1)}, bf16[160,128]{1,0:T(8,128)(2,1)S(1)}, u32[]{:S(2)}, u32[]{:S(2)}) collective-permute-start(bf16[160,128]{1,0:T(8,128)(2,1)S(1)} %get-tuple-element.141), channel_id=1, source_target_pairs={{0,255},{1,2},{2,1},{3,4},{4,3},{5,6},{6,5},{7,8},{8,7},{9,10},{10... | collective-permute-start | bytes 122888 | tf_op jit(solution)/shard_map/ppermute | solution.py:513
  24.6 2.6 %shard_map.95 = (bf16[1536,256]{1,0:T(8,128)(2,1)S(1)}, bf16[3,33,2,64,128]{4,3,2,1,0:T(8,128)(2,1)S(1)}, f32[32,2,64,128]{3,2,1,0:T(8,128)S(1)}) custom-call(s32[1]{0:T(128)} %bitcast.refs_0_.token.me, bf16[3,3,128,128]{3,2,1,0:T(8,128)(2,1)S(1)} %copy-done.10, bf16[32,2,64,128]{3,2,1,0:T(8,128)(2,1)S(1)} %bitcast.16), custom_call_target="tpu_custom_call" | custom-call | flops 1207959552 | bytes 4194304 | tf_op jit(solution)/shard_map/pallas_call | solution.py:610
  27.3 2.6 %shard_map.96 = (bf16[32,2,64,128]{3,2,1,0:T(8,128)(2,1)S(1)}, bf16[32,2,64,128]{3,2,1,0:T(8,128)(2,1)S(1)}, bf16[160,128]{1,0:T(8,128)(2,1)S(1)}, bf16[160,128]...) custom-call(s32[1]{0:T(128)} %bitcast.refs_0_.token.me, ...), custom_call_target="tpu_custom_call" | custom-call | flops 1207959552 | bytes 4194304 | tf_op jit(solution)/shard_map/pallas_call | solution.py:613
  29.9 6.5 %shard_map.97 = (f32[1152,128]{1,0:T(8,128)S(1)}, f32[1152,128]{1,0:T(8,128)S(1)}) custom-call(s32[1]{0:T(128)} %bitcast.refs_0_.token.me, s32[2,4,128]{2,1,0:T(4,128)S(1)} %bitcast.19, s32[2,4,128]{2,1,0:T(4,128)S(1)} %bitcast.23, bf16[160,128]{1,0:T(8,128)(2,1)S(1)} %get-tuple-element.75.refs_3_, bf16[160,128]{1,0:T(8,128)(2,1)S(1)} %get-tuple-element.76.refs_4_, ...), custom_call_target="tpu_custom_call" | custom-call | flops 2415919104 | bytes 4194304 | tf_op jit(solution)/shard_map/pallas_call | solution.py:623
  36.5 6.0 %collective-permute-start.4 = (f32[1152,128]{1,0:T(8,128)S(1)}, f32[1152,128]{1,0:T(8,128)S(1)}, u32[]{:S(2)}, u32[]{:S(2)}) collective-permute-start(f32[1152,128]{1,0:T(8,128)S(1)} %get-tuple-element.97), channel_id=1, source_target_pairs={{0,2},{1,3},{2,0},{3,1},{4,6},{5,7},{6,4},{7,5},{8,10},{9,11},{10,... | collective-permute-start | bytes 1769480 | tf_op jit(solution)/shard_map/ppermute | solution.py:502
  42.5 1.6 %collective-permute-done.4 = f32[1152,128]{1,0:T(8,128)S(1)} collective-permute-done((f32[1152,128]{1,0:T(8,128)S(1)}, f32[1152,128]{1,0:T(8,128)S(1)}, u32[]{:S(2)}, u32[]{:S(2)}) %collective-permute-start.4) | collective-permute-done | bytes 589856 | tf_op jit(solution)/shard_map/ppermute | solution.py:502
  45.4 2.3 %collective-permute-start.6 = (bf16[160,128]{1,0:T(8,128)(2,1)S(1)}, bf16[160,128]{1,0:T(8,128)(2,1)S(1)}, u32[]{:S(2)}, u32[]{:S(2)}) collective-permute-start(bf16[160,128]{1,0:T(8,128)(2,1)S(1)} %get-tuple-element.137), channel_id=1, source_target_pairs={{0,32},{1,33},{2,34},{3,35},{4,36},{5,37},{6,38},{7,39},{8,40},{9,... | collective-permute-start | bytes 122888 | tf_op jit(solution)/shard_map/ppermute | solution.py:512
  47.7 4.2 %all-to-all-start = ((bf16[16,72,128]{2,1,0:T(8,128)(2,1)}), bf16[16,72,128]{2,1,0:T(8,128)(2,1)}, u32[]{:S(2)}, u32[]{:S(2)}) async-start(bf16[16,72,128]{2,1,0:T(8,128)(2,1)} %bitcast.5), calls=%async_computation | async-start | bytes 589824 | tf_op jit(solution)/shard_map/all_to_all | solution.py:545
  52.8 2.7 %collective-permute-start.8 = (bf16[160,128]{1,0:T(8,128)(2,1)S(1)}, bf16[160,128]{1,0:T(8,128)(2,1)S(1)}, u32[]{:S(2)}, u32[]{:S(2)}) collective-permute-start(bf16[160,128]{1,0:T(8,128)(2,1)S(1)} %get-tuple-element.132), channel_id=1, source_target_pairs={{0,255},{1,2},{2,1},{3,4},{4,3},{5,6},{6,5},{7,8},{8,7},{9,10},{10... | collective-permute-start | bytes 122888 | tf_op jit(solution)/shard_map/ppermute | solution.py:513
  57.6 1.6 %collective-permute-done.8 = bf16[160,128]{1,0:T(8,128)(2,1)S(1)} collective-permute-done((bf16[160,128]{1,0:T(8,128)(2,1)S(1)}, bf16[160,128]{1,0:T(8,128)(2,1)S(1)}, u32[]{:S(2)}, u32[]{:S(2)}) %collective-permute-start.8) | collective-permute-done | bytes 40992 | tf_op jit(solution)/shard_map/ppermute | solution.py:513
  62.4 3.5 %shard_map.99 = bf16[32,2,64,128]{3,2,1,0:T(8,128)(2,1)} custom-call(bf16[32,2,64,128]{3,2,1,0:T(8,128)(2,1)S(1)} %copy-done.7, bf16[160,128]{1,0:T(8,128)(2,1)S(1)} %get-tuple-element.121.vp.refs_3_, bf16[160,128]{1,0:T(8,128)(2,1)S(1)} %get-tuple-element.122.vm.refs_4_, bf16[160,128]{1,0:T(8,128)(2,1)S(1)} %get-tuple-element.123.hp.refs_5_, ...), custom_call_target="tpu_custom_call" | custom-call | flops 1207959552 | bytes 4194304 | tf_op jit(solution)/shard_map/pallas_call | solution.py:639
  65.9 3.6 %collective-permute-start.10 = (f32[72,128]{1,0:T(8,128)S(1)}, f32[72,128]{1,0:T(8,128)S(1)}, u32[]{:S(2)}, u32[]{:S(2)}) collective-permute-start(f32[72,128]{1,0:T(8,128)S(1)} %add.35), channel_id=1, source_target_pairs={{0,8},{1,9},{2,10},{3,11},{4,12},{5,13},{6,14},{7,15},{8,0},{9,1},... | collective-permute-start | bytes 110600 | tf_op jit(solution)/shard_map/ppermute | solution.py:502
  69.6 4.7 %shard_map.100 = bf16[32,2,64,128]{3,2,1,0:T(8,128)(2,1)} custom-call(s32[1]{0:T(128)} %bitcast.refs_0_.token.me, s32[2,4,128]{2,1,0:T(4,128)S(1)} %bitcast.20, s32[2,4,128]{2,1,0:T(4,128)S(1)} %bitcast.24, bf16[160,128]{1,0:T(8,128)(2,1)S(1)} %get-tuple-element.121.vp.refs_3_, bf16[160,128]{1,0:T(8,128)(2,1)S(1)} %get-tuple-element.122.vm.refs_4_, ...), custom_call_target="tpu_custom_call" | custom-call | flops 1207959552 | bytes 4194304 | tf_op jit(solution)/shard_map/pallas_call | solution.py:645
  74.3 3.1 %collective-permute-start.11 = (f32[72,128]{1,0:T(8,128)S(1)}, f32[72,128]{1,0:T(8,128)S(1)}, u32[]{:S(2)}, u32[]{:S(2)}) collective-permute-start(f32[72,128]{1,0:T(8,128)S(1)} %add.36), channel_id=1, source_target_pairs={{0,16},{1,17},{2,18},{3,19},{4,20},{5,21},{6,22},{7,23},{8,24},{9,... | collective-permute-start | bytes 110600 | tf_op jit(solution)/shard_map/ppermute | solution.py:502
  77.4 3.7 %collective-permute-done.11 = f32[72,128]{1,0:T(8,128)S(1)} collective-permute-done((f32[72,128]{1,0:T(8,128)S(1)}, f32[72,128]{1,0:T(8,128)S(1)}, u32[]{:S(2)}, u32[]{:S(2)}) %collective-permute-start.11) | collective-permute-done | bytes 36896 | tf_op jit(solution)/shard_map/ppermute | solution.py:502
  81.2 12.7 %all_to_all.10 = bf16[16,72,128]{2,1,0:T(8,128)(2,1)S(1)} all-to-all(bf16[16,72,128]{2,1,0:T(8,128)(2,1)S(1)} %broadcast_in_dim.2), channel_id=1, replica_groups={{0,128,64,192,32,160,96,224,1,129,65,193,33,161,97,225},{2,130,66,194,3..., dimensions={0} | all-to-all | bytes 589824 | tf_op jit(solution)/shard_map/all_to_all | solution.py:545
  93.8 3.7 %collective-permute-start.12 = (bf16[1152,128]{1,0:T(8,128)(2,1)S(1)}, bf16[1152,128]{1,0:T(8,128)(2,1)S(1)}, u32[]{:S(2)}, u32[]{:S(2)}) collective-permute-start(bf16[1152,128]{1,0:T(8,128)(2,1)S(1)} %bitcast.11), channel_id=1, source_target_pairs={{0,2},{1,3},{2,0},{3,1},{4,6},{5,7},{6,4},{7,5},{8,10},{9,11},{10,... | collective-permute-start | bytes 884744 | tf_op jit(solution)/shard_map/ppermute | solution.py:502
  (69 shorter events, 15.9 us)
Async XLA Ops:
  0.7 22.7 %copy-start.10 = (bf16[3,3,128,128]{3,2,1,0:T(8,128)(2,1)S(1)}, bf16[3,3,128,128]{3,2,1,0:T(8,128)(2,1)}, u32[]{:S(2)}) copy-start(bf16[3,3,128,128]{3,2,1,0:T(8,128)(2,1)} %kernel_one.3) | copy-start | bytes 884740
  5.5 13.1 %collective-permute-start.1 = (bf16[160,128]{1,0:T(8,128)(2,1)}, bf16[160,128]{1,0:T(8,128)(2,1)}, u32[]{:S(2)}, u32[]{:S(2)}) collective-permute-start(bf16[160,128]{1,0:T(8,128)(2,1)} %get-tuple-element.144), channel_id=1, source_target_pairs={{0,32},{1,33},{2,34},{3,35},{4,36},{5,37},{6,38},{7,39},{8,40},{9,... | collective-permute-start | bytes 122888 | tf_op jit(solution)/shard_map/ppermute | solution.py:512
  9.2 9.4 %collective-permute-start = (bf16[160,128]{1,0:T(8,128)(2,1)}, bf16[160,128]{1,0:T(8,128)(2,1)}, u32[]{:S(2)}, u32[]{:S(2)}) collective-permute-start(bf16[160,128]{1,0:T(8,128)(2,1)} %get-tuple-element.145), channel_id=1, source_target_pairs={{0,224},{1,225},{2,226},{3,227},{4,228},{5,229},{6,230},{7,231},{8... | collective-permute-start | bytes 122888 | tf_op jit(solution)/shard_map/ppermute | solution.py:513
  18.6 8.6 %copy-start.13 = (s32[128,2,4]{0,2,1:T(4,128)S(1)}, s32[128,2,4]{0,2,1:T(4,128)}, u32[]{:S(2)}) copy-start(s32[128,2,4]{0,2,1:T(4,128)} %param.10) | copy-start | bytes 12292
  18.6 8.7 %copy-start.14 = (s32[128,2,4]{0,2,1:T(4,128)S(1)}, s32[128,2,4]{0,2,1:T(4,128)}, u32[]{:S(2)}) copy-start(s32[128,2,4]{0,2,1:T(4,128)} %param.11) | copy-start | bytes 12292
  18.6 8.7 %copy-start.1 = (f32[32,2,64,128]{3,2,1,0:T(8,128)S(1)}, f32[32,2,64,128]{3,2,1,0:T(8,128)}, u32[]{:S(2)}) copy-start(f32[32,2,64,128]{3,2,1,0:T(8,128)} %copy-done) | copy-start | bytes 6291460
  20.4 6.8 %collective-permute-start.3 = (bf16[160,128]{1,0:T(8,128)(2,1)S(1)}, bf16[160,128]{1,0:T(8,128)(2,1)S(1)}, u32[]{:S(2)}, u32[]{:S(2)}) collective-permute-start(bf16[160,128]{1,0:T(8,128)(2,1)S(1)} %get-tuple-element.140), channel_id=1, source_target_pairs={{0,1},{1,0},{2,3},{3,2},{4,5},{5,4},{6,7},{7,6},{8,9},{9,8},{10,11... | collective-permute-start | bytes 122888 | tf_op jit(solution)/shard_map/ppermute | solution.py:512
  21.8 5.4 %collective-permute-start.2 = (bf16[160,128]{1,0:T(8,128)(2,1)S(1)}, bf16[160,128]{1,0:T(8,128)(2,1)S(1)}, u32[]{:S(2)}, u32[]{:S(2)}) collective-permute-start(bf16[160,128]{1,0:T(8,128)(2,1)S(1)} %get-tuple-element.141), channel_id=1, source_target_pairs={{0,255},{1,2},{2,1},{3,4},{4,3},{5,6},{6,5},{7,8},{8,7},{9,10},{10... | collective-permute-start | bytes 122888 | tf_op jit(solution)/shard_map/ppermute | solution.py:513
  29.9 6.6 %copy-start.4 = (bf16[32,2,64,128]{3,2,1,0:T(8,128)(2,1)}, bf16[32,2,64,128]{3,2,1,0:T(8,128)(2,1)S(1)}, u32[]{:S(2)}) copy-start(bf16[32,2,64,128]{3,2,1,0:T(8,128)(2,1)S(1)} %get-tuple-element.89.refs_8_.refs_7_) | copy-start | bytes 3145732
  29.9 6.6 %copy-start.6 = (bf16[32,2,64,128]{3,2,1,0:T(8,128)(2,1)}, bf16[32,2,64,128]{3,2,1,0:T(8,128)(2,1)S(1)}, u32[]{:S(2)}) copy-start(bf16[32,2,64,128]{3,2,1,0:T(8,128)(2,1)S(1)} %get-tuple-element.88.refs_7_.hidden) | copy-start | bytes 3145732
  29.9 6.6 %copy-start.15 = (bf16[128,128]{1,0:T(8,128)(2,1)}, bf16[128,128]{1,0:T(8,128)(2,1)S(1)}, u32[]{:S(2)}) copy-start(bf16[128,128]{1,0:T(8,128)(2,1)S(1)} %get-tuple-element.101) | copy-start | bytes 98308
  29.9 6.6 %copy-start.16 = (bf16[128,128]{1,0:T(8,128)(2,1)}, bf16[128,128]{1,0:T(8,128)(2,1)S(1)}, u32[]{:S(2)}) copy-start(bf16[128,128]{1,0:T(8,128)(2,1)S(1)} %get-tuple-element.104) | copy-start | bytes 98308
  36.5 24.8 %copy-start.7 = (bf16[32,2,64,128]{3,2,1,0:T(8,128)(2,1)S(1)}, bf16[32,2,64,128]{3,2,1,0:T(8,128)(2,1)}, u32[]{:S(2)}) copy-start(bf16[32,2,64,128]{3,2,1,0:T(8,128)(2,1)} %copy-done.6) | copy-start | bytes 3145732
  36.5 7.7 %collective-permute-start.4 = (f32[1152,128]{1,0:T(8,128)S(1)}, f32[1152,128]{1,0:T(8,128)S(1)}, u32[]{:S(2)}, u32[]{:S(2)}) collective-permute-start(f32[1152,128]{1,0:T(8,128)S(1)} %get-tuple-element.97), channel_id=1, source_target_pairs={{0,2},{1,3},{2,0},{3,1},{4,6},{5,7},{6,4},{7,5},{8,10},{9,11},{10,... | collective-permute-start | bytes 1769480 | tf_op jit(solution)/shard_map/ppermute | solution.py:502
  44.9 7.0 %collective-permute-start.5 = (bf16[160,128]{1,0:T(8,128)(2,1)S(1)}, bf16[160,128]{1,0:T(8,128)(2,1)S(1)}, u32[]{:S(2)}, u32[]{:S(2)}) collective-permute-start(bf16[160,128]{1,0:T(8,128)(2,1)S(1)} %get-tuple-element.136), channel_id=1, source_target_pairs={{0,224},{1,225},{2,226},{3,227},{4,228},{5,229},{6,230},{7,231},{8... | collective-permute-start | bytes 122888 | tf_op jit(solution)/shard_map/ppermute | solution.py:513
  45.4 24.1 %copy-start.5 = (bf16[32,2,64,128]{3,2,1,0:T(8,128)(2,1)S(1)}, bf16[32,2,64,128]{3,2,1,0:T(8,128)(2,1)}, u32[]{:S(2)}) copy-start(bf16[32,2,64,128]{3,2,1,0:T(8,128)(2,1)} %copy-done.4) | copy-start | bytes 3145732
  45.4 6.5 %collective-permute-start.6 = (bf16[160,128]{1,0:T(8,128)(2,1)S(1)}, bf16[160,128]{1,0:T(8,128)(2,1)S(1)}, u32[]{:S(2)}, u32[]{:S(2)}) collective-permute-start(bf16[160,128]{1,0:T(8,128)(2,1)S(1)} %get-tuple-element.137), channel_id=1, source_target_pairs={{0,32},{1,33},{2,34},{3,35},{4,36},{5,37},{6,38},{7,39},{8,40},{9,... | collective-permute-start | bytes 122888 | tf_op jit(solution)/shard_map/ppermute | solution.py:512
  47.7 12.3 %all-to-all-start = ((bf16[16,72,128]{2,1,0:T(8,128)(2,1)}), bf16[16,72,128]{2,1,0:T(8,128)(2,1)}, u32[]{:S(2)}, u32[]{:S(2)}) async-start(bf16[16,72,128]{2,1,0:T(8,128)(2,1)} %bitcast.5), calls=%async_computation | async-start | bytes 589824 | tf_op jit(solution)/shard_map/all_to_all | solution.py:545
  52.8 6.4 %collective-permute-start.8 = (bf16[160,128]{1,0:T(8,128)(2,1)S(1)}, bf16[160,128]{1,0:T(8,128)(2,1)S(1)}, u32[]{:S(2)}, u32[]{:S(2)}) collective-permute-start(bf16[160,128]{1,0:T(8,128)(2,1)S(1)} %get-tuple-element.132), channel_id=1, source_target_pairs={{0,255},{1,2},{2,1},{3,4},{4,3},{5,6},{6,5},{7,8},{8,7},{9,10},{10... | collective-permute-start | bytes 122888 | tf_op jit(solution)/shard_map/ppermute | solution.py:513
  55.5 4.4 %collective-permute-start.7 = (bf16[160,128]{1,0:T(8,128)(2,1)S(1)}, bf16[160,128]{1,0:T(8,128)(2,1)S(1)}, u32[]{:S(2)}, u32[]{:S(2)}) collective-permute-start(bf16[160,128]{1,0:T(8,128)(2,1)S(1)} %get-tuple-element.133), channel_id=1, source_target_pairs={{0,1},{1,0},{2,3},{3,2},{4,5},{5,4},{6,7},{7,6},{8,9},{9,8},{10,11... | collective-permute-start | bytes 122888 | tf_op jit(solution)/shard_map/ppermute | solution.py:512
  61.0 4.9 %collective-permute-start.9 = (f32[72,128]{1,0:T(8,128)S(1)}, f32[72,128]{1,0:T(8,128)S(1)}, u32[]{:S(2)}, u32[]{:S(2)}) collective-permute-start(f32[72,128]{1,0:T(8,128)S(1)} %convert_reduce_fusion), channel_id=1, source_target_pairs={{0,4},{1,5},{2,6},{3,7},{4,0},{5,1},{6,2},{7,3},{8,12},{9,13},{10,... | collective-permute-start | bytes 110600 | tf_op jit(solution)/shard_map/ppermute | solution.py:502
  65.9 8.4 %collective-permute-start.10 = (f32[72,128]{1,0:T(8,128)S(1)}, f32[72,128]{1,0:T(8,128)S(1)}, u32[]{:S(2)}, u32[]{:S(2)}) collective-permute-start(f32[72,128]{1,0:T(8,128)S(1)} %add.35), channel_id=1, source_target_pairs={{0,8},{1,9},{2,10},{3,11},{4,12},{5,13},{6,14},{7,15},{8,0},{9,1},... | collective-permute-start | bytes 110600 | tf_op jit(solution)/shard_map/ppermute | solution.py:502
  74.3 6.8 %collective-permute-start.11 = (f32[72,128]{1,0:T(8,128)S(1)}, f32[72,128]{1,0:T(8,128)S(1)}, u32[]{:S(2)}, u32[]{:S(2)}) collective-permute-start(f32[72,128]{1,0:T(8,128)S(1)} %add.36), channel_id=1, source_target_pairs={{0,16},{1,17},{2,18},{3,19},{4,20},{5,21},{6,22},{7,23},{8,24},{9,... | collective-permute-start | bytes 110600 | tf_op jit(solution)/shard_map/ppermute | solution.py:502
  93.8 4.9 %collective-permute-start.12 = (bf16[1152,128]{1,0:T(8,128)(2,1)S(1)}, bf16[1152,128]{1,0:T(8,128)(2,1)S(1)}, u32[]{:S(2)}, u32[]{:S(2)}) collective-permute-start(bf16[1152,128]{1,0:T(8,128)(2,1)S(1)} %bitcast.11), channel_id=1, source_target_pairs={{0,2},{1,3},{2,0},{3,1},{4,6},{5,7},{6,4},{7,5},{8,10},{9,11},{10,... | collective-permute-start | bytes 884744 | tf_op jit(solution)/shard_map/ppermute | solution.py:502
  (9 other events, 11.3 us)

commit v5 on v4

--- a/solution.py
+++ b/solution.py
@@ -20,7 +20,6 @@
 NW, NE, SE, SW = 0, 1, 2, 3
 VMEM = pl.BlockSpec(memory_space=pltpu.VMEM)
 SMEM = pl.BlockSpec(memory_space=pltpu.SMEM)
-ANY = pl.BlockSpec(memory_space=pl.ANY)
 ROOM = 20 << 20
 
 
@@ -93,6 +92,26 @@
     vm[STRIPS + 16 : VROWS] = relayed(-width - 1, SE, NW)
     strips(hp, 1, W, E)
     strips(hm, -1, E, W)
+
+
+def choose(even, one, two, ahead, behind):
+    @pl.when(even)
+    def _():
+        ahead[...] = one[...]
+        behind[...] = two[...]
+
+    @pl.when(jnp.logical_not(even))
+    def _():
+        ahead[...] = two[...]
+        behind[...] = one[...]
+
+
+def even_row(me, width):
+    return (me // width) % 2 == 0
+
+
+def even_column(me):
+    return me % 2 == 0
 
 
 def put_row(dst, pair, part, row, west, east):
@@ -253,25 +272,32 @@
         adds[side] = adds[side] + jnp.where(row == place, given, 0.0)
 
 
-def pack_kernel(
-    count, width, me, edge, corner, fields, upstream, vp, vm, hp, hm, fore, back, rows, columns, sems
-):
-    copies = []
-    for k, source in enumerate((fields, upstream)):
-        for j, (part, dst) in enumerate((
-            (source.at[0, 0], rows.at[k, 0]),
-            (source.at[HALF - 1, 1], rows.at[k, 1]),
-            (source.at[:, :, pl.ds(0, 16), :], columns.at[k, 0]),
-            (source.at[:, :, pl.ds(SIDE - 16, 16), :], columns.at[k, 1]),
-        )):
-            copies.append(pltpu.make_async_copy(part, dst, sems.at[k, j]))
-    for copy in copies:
-        copy.start()
-    for copy in copies:
-        copy.wait()
-    for k, dst in enumerate((fore, back)):
-        strips_from(rows[k, 0], rows[k, 1], columns[k, 0], columns[k, 1], dst)
+def pack_kernel(count, width, me, edge, corner, fields, upstream, va, vb, hp, hm, here, fore, back, vp, vm):
+    here[...] = upstream[...]
+    side_strips(fields, fore)
+    side_strips(upstream, back)
     pack(me[0], edge, corner, count, width, fore, back, vp, vm, hp, hm)
+    choose(even_row(me[0], width), vp, vm, va, vb)
+
+
+def relay_kernel(width, me, one, two, hp, hm, vp, vm, ha, hb):
+    choose(even_row(me[0], width), two, one, vp, vm)
+
+    def send(even, right, left):
+        @pl.when(even)
+        def _():
+            for own, dst, start in ((hp, right, STRIPS), (hm, left, STRIPS + 16)):
+                dst[0:STRIPS] = own[...]
+                dst[STRIPS : STRIPS + 16] = vp[start : start + 16]
+                dst[STRIPS + 16 : VROWS] = vm[start : start + 16]
+
+    even = even_column(me[0])
+    send(even, ha, hb)
+    send(jnp.logical_not(even), hb, ha)
+
+
+def name_kernel(me, one, two, hp, hm):
+    choose(even_column(me[0]), two, one, hp, hm)
 
 
 def plain_weights(source, dst):
@@ -324,9 +350,11 @@
 
 
 def middle_kernel(
-    count, width, me, edge, corner, vp, vm, hp, hm, fwd_one, in_two, pre, grad,
-    hidden, grad_pre, vp2, vm2, hp2, hm2, fore, back, pieces, corners, grad_adds, pre_adds,
+    count, width, me, edge, corner, vp, vm, one_side, other_side, fwd_one, in_two, pre, grad,
+    hidden, grad_pre, va2, vb2, hp2, hm2, fore, back, pieces, corners, hp, hm,
+    grad_adds, pre_adds, vp2, vm2,
 ):
+    choose(even_column(me[0]), other_side, one_side, hp, hm)
     returned(me[0], edge, corner, count, width, in_two, vp, vm, hp, hm, grad_adds, pieces, corners)
     received(fwd_one, vp, vm, hp, hm, pre_adds)
 
@@ -351,11 +379,12 @@
     side_strips(hidden, fore)
     side_strips(grad_pre, back)
     pack(me[0], edge, corner, count, width, fore, back, vp2, vm2, hp2, hm2)
+    choose(even_row(me[0], width), vp2, vm2, va2, vb2)
 
 
 def sums_kernel(
-    count, width, scale, me, edge, corner, vp, vm, hp, hm, hidden, grad_pre, field_copies, up_copies,
-    fore, back, pieces, corners, keep, send, acc, sums,
+    count, width, scale, kept, me, edge, corner, vp, vm, hp, hm, hidden, grad_pre, field_copies, up_copies,
+    fore, back, pieces, corners, sums, acc,
 ):
     gb = 8
     first = (((0,), (0,)), ((), ()))
@@ -377,51 +406,53 @@
         high = low + 3 * CH
         return acc[0:CH, low : low + CH] + acc[CH : 2 * CH, high : high + CH]
 
-    def add(half, tap, term):
+    def add(tap, term):
         at = (tap[0] * 3 + tap[1]) * CH
-        sums[half, at : at + CH] = sums[half, at : at + CH] + term * scale
+        sums[at : at + CH] = sums[at : at + CH] + term * scale
 
     def block(offset):
         return lax.rem(me[0] + offset + 2 * count, count)
 
     row = iota((16, CH), 0)
-    gather(grad_pre, field_copies)
-    for a in range(3):
-        for b in range(3):
-            at = (a * 3 + b) * CH
-            sums[0, at : at + CH] = from_acc(a, b).T * scale
-    for side, message in pad_sides(vp, vm, hp, hm):
-        strip = back[side]
-        up, down = neighbours(strip)
-        joined = jnp.concatenate([up, strip, down], axis=1).astype(BF16)
-        term = lax.dot_general(message[0:SIDE], joined, first, preferred_element_type=F32)
-        for k in range(3):
-            add(0, edge_tap(side, k), term[:, k * CH : (k + 1) * CH])
-    own = corner_rows(back)
-    for q, message, start in pad_corners(hp, hm):
-        right = jnp.where(row == 0, own[q], 0.0).astype(BF16)
-        add(0, CORNER_TAP[q], lax.dot_general(message[start : start + 16], right, first, preferred_element_type=F32))
-
-    gather(hidden, up_copies)
-    for a in range(3):
-        for b in range(3):
-            at = (a * 3 + b) * CH
-            sums[1, at : at + CH] = from_acc(2 - a, 2 - b) * scale
-    for side, offset in ((N, width), (E, -1), (S, -width), (W, 1)):
-        code = lax.rem(code_at(edge, block(offset), side), 4)
-        term = lax.dot_general(fore[code].astype(BF16), pieces[side], first, preferred_element_type=F32)
-        for k in range(3):
-            add(1, edge_tap(side, k), term[:, k * CH : (k + 1) * CH])
-    own = corner_rows(fore)
-    for q, offset in ((NW, width + 1), (NE, width - 1), (SE, -width - 1), (SW, -width + 1)):
-        code = code_at(corner, block(offset), q)
-        cell = jnp.where(code == 0, own[0], jnp.where(code == 1, own[1], jnp.where(code == 2, own[2], own[3])))
-        left = jnp.where(row == 1, cell, 0.0).astype(BF16)
-        add(1, CORNER_TAP[q], lax.dot_general(left, corners[q], first, preferred_element_type=F32))
-
-    high = (me[0] // 2) % 2
-    keep[...] = sums[high]
-    send[...] = sums[1 - high]
+    high = (me[0] // FIRST) % 2
+
+    @pl.when(high == (0 if kept else 1))
+    def _():
+        gather(grad_pre, field_copies)
+        for a in range(3):
+            for b in range(3):
+                at = (a * 3 + b) * CH
+                sums[at : at + CH] = from_acc(a, b).T * scale
+        for side, message in pad_sides(vp, vm, hp, hm):
+            strip = back[side]
+            up, down = neighbours(strip)
+            joined = jnp.concatenate([up, strip, down], axis=1).astype(BF16)
+            term = lax.dot_general(message[0:SIDE], joined, first, preferred_element_type=F32)
+            for k in range(3):
+                add(edge_tap(side, k), term[:, k * CH : (k + 1) * CH])
+        own = corner_rows(back)
+        for q, message, start in pad_corners(hp, hm):
+            right = jnp.where(row == 0, own[q], 0.0).astype(BF16)
+            add(CORNER_TAP[q], lax.dot_general(message[start : start + 16], right, first, preferred_element_type=F32))
+
+    @pl.when(high == (1 if kept else 0))
+    def _():
+        gather(hidden, up_copies)
+        for a in range(3):
+            for b in range(3):
+                at = (a * 3 + b) * CH
+                sums[at : at + CH] = from_acc(2 - a, 2 - b) * scale
+        for side, offset in ((N, width), (E, -1), (S, -width), (W, 1)):
+            code = lax.rem(code_at(edge, block(offset), side), 4)
+            term = lax.dot_general(fore[code].astype(BF16), pieces[side], first, preferred_element_type=F32)
+            for k in range(3):
+                add(edge_tap(side, k), term[:, k * CH : (k + 1) * CH])
+        own = corner_rows(fore)
+        for q, offset in ((NW, width + 1), (NE, width - 1), (SE, -width - 1), (SW, -width + 1)):
+            code = code_at(corner, block(offset), q)
+            cell = jnp.where(code == 0, own[0], jnp.where(code == 1, own[1], jnp.where(code == 2, own[2], own[3])))
+            left = jnp.where(row == 1, cell, 0.0).astype(BF16)
+            add(CORNER_TAP[q], lax.dot_general(left, corners[q], first, preferred_element_type=F32))
 
 
 def weights_kernel(token, kernel_one, kernel_two, in_one, fwd_two):
@@ -485,14 +516,14 @@
 WEIGHTS = (12 * CH, 2 * CH)
 
 
-def call(body, tables, arrays, outs, scratch=(), flops=0, moved=4 << 20, space=VMEM, room=ROOM):
+def call(body, tables, arrays, outs, scratch=(), flops=0, moved=4 << 20):
     return pl.pallas_call(
         body,
         out_shape=outs,
-        in_specs=[SMEM] * tables + [space] * arrays,
+        in_specs=[SMEM] * tables + [VMEM] * arrays,
         out_specs=tuple(VMEM for _ in outs),
         scratch_shapes=list(scratch),
-        compiler_params=pltpu.CompilerParams(vmem_limit_bytes=room),
+        compiler_params=pltpu.CompilerParams(vmem_limit_bytes=ROOM),
         cost_estimate=pl.CostEstimate(flops=flops, bytes_accessed=moved, transcendentals=0),
     )
 
@@ -502,26 +533,13 @@
     return lax.ppermute(x, AXES, [(i, i ^ bit) for i in range(size)])
 
 
-def both_ways(ahead, behind, step):
+def both_ways(one, two, step):
     size = lax.axis_size(AXES)
-    even = (lax.axis_index(AXES) // step) % 2 == 0
 
     def pairs(turn):
         return [(i, (i + (step if (i // step + turn) % 2 == 0 else -step)) % size) for i in range(size)]
 
-    one = lax.ppermute(jnp.where(even, ahead, behind), AXES, pairs(0))
-    two = lax.ppermute(jnp.where(even, behind, ahead), AXES, pairs(1))
-    return jnp.where(even, two, one), jnp.where(even, one, two)
-
-
-def vertical(vp, vm, width):
-    return both_ways(vp, vm, width)
-
-
-def horizontal(vp, vm, hp, hm):
-    hp = jnp.concatenate([hp, vp[STRIPS : STRIPS + 16], vm[STRIPS : STRIPS + 16]])
-    hm = jnp.concatenate([hm, vp[STRIPS + 16 : VROWS], vm[STRIPS + 16 : VROWS]])
-    return both_ways(hp, hm, 1)
+    return lax.ppermute(one, AXES, pairs(0)), lax.ppermute(two, AXES, pairs(1))
 
 
 FIRST = 2
@@ -536,7 +554,7 @@
     return [[base + member for member in members] for base in rest]
 
 
-def total(keep, send, done, works):
+def total(send, done, works):
     me = lax.axis_index(AXES).astype(jnp.int32)
     groups = plane_groups(lax.axis_size(AXES))
     steps = [0]
@@ -558,7 +576,8 @@
         done.update(gave)
         return got
 
-    x = keep + beside(send, FIRST)
+    x = beside(send, FIRST)
+    x = done["keep"] + x
     parts = (len(groups[0]), x.shape[0] // len(groups[0]), CH)
     spread = beside(x.astype(BF16).reshape(parts), None)
     x = jnp.sum(spread.astype(F32), axis=0)
@@ -583,53 +602,68 @@
     own = struct((STRIPS, CH))
     weights = struct(WEIGHTS)
     block = struct(BLOCK)
+    taps = struct((3, 3, CH, CH))
     copies = struct(COPIES)
     wide = struct(BLOCK, F32)
     sides = (4, SIDE, CH)
     strips = pltpu.VMEM(sides, F32)
+    vertical_pair = pltpu.VMEM((VROWS, CH), BF16)
     column = pltpu.VMEM((SIDE, CH), F32)
     conv_flops = 2 * SIDE * SIDE * 9 * CH * CH
 
-    vp, vm, hp, hm = call(
-        lambda *refs: pack_kernel(count, width, *refs), 3, 2, (message, message, own, own),
-        [
-            strips, strips, pltpu.VMEM((2, 2, SIDE, CH), BF16),
-            pltpu.VMEM((2, 2, HALF, 2, 16, CH), BF16), pltpu.SemaphoreType.DMA((2, 4)),
-        ],
-        space=ANY, room=56 << 20,
+    va, vb, hp, hm, upstream = call(
+        lambda *refs: pack_kernel(count, width, *refs), 3, 2, (message, message, own, own, block),
+        [strips, strips, vertical_pair, vertical_pair],
     )(*tables, fields, upstream)
-    vp, vm, token = lax.optimization_barrier((vp, vm, me))
-    vp, vm = vertical(vp, vm, width)
+    va, vb, token = lax.optimization_barrier((va, vb, me))
+    va, vb = both_ways(va, vb, width)
     in_two, up_copies, grad = call(back_kernel, 1, 2, (weights, copies, wide), (), conv_flops)(
         token, kernel_two, upstream
     )
-    vp, vm, in_two, up_copies, grad, token = lax.optimization_barrier(
-        (vp, vm, in_two, up_copies, grad, token)
-    )
-    hp, hm = horizontal(vp, vm, hp, hm)
+    va, vb, in_two, up_copies, grad, token = lax.optimization_barrier(
+        (va, vb, in_two, up_copies, grad, token)
+    )
+
+    def relay(token, va, vb, hp, hm):
+        return call(
+            lambda *refs: relay_kernel(width, *refs), 1, 4, (message, message, message, message), (), 0, 1 << 18
+        )(token, va, vb, hp, hm)
+
+    vp, vm, ha, hb = relay(token, va, vb, hp, hm)
+    ha, hb, token = lax.optimization_barrier((ha, hb, token))
+    ha, hb = both_ways(ha, hb, 1)
     fwd_one, field_copies, pre = call(fore_kernel, 1, 2, (weights, copies, wide), (), conv_flops)(
         token, kernel_one, fields
     )
-    hidden, grad_pre, vp2, vm2, hp2, hm2, fore, back, pieces, corners = call(
+    hidden, grad_pre, va2, vb2, hp2, hm2, fore, back, pieces, corners, hp, hm = call(
         lambda *refs: middle_kernel(count, width, *refs), 3, 8,
         (
             block, block, message, message, own, own, struct(sides, F32), struct(sides, F32),
             struct((4, SIDE, 3 * CH)), struct((4, 16, CH)),
+            message, message,
         ),
-        [strips, strips], conv_flops,
-    )(*tables, vp, vm, hp, hm, fwd_one, in_two, pre, grad)
-    hidden, grad_pre, vp2, vm2, token = lax.optimization_barrier((hidden, grad_pre, vp2, vm2, token))
+        [strips, strips, vertical_pair, vertical_pair], conv_flops,
+    )(*tables, vp, vm, ha, hb, fwd_one, in_two, pre, grad)
+    hidden, grad_pre, va2, vb2, token = lax.optimization_barrier((hidden, grad_pre, va2, vb2, token))
     in_one, fwd_two = call(weights_kernel, 1, 2, (weights, weights))(token, kernel_one, kernel_two)
-    keep, send = call(
-        lambda *refs: sums_kernel(count, width, scale, *refs), 3, 12,
-        (struct((9 * CH, CH), F32), struct((9 * CH, CH), F32)),
-        [pltpu.VMEM((2 * CH, 12 * CH), F32), pltpu.VMEM((2, 9 * CH, CH), F32)],
-        2 * conv_flops,
-    )(*tables, vp, vm, hp, hm, hidden, grad_pre, field_copies, up_copies, fore, back, pieces, corners)
+    def half(kept, token):
+        got, = call(
+            lambda me, *refs: sums_kernel(count, width, scale, kept, me, *refs), 3, 12,
+            (struct((9 * CH, CH), F32),), [pltpu.VMEM((2 * CH, 12 * CH), F32)], conv_flops,
+        )(
+            token, *tables[1:], vp, vm, hp, hm, hidden, grad_pre, field_copies, up_copies,
+            fore, back, pieces, corners,
+        )
+        return got
+
+    def keep_half(done):
+        return dict(keep=half(True, done["token"]))
 
     def second_round(done):
-        vp, vm = vertical(done["vp"], done["vm"], width)
-        hp, hm = horizontal(vp, vm, hp2, hm2)
+        va, vb = both_ways(done["va"], done["vb"], width)
+        vp, vm, ha, hb = relay(me, va, vb, hp2, hm2)
+        ha, hb = both_ways(ha, hb, 1)
+        hp, hm = call(name_kernel, 1, 2, (message, message), (), 0, 1 << 18)(me, ha, hb)
         return dict(vp=vp, vm=vm, hp=hp, hm=hm)
 
     def messages(done):
@@ -649,14 +683,13 @@
         return dict(grad_fields=grad_fields)
 
     grads, done = total(
-        keep, send, dict(vp=vp2, vm=vm2),
-        {1: second_round, 2: make_outputs, 3: make_grads},
+        half(False, token), dict(va=va2, vb=vb2, token=token),
+        {0: keep_half, 1: second_round, 2: make_outputs, 3: make_grads},
     )
     shape = (1, 1, SIDE, SIDE, CH)
-    taps = (3, 3, CH, CH)
     return (
         done["outputs"].reshape(shape), done["grad_fields"].reshape(shape),
-        grads[0].reshape(taps), grads[1].reshape(taps),
+        grads[0].reshape(taps.shape), grads[1].reshape(taps.shape),
     )
 
 

time: 100 us -> 99 us (0.990)
  other arithmetic: 5.85 us -> 1.81 us
  starting transfers between devices: 35.3 us -> 38.4 us
  Pallas kernels: 27.4 us -> 25.9 us
    select_n x8 -> x0, other arithmetic: 4.05 us -> none  [the longest x2 2.24 us: both_ways(): one = lax.ppermute(jnp.where(even, ahead, behind), AXES, pairs(0))]
    ppermute x8, waiting for transfers between devices: 2.29 us -> 5.93 us  [the longest x4 4.77 us: both_ways(): lax.ppermute(two, AXES, pairs(1))]
    ppermute x8, starting transfers between devices: 14.4 us -> 18 us  [the longest x4 10.2 us: both_ways(): lax.ppermute(two, AXES, pairs(1))]
    ppermute x5, waiting for transfers between devices: 6.55 us -> 3.75 us  [swap(): return lax.ppermute(x, AXES, [(i, i ^ bit) for i in range(size)])]
    pallas_call x1, Pallas kernels: 3.34 us -> 1.2 us  [local(): call(lambda *refs: pack_kernel(count, width, *refs), 3, 2, (message, mess...]
    pallas_call x1 -> x5, Pallas kernels: 6.55 us -> 7.19 us  [the longest x2 7.16 us: half(): call(lambda me, *refs: sums_kernel(count, width, scale, kept, me, *refs),...]
    unnamed x38 -> x28, local copies, waits for them, and re-layouts: 8.63 us -> 8.19 us
  transfers between devices with their start and end apart: 14 -> 14, of which waited for: 6 -> 6; matrix products, arithmetic and copies ran while one was open for 1% -> 0% of each run, Pallas kernels for 14% -> 18%
where the time goes in v5:
time: 99 us; the launch traced here: 98.4 us
  starting transfers between devices  38.4 us (39%)
  Pallas kernels  25.9 us (26%)
  blocking collectives  13.6 us (14%)
  waiting for transfers between devices  9.68 us (10%)
  local copies, waits for them, and re-layouts  8.23 us (8%)
  other arithmetic  1.81 us (2%)
    ppermute x5, starting transfers between devices, swap(): return lax.ppermute(x, AXES, [(i, i ^ bit) for i in range(size)])  16.2 us
    all_to_all x1, blocking collectives, scatter(): lax.all_to_all(sent, AXES, 0, 0, axis_index_groups=groups, tiled=True)  13.6 us
    ppermute x4, starting transfers between devices, both_ways(): lax.ppermute(two, AXES, pairs(1))  10.2 us
    unnamed x28, local copies, waits for them, and re-layouts  8.19 us
    ppermute x4, starting transfers between devices, both_ways(): lax.ppermute(one, AXES, pairs(0))  7.79 us
    pallas_call x2, Pallas kernels, half(): call(lambda me, *refs: sums_kernel(count, width, scale, kept, me, *refs),...  7.16 us
    ppermute x4, waiting for transfers between devices, both_ways(): lax.ppermute(two, AXES, pairs(1))  4.77 us
    pallas_call x1, Pallas kernels, make_grads(): call(lambda *refs: grads_kernel(count, width, *refs), 3, 6, (block,), [pl...  4.73 us
  transfers between devices with their start and end apart: 14, of which 6 were waited for; matrix products, arithmetic and copies ran while one was open for 0% of the time, Pallas kernels for 18%

profile of v5, /device:TPU:1, one launch (start us, length us, event | category | flops | bytes accessed | tf_op | source)
XLA Modules:
  0.0 98.4 jit_solution(5096296769882956115)
XLA Ops:
  0.6 1.2 %copy-done = bf16[1,1,64,64,128]{4,3,2,1,0:T(8,128)(2,1)S(1)} copy-done((bf16[1,1,64,64,128]{4,3,2,1,0:T(8,128)(2,1)S(1)}, bf16[1,1,64,64,128]{4,3,2,1,0:T(8,128)(2,1)}, u32[]{:S(2)}) %copy-start) | copy-done | bytes 1048600
  1.9 1.2 %copy-done.1 = bf16[1,1,64,64,128]{4,3,2,1,0:T(8,128)(2,1)S(1)} copy-done((bf16[1,1,64,64,128]{4,3,2,1,0:T(8,128)(2,1)S(1)}, bf16[1,1,64,64,128]{4,3,2,1,0:T(8,128)(2,1)}, u32[]{:S(2)}) %copy-start.1) | copy-done | bytes 1048600
  5.7 3.8 %collective-permute-start = (bf16[160,128]{1,0:T(8,128)(2,1)S(1)}, bf16[160,128]{1,0:T(8,128)(2,1)S(1)}, u32[]{:S(2)}, u32[]{:S(2)}) collective-permute-start(bf16[160,128]{1,0:T(8,128)(2,1)S(1)} %get-tuple-element.89), channel_id=1, source_target_pairs={{0,32},{1,33},{2,34},{3,35},{4,36},{5,37},{6,38},{7,39},{8,40},{9,... | collective-permute-start | bytes 122888 | tf_op jit(solution)/shard_map/ppermute | solution.py:542
  9.5 2.3 %collective-permute-start.1 = (bf16[160,128]{1,0:T(8,128)(2,1)S(1)}, bf16[160,128]{1,0:T(8,128)(2,1)S(1)}, u32[]{:S(2)}, u32[]{:S(2)}) collective-permute-start(bf16[160,128]{1,0:T(8,128)(2,1)S(1)} %get-tuple-element.90), channel_id=1, source_target_pairs={{0,224},{1,225},{2,226},{3,227},{4,228},{5,229},{6,230},{7,231},{8... | collective-permute-start | bytes 122888 | tf_op jit(solution)/shard_map/ppermute | solution.py:542
  12.8 2.7 %shard_map.94 = (bf16[1536,256]{1,0:T(8,128)(2,1)S(1)}, bf16[3,33,2,64,128]{4,3,2,1,0:T(8,128)(2,1)S(1)}, f32[32,2,64,128]{3,2,1,0:T(8,128)S(1)}) custom-call(s32[1]{0:T(128)} %bitcast.refs_0_.token.me, bf16[3,3,128,128]{3,2,1,0:T(8,128)(2,1)S(1)} %copy-done.4, bf16[32,2,64,128]{3,2,1,0:T(8,128)(2,1)S(1)} %get-tuple-element.92.upstream), custom_call_target="tpu_custom_call" | custom-call | flops 1207959552 | bytes 4194304 | tf_op jit(solution)/shard_map/pallas_call | solution.py:620
  16.9 2.9 %collective-permute-start.3 = (bf16[160,128]{1,0:T(8,128)(2,1)S(1)}, bf16[160,128]{1,0:T(8,128)(2,1)S(1)}, u32[]{:S(2)}, u32[]{:S(2)}) collective-permute-start(bf16[160,128]{1,0:T(8,128)(2,1)S(1)} %get-tuple-element.106), channel_id=1, source_target_pairs={{0,255},{1,2},{2,1},{3,4},{4,3},{5,6},{6,5},{7,8},{8,7},{9,10},{10... | collective-permute-start | bytes 122888 | tf_op jit(solution)/shard_map/ppermute | solution.py:542
  19.8 2.6 %shard_map.96 = (bf16[1536,256]{1,0:T(8,128)(2,1)S(1)}, bf16[3,33,2,64,128]{4,3,2,1,0:T(8,128)(2,1)S(1)}, f32[32,2,64,128]{3,2,1,0:T(8,128)S(1)}) custom-call(s32[1]{0:T(128)} %bitcast.refs_0_.token.me, bf16[3,3,128,128]{3,2,1,0:T(8,128)(2,1)S(1)} %copy-done.3, bf16[32,2,64,128]{3,2,1,0:T(8,128)(2,1)S(1)} %bitcast.15), custom_call_target="tpu_custom_call" | custom-call | flops 1207959552 | bytes 4194304 | tf_op jit(solution)/shard_map/pallas_call | solution.py:635
  22.5 2.6 %shard_map.97 = (bf16[32,2,64,128]{3,2,1,0:T(8,128)(2,1)S(1)}, bf16[32,2,64,128]{3,2,1,0:T(8,128)(2,1)S(1)}, bf16[160,128]{1,0:T(8,128)(2,1)S(1)}, bf16[160,128]...) custom-call(s32[1]{0:T(128)} %bitcast.refs_0_.token.me, ...), custom_call_target="tpu_custom_call" | custom-call | flops 1207959552 | bytes 4194304 | tf_op jit(solution)/shard_map/pallas_call | solution.py:638
  25.1 3.6 %shard_map.98 = f32[1152,128]{1,0:T(8,128)S(1)} custom-call(s32[1]{0:T(128)} %bitcast.refs_0_.token.me, s32[2,4,128]{2,1,0:T(4,128)S(1)} %bitcast.18, s32[2,4,128]{2,1,0:T(4,128)S(1)} %bitcast.23, bf16[160,128]{1,0:T(8,128)(2,1)S(1)} %get-tuple-element.101.refs_3_.refs_2_, bf16[160,128]{1,0:T(8,128)(2,1)S(1)} %get-tuple-element.102.refs_4_.refs_3_, ...), custom_call_target="tpu_custom_call" | custom-call | flops 1207959552 | bytes 4194304 | tf_op jit(solution)/shard_map/pallas_call | solution.py:650
  28.7 5.3 %collective-permute-start.4 = (f32[1152,128]{1,0:T(8,128)S(1)}, f32[1152,128]{1,0:T(8,128)S(1)}, u32[]{:S(2)}, u32[]{:S(2)}) collective-permute-start(f32[1152,128]{1,0:T(8,128)S(1)} %shard_map.98), channel_id=1, source_target_pairs={{0,2},{1,3},{2,0},{3,1},{4,6},{5,7},{6,4},{7,5},{8,10},{9,11},{10,... | collective-permute-start | bytes 1769480 | tf_op jit(solution)/shard_map/ppermute | solution.py:533
  34.0 3.6 %shard_map.99 = f32[1152,128]{1,0:T(8,128)S(1)} custom-call(s32[1]{0:T(128)} %bitcast.refs_0_.token.me, s32[2,4,128]{2,1,0:T(4,128)S(1)} %bitcast.19, s32[2,4,128]{2,1,0:T(4,128)S(1)} %bitcast.24, bf16[160,128]{1,0:T(8,128)(2,1)S(1)} %get-tuple-element.101.refs_3_.refs_2_, bf16[160,128]{1,0:T(8,128)(2,1)S(1)} %get-tuple-element.102.refs_4_.refs_3_, ...), custom_call_target="tpu_custom_call" | custom-call | flops 1207959552 | bytes 4194304 | tf_op jit(solution)/shard_map/pallas_call | solution.py:650
  38.4 4.2 %all-to-all-start = ((bf16[16,72,128]{2,1,0:T(8,128)(2,1)}), bf16[16,72,128]{2,1,0:T(8,128)(2,1)}, u32[]{:S(2)}, u32[]{:S(2)}) async-start(bf16[16,72,128]{2,1,0:T(8,128)(2,1)} %bitcast.5), calls=%async_computation | async-start | bytes 589824 | tf_op jit(solution)/shard_map/all_to_all | solution.py:563
  42.6 2.7 %collective-permute-start.5 = (bf16[160,128]{1,0:T(8,128)(2,1)S(1)}, bf16[160,128]{1,0:T(8,128)(2,1)S(1)}, u32[]{:S(2)}, u32[]{:S(2)}) collective-permute-start(bf16[160,128]{1,0:T(8,128)(2,1)S(1)} %get-tuple-element.136), channel_id=1, source_target_pairs={{0,32},{1,33},{2,34},{3,35},{4,36},{5,37},{6,38},{7,39},{8,40},{9,... | collective-permute-start | bytes 122888 | tf_op jit(solution)/shard_map/ppermute | solution.py:542
  45.3 2.4 %collective-permute-start.6 = (bf16[160,128]{1,0:T(8,128)(2,1)S(1)}, bf16[160,128]{1,0:T(8,128)(2,1)S(1)}, u32[]{:S(2)}, u32[]{:S(2)}) collective-permute-start(bf16[160,128]{1,0:T(8,128)(2,1)S(1)} %get-tuple-element.137), channel_id=1, source_target_pairs={{0,224},{1,225},{2,226},{3,227},{4,228},{5,229},{6,230},{7,231},{8... | collective-permute-start | bytes 122888 | tf_op jit(solution)/shard_map/ppermute | solution.py:542
  48.9 3.3 %collective-permute-done.6.refs_2_ = bf16[160,128]{1,0:T(8,128)(2,1)S(1)} collective-permute-done((bf16[160,128]{1,0:T(8,128)(2,1)S(1)}, bf16[160,128]{1,0:T(8,128)(2,1)S(1)}, u32[]{:S(2)}, u32[]{:S(2)}) %collective-permute-start.6) | collective-permute-done | bytes 40992 | tf_op jit(solution)/shard_map/ppermute | solution.py:542
  53.2 2.6 %collective-permute-start.8 = (bf16[160,128]{1,0:T(8,128)(2,1)S(1)}, bf16[160,128]{1,0:T(8,128)(2,1)S(1)}, u32[]{:S(2)}, u32[]{:S(2)}) collective-permute-start(bf16[160,128]{1,0:T(8,128)(2,1)S(1)} %get-tuple-element.141), channel_id=1, source_target_pairs={{0,255},{1,2},{2,1},{3,4},{4,3},{5,6},{6,5},{7,8},{8,7},{9,10},{10... | collective-permute-start | bytes 122888 | tf_op jit(solution)/shard_map/ppermute | solution.py:542
  60.9 3.5 %shard_map.103 = bf16[32,2,64,128]{3,2,1,0:T(8,128)(2,1)} custom-call(bf16[32,2,64,128]{3,2,1,0:T(8,128)(2,1)S(1)} %get-tuple-element.119.refs_6_.hidden, bf16[160,128]{1,0:T(8,128)(2,1)S(1)} %get-tuple-element.161.vp.refs_3_, bf16[160,128]{1,0:T(8,128)(2,1)S(1)} %copy-done.13, bf16[160,128]{1,0:T(8,128)(2,1)S(1)} %get-tuple-element.163.hp.refs_5_, ...), custom_call_target="tpu_custom_call" | custom-call | flops 1207959552 | bytes 4194304 | tf_op jit(solution)/shard_map/pallas_call | solution.py:673
  64.4 3.1 %collective-permute-start.10 = (f32[72,128]{1,0:T(8,128)S(1)}, f32[72,128]{1,0:T(8,128)S(1)}, u32[]{:S(2)}, u32[]{:S(2)}) collective-permute-start(f32[72,128]{1,0:T(8,128)S(1)} %add.18), channel_id=1, source_target_pairs={{0,8},{1,9},{2,10},{3,11},{4,12},{5,13},{6,14},{7,15},{8,0},{9,1},... | collective-permute-start | bytes 110600 | tf_op jit(solution)/shard_map/ppermute | solution.py:533
  67.5 4.7 %shard_map.104 = bf16[32,2,64,128]{3,2,1,0:T(8,128)(2,1)} custom-call(s32[1]{0:T(128)} %bitcast.refs_0_.token.me, s32[2,4,128]{2,1,0:T(4,128)S(1)} %bitcast.20, s32[2,4,128]{2,1,0:T(4,128)S(1)} %bitcast.25, bf16[160,128]{1,0:T(8,128)(2,1)S(1)} %get-tuple-element.161.vp.refs_3_, bf16[160,128]{1,0:T(8,128)(2,1)S(1)} %copy-done.13, ...), custom_call_target="tpu_custom_call" | custom-call | flops 1207959552 | bytes 4194304 | tf_op jit(solution)/shard_map/pallas_call | solution.py:679
  72.3 4.3 %collective-permute-start.11 = (f32[72,128]{1,0:T(8,128)S(1)}, f32[72,128]{1,0:T(8,128)S(1)}, u32[]{:S(2)}, u32[]{:S(2)}) collective-permute-start(f32[72,128]{1,0:T(8,128)S(1)} %add.19), channel_id=1, source_target_pairs={{0,16},{1,17},{2,18},{3,19},{4,20},{5,21},{6,22},{7,23},{8,24},{9,... | collective-permute-start | bytes 110600 | tf_op jit(solution)/shard_map/ppermute | solution.py:533
  76.6 2.5 %collective-permute-done.11 = f32[72,128]{1,0:T(8,128)S(1)} collective-permute-done((f32[72,128]{1,0:T(8,128)S(1)}, f32[72,128]{1,0:T(8,128)S(1)}, u32[]{:S(2)}, u32[]{:S(2)}) %collective-permute-start.11) | collective-permute-done | bytes 36896 | tf_op jit(solution)/shard_map/ppermute | solution.py:533
  79.2 13.6 %all_to_all.10 = bf16[16,72,128]{2,1,0:T(8,128)(2,1)S(1)} all-to-all(bf16[16,72,128]{2,1,0:T(8,128)(2,1)S(1)} %broadcast_in_dim.2), channel_id=1, replica_groups={{0,128,64,192,32,160,96,224,1,129,65,193,33,161,97,225},{2,130,66,194,3..., dimensions={0} | all-to-all | bytes 589824 | tf_op jit(solution)/shard_map/all_to_all | solution.py:563
  92.7 3.4 %collective-permute-start.12 = (bf16[1152,128]{1,0:T(8,128)(2,1)S(1)}, bf16[1152,128]{1,0:T(8,128)(2,1)S(1)}, u32[]{:S(2)}, u32[]{:S(2)}) collective-permute-start(bf16[1152,128]{1,0:T(8,128)(2,1)S(1)} %bitcast.11), channel_id=1, source_target_pairs={{0,2},{1,3},{2,0},{3,1},{4,6},{5,7},{6,4},{7,5},{8,10},{9,11},{10,... | collective-permute-start | bytes 884744 | tf_op jit(solution)/shard_map/ppermute | solution.py:533
  96.1 1.2 %collective-permute-done.12.other = bf16[1152,128]{1,0:T(8,128)(2,1)S(1)} collective-permute-done((bf16[1152,128]{1,0:T(8,128)(2,1)S(1)}, bf16[1152,128]{1,0:T(8,128)(2,1)S(1)}, u32[]{:S(2)}, u32[]{:S(2)}) %collective-permute-start.12) | collective-permute-done | bytes 294944 | tf_op jit(solution)/shard_map/ppermute | solution.py:533
  (52 shorter events, 14.1 us)
Async XLA Ops:
  0.6 1.2 %copy-start = (bf16[1,1,64,64,128]{4,3,2,1,0:T(8,128)(2,1)S(1)}, bf16[1,1,64,64,128]{4,3,2,1,0:T(8,128)(2,1)}, u32[]{:S(2)}) copy-start(bf16[1,1,64,64,128]{4,3,2,1,0:T(8,128)(2,1)} %param.9) | copy-start | bytes 3145732
  1.9 1.2 %copy-start.1 = (bf16[1,1,64,64,128]{4,3,2,1,0:T(8,128)(2,1)S(1)}, bf16[1,1,64,64,128]{4,3,2,1,0:T(8,128)(2,1)}, u32[]{:S(2)}) copy-start(bf16[1,1,64,64,128]{4,3,2,1,0:T(8,128)(2,1)} %param.6) | copy-start | bytes 3145732
  4.5 15.4 %copy-start.2 = (bf16[1,1,64,64,128]{4,3,2,1,0:T(8,128)(2,1)S(1)}, bf16[1,1,64,64,128]{4,3,2,1,0:T(8,128)(2,1)}, u32[]{:S(2)}) copy-start(bf16[1,1,64,64,128]{4,3,2,1,0:T(8,128)(2,1)} %param.6) | copy-start | bytes 3145732
  4.5 15.4 %copy-start.3 = (bf16[3,3,128,128]{3,2,1,0:T(8,128)(2,1)S(1)}, bf16[3,3,128,128]{3,2,1,0:T(8,128)(2,1)}, u32[]{:S(2)}) copy-start(bf16[3,3,128,128]{3,2,1,0:T(8,128)(2,1)} %kernel_one.3) | copy-start | bytes 884740
  5.7 9.8 %collective-permute-start = (bf16[160,128]{1,0:T(8,128)(2,1)S(1)}, bf16[160,128]{1,0:T(8,128)(2,1)S(1)}, u32[]{:S(2)}, u32[]{:S(2)}) collective-permute-start(bf16[160,128]{1,0:T(8,128)(2,1)S(1)} %get-tuple-element.89), channel_id=1, source_target_pairs={{0,32},{1,33},{2,34},{3,35},{4,36},{5,37},{6,38},{7,39},{8,40},{9,... | collective-permute-start | bytes 122888 | tf_op jit(solution)/shard_map/ppermute | solution.py:542
  9.5 6.5 %collective-permute-start.1 = (bf16[160,128]{1,0:T(8,128)(2,1)S(1)}, bf16[160,128]{1,0:T(8,128)(2,1)S(1)}, u32[]{:S(2)}, u32[]{:S(2)}) collective-permute-start(bf16[160,128]{1,0:T(8,128)(2,1)S(1)} %get-tuple-element.90), channel_id=1, source_target_pairs={{0,224},{1,225},{2,226},{3,227},{4,228},{5,229},{6,230},{7,231},{8... | collective-permute-start | bytes 122888 | tf_op jit(solution)/shard_map/ppermute | solution.py:542
  11.8 1.0 copy-start.4
  15.5 7.0 %copy-start.7 = (s32[128,2,4]{0,2,1:T(4,128)S(1)}, s32[128,2,4]{0,2,1:T(4,128)}, u32[]{:S(2)}) copy-start(s32[128,2,4]{0,2,1:T(4,128)} %param.10) | copy-start | bytes 12292
  15.5 7.0 %copy-start.9 = (s32[128,2,4]{0,2,1:T(4,128)S(1)}, s32[128,2,4]{0,2,1:T(4,128)}, u32[]{:S(2)}) copy-start(s32[128,2,4]{0,2,1:T(4,128)} %param.11) | copy-start | bytes 12292
  16.0 6.4 %collective-permute-start.2 = (bf16[160,128]{1,0:T(8,128)(2,1)S(1)}, bf16[160,128]{1,0:T(8,128)(2,1)S(1)}, u32[]{:S(2)}, u32[]{:S(2)}) collective-permute-start(bf16[160,128]{1,0:T(8,128)(2,1)S(1)} %get-tuple-element.105), channel_id=1, source_target_pairs={{0,1},{1,0},{2,3},{3,2},{4,5},{5,4},{6,7},{7,6},{8,9},{9,8},{10,11... | collective-permute-start | bytes 122888 | tf_op jit(solution)/shard_map/ppermute | solution.py:542
  16.9 5.6 %collective-permute-start.3 = (bf16[160,128]{1,0:T(8,128)(2,1)S(1)}, bf16[160,128]{1,0:T(8,128)(2,1)S(1)}, u32[]{:S(2)}, u32[]{:S(2)}) collective-permute-start(bf16[160,128]{1,0:T(8,128)(2,1)S(1)} %get-tuple-element.106), channel_id=1, source_target_pairs={{0,255},{1,2},{2,1},{3,4},{4,3},{5,6},{6,5},{7,8},{8,7},{9,10},{10... | collective-permute-start | bytes 122888 | tf_op jit(solution)/shard_map/ppermute | solution.py:542
  28.7 27.1 %copy-start.5 = (bf16[3,3,128,128]{3,2,1,0:T(8,128)(2,1)S(1)}, bf16[3,3,128,128]{3,2,1,0:T(8,128)(2,1)}, u32[]{:S(2)}) copy-start(bf16[3,3,128,128]{3,2,1,0:T(8,128)(2,1)} %kernel_two.3) | copy-start | bytes 884740
  28.7 8.9 %collective-permute-start.4 = (f32[1152,128]{1,0:T(8,128)S(1)}, f32[1152,128]{1,0:T(8,128)S(1)}, u32[]{:S(2)}, u32[]{:S(2)}) collective-permute-start(f32[1152,128]{1,0:T(8,128)S(1)} %shard_map.98), channel_id=1, source_target_pairs={{0,2},{1,3},{2,0},{3,1},{4,6},{5,7},{6,4},{7,5},{8,10},{9,11},{10,... | collective-permute-start | bytes 1769480 | tf_op jit(solution)/shard_map/ppermute | solution.py:533
  38.4 19.5 %all-to-all-start = ((bf16[16,72,128]{2,1,0:T(8,128)(2,1)}), bf16[16,72,128]{2,1,0:T(8,128)(2,1)}, u32[]{:S(2)}, u32[]{:S(2)}) async-start(bf16[16,72,128]{2,1,0:T(8,128)(2,1)} %bitcast.5), calls=%async_computation | async-start | bytes 589824 | tf_op jit(solution)/shard_map/all_to_all | solution.py:563
  42.6 6.3 %collective-permute-start.5 = (bf16[160,128]{1,0:T(8,128)(2,1)S(1)}, bf16[160,128]{1,0:T(8,128)(2,1)S(1)}, u32[]{:S(2)}, u32[]{:S(2)}) collective-permute-start(bf16[160,128]{1,0:T(8,128)(2,1)S(1)} %get-tuple-element.136), channel_id=1, source_target_pairs={{0,32},{1,33},{2,34},{3,35},{4,36},{5,37},{6,38},{7,39},{8,40},{9,... | collective-permute-start | bytes 122888 | tf_op jit(solution)/shard_map/ppermute | solution.py:542
  45.3 6.9 %collective-permute-start.6 = (bf16[160,128]{1,0:T(8,128)(2,1)S(1)}, bf16[160,128]{1,0:T(8,128)(2,1)S(1)}, u32[]{:S(2)}, u32[]{:S(2)}) collective-permute-start(bf16[160,128]{1,0:T(8,128)(2,1)S(1)} %get-tuple-element.137), channel_id=1, source_target_pairs={{0,224},{1,225},{2,226},{3,227},{4,228},{5,229},{6,230},{7,231},{8... | collective-permute-start | bytes 122888 | tf_op jit(solution)/shard_map/ppermute | solution.py:542
  52.8 4.1 %collective-permute-start.7 = (bf16[160,128]{1,0:T(8,128)(2,1)S(1)}, bf16[160,128]{1,0:T(8,128)(2,1)S(1)}, u32[]{:S(2)}, u32[]{:S(2)}) collective-permute-start(bf16[160,128]{1,0:T(8,128)(2,1)S(1)} %get-tuple-element.140), channel_id=1, source_target_pairs={{0,1},{1,0},{2,3},{3,2},{4,5},{5,4},{6,7},{7,6},{8,9},{9,8},{10,11... | collective-permute-start | bytes 122888 | tf_op jit(solution)/shard_map/ppermute | solution.py:542
  53.2 4.7 %collective-permute-start.8 = (bf16[160,128]{1,0:T(8,128)(2,1)S(1)}, bf16[160,128]{1,0:T(8,128)(2,1)S(1)}, u32[]{:S(2)}, u32[]{:S(2)}) collective-permute-start(bf16[160,128]{1,0:T(8,128)(2,1)S(1)} %get-tuple-element.141), channel_id=1, source_target_pairs={{0,255},{1,2},{2,1},{3,4},{4,3},{5,6},{6,5},{7,8},{8,7},{9,10},{10... | collective-permute-start | bytes 122888 | tf_op jit(solution)/shard_map/ppermute | solution.py:542
  56.1 0.9 copy-start.10
  58.9 5.5 %collective-permute-start.9 = (f32[72,128]{1,0:T(8,128)S(1)}, f32[72,128]{1,0:T(8,128)S(1)}, u32[]{:S(2)}, u32[]{:S(2)}) collective-permute-start(f32[72,128]{1,0:T(8,128)S(1)} %convert_reduce_fusion), channel_id=1, source_target_pairs={{0,4},{1,5},{2,6},{3,7},{4,0},{5,1},{6,2},{7,3},{8,12},{9,13},{10,... | collective-permute-start | bytes 110600 | tf_op jit(solution)/shard_map/ppermute | solution.py:533
  59.0 1.1 %copy-start.11 = (bf16[1536,256]{1,0:T(8,128)(2,1)S(1)}, bf16[1536,256]{1,0:T(8,128)(2,1)}, u32[]{:S(2)}) copy-start(bf16[1536,256]{1,0:T(8,128)(2,1)} %copy-done.10) | copy-start | bytes 2359300
  64.4 7.8 %collective-permute-start.10 = (f32[72,128]{1,0:T(8,128)S(1)}, f32[72,128]{1,0:T(8,128)S(1)}, u32[]{:S(2)}, u32[]{:S(2)}) collective-permute-start(f32[72,128]{1,0:T(8,128)S(1)} %add.18), channel_id=1, source_target_pairs={{0,8},{1,9},{2,10},{3,11},{4,12},{5,13},{6,14},{7,15},{8,0},{9,1},... | collective-permute-start | bytes 110600 | tf_op jit(solution)/shard_map/ppermute | solution.py:533
  72.3 6.8 %collective-permute-start.11 = (f32[72,128]{1,0:T(8,128)S(1)}, f32[72,128]{1,0:T(8,128)S(1)}, u32[]{:S(2)}, u32[]{:S(2)}) collective-permute-start(f32[72,128]{1,0:T(8,128)S(1)} %add.19), channel_id=1, source_target_pairs={{0,16},{1,17},{2,18},{3,19},{4,20},{5,21},{6,22},{7,23},{8,24},{9,... | collective-permute-start | bytes 110600 | tf_op jit(solution)/shard_map/ppermute | solution.py:533
  92.7 4.6 %collective-permute-start.12 = (bf16[1152,128]{1,0:T(8,128)(2,1)S(1)}, bf16[1152,128]{1,0:T(8,128)(2,1)S(1)}, u32[]{:S(2)}, u32[]{:S(2)}) collective-permute-start(bf16[1152,128]{1,0:T(8,128)(2,1)S(1)} %bitcast.11), channel_id=1, source_target_pairs={{0,2},{1,3},{2,0},{3,1},{4,6},{5,7},{6,4},{7,5},{8,10},{9,11},{10,... | collective-permute-start | bytes 884744 | tf_op jit(solution)/shard_map/ppermute | solution.py:533
  (4 other events, 2.8 us)

commit v6 on v5

--- a/solution.py
+++ b/solution.py
@@ -493,6 +493,10 @@
     rows(HALF // mb - 1, last=True)
 
 
+def fold_kernel(parts, total):
+    total[...] = jnp.sum(parts[...].astype(F32), axis=0)
+
+
 def finish_kernel(me, mine, other, first, second):
     high = (me[0] // FIRST) % 2
 
@@ -558,6 +562,7 @@
     me = lax.axis_index(AXES).astype(jnp.int32)
     groups = plane_groups(lax.axis_size(AXES))
     steps = [0]
+    free = {}
 
     def scatter(sent):
         return lax.all_to_all(sent, AXES, 0, 0, axis_index_groups=groups, tiled=True)
@@ -571,16 +576,17 @@
         sent, held = lax.optimization_barrier((sent, done.copy()))
         done.update(held)
         got = move(sent)
-        gave = work(done)
+        gave, loose = work(done, free)
         got, gave = lax.optimization_barrier((got, gave))
         done.update(gave)
+        free.update(loose)
         return got
 
     x = beside(send, FIRST)
     x = done["keep"] + x
     parts = (len(groups[0]), x.shape[0] // len(groups[0]), CH)
     spread = beside(x.astype(BF16).reshape(parts), None)
-    x = jnp.sum(spread.astype(F32), axis=0)
+    x, = call(fold_kernel, 0, 1, (struct(parts[1:], F32),), (), 0, 1 << 19)(spread)
     for bit in WHOLE:
         x = x + beside(x, bit)
     spread = jnp.broadcast_to(x.astype(BF16)[None], parts)
@@ -645,7 +651,6 @@
         [strips, strips, vertical_pair, vertical_pair], conv_flops,
     )(*tables, vp, vm, ha, hb, fwd_one, in_two, pre, grad)
     hidden, grad_pre, va2, vb2, token = lax.optimization_barrier((hidden, grad_pre, va2, vb2, token))
-    in_one, fwd_two = call(weights_kernel, 1, 2, (weights, weights))(token, kernel_one, kernel_two)
     def half(kept, token):
         got, = call(
             lambda me, *refs: sums_kernel(count, width, scale, kept, me, *refs), 3, 12,
@@ -656,35 +661,43 @@
         )
         return got
 
-    def keep_half(done):
-        return dict(keep=half(True, done["token"]))
-
-    def second_round(done):
+    def first_work(done, free):
         va, vb = both_ways(done["va"], done["vb"], width)
-        vp, vm, ha, hb = relay(me, va, vb, hp2, hm2)
+        return dict(keep=half(True, done["token"]), va=va, vb=vb), {}
+
+    def second_work(done, free):
+        vp, vm, ha, hb = relay(done["token"], done["va"], done["vb"], hp2, hm2)
         ha, hb = both_ways(ha, hb, 1)
-        hp, hm = call(name_kernel, 1, 2, (message, message), (), 0, 1 << 18)(me, ha, hb)
-        return dict(vp=vp, vm=vm, hp=hp, hm=hm)
-
-    def messages(done):
-        return done["vp"], done["vm"], done["hp"], done["hm"]
-
-    def make_outputs(done):
+        return {}, dict(vp=vp, vm=vm, ha=ha, hb=hb)
+
+    def third_work(done, free):
+        hp, hm = call(name_kernel, 1, 2, (message, message), (), 0, 1 << 18)(
+            done["token"], free["ha"], free["hb"]
+        )
+        in_one, fwd_two = call(weights_kernel, 1, 2, (weights, weights))(
+            done["token"], kernel_one, kernel_two
+        )
+        return dict(in_one=in_one, fwd_two=fwd_two, hp=hp, hm=hm), {}
+
+    def messages(done, free):
+        return free["vp"], free["vm"], done["hp"], done["hm"]
+
+    def make_outputs(done, free):
         outputs, = call(
             outputs_kernel, 0, 6, (block,), [pltpu.VMEM(COPIES, BF16), column, column], conv_flops
-        )(hidden, *messages(done), fwd_two)
-        return dict(outputs=outputs)
-
-    def make_grads(done):
+        )(hidden, *messages(done, free), done["fwd_two"])
+        return dict(outputs=outputs), {}
+
+    def make_grads(done, free):
         grad_fields, = call(
             lambda *refs: grads_kernel(count, width, *refs), 3, 6, (block,),
             [pltpu.VMEM(COPIES, BF16), strips], conv_flops,
-        )(*tables, *messages(done), grad_pre, in_one)
-        return dict(grad_fields=grad_fields)
+        )(*tables, *messages(done, free), grad_pre, done["in_one"])
+        return dict(grad_fields=grad_fields), {}
 
     grads, done = total(
         half(False, token), dict(va=va2, vb=vb2, token=token),
-        {0: keep_half, 1: second_round, 2: make_outputs, 3: make_grads},
+        {0: first_work, 1: second_work, 2: third_work, 3: make_outputs, 4: make_grads},
     )
     shape = (1, 1, SIDE, SIDE, CH)
     return (

time: 99 us -> 90 us (0.909)
  local copies, waits for them, and re-layouts: 8.23 us -> 4.84 us
  blocking collectives: 13.6 us -> 10.7 us
  other arithmetic: 1.81 us -> 0.79 us
  starting transfers between devices: 38.4 us -> 37.4 us
    all_to_all x1, waiting for transfers between devices: 0.01 us -> 4.54 us  [scatter(): lax.all_to_all(sent, AXES, 0, 0, axis_index_groups=groups, tiled=True)]
    ppermute x4, waiting for transfers between devices: 4.77 us -> 0.49 us  [both_ways(): lax.ppermute(two, AXES, pairs(1))]
    unnamed x28 -> x20, local copies, waits for them, and re-layouts: 8.19 us -> 4.8 us
    all_to_all x1, blocking collectives: 13.6 us -> 10.7 us  [scatter(): lax.all_to_all(sent, AXES, 0, 0, axis_index_groups=groups, tiled=True)]
    ppermute x4, starting transfers between devices: 7.79 us -> 6.19 us  [both_ways(): lax.ppermute(one, AXES, pairs(0))]
    ppermute x4, waiting for transfers between devices: 1.16 us -> 0.01 us  [both_ways(): lax.ppermute(one, AXES, pairs(0))]
    reduce_sum x1 -> x0, other arithmetic: 1.01 us -> none  [total(): x = jnp.sum(spread.astype(F32), axis=0)]
  transfers between devices with their start and end apart: 14 -> 14, of which waited for: 6 -> 4; matrix products, arithmetic and copies ran while one was open for 0% -> 0% of each run, Pallas kernels for 18% -> 19%
where the time goes in v6:
time: 90 us; the launch traced here: 89.7 us
  starting transfers between devices  37.4 us (42%)
  Pallas kernels  26 us (29%)
  blocking collectives  10.7 us (12%)
  waiting for transfers between devices  9 us (10%)
  local copies, waits for them, and re-layouts  4.84 us (5%)
    ppermute x5, starting transfers between devices, swap(): return lax.ppermute(x, AXES, [(i, i ^ bit) for i in range(size)])  16.4 us
    all_to_all x1, blocking collectives, scatter(): lax.all_to_all(sent, AXES, 0, 0, axis_index_groups=groups, tiled=True)  10.7 us
    ppermute x4, starting transfers between devices, both_ways(): lax.ppermute(two, AXES, pairs(1))  10.6 us
    pallas_call x2, Pallas kernels, half(): call(lambda me, *refs: sums_kernel(count, width, scale, kept, me, *refs),...  7.15 us
    ppermute x4, starting transfers between devices, both_ways(): lax.ppermute(one, AXES, pairs(0))  6.19 us
    unnamed x20, local copies, waits for them, and re-layouts  4.8 us
    pallas_call x1, Pallas kernels, make_grads(): call(lambda *refs: grads_kernel(count, width, *refs), 3, 6, (block,), [pl...  4.73 us
    all_to_all x1, waiting for transfers between devices, scatter(): lax.all_to_all(sent, AXES, 0, 0, axis_index_groups=groups, tiled=True)  4.54 us
  transfers between devices with their start and end apart: 14, of which 4 were waited for; matrix products, arithmetic and copies ran while one was open for 0% of the time, Pallas kernels for 19%

profile of v6, /device:TPU:1, one launch (start us, length us, event | category | flops | bytes accessed | tf_op | source)
XLA Modules:
  0.0 89.7 jit_solution(2197377422688474400)
XLA Ops:
  0.6 1.2 %copy-done = bf16[1,1,64,64,128]{4,3,2,1,0:T(8,128)(2,1)S(1)} copy-done((bf16[1,1,64,64,128]{4,3,2,1,0:T(8,128)(2,1)S(1)}, bf16[1,1,64,64,128]{4,3,2,1,0:T(8,128)(2,1)}, u32[]{:S(2)}) %copy-start) | copy-done | bytes 1048600
  1.9 1.2 %copy-done.1 = bf16[1,1,64,64,128]{4,3,2,1,0:T(8,128)(2,1)S(1)} copy-done((bf16[1,1,64,64,128]{4,3,2,1,0:T(8,128)(2,1)S(1)}, bf16[1,1,64,64,128]{4,3,2,1,0:T(8,128)(2,1)}, u32[]{:S(2)}) %copy-start.1) | copy-done | bytes 1048600
  4.5 1.2 %shard_map.93 = (bf16[160,128]{1,0:T(8,128)(2,1)S(1)}, bf16[160,128]{1,0:T(8,128)(2,1)S(1)}, bf16[128,128]{1,0:T(8,128)(2,1)S(1)}, bf16[128,128]{1,0:T(8,128)(2,1)S(1)}, bf16[32,2,64,128]{3,2,1,0:T(8,128)(2,1)S(1)}) custom-call(s32[1]{0:T(128)} %bitcast.refs_0_.token.me, s32[2,4,128]{2,1,0:T(4,128)S(1)} %bitcast.16, s32[2,4,128]{2,1,0:T(4,128)S(1)} %bitcast.21, ...), custom_call_target="tpu_custom_call" | custom-call | bytes 4194304 | tf_op jit(solution)/shard_map/pallas_call | solution.py:620
  5.7 3.8 %collective-permute-start = (bf16[160,128]{1,0:T(8,128)(2,1)S(1)}, bf16[160,128]{1,0:T(8,128)(2,1)S(1)}, u32[]{:S(2)}, u32[]{:S(2)}) collective-permute-start(bf16[160,128]{1,0:T(8,128)(2,1)S(1)} %get-tuple-element.93), channel_id=1, source_target_pairs={{0,32},{1,33},{2,34},{3,35},{4,36},{5,37},{6,38},{7,39},{8,40},{9,... | collective-permute-start | bytes 122888 | tf_op jit(solution)/shard_map/ppermute | solution.py:546
  9.5 2.3 %collective-permute-start.1 = (bf16[160,128]{1,0:T(8,128)(2,1)S(1)}, bf16[160,128]{1,0:T(8,128)(2,1)S(1)}, u32[]{:S(2)}, u32[]{:S(2)}) collective-permute-start(bf16[160,128]{1,0:T(8,128)(2,1)S(1)} %get-tuple-element.94), channel_id=1, source_target_pairs={{0,224},{1,225},{2,226},{3,227},{4,228},{5,229},{6,230},{7,231},{8... | collective-permute-start | bytes 122888 | tf_op jit(solution)/shard_map/ppermute | solution.py:546
  12.8 2.7 %shard_map.94 = (bf16[1536,256]{1,0:T(8,128)(2,1)S(1)}, bf16[3,33,2,64,128]{4,3,2,1,0:T(8,128)(2,1)S(1)}, f32[32,2,64,128]{3,2,1,0:T(8,128)S(1)}) custom-call(s32[1]{0:T(128)} %bitcast.refs_0_.token.me, bf16[3,3,128,128]{3,2,1,0:T(8,128)(2,1)S(1)} %copy-done.4, bf16[32,2,64,128]{3,2,1,0:T(8,128)(2,1)S(1)} %get-tuple-element.96.upstream), custom_call_target="tpu_custom_call" | custom-call | flops 1207959552 | bytes 4194304 | tf_op jit(solution)/shard_map/pallas_call | solution.py:626
  16.9 2.9 %collective-permute-start.3 = (bf16[160,128]{1,0:T(8,128)(2,1)S(1)}, bf16[160,128]{1,0:T(8,128)(2,1)S(1)}, u32[]{:S(2)}, u32[]{:S(2)}) collective-permute-start(bf16[160,128]{1,0:T(8,128)(2,1)S(1)} %get-tuple-element.110), channel_id=1, source_target_pairs={{0,255},{1,2},{2,1},{3,4},{4,3},{5,6},{6,5},{7,8},{8,7},{9,10},{10... | collective-permute-start | bytes 122888 | tf_op jit(solution)/shard_map/ppermute | solution.py:546
  19.8 2.6 %shard_map.96 = (bf16[1536,256]{1,0:T(8,128)(2,1)S(1)}, bf16[3,33,2,64,128]{4,3,2,1,0:T(8,128)(2,1)S(1)}, f32[32,2,64,128]{3,2,1,0:T(8,128)S(1)}) custom-call(s32[1]{0:T(128)} %bitcast.refs_0_.token.me, bf16[3,3,128,128]{3,2,1,0:T(8,128)(2,1)S(1)} %copy-done.3, bf16[32,2,64,128]{3,2,1,0:T(8,128)(2,1)S(1)} %bitcast.15), custom_call_target="tpu_custom_call" | custom-call | flops 1207959552 | bytes 4194304 | tf_op jit(solution)/shard_map/pallas_call | solution.py:641
  22.5 2.6 %shard_map.97 = (bf16[32,2,64,128]{3,2,1,0:T(8,128)(2,1)S(1)}, bf16[32,2,64,128]{3,2,1,0:T(8,128)(2,1)S(1)}, bf16[160,128]{1,0:T(8,128)(2,1)S(1)}, bf16[160,128]...) custom-call(s32[1]{0:T(128)} %bitcast.refs_0_.token.me, ...), custom_call_target="tpu_custom_call" | custom-call | flops 1207959552 | bytes 4194304 | tf_op jit(solution)/shard_map/pallas_call | solution.py:644
  25.1 3.6 %shard_map.98 = f32[1152,128]{1,0:T(8,128)S(1)} custom-call(s32[1]{0:T(128)} %bitcast.refs_0_.token.me, s32[2,4,128]{2,1,0:T(4,128)S(1)} %bitcast.18, s32[2,4,128]{2,1,0:T(4,128)S(1)} %bitcast.23, bf16[160,128]{1,0:T(8,128)(2,1)S(1)} %get-tuple-element.105.refs_3_.refs_2_, bf16[160,128]{1,0:T(8,128)(2,1)S(1)} %get-tuple-element.106.refs_4_.refs_3_, ...), custom_call_target="tpu_custom_call" | custom-call | flops 1207959552 | bytes 4194304 | tf_op jit(solution)/shard_map/pallas_call | solution.py:655
  28.7 5.3 %collective-permute-start.4 = (f32[1152,128]{1,0:T(8,128)S(1)}, f32[1152,128]{1,0:T(8,128)S(1)}, u32[]{:S(2)}, u32[]{:S(2)}) collective-permute-start(f32[1152,128]{1,0:T(8,128)S(1)} %shard_map.98), channel_id=1, source_target_pairs={{0,2},{1,3},{2,0},{3,1},{4,6},{5,7},{6,4},{7,5},{8,10},{9,11},{10,... | collective-permute-start | bytes 1769480 | tf_op jit(solution)/shard_map/ppermute | solution.py:537
  34.0 3.3 %collective-permute-start.6 = (bf16[160,128]{1,0:T(8,128)(2,1)S(1)}, bf16[160,128]{1,0:T(8,128)(2,1)S(1)}, u32[]{:S(2)}, u32[]{:S(2)}) collective-permute-start(bf16[160,128]{1,0:T(8,128)(2,1)S(1)} %get-tuple-element.136), channel_id=1, source_target_pairs={{0,224},{1,225},{2,226},{3,227},{4,228},{5,229},{6,230},{7,231},{8... | collective-permute-start | bytes 122888 | tf_op jit(solution)/shard_map/ppermute | solution.py:546
  37.4 3.6 %shard_map.99 = f32[1152,128]{1,0:T(8,128)S(1)} custom-call(s32[1]{0:T(128)} %bitcast.refs_0_.token.me, s32[2,4,128]{2,1,0:T(4,128)S(1)} %bitcast.19, s32[2,4,128]{2,1,0:T(4,128)S(1)} %bitcast.24, bf16[160,128]{1,0:T(8,128)(2,1)S(1)} %get-tuple-element.105.refs_3_.refs_2_, bf16[160,128]{1,0:T(8,128)(2,1)S(1)} %get-tuple-element.106.refs_4_.refs_3_, ...), custom_call_target="tpu_custom_call" | custom-call | flops 1207959552 | bytes 4194304 | tf_op jit(solution)/shard_map/pallas_call | solution.py:655
  41.8 4.2 %all-to-all-start = ((bf16[16,72,128]{2,1,0:T(8,128)(2,1)}), bf16[16,72,128]{2,1,0:T(8,128)(2,1)S(1)}, u32[]{:S(2)}, u32[]{:S(2)}) async-start(bf16[16,72,128]{2,1,0:T(8,128)(2,1)} %bitcast.5), calls=%async_computation | async-start | bytes 589824 | tf_op jit(solution)/shard_map/all_to_all | solution.py:568
  46.1 1.4 %collective-permute-start.8 = (bf16[160,128]{1,0:T(8,128)(2,1)S(1)}, bf16[160,128]{1,0:T(8,128)(2,1)S(1)}, u32[]{:S(2)}, u32[]{:S(2)}) collective-permute-start(bf16[160,128]{1,0:T(8,128)(2,1)S(1)} %get-tuple-element.150), channel_id=1, source_target_pairs={{0,1},{1,0},{2,3},{3,2},{4,5},{5,4},{6,7},{7,6},{8,9},{9,8},{10,11... | collective-permute-start | bytes 122888 | tf_op jit(solution)/shard_map/ppermute | solution.py:546
  47.5 2.1 %collective-permute-start.9 = (bf16[160,128]{1,0:T(8,128)(2,1)S(1)}, bf16[160,128]{1,0:T(8,128)(2,1)S(1)}, u32[]{:S(2)}, u32[]{:S(2)}) collective-permute-start(bf16[160,128]{1,0:T(8,128)(2,1)S(1)} %get-tuple-element.151), channel_id=1, source_target_pairs={{0,255},{1,2},{2,1},{3,4},{4,3},{5,6},{6,5},{7,8},{8,7},{9,10},{10... | collective-permute-start | bytes 122888 | tf_op jit(solution)/shard_map/ppermute | solution.py:546
  49.6 4.5 %all-to-all-done.parts = bf16[16,72,128]{2,1,0:T(8,128)(2,1)S(1)} async-done(((bf16[16,72,128]{2,1,0:T(8,128)(2,1)}), bf16[16,72,128]{2,1,0:T(8,128)(2,1)S(1)}, u32[]{:S(2)}, u32[]{:S(2)}) %all-to-all-start) | async-done | bytes 294944 | tf_op jit(solution)/shard_map/all_to_all | solution.py:568
  54.8 2.7 %collective-permute-done.7 = f32[72,128]{1,0:T(8,128)S(1)} collective-permute-done((f32[72,128]{1,0:T(8,128)S(1)}, f32[72,128]{1,0:T(8,128)S(1)}, u32[]{:S(2)}, u32[]{:S(2)}) %collective-permute-start.7) | collective-permute-done | bytes 36896 | tf_op jit(solution)/shard_map/ppermute | solution.py:537
  58.4 3.5 %shard_map.104 = bf16[32,2,64,128]{3,2,1,0:T(8,128)(2,1)} custom-call(bf16[32,2,64,128]{3,2,1,0:T(8,128)(2,1)S(1)} %get-tuple-element.123.refs_6_.hidden, bf16[160,128]{1,0:T(8,128)(2,1)S(1)} %get-tuple-element.161.vp.refs_3_, bf16[160,128]{1,0:T(8,128)(2,1)S(1)} %get-tuple-element.162.vm.refs_4_, bf16[160,128]{1,0:T(8,128)(2,1)S(1)} %get-tuple-element.171.hp.refs_5_, ...), custom_call_target="tpu_custom_call" | custom-call | flops 1207959552 | bytes 4194304 | tf_op jit(solution)/shard_map/pallas_call | solution.py:686
  61.8 4.3 %collective-permute-start.11 = (f32[72,128]{1,0:T(8,128)S(1)}, f32[72,128]{1,0:T(8,128)S(1)}, u32[]{:S(2)}, u32[]{:S(2)}) collective-permute-start(f32[72,128]{1,0:T(8,128)S(1)} %add.19), channel_id=1, source_target_pairs={{0,16},{1,17},{2,18},{3,19},{4,20},{5,21},{6,22},{7,23},{8,24},{9,... | collective-permute-start | bytes 110600 | tf_op jit(solution)/shard_map/ppermute | solution.py:537
  66.1 4.7 %shard_map.105 = bf16[32,2,64,128]{3,2,1,0:T(8,128)(2,1)} custom-call(s32[1]{0:T(128)} %bitcast.refs_0_.token.me, s32[2,4,128]{2,1,0:T(4,128)S(1)} %bitcast.20, s32[2,4,128]{2,1,0:T(4,128)S(1)} %bitcast.25, bf16[160,128]{1,0:T(8,128)(2,1)S(1)} %get-tuple-element.161.vp.refs_3_, bf16[160,128]{1,0:T(8,128)(2,1)S(1)} %get-tuple-element.162.vm.refs_4_, ...), custom_call_target="tpu_custom_call" | custom-call | flops 1207959552 | bytes 4194304 | tf_op jit(solution)/shard_map/pallas_call | solution.py:692
  70.9 10.7 %all_to_all.10 = bf16[16,72,128]{2,1,0:T(8,128)(2,1)S(1)} all-to-all(bf16[16,72,128]{2,1,0:T(8,128)(2,1)S(1)} %broadcast_in_dim.2), channel_id=1, replica_groups={{0,128,64,192,32,160,96,224,1,129,65,193,33,161,97,225},{2,130,66,194,3..., dimensions={0} | all-to-all | bytes 589824 | tf_op jit(solution)/shard_map/all_to_all | solution.py:568
  81.6 5.7 %collective-permute-start.12 = (bf16[1152,128]{1,0:T(8,128)(2,1)S(1)}, bf16[1152,128]{1,0:T(8,128)(2,1)S(1)}, u32[]{:S(2)}, u32[]{:S(2)}) collective-permute-start(bf16[1152,128]{1,0:T(8,128)(2,1)S(1)} %bitcast.11), channel_id=1, source_target_pairs={{0,2},{1,3},{2,0},{3,1},{4,6},{5,7},{6,4},{7,5},{8,10},{9,11},{10,... | collective-permute-start | bytes 884744 | tf_op jit(solution)/shard_map/ppermute | solution.py:537
  87.4 1.2 %collective-permute-done.12.other = bf16[1152,128]{1,0:T(8,128)(2,1)S(1)} collective-permute-done((bf16[1152,128]{1,0:T(8,128)(2,1)S(1)}, bf16[1152,128]{1,0:T(8,128)(2,1)S(1)}, u32[]{:S(2)}, u32[]{:S(2)}) %collective-permute-start.12) | collective-permute-done | bytes 294944 | tf_op jit(solution)/shard_map/ppermute | solution.py:537
  (44 shorter events, 7.2 us)
Async XLA Ops:
  0.6 1.2 %copy-start = (bf16[1,1,64,64,128]{4,3,2,1,0:T(8,128)(2,1)S(1)}, bf16[1,1,64,64,128]{4,3,2,1,0:T(8,128)(2,1)}, u32[]{:S(2)}) copy-start(bf16[1,1,64,64,128]{4,3,2,1,0:T(8,128)(2,1)} %param.9) | copy-start | bytes 3145732
  1.9 1.2 %copy-start.1 = (bf16[1,1,64,64,128]{4,3,2,1,0:T(8,128)(2,1)S(1)}, bf16[1,1,64,64,128]{4,3,2,1,0:T(8,128)(2,1)}, u32[]{:S(2)}) copy-start(bf16[1,1,64,64,128]{4,3,2,1,0:T(8,128)(2,1)} %param.6) | copy-start | bytes 3145732
  3.1 0.7 copy-start.6
  3.8 0.7 copy-start.8
  4.5 15.4 %copy-start.2 = (bf16[1,1,64,64,128]{4,3,2,1,0:T(8,128)(2,1)S(1)}, bf16[1,1,64,64,128]{4,3,2,1,0:T(8,128)(2,1)}, u32[]{:S(2)}) copy-start(bf16[1,1,64,64,128]{4,3,2,1,0:T(8,128)(2,1)} %param.6) | copy-start | bytes 3145732
  4.5 15.4 %copy-start.3 = (bf16[3,3,128,128]{3,2,1,0:T(8,128)(2,1)S(1)}, bf16[3,3,128,128]{3,2,1,0:T(8,128)(2,1)}, u32[]{:S(2)}) copy-start(bf16[3,3,128,128]{3,2,1,0:T(8,128)(2,1)} %kernel_one.3) | copy-start | bytes 884740
  5.7 9.8 %collective-permute-start = (bf16[160,128]{1,0:T(8,128)(2,1)S(1)}, bf16[160,128]{1,0:T(8,128)(2,1)S(1)}, u32[]{:S(2)}, u32[]{:S(2)}) collective-permute-start(bf16[160,128]{1,0:T(8,128)(2,1)S(1)} %get-tuple-element.93), channel_id=1, source_target_pairs={{0,32},{1,33},{2,34},{3,35},{4,36},{5,37},{6,38},{7,39},{8,40},{9,... | collective-permute-start | bytes 122888 | tf_op jit(solution)/shard_map/ppermute | solution.py:546
  9.5 6.5 %collective-permute-start.1 = (bf16[160,128]{1,0:T(8,128)(2,1)S(1)}, bf16[160,128]{1,0:T(8,128)(2,1)S(1)}, u32[]{:S(2)}, u32[]{:S(2)}) collective-permute-start(bf16[160,128]{1,0:T(8,128)(2,1)S(1)} %get-tuple-element.94), channel_id=1, source_target_pairs={{0,224},{1,225},{2,226},{3,227},{4,228},{5,229},{6,230},{7,231},{8... | collective-permute-start | bytes 122888 | tf_op jit(solution)/shard_map/ppermute | solution.py:546
  11.8 1.0 %copy-start.4 = (bf16[3,3,128,128]{3,2,1,0:T(8,128)(2,1)S(1)}, bf16[3,3,128,128]{3,2,1,0:T(8,128)(2,1)}, u32[]{:S(2)}) copy-start(bf16[3,3,128,128]{3,2,1,0:T(8,128)(2,1)} %kernel_two.3) | copy-start | bytes 884740
  15.5 7.0 %copy-start.7 = (s32[128,2,4]{0,2,1:T(4,128)S(1)}, s32[128,2,4]{0,2,1:T(4,128)}, u32[]{:S(2)}) copy-start(s32[128,2,4]{0,2,1:T(4,128)} %param.10) | copy-start | bytes 12292
  15.5 7.0 %copy-start.9 = (s32[128,2,4]{0,2,1:T(4,128)S(1)}, s32[128,2,4]{0,2,1:T(4,128)}, u32[]{:S(2)}) copy-start(s32[128,2,4]{0,2,1:T(4,128)} %param.11) | copy-start | bytes 12292
  16.0 6.4 %collective-permute-start.2 = (bf16[160,128]{1,0:T(8,128)(2,1)S(1)}, bf16[160,128]{1,0:T(8,128)(2,1)S(1)}, u32[]{:S(2)}, u32[]{:S(2)}) collective-permute-start(bf16[160,128]{1,0:T(8,128)(2,1)S(1)} %get-tuple-element.109), channel_id=1, source_target_pairs={{0,1},{1,0},{2,3},{3,2},{4,5},{5,4},{6,7},{7,6},{8,9},{9,8},{10,11... | collective-permute-start | bytes 122888 | tf_op jit(solution)/shard_map/ppermute | solution.py:546
  16.9 5.6 %collective-permute-start.3 = (bf16[160,128]{1,0:T(8,128)(2,1)S(1)}, bf16[160,128]{1,0:T(8,128)(2,1)S(1)}, u32[]{:S(2)}, u32[]{:S(2)}) collective-permute-start(bf16[160,128]{1,0:T(8,128)(2,1)S(1)} %get-tuple-element.110), channel_id=1, source_target_pairs={{0,255},{1,2},{2,1},{3,4},{4,3},{5,6},{6,5},{7,8},{8,7},{9,10},{10... | collective-permute-start | bytes 122888 | tf_op jit(solution)/shard_map/ppermute | solution.py:546
  28.7 25.7 %copy-start.5 = (bf16[3,3,128,128]{3,2,1,0:T(8,128)(2,1)S(1)}, bf16[3,3,128,128]{3,2,1,0:T(8,128)(2,1)}, u32[]{:S(2)}) copy-start(bf16[3,3,128,128]{3,2,1,0:T(8,128)(2,1)} %kernel_two.3) | copy-start | bytes 884740
  28.7 12.3 %collective-permute-start.4 = (f32[1152,128]{1,0:T(8,128)S(1)}, f32[1152,128]{1,0:T(8,128)S(1)}, u32[]{:S(2)}, u32[]{:S(2)}) collective-permute-start(f32[1152,128]{1,0:T(8,128)S(1)} %shard_map.98), channel_id=1, source_target_pairs={{0,2},{1,3},{2,0},{3,1},{4,6},{5,7},{6,4},{7,5},{8,10},{9,11},{10,... | collective-permute-start | bytes 1769480 | tf_op jit(solution)/shard_map/ppermute | solution.py:537
  34.0 6.9 %collective-permute-start.5 = (bf16[160,128]{1,0:T(8,128)(2,1)S(1)}, bf16[160,128]{1,0:T(8,128)(2,1)S(1)}, u32[]{:S(2)}, u32[]{:S(2)}) collective-permute-start(bf16[160,128]{1,0:T(8,128)(2,1)S(1)} %get-tuple-element.135), channel_id=1, source_target_pairs={{0,32},{1,33},{2,34},{3,35},{4,36},{5,37},{6,38},{7,39},{8,40},{9,... | collective-permute-start | bytes 122888 | tf_op jit(solution)/shard_map/ppermute | solution.py:546
  34.0 6.9 %collective-permute-start.6 = (bf16[160,128]{1,0:T(8,128)(2,1)S(1)}, bf16[160,128]{1,0:T(8,128)(2,1)S(1)}, u32[]{:S(2)}, u32[]{:S(2)}) collective-permute-start(bf16[160,128]{1,0:T(8,128)(2,1)S(1)} %get-tuple-element.136), channel_id=1, source_target_pairs={{0,224},{1,225},{2,226},{3,227},{4,228},{5,229},{6,230},{7,231},{8... | collective-permute-start | bytes 122888 | tf_op jit(solution)/shard_map/ppermute | solution.py:546
  41.8 12.3 %all-to-all-start = ((bf16[16,72,128]{2,1,0:T(8,128)(2,1)}), bf16[16,72,128]{2,1,0:T(8,128)(2,1)S(1)}, u32[]{:S(2)}, u32[]{:S(2)}) async-start(bf16[16,72,128]{2,1,0:T(8,128)(2,1)} %bitcast.5), calls=%async_computation | async-start | bytes 589824 | tf_op jit(solution)/shard_map/all_to_all | solution.py:568
  46.1 8.7 %collective-permute-start.8 = (bf16[160,128]{1,0:T(8,128)(2,1)S(1)}, bf16[160,128]{1,0:T(8,128)(2,1)S(1)}, u32[]{:S(2)}, u32[]{:S(2)}) collective-permute-start(bf16[160,128]{1,0:T(8,128)(2,1)S(1)} %get-tuple-element.150), channel_id=1, source_target_pairs={{0,1},{1,0},{2,3},{3,2},{4,5},{5,4},{6,7},{7,6},{8,9},{9,8},{10,11... | collective-permute-start | bytes 122888 | tf_op jit(solution)/shard_map/ppermute | solution.py:546
  47.5 7.3 %collective-permute-start.9 = (bf16[160,128]{1,0:T(8,128)(2,1)S(1)}, bf16[160,128]{1,0:T(8,128)(2,1)S(1)}, u32[]{:S(2)}, u32[]{:S(2)}) collective-permute-start(bf16[160,128]{1,0:T(8,128)(2,1)S(1)} %get-tuple-element.151), channel_id=1, source_target_pairs={{0,255},{1,2},{2,1},{3,4},{4,3},{5,6},{6,5},{7,8},{8,7},{9,10},{10... | collective-permute-start | bytes 122888 | tf_op jit(solution)/shard_map/ppermute | solution.py:546
  54.2 3.4 %collective-permute-start.7 = (f32[72,128]{1,0:T(8,128)S(1)}, f32[72,128]{1,0:T(8,128)S(1)}, u32[]{:S(2)}, u32[]{:S(2)}) collective-permute-start(f32[72,128]{1,0:T(8,128)S(1)} %shard_map.100), channel_id=1, source_target_pairs={{0,4},{1,5},{2,6},{3,7},{4,0},{5,1},{6,2},{7,3},{8,12},{9,13},{10,... | collective-permute-start | bytes 110600 | tf_op jit(solution)/shard_map/ppermute | solution.py:537
  57.5 4.3 %collective-permute-start.10 = (f32[72,128]{1,0:T(8,128)S(1)}, f32[72,128]{1,0:T(8,128)S(1)}, u32[]{:S(2)}, u32[]{:S(2)}) collective-permute-start(f32[72,128]{1,0:T(8,128)S(1)} %add.18), channel_id=1, source_target_pairs={{0,8},{1,9},{2,10},{3,11},{4,12},{5,13},{6,14},{7,15},{8,0},{9,1},... | collective-permute-start | bytes 110600 | tf_op jit(solution)/shard_map/ppermute | solution.py:537
  61.8 9.0 %collective-permute-start.11 = (f32[72,128]{1,0:T(8,128)S(1)}, f32[72,128]{1,0:T(8,128)S(1)}, u32[]{:S(2)}, u32[]{:S(2)}) collective-permute-start(f32[72,128]{1,0:T(8,128)S(1)} %add.19), channel_id=1, source_target_pairs={{0,16},{1,17},{2,18},{3,19},{4,20},{5,21},{6,22},{7,23},{8,24},{9,... | collective-permute-start | bytes 110600 | tf_op jit(solution)/shard_map/ppermute | solution.py:537
  81.6 6.9 %collective-permute-start.12 = (bf16[1152,128]{1,0:T(8,128)(2,1)S(1)}, bf16[1152,128]{1,0:T(8,128)(2,1)S(1)}, u32[]{:S(2)}, u32[]{:S(2)}) collective-permute-start(bf16[1152,128]{1,0:T(8,128)(2,1)S(1)} %bitcast.11), channel_id=1, source_target_pairs={{0,2},{1,3},{2,0},{3,1},{4,6},{5,7},{6,4},{7,5},{8,10},{9,11},{10,... | collective-permute-start | bytes 884744 | tf_op jit(solution)/shard_map/ppermute | solution.py:537

commit v7 on v6

--- a/solution.py
+++ b/solution.py
@@ -493,8 +493,10 @@
     rows(HALF // mb - 1, last=True)
 
 
-def fold_kernel(parts, total):
-    total[...] = jnp.sum(parts[...].astype(F32), axis=0)
+def fold_kernel(parts, copies):
+    folded = jnp.sum(parts[...].astype(F32), axis=0).astype(copies.dtype)
+    for k in range(copies.shape[0]):
+        copies[k] = folded
 
 
 def finish_kernel(me, mine, other, first, second):
@@ -548,27 +550,24 @@
 
 FIRST = 2
 PLANE = (128, 64, 32, 1)
-WHOLE = (4, 8, 16)
-
-
-def plane_groups(size):
-    mask = sum(PLANE)
-    rest = [i for i in range(size) if i & mask == 0]
-    members = [sum(bit for k, bit in enumerate(PLANE) if n >> k & 1) for n in range(1 << len(PLANE))]
+RING = (16, 8, 4)
+
+
+def groups_over(bits, size):
+    rest = [i for i in range(size) if i & sum(bits) == 0]
+    members = [sum(bit for k, bit in enumerate(bits) if n >> k & 1) for n in range(1 << len(bits))]
     return [[base + member for member in members] for base in rest]
 
 
 def total(send, done, works):
     me = lax.axis_index(AXES).astype(jnp.int32)
-    groups = plane_groups(lax.axis_size(AXES))
+    plane, ring = [groups_over(bits, lax.axis_size(AXES)) for bits in (PLANE, RING)]
     steps = [0]
-    free = {}
-
-    def scatter(sent):
-        return lax.all_to_all(sent, AXES, 0, 0, axis_index_groups=groups, tiled=True)
-
-    def beside(sent, bit):
-        move = scatter if bit is None else lambda sent: swap(sent, bit)
+
+    def scatter(groups):
+        return lambda sent: lax.all_to_all(sent, AXES, 0, 0, axis_index_groups=groups, tiled=True)
+
+    def beside(sent, move):
         work = works.get(steps[0])
         steps[0] += 1
         if work is None:
@@ -576,23 +575,26 @@
         sent, held = lax.optimization_barrier((sent, done.copy()))
         done.update(held)
         got = move(sent)
-        gave, loose = work(done, free)
+        gave = work(done)
         got, gave = lax.optimization_barrier((got, gave))
         done.update(gave)
-        free.update(loose)
         return got
 
-    x = beside(send, FIRST)
-    x = done["keep"] + x
-    parts = (len(groups[0]), x.shape[0] // len(groups[0]), CH)
-    spread = beside(x.astype(BF16).reshape(parts), None)
-    x, = call(fold_kernel, 0, 1, (struct(parts[1:], F32),), (), 0, 1 << 19)(spread)
-    for bit in WHOLE:
-        x = x + beside(x, bit)
-    spread = jnp.broadcast_to(x.astype(BF16)[None], parts)
-    x = beside(spread, None).reshape(-1, CH)
+    def fold(x, parts, dtype):
+        folded, = call(fold_kernel, 0, 1, (struct((parts,) + x.shape[1:], dtype),), (), 0, 1 << 19)(x)
+        return folded
+
+    def across(sent):
+        return swap(sent, FIRST)
+
+    x = beside(send, across)
+    x = (done["keep"] + x).astype(BF16)
+    parts = len(plane[0])
+    x = beside(x.reshape(parts, x.shape[0] // parts, CH), scatter(plane))
+    x = beside(fold(x, len(ring[0]), F32), scatter(ring))
+    x = beside(fold(x, parts, BF16), scatter(plane)).reshape(-1, CH)
     out = struct(x.shape, F32)
-    grads = call(finish_kernel, 1, 2, (out, out))(me.reshape(1), x, beside(x, FIRST))
+    grads = call(finish_kernel, 1, 2, (out, out))(me.reshape(1), x, beside(x, across))
     return grads, done
 
 
@@ -661,43 +663,37 @@
         )
         return got
 
-    def first_work(done, free):
+    def first_work(done):
         va, vb = both_ways(done["va"], done["vb"], width)
-        return dict(keep=half(True, done["token"]), va=va, vb=vb), {}
-
-    def second_work(done, free):
+        return dict(keep=half(True, done["token"]), va=va, vb=vb)
+
+    def second_work(done):
         vp, vm, ha, hb = relay(done["token"], done["va"], done["vb"], hp2, hm2)
         ha, hb = both_ways(ha, hb, 1)
-        return {}, dict(vp=vp, vm=vm, ha=ha, hb=hb)
-
-    def third_work(done, free):
+        return dict(vp=vp, vm=vm, ha=ha, hb=hb)
+
+    def third_work(done):
         hp, hm = call(name_kernel, 1, 2, (message, message), (), 0, 1 << 18)(
-            done["token"], free["ha"], free["hb"]
+            done["token"], done["ha"], done["hb"]
         )
         in_one, fwd_two = call(weights_kernel, 1, 2, (weights, weights))(
             done["token"], kernel_one, kernel_two
         )
-        return dict(in_one=in_one, fwd_two=fwd_two, hp=hp, hm=hm), {}
-
-    def messages(done, free):
-        return free["vp"], free["vm"], done["hp"], done["hm"]
-
-    def make_outputs(done, free):
         outputs, = call(
             outputs_kernel, 0, 6, (block,), [pltpu.VMEM(COPIES, BF16), column, column], conv_flops
-        )(hidden, *messages(done, free), done["fwd_two"])
-        return dict(outputs=outputs), {}
-
-    def make_grads(done, free):
+        )(hidden, done["vp"], done["vm"], hp, hm, fwd_two)
+        return dict(in_one=in_one, hp=hp, hm=hm, outputs=outputs)
+
+    def fourth_work(done):
         grad_fields, = call(
             lambda *refs: grads_kernel(count, width, *refs), 3, 6, (block,),
             [pltpu.VMEM(COPIES, BF16), strips], conv_flops,
-        )(*tables, *messages(done, free), grad_pre, done["in_one"])
-        return dict(grad_fields=grad_fields), {}
+        )(*tables, done["vp"], done["vm"], done["hp"], done["hm"], grad_pre, done["in_one"])
+        return dict(grad_fields=grad_fields)
 
     grads, done = total(
         half(False, token), dict(va=va2, vb=vb2, token=token),
-        {0: first_work, 1: second_work, 2: third_work, 3: make_outputs, 4: make_grads},
+        {0: first_work, 1: second_work, 2: third_work, 3: fourth_work},
     )
     shape = (1, 1, SIDE, SIDE, CH)
     return (

time: 90 us -> 91.3 us (1.014)
  blocking collectives: 10.7 us -> 0 us
  starting transfers between devices: 37.4 us -> 44.2 us
  local copies, waits for them, and re-layouts: 4.84 us -> 6.8 us
  waiting for transfers between devices: 9 us -> 10.7 us
  Pallas kernels: 26 us -> 27.4 us
    all_to_all x1 -> x3, starting transfers between devices: 4.23 us -> 20 us  [scatter(): lax.all_to_all(sent, AXES, 0, 0, axis_index_groups=groups, tiled=True)]
    all_to_all x1 -> x0, blocking collectives: 10.7 us -> none  [scatter(): lax.all_to_all(sent, AXES, 0, 0, axis_index_groups=groups, tiled=True)]
    ppermute x5 -> x2, starting transfers between devices: 16.4 us -> 7.43 us  [swap(): return lax.ppermute(x, AXES, [(i, i ^ bit) for i in range(size)])]
    ppermute x4, waiting for transfers between devices: 0.49 us -> 4.9 us  [both_ways(): lax.ppermute(two, AXES, pairs(1))]
    ppermute x5 -> x2, waiting for transfers between devices: 3.96 us -> 1.21 us  [swap(): return lax.ppermute(x, AXES, [(i, i ^ bit) for i in range(size)])]
    unnamed x20 -> x24, local copies, waits for them, and re-layouts: 4.8 us -> 6.8 us
    pallas_call x4 -> x5, Pallas kernels: 9.33 us -> 10.8 us  [the longest x1 4.72 us: fourth_work(): call(lambda *refs: grads_kernel(count, width, *refs), 3, 6, (block,), [pl...]
    all_to_all x1 -> x3, waiting for transfers between devices: 4.54 us -> 4.58 us  [scatter(): lax.all_to_all(sent, AXES, 0, 0, axis_index_groups=groups, tiled=True)]
  transfers between devices with their start and end apart: 14 -> 13, of which waited for: 4 -> 6; matrix products, arithmetic and copies ran while one was open for 0% -> 0% of each run, Pallas kernels for 19% -> 19%
where the time goes in v7:
time: 91.3 us; the launch traced here: 90.7 us
  starting transfers between devices  44.2 us (48%)
  Pallas kernels  27.4 us (30%)
  waiting for transfers between devices  10.7 us (12%)
  local copies, waits for them, and re-layouts  6.8 us (7%)
    all_to_all x3, starting transfers between devices, scatter(): lax.all_to_all(sent, AXES, 0, 0, axis_index_groups=groups, tiled=True)  20 us
    ppermute x4, starting transfers between devices, both_ways(): lax.ppermute(two, AXES, pairs(1))  10.6 us
    ppermute x2, starting transfers between devices, swap(): return lax.ppermute(x, AXES, [(i, i ^ bit) for i in range(size)])  7.43 us
    pallas_call x2, Pallas kernels, half(): call(lambda me, *refs: sums_kernel(count, width, scale, kept, me, *refs),...  7.15 us
    unnamed x24, local copies, waits for them, and re-layouts  6.8 us
    ppermute x4, starting transfers between devices, both_ways(): lax.ppermute(one, AXES, pairs(0))  6.18 us
    ppermute x4, waiting for transfers between devices, both_ways(): lax.ppermute(two, AXES, pairs(1))  4.9 us
    pallas_call x1, Pallas kernels, fourth_work(): call(lambda *refs: grads_kernel(count, width, *refs), 3, 6, (block,), [pl...  4.72 us
  transfers between devices with their start and end apart: 13, of which 6 were waited for; matrix products, arithmetic and copies ran while one was open for 0% of the time, Pallas kernels for 19%

profile of v7, /device:TPU:1, one launch (start us, length us, event | category | flops | bytes accessed | tf_op | source)
XLA Modules:
  0.0 90.7 jit_solution(15303651343844663145)
XLA Ops:
  0.6 1.2 %copy-done = bf16[1,1,64,64,128]{4,3,2,1,0:T(8,128)(2,1)S(1)} copy-done((bf16[1,1,64,64,128]{4,3,2,1,0:T(8,128)(2,1)S(1)}, bf16[1,1,64,64,128]{4,3,2,1,0:T(8,128)(2,1)}, u32[]{:S(2)}) %copy-start) | copy-done | bytes 1048600
  1.9 1.2 %copy-done.1 = bf16[1,1,64,64,128]{4,3,2,1,0:T(8,128)(2,1)S(1)} copy-done((bf16[1,1,64,64,128]{4,3,2,1,0:T(8,128)(2,1)S(1)}, bf16[1,1,64,64,128]{4,3,2,1,0:T(8,128)(2,1)}, u32[]{:S(2)}) %copy-start.1) | copy-done | bytes 1048600
  5.7 3.8 %collective-permute-start = (bf16[160,128]{1,0:T(8,128)(2,1)S(1)}, bf16[160,128]{1,0:T(8,128)(2,1)S(1)}, u32[]{:S(2)}, u32[]{:S(2)}) collective-permute-start(bf16[160,128]{1,0:T(8,128)(2,1)S(1)} %get-tuple-element.97), channel_id=1, source_target_pairs={{0,32},{1,33},{2,34},{3,35},{4,36},{5,37},{6,38},{7,39},{8,40},{9,... | collective-permute-start | bytes 122888 | tf_op jit(solution)/shard_map/ppermute | solution.py:548
  9.5 2.3 %collective-permute-start.1 = (bf16[160,128]{1,0:T(8,128)(2,1)S(1)}, bf16[160,128]{1,0:T(8,128)(2,1)S(1)}, u32[]{:S(2)}, u32[]{:S(2)}) collective-permute-start(bf16[160,128]{1,0:T(8,128)(2,1)S(1)} %get-tuple-element.98), channel_id=1, source_target_pairs={{0,224},{1,225},{2,226},{3,227},{4,228},{5,229},{6,230},{7,231},{8... | collective-permute-start | bytes 122888 | tf_op jit(solution)/shard_map/ppermute | solution.py:548
  12.8 2.7 %shard_map.94 = (bf16[1536,256]{1,0:T(8,128)(2,1)S(1)}, bf16[3,33,2,64,128]{4,3,2,1,0:T(8,128)(2,1)S(1)}, f32[32,2,64,128]{3,2,1,0:T(8,128)S(1)}) custom-call(s32[1]{0:T(128)} %bitcast.refs_0_.token.me, bf16[3,3,128,128]{3,2,1,0:T(8,128)(2,1)S(1)} %copy-done.4, bf16[32,2,64,128]{3,2,1,0:T(8,128)(2,1)S(1)} %get-tuple-element.100.upstream), custom_call_target="tpu_custom_call" | custom-call | flops 1207959552 | bytes 4194304 | tf_op jit(solution)/shard_map/pallas_call | solution.py:628
  16.9 2.9 %collective-permute-start.3 = (bf16[160,128]{1,0:T(8,128)(2,1)S(1)}, bf16[160,128]{1,0:T(8,128)(2,1)S(1)}, u32[]{:S(2)}, u32[]{:S(2)}) collective-permute-start(bf16[160,128]{1,0:T(8,128)(2,1)S(1)} %get-tuple-element.114), channel_id=1, source_target_pairs={{0,255},{1,2},{2,1},{3,4},{4,3},{5,6},{6,5},{7,8},{8,7},{9,10},{10... | collective-permute-start | bytes 122888 | tf_op jit(solution)/shard_map/ppermute | solution.py:548
  19.8 2.6 %shard_map.96 = (bf16[1536,256]{1,0:T(8,128)(2,1)S(1)}, bf16[3,33,2,64,128]{4,3,2,1,0:T(8,128)(2,1)S(1)}, f32[32,2,64,128]{3,2,1,0:T(8,128)S(1)}) custom-call(s32[1]{0:T(128)} %bitcast.refs_0_.token.me, bf16[3,3,128,128]{3,2,1,0:T(8,128)(2,1)S(1)} %copy-done.3, bf16[32,2,64,128]{3,2,1,0:T(8,128)(2,1)S(1)} %bitcast.15), custom_call_target="tpu_custom_call" | custom-call | flops 1207959552 | bytes 4194304 | tf_op jit(solution)/shard_map/pallas_call | solution.py:643
  22.5 2.6 %shard_map.97 = (bf16[32,2,64,128]{3,2,1,0:T(8,128)(2,1)S(1)}, bf16[32,2,64,128]{3,2,1,0:T(8,128)(2,1)S(1)}, bf16[160,128]{1,0:T(8,128)(2,1)S(1)}, bf16[160,128]...) custom-call(s32[1]{0:T(128)} %bitcast.refs_0_.token.me, ...), custom_call_target="tpu_custom_call" | custom-call | flops 1207959552 | bytes 4194304 | tf_op jit(solution)/shard_map/pallas_call | solution.py:646
  25.1 3.6 %shard_map.98 = f32[1152,128]{1,0:T(8,128)S(1)} custom-call(s32[1]{0:T(128)} %bitcast.refs_0_.token.me, s32[2,4,128]{2,1,0:T(4,128)S(1)} %bitcast.18, s32[2,4,128]{2,1,0:T(4,128)S(1)} %bitcast.23, bf16[160,128]{1,0:T(8,128)(2,1)S(1)} %get-tuple-element.109.refs_3_.refs_2_, bf16[160,128]{1,0:T(8,128)(2,1)S(1)} %get-tuple-element.110.refs_4_.refs_3_, ...), custom_call_target="tpu_custom_call" | custom-call | flops 1207959552 | bytes 4194304 | tf_op jit(solution)/shard_map/pallas_call | solution.py:657
  28.7 5.3 %collective-permute-start.4 = (f32[1152,128]{1,0:T(8,128)S(1)}, f32[1152,128]{1,0:T(8,128)S(1)}, u32[]{:S(2)}, u32[]{:S(2)}) collective-permute-start(f32[1152,128]{1,0:T(8,128)S(1)} %shard_map.98), channel_id=1, source_target_pairs={{0,2},{1,3},{2,0},{3,1},{4,6},{5,7},{6,4},{7,5},{8,10},{9,11},{10,... | collective-permute-start | bytes 1769480 | tf_op jit(solution)/shard_map/ppermute | solution.py:539
  34.0 3.3 %collective-permute-start.6 = (bf16[160,128]{1,0:T(8,128)(2,1)S(1)}, bf16[160,128]{1,0:T(8,128)(2,1)S(1)}, u32[]{:S(2)}, u32[]{:S(2)}) collective-permute-start(bf16[160,128]{1,0:T(8,128)(2,1)S(1)} %get-tuple-element.140), channel_id=1, source_target_pairs={{0,224},{1,225},{2,226},{3,227},{4,228},{5,229},{6,230},{7,231},{8... | collective-permute-start | bytes 122888 | tf_op jit(solution)/shard_map/ppermute | solution.py:548
  37.4 3.6 %shard_map.99 = f32[1152,128]{1,0:T(8,128)S(1)} custom-call(s32[1]{0:T(128)} %bitcast.refs_0_.token.me, s32[2,4,128]{2,1,0:T(4,128)S(1)} %bitcast.19, s32[2,4,128]{2,1,0:T(4,128)S(1)} %bitcast.24, bf16[160,128]{1,0:T(8,128)(2,1)S(1)} %get-tuple-element.109.refs_3_.refs_2_, bf16[160,128]{1,0:T(8,128)(2,1)S(1)} %get-tuple-element.110.refs_4_.refs_3_, ...), custom_call_target="tpu_custom_call" | custom-call | flops 1207959552 | bytes 4194304 | tf_op jit(solution)/shard_map/pallas_call | solution.py:657
  41.8 4.2 %all-to-all-start = ((bf16[16,72,128]{2,1,0:T(8,128)(2,1)}), bf16[16,72,128]{2,1,0:T(8,128)(2,1)S(1)}, u32[]{:S(2)}, u32[]{:S(2)}) async-start(bf16[16,72,128]{2,1,0:T(8,128)(2,1)} %bitcast.5), calls=%async_computation | async-start | bytes 589824 | tf_op jit(solution)/shard_map/all_to_all | solution.py:568
  46.0 1.4 %collective-permute-start.7 = (bf16[160,128]{1,0:T(8,128)(2,1)S(1)}, bf16[160,128]{1,0:T(8,128)(2,1)S(1)}, u32[]{:S(2)}, u32[]{:S(2)}) collective-permute-start(bf16[160,128]{1,0:T(8,128)(2,1)S(1)} %get-tuple-element.151), channel_id=1, source_target_pairs={{0,1},{1,0},{2,3},{3,2},{4,5},{5,4},{6,7},{7,6},{8,9},{9,8},{10,11... | collective-permute-start | bytes 122888 | tf_op jit(solution)/shard_map/ppermute | solution.py:548
  47.5 2.1 %collective-permute-start.8 = (bf16[160,128]{1,0:T(8,128)(2,1)S(1)}, bf16[160,128]{1,0:T(8,128)(2,1)S(1)}, u32[]{:S(2)}, u32[]{:S(2)}) collective-permute-start(bf16[160,128]{1,0:T(8,128)(2,1)S(1)} %get-tuple-element.152), channel_id=1, source_target_pairs={{0,255},{1,2},{2,1},{3,4},{4,3},{5,6},{6,5},{7,8},{8,7},{9,10},{10... | collective-permute-start | bytes 122888 | tf_op jit(solution)/shard_map/ppermute | solution.py:548
  49.6 4.4 %collective-permute-done.8.two = bf16[160,128]{1,0:T(8,128)(2,1)S(1)} collective-permute-done((bf16[160,128]{1,0:T(8,128)(2,1)S(1)}, bf16[160,128]{1,0:T(8,128)(2,1)S(1)}, u32[]{:S(2)}, u32[]{:S(2)}) %collective-permute-start.8) | collective-permute-done | bytes 40992 | tf_op jit(solution)/shard_map/ppermute | solution.py:548
  54.9 6.5 %all-to-all-start.1 = ((f32[8,72,128]{2,1,0:T(8,128)}), f32[8,72,128]{2,1,0:T(8,128)S(1)}, u32[]{:S(2)}, u32[]{:S(2)}) async-start(f32[8,72,128]{2,1,0:T(8,128)} %shard_map.101), calls=%async_computation.1 | async-start | bytes 589824 | tf_op jit(solution)/shard_map/all_to_all | solution.py:568
  62.6 3.5 %shard_map.104 = bf16[32,2,64,128]{3,2,1,0:T(8,128)(2,1)} custom-call(bf16[32,2,64,128]{3,2,1,0:T(8,128)(2,1)S(1)} %get-tuple-element.127.refs_6_.hidden, bf16[160,128]{1,0:T(8,128)(2,1)S(1)} %get-tuple-element.177.vp.refs_3_, bf16[160,128]{1,0:T(8,128)(2,1)S(1)} %get-tuple-element.178.vm.refs_4_, bf16[160,128]{1,0:T(8,128)(2,1)S(1)} %get-tuple-element.179.hp.refs_5_, ...), custom_call_target="tpu_custom_call" | custom-call | flops 1207959552 | bytes 4194304 | tf_op jit(solution)/shard_map/pallas_call | solution.py:682
  66.0 2.5 %all-to-all-done.1.parts = f32[8,72,128]{2,1,0:T(8,128)S(1)} async-done(((f32[8,72,128]{2,1,0:T(8,128)}), f32[8,72,128]{2,1,0:T(8,128)S(1)}, u32[]{:S(2)}, u32[]{:S(2)}) %all-to-all-start.1) | async-done | bytes 294944 | tf_op jit(solution)/shard_map/all_to_all | solution.py:568
  69.3 9.2 %all-to-all-start.2 = ((bf16[16,72,128]{2,1,0:T(8,128)(2,1)}), bf16[16,72,128]{2,1,0:T(8,128)(2,1)S(1)}, u32[]{:S(2)}, u32[]{:S(2)}) async-start(bf16[16,72,128]{2,1,0:T(8,128)(2,1)} %shard_map.105), calls=%async_computation.2 | async-start | bytes 589824 | tf_op jit(solution)/shard_map/all_to_all | solution.py:568
  79.7 4.7 %shard_map.106 = bf16[32,2,64,128]{3,2,1,0:T(8,128)(2,1)} custom-call(s32[1]{0:T(128)} %bitcast.refs_0_.token.me, s32[2,4,128]{2,1,0:T(4,128)S(1)} %bitcast.20, s32[2,4,128]{2,1,0:T(4,128)S(1)} %bitcast.25, bf16[160,128]{1,0:T(8,128)(2,1)S(1)} %get-tuple-element.177.vp.refs_3_, bf16[160,128]{1,0:T(8,128)(2,1)S(1)} %get-tuple-element.178.vm.refs_4_, ...), custom_call_target="tpu_custom_call" | custom-call | flops 1207959552 | bytes 4194304 | tf_op jit(solution)/shard_map/pallas_call | solution.py:688
  84.4 1.9 %all-to-all-done.2 = bf16[16,72,128]{2,1,0:T(8,128)(2,1)S(1)} async-done(((bf16[16,72,128]{2,1,0:T(8,128)(2,1)}), bf16[16,72,128]{2,1,0:T(8,128)(2,1)S(1)}, u32[]{:S(2)}, u32[]{:S(2)}) %all-to-all-start.2) | async-done | bytes 294944 | tf_op jit(solution)/shard_map/all_to_all | solution.py:568
  86.3 2.1 %collective-permute-start.9 = (bf16[1152,128]{1,0:T(8,128)(2,1)S(1)}, bf16[1152,128]{1,0:T(8,128)(2,1)S(1)}, u32[]{:S(2)}, u32[]{:S(2)}) collective-permute-start(bf16[1152,128]{1,0:T(8,128)(2,1)S(1)} %bitcast.11), channel_id=1, source_target_pairs={{0,2},{1,3},{2,0},{3,1},{4,6},{5,7},{6,4},{7,5},{8,10},{9,11},{10,... | collective-permute-start | bytes 884744 | tf_op jit(solution)/shard_map/ppermute | solution.py:539
  88.4 1.2 %collective-permute-done.9.other = bf16[1152,128]{1,0:T(8,128)(2,1)S(1)} collective-permute-done((bf16[1152,128]{1,0:T(8,128)(2,1)S(1)}, bf16[1152,128]{1,0:T(8,128)(2,1)S(1)}, u32[]{:S(2)}, u32[]{:S(2)}) %collective-permute-start.9) | collective-permute-done | bytes 294944 | tf_op jit(solution)/shard_map/ppermute | solution.py:539
  (42 shorter events, 10.8 us)
Async XLA Ops:
  0.6 1.2 %copy-start = (bf16[1,1,64,64,128]{4,3,2,1,0:T(8,128)(2,1)S(1)}, bf16[1,1,64,64,128]{4,3,2,1,0:T(8,128)(2,1)}, u32[]{:S(2)}) copy-start(bf16[1,1,64,64,128]{4,3,2,1,0:T(8,128)(2,1)} %param.9) | copy-start | bytes 3145732
  1.9 1.2 %copy-start.1 = (bf16[1,1,64,64,128]{4,3,2,1,0:T(8,128)(2,1)S(1)}, bf16[1,1,64,64,128]{4,3,2,1,0:T(8,128)(2,1)}, u32[]{:S(2)}) copy-start(bf16[1,1,64,64,128]{4,3,2,1,0:T(8,128)(2,1)} %param.6) | copy-start | bytes 3145732
  3.1 0.7 copy-start.6
  4.5 15.4 %copy-start.2 = (bf16[1,1,64,64,128]{4,3,2,1,0:T(8,128)(2,1)S(1)}, bf16[1,1,64,64,128]{4,3,2,1,0:T(8,128)(2,1)}, u32[]{:S(2)}) copy-start(bf16[1,1,64,64,128]{4,3,2,1,0:T(8,128)(2,1)} %param.6) | copy-start | bytes 3145732
  4.5 15.4 %copy-start.3 = (bf16[3,3,128,128]{3,2,1,0:T(8,128)(2,1)S(1)}, bf16[3,3,128,128]{3,2,1,0:T(8,128)(2,1)}, u32[]{:S(2)}) copy-start(bf16[3,3,128,128]{3,2,1,0:T(8,128)(2,1)} %kernel_one.3) | copy-start | bytes 884740
  5.7 9.8 %collective-permute-start = (bf16[160,128]{1,0:T(8,128)(2,1)S(1)}, bf16[160,128]{1,0:T(8,128)(2,1)S(1)}, u32[]{:S(2)}, u32[]{:S(2)}) collective-permute-start(bf16[160,128]{1,0:T(8,128)(2,1)S(1)} %get-tuple-element.97), channel_id=1, source_target_pairs={{0,32},{1,33},{2,34},{3,35},{4,36},{5,37},{6,38},{7,39},{8,40},{9,... | collective-permute-start | bytes 122888 | tf_op jit(solution)/shard_map/ppermute | solution.py:548
  9.5 6.5 %collective-permute-start.1 = (bf16[160,128]{1,0:T(8,128)(2,1)S(1)}, bf16[160,128]{1,0:T(8,128)(2,1)S(1)}, u32[]{:S(2)}, u32[]{:S(2)}) collective-permute-start(bf16[160,128]{1,0:T(8,128)(2,1)S(1)} %get-tuple-element.98), channel_id=1, source_target_pairs={{0,224},{1,225},{2,226},{3,227},{4,228},{5,229},{6,230},{7,231},{8... | collective-permute-start | bytes 122888 | tf_op jit(solution)/shard_map/ppermute | solution.py:548
  11.8 1.0 %copy-start.4 = (bf16[3,3,128,128]{3,2,1,0:T(8,128)(2,1)S(1)}, bf16[3,3,128,128]{3,2,1,0:T(8,128)(2,1)}, u32[]{:S(2)}) copy-start(bf16[3,3,128,128]{3,2,1,0:T(8,128)(2,1)} %kernel_two.3) | copy-start | bytes 884740
  15.5 7.0 %copy-start.7 = (s32[128,2,4]{0,2,1:T(4,128)S(1)}, s32[128,2,4]{0,2,1:T(4,128)}, u32[]{:S(2)}) copy-start(s32[128,2,4]{0,2,1:T(4,128)} %param.10) | copy-start | bytes 12292
  15.5 7.0 %copy-start.9 = (s32[128,2,4]{0,2,1:T(4,128)S(1)}, s32[128,2,4]{0,2,1:T(4,128)}, u32[]{:S(2)}) copy-start(s32[128,2,4]{0,2,1:T(4,128)} %param.11) | copy-start | bytes 12292
  16.0 6.4 %collective-permute-start.2 = (bf16[160,128]{1,0:T(8,128)(2,1)S(1)}, bf16[160,128]{1,0:T(8,128)(2,1)S(1)}, u32[]{:S(2)}, u32[]{:S(2)}) collective-permute-start(bf16[160,128]{1,0:T(8,128)(2,1)S(1)} %get-tuple-element.113), channel_id=1, source_target_pairs={{0,1},{1,0},{2,3},{3,2},{4,5},{5,4},{6,7},{7,6},{8,9},{9,8},{10,11... | collective-permute-start | bytes 122888 | tf_op jit(solution)/shard_map/ppermute | solution.py:548
  16.9 5.6 %collective-permute-start.3 = (bf16[160,128]{1,0:T(8,128)(2,1)S(1)}, bf16[160,128]{1,0:T(8,128)(2,1)S(1)}, u32[]{:S(2)}, u32[]{:S(2)}) collective-permute-start(bf16[160,128]{1,0:T(8,128)(2,1)S(1)} %get-tuple-element.114), channel_id=1, source_target_pairs={{0,255},{1,2},{2,1},{3,4},{4,3},{5,6},{6,5},{7,8},{8,7},{9,10},{10... | collective-permute-start | bytes 122888 | tf_op jit(solution)/shard_map/ppermute | solution.py:548
  28.7 12.3 %collective-permute-start.4 = (f32[1152,128]{1,0:T(8,128)S(1)}, f32[1152,128]{1,0:T(8,128)S(1)}, u32[]{:S(2)}, u32[]{:S(2)}) collective-permute-start(f32[1152,128]{1,0:T(8,128)S(1)} %shard_map.98), channel_id=1, source_target_pairs={{0,2},{1,3},{2,0},{3,1},{4,6},{5,7},{6,4},{7,5},{8,10},{9,11},{10,... | collective-permute-start | bytes 1769480 | tf_op jit(solution)/shard_map/ppermute | solution.py:539
  34.0 6.9 %collective-permute-start.5 = (bf16[160,128]{1,0:T(8,128)(2,1)S(1)}, bf16[160,128]{1,0:T(8,128)(2,1)S(1)}, u32[]{:S(2)}, u32[]{:S(2)}) collective-permute-start(bf16[160,128]{1,0:T(8,128)(2,1)S(1)} %get-tuple-element.139), channel_id=1, source_target_pairs={{0,32},{1,33},{2,34},{3,35},{4,36},{5,37},{6,38},{7,39},{8,40},{9,... | collective-permute-start | bytes 122888 | tf_op jit(solution)/shard_map/ppermute | solution.py:548
  34.0 6.9 %collective-permute-start.6 = (bf16[160,128]{1,0:T(8,128)(2,1)S(1)}, bf16[160,128]{1,0:T(8,128)(2,1)S(1)}, u32[]{:S(2)}, u32[]{:S(2)}) collective-permute-start(bf16[160,128]{1,0:T(8,128)(2,1)S(1)} %get-tuple-element.140), channel_id=1, source_target_pairs={{0,224},{1,225},{2,226},{3,227},{4,228},{5,229},{6,230},{7,231},{8... | collective-permute-start | bytes 122888 | tf_op jit(solution)/shard_map/ppermute | solution.py:548
  40.9 20.4 %copy-start.5 = (bf16[3,3,128,128]{3,2,1,0:T(8,128)(2,1)S(1)}, bf16[3,3,128,128]{3,2,1,0:T(8,128)(2,1)}, u32[]{:S(2)}) copy-start(bf16[3,3,128,128]{3,2,1,0:T(8,128)(2,1)} %kernel_two.3) | copy-start | bytes 884740
  41.8 12.3 %all-to-all-start = ((bf16[16,72,128]{2,1,0:T(8,128)(2,1)}), bf16[16,72,128]{2,1,0:T(8,128)(2,1)S(1)}, u32[]{:S(2)}, u32[]{:S(2)}) async-start(bf16[16,72,128]{2,1,0:T(8,128)(2,1)} %bitcast.5), calls=%async_computation | async-start | bytes 589824 | tf_op jit(solution)/shard_map/all_to_all | solution.py:568
  46.0 3.5 %collective-permute-start.7 = (bf16[160,128]{1,0:T(8,128)(2,1)S(1)}, bf16[160,128]{1,0:T(8,128)(2,1)S(1)}, u32[]{:S(2)}, u32[]{:S(2)}) collective-permute-start(bf16[160,128]{1,0:T(8,128)(2,1)S(1)} %get-tuple-element.151), channel_id=1, source_target_pairs={{0,1},{1,0},{2,3},{3,2},{4,5},{5,4},{6,7},{7,6},{8,9},{9,8},{10,11... | collective-permute-start | bytes 122888 | tf_op jit(solution)/shard_map/ppermute | solution.py:548
  47.5 6.5 %collective-permute-start.8 = (bf16[160,128]{1,0:T(8,128)(2,1)S(1)}, bf16[160,128]{1,0:T(8,128)(2,1)S(1)}, u32[]{:S(2)}, u32[]{:S(2)}) collective-permute-start(bf16[160,128]{1,0:T(8,128)(2,1)S(1)} %get-tuple-element.152), channel_id=1, source_target_pairs={{0,255},{1,2},{2,1},{3,4},{4,3},{5,6},{6,5},{7,8},{8,7},{9,10},{10... | collective-permute-start | bytes 122888 | tf_op jit(solution)/shard_map/ppermute | solution.py:548
  54.9 13.7 %all-to-all-start.1 = ((f32[8,72,128]{2,1,0:T(8,128)}), f32[8,72,128]{2,1,0:T(8,128)S(1)}, u32[]{:S(2)}, u32[]{:S(2)}) async-start(f32[8,72,128]{2,1,0:T(8,128)} %shard_map.101), calls=%async_computation.1 | async-start | bytes 589824 | tf_op jit(solution)/shard_map/all_to_all | solution.py:568
  61.7 0.9 copy-start.10
  69.3 17.0 %all-to-all-start.2 = ((bf16[16,72,128]{2,1,0:T(8,128)(2,1)}), bf16[16,72,128]{2,1,0:T(8,128)(2,1)S(1)}, u32[]{:S(2)}, u32[]{:S(2)}) async-start(bf16[16,72,128]{2,1,0:T(8,128)(2,1)} %shard_map.105), calls=%async_computation.2 | async-start | bytes 589824 | tf_op jit(solution)/shard_map/all_to_all | solution.py:568
  78.5 1.1 %copy-start.11 = (bf16[1536,256]{1,0:T(8,128)(2,1)S(1)}, bf16[1536,256]{1,0:T(8,128)(2,1)}, u32[]{:S(2)}) copy-start(bf16[1536,256]{1,0:T(8,128)(2,1)} %copy-done.10) | copy-start | bytes 2359300
  86.3 3.3 %collective-permute-start.9 = (bf16[1152,128]{1,0:T(8,128)(2,1)S(1)}, bf16[1152,128]{1,0:T(8,128)(2,1)S(1)}, u32[]{:S(2)}, u32[]{:S(2)}) collective-permute-start(bf16[1152,128]{1,0:T(8,128)(2,1)S(1)} %bitcast.11), channel_id=1, source_target_pairs={{0,2},{1,3},{2,0},{3,1},{4,6},{5,7},{6,4},{7,5},{8,10},{9,11},{10,... | collective-permute-start | bytes 884744 | tf_op jit(solution)/shard_map/ppermute | solution.py:539
  (1 other events, 0.7 us)

commit v8 on v7

--- a/solution.py
+++ b/solution.py
@@ -682,18 +682,15 @@
         outputs, = call(
             outputs_kernel, 0, 6, (block,), [pltpu.VMEM(COPIES, BF16), column, column], conv_flops
         )(hidden, done["vp"], done["vm"], hp, hm, fwd_two)
-        return dict(in_one=in_one, hp=hp, hm=hm, outputs=outputs)
-
-    def fourth_work(done):
         grad_fields, = call(
             lambda *refs: grads_kernel(count, width, *refs), 3, 6, (block,),
             [pltpu.VMEM(COPIES, BF16), strips], conv_flops,
-        )(*tables, done["vp"], done["vm"], done["hp"], done["hm"], grad_pre, done["in_one"])
-        return dict(grad_fields=grad_fields)
+        )(*tables, done["vp"], done["vm"], hp, hm, grad_pre, in_one)
+        return dict(outputs=outputs, grad_fields=grad_fields)
 
     grads, done = total(
         half(False, token), dict(va=va2, vb=vb2, token=token),
-        {0: first_work, 1: second_work, 2: third_work, 3: fourth_work},
+        {0: first_work, 1: second_work, 2: third_work},
     )
     shape = (1, 1, SIDE, SIDE, CH)
     return (

time: 91.3 us -> 90.3 us (0.989)
  blocking collectives: 0 us -> 15.5 us
  starting transfers between devices: 44.2 us -> 35 us
  waiting for transfers between devices: 10.7 us -> 6.24 us
  local copies, waits for them, and re-layouts: 6.8 us -> 4.8 us
    all_to_all x0 -> x1, blocking collectives: none -> 15.5 us  [scatter(): lax.all_to_all(sent, AXES, 0, 0, axis_index_groups=groups, tiled=True)]
    all_to_all x3 -> x2, starting transfers between devices: 20 us -> 10.7 us  [scatter(): lax.all_to_all(sent, AXES, 0, 0, axis_index_groups=groups, tiled=True)]
    all_to_all x3 -> x2, waiting for transfers between devices: 4.58 us -> 0.13 us  [scatter(): lax.all_to_all(sent, AXES, 0, 0, axis_index_groups=groups, tiled=True)]
    unnamed x24 -> x20, local copies, waits for them, and re-layouts: 6.8 us -> 4.8 us
  transfers between devices with their start and end apart: 13 -> 12, of which waited for: 6 -> 4; matrix products, arithmetic and copies ran while one was open for 0% -> 0% of each run, Pallas kernels for 19% -> 19%
where the time goes in v8:
time: 90.3 us; the launch traced here: 89.8 us
  starting transfers between devices  35 us (39%)
  Pallas kernels  26.7 us (30%)
  blocking collectives  15.5 us (17%)
  waiting for transfers between devices  6.24 us (7%)
  local copies, waits for them, and re-layouts  4.8 us (5%)
    all_to_all x1, blocking collectives, scatter(): lax.all_to_all(sent, AXES, 0, 0, axis_index_groups=groups, tiled=True)  15.5 us
    all_to_all x2, starting transfers between devices, scatter(): lax.all_to_all(sent, AXES, 0, 0, axis_index_groups=groups, tiled=True)  10.7 us
    ppermute x4, starting transfers between devices, both_ways(): lax.ppermute(two, AXES, pairs(1))  10.6 us
    ppermute x2, starting transfers between devices, swap(): return lax.ppermute(x, AXES, [(i, i ^ bit) for i in range(size)])  7.43 us
    pallas_call x2, Pallas kernels, half(): call(lambda me, *refs: sums_kernel(count, width, scale, kept, me, *refs),...  7.15 us
    ppermute x4, starting transfers between devices, both_ways(): lax.ppermute(one, AXES, pairs(0))  6.18 us
    ppermute x4, waiting for transfers between devices, both_ways(): lax.ppermute(two, AXES, pairs(1))  4.89 us
    unnamed x20, local copies, waits for them, and re-layouts  4.8 us
  transfers between devices with their start and end apart: 12, of which 4 were waited for; matrix products, arithmetic and copies ran while one was open for 0% of the time, Pallas kernels for 19%

profile of v8, /device:TPU:1, one launch (start us, length us, event | category | flops | bytes accessed | tf_op | source)
XLA Modules:
  0.0 89.8 jit_solution(16929843474349235541)
XLA Ops:
  0.6 1.2 %copy-done = bf16[1,1,64,64,128]{4,3,2,1,0:T(8,128)(2,1)S(1)} copy-done((bf16[1,1,64,64,128]{4,3,2,1,0:T(8,128)(2,1)S(1)}, bf16[1,1,64,64,128]{4,3,2,1,0:T(8,128)(2,1)}, u32[]{:S(2)}) %copy-start) | copy-done | bytes 1048600
  1.9 1.2 %copy-done.1 = bf16[1,1,64,64,128]{4,3,2,1,0:T(8,128)(2,1)S(1)} copy-done((bf16[1,1,64,64,128]{4,3,2,1,0:T(8,128)(2,1)S(1)}, bf16[1,1,64,64,128]{4,3,2,1,0:T(8,128)(2,1)}, u32[]{:S(2)}) %copy-start.1) | copy-done | bytes 1048600
  4.5 1.2 %shard_map.93 = (bf16[160,128]{1,0:T(8,128)(2,1)S(1)}, bf16[160,128]{1,0:T(8,128)(2,1)S(1)}, bf16[128,128]{1,0:T(8,128)(2,1)S(1)}, bf16[128,128]{1,0:T(8,128)(2,1)S(1)}, bf16[32,2,64,128]{3,2,1,0:T(8,128)(2,1)S(1)}) custom-call(s32[1]{0:T(128)} %bitcast.refs_0_.token.me, s32[2,4,128]{2,1,0:T(4,128)S(1)} %bitcast.16, s32[2,4,128]{2,1,0:T(4,128)S(1)} %bitcast.21, ...), custom_call_target="tpu_custom_call" | custom-call | bytes 4194304 | tf_op jit(solution)/shard_map/pallas_call | solution.py:622
  5.7 3.8 %collective-permute-start = (bf16[160,128]{1,0:T(8,128)(2,1)S(1)}, bf16[160,128]{1,0:T(8,128)(2,1)S(1)}, u32[]{:S(2)}, u32[]{:S(2)}) collective-permute-start(bf16[160,128]{1,0:T(8,128)(2,1)S(1)} %get-tuple-element.86), channel_id=1, source_target_pairs={{0,32},{1,33},{2,34},{3,35},{4,36},{5,37},{6,38},{7,39},{8,40},{9,... | collective-permute-start | bytes 122888 | tf_op jit(solution)/shard_map/ppermute | solution.py:548
  9.5 2.3 %collective-permute-start.1 = (bf16[160,128]{1,0:T(8,128)(2,1)S(1)}, bf16[160,128]{1,0:T(8,128)(2,1)S(1)}, u32[]{:S(2)}, u32[]{:S(2)}) collective-permute-start(bf16[160,128]{1,0:T(8,128)(2,1)S(1)} %get-tuple-element.87), channel_id=1, source_target_pairs={{0,224},{1,225},{2,226},{3,227},{4,228},{5,229},{6,230},{7,231},{8... | collective-permute-start | bytes 122888 | tf_op jit(solution)/shard_map/ppermute | solution.py:548
  12.8 2.7 %shard_map.94 = (bf16[1536,256]{1,0:T(8,128)(2,1)S(1)}, bf16[3,33,2,64,128]{4,3,2,1,0:T(8,128)(2,1)S(1)}, f32[32,2,64,128]{3,2,1,0:T(8,128)S(1)}) custom-call(s32[1]{0:T(128)} %bitcast.refs_0_.token.me, bf16[3,3,128,128]{3,2,1,0:T(8,128)(2,1)S(1)} %copy-done.4, bf16[32,2,64,128]{3,2,1,0:T(8,128)(2,1)S(1)} %get-tuple-element.89.upstream), custom_call_target="tpu_custom_call" | custom-call | flops 1207959552 | bytes 4194304 | tf_op jit(solution)/shard_map/pallas_call | solution.py:628
  16.9 2.9 %collective-permute-start.3 = (bf16[160,128]{1,0:T(8,128)(2,1)S(1)}, bf16[160,128]{1,0:T(8,128)(2,1)S(1)}, u32[]{:S(2)}, u32[]{:S(2)}) collective-permute-start(bf16[160,128]{1,0:T(8,128)(2,1)S(1)} %get-tuple-element.103), channel_id=1, source_target_pairs={{0,255},{1,2},{2,1},{3,4},{4,3},{5,6},{6,5},{7,8},{8,7},{9,10},{10... | collective-permute-start | bytes 122888 | tf_op jit(solution)/shard_map/ppermute | solution.py:548
  19.8 2.6 %shard_map.96 = (bf16[1536,256]{1,0:T(8,128)(2,1)S(1)}, bf16[3,33,2,64,128]{4,3,2,1,0:T(8,128)(2,1)S(1)}, f32[32,2,64,128]{3,2,1,0:T(8,128)S(1)}) custom-call(s32[1]{0:T(128)} %bitcast.refs_0_.token.me, bf16[3,3,128,128]{3,2,1,0:T(8,128)(2,1)S(1)} %copy-done.3, bf16[32,2,64,128]{3,2,1,0:T(8,128)(2,1)S(1)} %bitcast.15), custom_call_target="tpu_custom_call" | custom-call | flops 1207959552 | bytes 4194304 | tf_op jit(solution)/shard_map/pallas_call | solution.py:643
  22.5 2.6 %shard_map.97 = (bf16[32,2,64,128]{3,2,1,0:T(8,128)(2,1)S(1)}, bf16[32,2,64,128]{3,2,1,0:T(8,128)(2,1)S(1)}, bf16[160,128]{1,0:T(8,128)(2,1)S(1)}, bf16[160,128]...) custom-call(s32[1]{0:T(128)} %bitcast.refs_0_.token.me, ...), custom_call_target="tpu_custom_call" | custom-call | flops 1207959552 | bytes 4194304 | tf_op jit(solution)/shard_map/pallas_call | solution.py:646
  25.1 3.6 %shard_map.98 = f32[1152,128]{1,0:T(8,128)S(1)} custom-call(s32[1]{0:T(128)} %bitcast.refs_0_.token.me, s32[2,4,128]{2,1,0:T(4,128)S(1)} %bitcast.18, s32[2,4,128]{2,1,0:T(4,128)S(1)} %bitcast.23, bf16[160,128]{1,0:T(8,128)(2,1)S(1)} %get-tuple-element.98.refs_3_.refs_2_, bf16[160,128]{1,0:T(8,128)(2,1)S(1)} %get-tuple-element.99.refs_4_.refs_3_, ...), custom_call_target="tpu_custom_call" | custom-call | flops 1207959552 | bytes 4194304 | tf_op jit(solution)/shard_map/pallas_call | solution.py:657
  28.7 5.3 %collective-permute-start.4 = (f32[1152,128]{1,0:T(8,128)S(1)}, f32[1152,128]{1,0:T(8,128)S(1)}, u32[]{:S(2)}, u32[]{:S(2)}) collective-permute-start(f32[1152,128]{1,0:T(8,128)S(1)} %shard_map.98), channel_id=1, source_target_pairs={{0,2},{1,3},{2,0},{3,1},{4,6},{5,7},{6,4},{7,5},{8,10},{9,11},{10,... | collective-permute-start | bytes 1769480 | tf_op jit(solution)/shard_map/ppermute | solution.py:539
  34.0 3.3 %collective-permute-start.6 = (bf16[160,128]{1,0:T(8,128)(2,1)S(1)}, bf16[160,128]{1,0:T(8,128)(2,1)S(1)}, u32[]{:S(2)}, u32[]{:S(2)}) collective-permute-start(bf16[160,128]{1,0:T(8,128)(2,1)S(1)} %get-tuple-element.129), channel_id=1, source_target_pairs={{0,224},{1,225},{2,226},{3,227},{4,228},{5,229},{6,230},{7,231},{8... | collective-permute-start | bytes 122888 | tf_op jit(solution)/shard_map/ppermute | solution.py:548
  37.4 3.6 %shard_map.99 = f32[1152,128]{1,0:T(8,128)S(1)} custom-call(s32[1]{0:T(128)} %bitcast.refs_0_.token.me, s32[2,4,128]{2,1,0:T(4,128)S(1)} %bitcast.19, s32[2,4,128]{2,1,0:T(4,128)S(1)} %bitcast.24, bf16[160,128]{1,0:T(8,128)(2,1)S(1)} %get-tuple-element.98.refs_3_.refs_2_, bf16[160,128]{1,0:T(8,128)(2,1)S(1)} %get-tuple-element.99.refs_4_.refs_3_, ...), custom_call_target="tpu_custom_call" | custom-call | flops 1207959552 | bytes 4194304 | tf_op jit(solution)/shard_map/pallas_call | solution.py:657
  41.8 4.2 %all-to-all-start = ((bf16[16,72,128]{2,1,0:T(8,128)(2,1)}), bf16[16,72,128]{2,1,0:T(8,128)(2,1)S(1)}, u32[]{:S(2)}, u32[]{:S(2)}) async-start(bf16[16,72,128]{2,1,0:T(8,128)(2,1)} %bitcast.5), calls=%async_computation | async-start | bytes 589824 | tf_op jit(solution)/shard_map/all_to_all | solution.py:568
  46.0 1.4 %collective-permute-start.7 = (bf16[160,128]{1,0:T(8,128)(2,1)S(1)}, bf16[160,128]{1,0:T(8,128)(2,1)S(1)}, u32[]{:S(2)}, u32[]{:S(2)}) collective-permute-start(bf16[160,128]{1,0:T(8,128)(2,1)S(1)} %get-tuple-element.140), channel_id=1, source_target_pairs={{0,1},{1,0},{2,3},{3,2},{4,5},{5,4},{6,7},{7,6},{8,9},{9,8},{10,11... | collective-permute-start | bytes 122888 | tf_op jit(solution)/shard_map/ppermute | solution.py:548
  47.5 2.1 %collective-permute-start.8 = (bf16[160,128]{1,0:T(8,128)(2,1)S(1)}, bf16[160,128]{1,0:T(8,128)(2,1)S(1)}, u32[]{:S(2)}, u32[]{:S(2)}) collective-permute-start(bf16[160,128]{1,0:T(8,128)(2,1)S(1)} %get-tuple-element.141), channel_id=1, source_target_pairs={{0,255},{1,2},{2,1},{3,4},{4,3},{5,6},{6,5},{7,8},{8,7},{9,10},{10... | collective-permute-start | bytes 122888 | tf_op jit(solution)/shard_map/ppermute | solution.py:548
  49.6 4.4 %collective-permute-done.8.two = bf16[160,128]{1,0:T(8,128)(2,1)S(1)} collective-permute-done((bf16[160,128]{1,0:T(8,128)(2,1)S(1)}, bf16[160,128]{1,0:T(8,128)(2,1)S(1)}, u32[]{:S(2)}, u32[]{:S(2)}) %collective-permute-start.8) | collective-permute-done | bytes 40992 | tf_op jit(solution)/shard_map/ppermute | solution.py:548
  54.9 6.5 %all-to-all-start.1 = ((f32[8,72,128]{2,1,0:T(8,128)}), f32[8,72,128]{2,1,0:T(8,128)S(1)}, u32[]{:S(2)}, u32[]{:S(2)}) async-start(f32[8,72,128]{2,1,0:T(8,128)} %shard_map.101), calls=%async_computation.1 | async-start | bytes 589824 | tf_op jit(solution)/shard_map/all_to_all | solution.py:568
  61.7 4.7 %shard_map.104 = bf16[32,2,64,128]{3,2,1,0:T(8,128)(2,1)} custom-call(s32[1]{0:T(128)} %bitcast.refs_0_.token.me, s32[2,4,128]{2,1,0:T(4,128)S(1)} %bitcast.20, s32[2,4,128]{2,1,0:T(4,128)S(1)} %bitcast.25, bf16[160,128]{1,0:T(8,128)(2,1)S(1)} %get-tuple-element.150.refs_3_.vp, bf16[160,128]{1,0:T(8,128)(2,1)S(1)} %get-tuple-element.151.refs_4_.vm, ...), custom_call_target="tpu_custom_call" | custom-call | flops 1207959552 | bytes 4194304 | tf_op jit(solution)/shard_map/pallas_call | solution.py:685
  66.4 3.5 %shard_map.105 = bf16[32,2,64,128]{3,2,1,0:T(8,128)(2,1)} custom-call(bf16[32,2,64,128]{3,2,1,0:T(8,128)(2,1)S(1)} %get-tuple-element.116.refs_6_.hidden, bf16[160,128]{1,0:T(8,128)(2,1)S(1)} %get-tuple-element.150.refs_3_.vp, bf16[160,128]{1,0:T(8,128)(2,1)S(1)} %get-tuple-element.151.refs_4_.vm, bf16[160,128]{1,0:T(8,128)(2,1)S(1)} %get-tuple-element.155.refs_5_.hp, ...), custom_call_target="tpu_custom_call" | custom-call | flops 1207959552 | bytes 4194304 | tf_op jit(solution)/shard_map/pallas_call | solution.py:682
  69.9 15.5 %all_to_all.15 = bf16[16,72,128]{2,1,0:T(8,128)(2,1)S(1)} all-to-all(bf16[16,72,128]{2,1,0:T(8,128)(2,1)S(1)} %shard_map.106), channel_id=1, replica_groups={{0,128,64,192,32,160,96,224,1,129,65,193,33,161,97,225},{2,130,66,194,3..., dimensions={0} | all-to-all | bytes 589824 | tf_op jit(solution)/shard_map/all_to_all | solution.py:568
  85.4 2.1 %collective-permute-start.9 = (bf16[1152,128]{1,0:T(8,128)(2,1)S(1)}, bf16[1152,128]{1,0:T(8,128)(2,1)S(1)}, u32[]{:S(2)}, u32[]{:S(2)}) collective-permute-start(bf16[1152,128]{1,0:T(8,128)(2,1)S(1)} %bitcast.11), channel_id=1, source_target_pairs={{0,2},{1,3},{2,0},{3,1},{4,6},{5,7},{6,4},{7,5},{8,10},{9,11},{10,... | collective-permute-start | bytes 884744 | tf_op jit(solution)/shard_map/ppermute | solution.py:539
  87.5 1.2 %collective-permute-done.9.other = bf16[1152,128]{1,0:T(8,128)(2,1)S(1)} collective-permute-done((bf16[1152,128]{1,0:T(8,128)(2,1)S(1)}, bf16[1152,128]{1,0:T(8,128)(2,1)S(1)}, u32[]{:S(2)}, u32[]{:S(2)}) %collective-permute-start.9) | collective-permute-done | bytes 294944 | tf_op jit(solution)/shard_map/ppermute | solution.py:539
  88.7 1.1 %shard_map.107 = (f32[1152,128]{1,0:T(8,128)}, f32[1152,128]{1,0:T(8,128)}) custom-call(s32[1]{0:T(128)} %bitcast.refs_0_.token.me, bf16[1152,128]{1,0:T(8,128)(2,1)S(1)} %bitcast.12, bf16[1152,128]{1,0:T(8,128)(2,1)S(1)} %collective-permute-done.9.other), custom_call_target="tpu_custom_call" | custom-call | bytes 4194304 | tf_op jit(solution)/shard_map/pallas_call | solution.py:597
  (37 shorter events, 5.8 us)
Async XLA Ops:
  0.6 1.2 %copy-start = (bf16[1,1,64,64,128]{4,3,2,1,0:T(8,128)(2,1)S(1)}, bf16[1,1,64,64,128]{4,3,2,1,0:T(8,128)(2,1)}, u32[]{:S(2)}) copy-start(bf16[1,1,64,64,128]{4,3,2,1,0:T(8,128)(2,1)} %param.9) | copy-start | bytes 3145732
  1.9 1.2 %copy-start.1 = (bf16[1,1,64,64,128]{4,3,2,1,0:T(8,128)(2,1)S(1)}, bf16[1,1,64,64,128]{4,3,2,1,0:T(8,128)(2,1)}, u32[]{:S(2)}) copy-start(bf16[1,1,64,64,128]{4,3,2,1,0:T(8,128)(2,1)} %param.6) | copy-start | bytes 3145732
  3.1 0.7 copy-start.6
  3.8 0.7 copy-start.8
  4.5 15.4 %copy-start.2 = (bf16[1,1,64,64,128]{4,3,2,1,0:T(8,128)(2,1)S(1)}, bf16[1,1,64,64,128]{4,3,2,1,0:T(8,128)(2,1)}, u32[]{:S(2)}) copy-start(bf16[1,1,64,64,128]{4,3,2,1,0:T(8,128)(2,1)} %param.6) | copy-start | bytes 3145732
  4.5 15.4 %copy-start.3 = (bf16[3,3,128,128]{3,2,1,0:T(8,128)(2,1)S(1)}, bf16[3,3,128,128]{3,2,1,0:T(8,128)(2,1)}, u32[]{:S(2)}) copy-start(bf16[3,3,128,128]{3,2,1,0:T(8,128)(2,1)} %kernel_one.3) | copy-start | bytes 884740
  5.7 9.8 %collective-permute-start = (bf16[160,128]{1,0:T(8,128)(2,1)S(1)}, bf16[160,128]{1,0:T(8,128)(2,1)S(1)}, u32[]{:S(2)}, u32[]{:S(2)}) collective-permute-start(bf16[160,128]{1,0:T(8,128)(2,1)S(1)} %get-tuple-element.86), channel_id=1, source_target_pairs={{0,32},{1,33},{2,34},{3,35},{4,36},{5,37},{6,38},{7,39},{8,40},{9,... | collective-permute-start | bytes 122888 | tf_op jit(solution)/shard_map/ppermute | solution.py:548
  9.5 6.5 %collective-permute-start.1 = (bf16[160,128]{1,0:T(8,128)(2,1)S(1)}, bf16[160,128]{1,0:T(8,128)(2,1)S(1)}, u32[]{:S(2)}, u32[]{:S(2)}) collective-permute-start(bf16[160,128]{1,0:T(8,128)(2,1)S(1)} %get-tuple-element.87), channel_id=1, source_target_pairs={{0,224},{1,225},{2,226},{3,227},{4,228},{5,229},{6,230},{7,231},{8... | collective-permute-start | bytes 122888 | tf_op jit(solution)/shard_map/ppermute | solution.py:548
  11.8 1.0 %copy-start.4 = (bf16[3,3,128,128]{3,2,1,0:T(8,128)(2,1)S(1)}, bf16[3,3,128,128]{3,2,1,0:T(8,128)(2,1)}, u32[]{:S(2)}) copy-start(bf16[3,3,128,128]{3,2,1,0:T(8,128)(2,1)} %kernel_two.3) | copy-start | bytes 884740
  15.5 7.0 %copy-start.7 = (s32[128,2,4]{0,2,1:T(4,128)S(1)}, s32[128,2,4]{0,2,1:T(4,128)}, u32[]{:S(2)}) copy-start(s32[128,2,4]{0,2,1:T(4,128)} %param.10) | copy-start | bytes 12292
  15.5 7.0 %copy-start.9 = (s32[128,2,4]{0,2,1:T(4,128)S(1)}, s32[128,2,4]{0,2,1:T(4,128)}, u32[]{:S(2)}) copy-start(s32[128,2,4]{0,2,1:T(4,128)} %param.11) | copy-start | bytes 12292
  16.0 6.4 %collective-permute-start.2 = (bf16[160,128]{1,0:T(8,128)(2,1)S(1)}, bf16[160,128]{1,0:T(8,128)(2,1)S(1)}, u32[]{:S(2)}, u32[]{:S(2)}) collective-permute-start(bf16[160,128]{1,0:T(8,128)(2,1)S(1)} %get-tuple-element.102), channel_id=1, source_target_pairs={{0,1},{1,0},{2,3},{3,2},{4,5},{5,4},{6,7},{7,6},{8,9},{9,8},{10,11... | collective-permute-start | bytes 122888 | tf_op jit(solution)/shard_map/ppermute | solution.py:548
  16.9 5.6 %collective-permute-start.3 = (bf16[160,128]{1,0:T(8,128)(2,1)S(1)}, bf16[160,128]{1,0:T(8,128)(2,1)S(1)}, u32[]{:S(2)}, u32[]{:S(2)}) collective-permute-start(bf16[160,128]{1,0:T(8,128)(2,1)S(1)} %get-tuple-element.103), channel_id=1, source_target_pairs={{0,255},{1,2},{2,1},{3,4},{4,3},{5,6},{6,5},{7,8},{8,7},{9,10},{10... | collective-permute-start | bytes 122888 | tf_op jit(solution)/shard_map/ppermute | solution.py:548
  28.7 12.3 %collective-permute-start.4 = (f32[1152,128]{1,0:T(8,128)S(1)}, f32[1152,128]{1,0:T(8,128)S(1)}, u32[]{:S(2)}, u32[]{:S(2)}) collective-permute-start(f32[1152,128]{1,0:T(8,128)S(1)} %shard_map.98), channel_id=1, source_target_pairs={{0,2},{1,3},{2,0},{3,1},{4,6},{5,7},{6,4},{7,5},{8,10},{9,11},{10,... | collective-permute-start | bytes 1769480 | tf_op jit(solution)/shard_map/ppermute | solution.py:539
  34.0 6.9 %collective-permute-start.5 = (bf16[160,128]{1,0:T(8,128)(2,1)S(1)}, bf16[160,128]{1,0:T(8,128)(2,1)S(1)}, u32[]{:S(2)}, u32[]{:S(2)}) collective-permute-start(bf16[160,128]{1,0:T(8,128)(2,1)S(1)} %get-tuple-element.128), channel_id=1, source_target_pairs={{0,32},{1,33},{2,34},{3,35},{4,36},{5,37},{6,38},{7,39},{8,40},{9,... | collective-permute-start | bytes 122888 | tf_op jit(solution)/shard_map/ppermute | solution.py:548
  34.0 6.9 %collective-permute-start.6 = (bf16[160,128]{1,0:T(8,128)(2,1)S(1)}, bf16[160,128]{1,0:T(8,128)(2,1)S(1)}, u32[]{:S(2)}, u32[]{:S(2)}) collective-permute-start(bf16[160,128]{1,0:T(8,128)(2,1)S(1)} %get-tuple-element.129), channel_id=1, source_target_pairs={{0,224},{1,225},{2,226},{3,227},{4,228},{5,229},{6,230},{7,231},{8... | collective-permute-start | bytes 122888 | tf_op jit(solution)/shard_map/ppermute | solution.py:548
  40.9 20.4 %copy-start.5 = (bf16[3,3,128,128]{3,2,1,0:T(8,128)(2,1)S(1)}, bf16[3,3,128,128]{3,2,1,0:T(8,128)(2,1)}, u32[]{:S(2)}) copy-start(bf16[3,3,128,128]{3,2,1,0:T(8,128)(2,1)} %kernel_two.3) | copy-start | bytes 884740
  41.8 12.3 %all-to-all-start = ((bf16[16,72,128]{2,1,0:T(8,128)(2,1)}), bf16[16,72,128]{2,1,0:T(8,128)(2,1)S(1)}, u32[]{:S(2)}, u32[]{:S(2)}) async-start(bf16[16,72,128]{2,1,0:T(8,128)(2,1)} %bitcast.5), calls=%async_computation | async-start | bytes 589824 | tf_op jit(solution)/shard_map/all_to_all | solution.py:568
  46.0 3.5 %collective-permute-start.7 = (bf16[160,128]{1,0:T(8,128)(2,1)S(1)}, bf16[160,128]{1,0:T(8,128)(2,1)S(1)}, u32[]{:S(2)}, u32[]{:S(2)}) collective-permute-start(bf16[160,128]{1,0:T(8,128)(2,1)S(1)} %get-tuple-element.140), channel_id=1, source_target_pairs={{0,1},{1,0},{2,3},{3,2},{4,5},{5,4},{6,7},{7,6},{8,9},{9,8},{10,11... | collective-permute-start | bytes 122888 | tf_op jit(solution)/shard_map/ppermute | solution.py:548
  47.5 6.5 %collective-permute-start.8 = (bf16[160,128]{1,0:T(8,128)(2,1)S(1)}, bf16[160,128]{1,0:T(8,128)(2,1)S(1)}, u32[]{:S(2)}, u32[]{:S(2)}) collective-permute-start(bf16[160,128]{1,0:T(8,128)(2,1)S(1)} %get-tuple-element.141), channel_id=1, source_target_pairs={{0,255},{1,2},{2,1},{3,4},{4,3},{5,6},{6,5},{7,8},{8,7},{9,10},{10... | collective-permute-start | bytes 122888 | tf_op jit(solution)/shard_map/ppermute | solution.py:548
  54.9 15.0 %all-to-all-start.1 = ((f32[8,72,128]{2,1,0:T(8,128)}), f32[8,72,128]{2,1,0:T(8,128)S(1)}, u32[]{:S(2)}, u32[]{:S(2)}) async-start(f32[8,72,128]{2,1,0:T(8,128)} %shard_map.101), calls=%async_computation.1 | async-start | bytes 589824 | tf_op jit(solution)/shard_map/all_to_all | solution.py:568
  85.4 3.3 %collective-permute-start.9 = (bf16[1152,128]{1,0:T(8,128)(2,1)S(1)}, bf16[1152,128]{1,0:T(8,128)(2,1)S(1)}, u32[]{:S(2)}, u32[]{:S(2)}) collective-permute-start(bf16[1152,128]{1,0:T(8,128)(2,1)S(1)} %bitcast.11), channel_id=1, source_target_pairs={{0,2},{1,3},{2,0},{3,1},{4,6},{5,7},{6,4},{7,5},{8,10},{9,11},{10,... | collective-permute-start | bytes 884744 | tf_op jit(solution)/shard_map/ppermute | solution.py:539

commit v9 on v8

--- a/solution.py
+++ b/solution.py
@@ -591,7 +591,7 @@
     x = (done["keep"] + x).astype(BF16)
     parts = len(plane[0])
     x = beside(x.reshape(parts, x.shape[0] // parts, CH), scatter(plane))
-    x = beside(fold(x, len(ring[0]), F32), scatter(ring))
+    x = beside(fold(x, len(ring[0]), BF16), scatter(ring))
     x = beside(fold(x, parts, BF16), scatter(plane)).reshape(-1, CH)
     out = struct(x.shape, F32)
     grads = call(finish_kernel, 1, 2, (out, out))(me.reshape(1), x, beside(x, across))

time: 90.3 us -> 88.4 us (0.979)
  blocking collectives: 15.5 us -> 13.6 us
    all_to_all x1, blocking collectives: 15.5 us -> 13.6 us  [scatter(): lax.all_to_all(sent, AXES, 0, 0, axis_index_groups=groups, tiled=True)]
  transfers between devices with their start and end apart: 12 -> 12, of which waited for: 4 -> 4; matrix products, arithmetic and copies ran while one was open for 0% -> 0% of each run, Pallas kernels for 19% -> 20%
where the time goes in v9:
time: 88.4 us; the launch traced here: 88 us
  starting transfers between devices  35 us (40%)
  Pallas kernels  26.7 us (30%)
  blocking collectives  13.6 us (15%)
  waiting for transfers between devices  6.25 us (7%)
  local copies, waits for them, and re-layouts  4.8 us (5%)
    all_to_all x1, blocking collectives, scatter(): lax.all_to_all(sent, AXES, 0, 0, axis_index_groups=groups, tiled=True)  13.6 us
    all_to_all x2, starting transfers between devices, scatter(): lax.all_to_all(sent, AXES, 0, 0, axis_index_groups=groups, tiled=True)  10.7 us
    ppermute x4, starting transfers between devices, both_ways(): lax.ppermute(two, AXES, pairs(1))  10.6 us
    ppermute x2, starting transfers between devices, swap(): return lax.ppermute(x, AXES, [(i, i ^ bit) for i in range(size)])  7.48 us
    pallas_call x2, Pallas kernels, half(): call(lambda me, *refs: sums_kernel(count, width, scale, kept, me, *refs),...  7.15 us
    ppermute x4, starting transfers between devices, both_ways(): lax.ppermute(one, AXES, pairs(0))  6.18 us
    ppermute x4, waiting for transfers between devices, both_ways(): lax.ppermute(two, AXES, pairs(1))  4.9 us
    unnamed x20, local copies, waits for them, and re-layouts  4.8 us
  transfers between devices with their start and end apart: 12, of which 4 were waited for; matrix products, arithmetic and copies ran while one was open for 0% of the time, Pallas kernels for 20%

profile of v9, /device:TPU:1, one launch (start us, length us, event | category | flops | bytes accessed | tf_op | source)
XLA Modules:
  0.0 88.0 jit_solution(10186741476736951497)
XLA Ops:
  0.6 1.2 %copy-done = bf16[1,1,64,64,128]{4,3,2,1,0:T(8,128)(2,1)S(1)} copy-done((bf16[1,1,64,64,128]{4,3,2,1,0:T(8,128)(2,1)S(1)}, bf16[1,1,64,64,128]{4,3,2,1,0:T(8,128)(2,1)}, u32[]{:S(2)}) %copy-start) | copy-done | bytes 1048600
  1.9 1.2 %copy-done.1 = bf16[1,1,64,64,128]{4,3,2,1,0:T(8,128)(2,1)S(1)} copy-done((bf16[1,1,64,64,128]{4,3,2,1,0:T(8,128)(2,1)S(1)}, bf16[1,1,64,64,128]{4,3,2,1,0:T(8,128)(2,1)}, u32[]{:S(2)}) %copy-start.1) | copy-done | bytes 1048600
  4.5 1.2 %shard_map.93 = (bf16[160,128]{1,0:T(8,128)(2,1)S(1)}, bf16[160,128]{1,0:T(8,128)(2,1)S(1)}, bf16[128,128]{1,0:T(8,128)(2,1)S(1)}, bf16[128,128]{1,0:T(8,128)(2,1)S(1)}, bf16[32,2,64,128]{3,2,1,0:T(8,128)(2,1)S(1)}) custom-call(s32[1]{0:T(128)} %bitcast.refs_0_.token.me, s32[2,4,128]{2,1,0:T(4,128)S(1)} %bitcast.16, s32[2,4,128]{2,1,0:T(4,128)S(1)} %bitcast.21, ...), custom_call_target="tpu_custom_call" | custom-call | bytes 4194304 | tf_op jit(solution)/shard_map/pallas_call | solution.py:622
  5.7 3.8 %collective-permute-start = (bf16[160,128]{1,0:T(8,128)(2,1)S(1)}, bf16[160,128]{1,0:T(8,128)(2,1)S(1)}, u32[]{:S(2)}, u32[]{:S(2)}) collective-permute-start(bf16[160,128]{1,0:T(8,128)(2,1)S(1)} %get-tuple-element.86), channel_id=1, source_target_pairs={{0,32},{1,33},{2,34},{3,35},{4,36},{5,37},{6,38},{7,39},{8,40},{9,... | collective-permute-start | bytes 122888 | tf_op jit(solution)/shard_map/ppermute | solution.py:548
  9.5 2.3 %collective-permute-start.1 = (bf16[160,128]{1,0:T(8,128)(2,1)S(1)}, bf16[160,128]{1,0:T(8,128)(2,1)S(1)}, u32[]{:S(2)}, u32[]{:S(2)}) collective-permute-start(bf16[160,128]{1,0:T(8,128)(2,1)S(1)} %get-tuple-element.87), channel_id=1, source_target_pairs={{0,224},{1,225},{2,226},{3,227},{4,228},{5,229},{6,230},{7,231},{8... | collective-permute-start | bytes 122888 | tf_op jit(solution)/shard_map/ppermute | solution.py:548
  12.8 2.7 %shard_map.94 = (bf16[1536,256]{1,0:T(8,128)(2,1)S(1)}, bf16[3,33,2,64,128]{4,3,2,1,0:T(8,128)(2,1)S(1)}, f32[32,2,64,128]{3,2,1,0:T(8,128)S(1)}) custom-call(s32[1]{0:T(128)} %bitcast.refs_0_.token.me, bf16[3,3,128,128]{3,2,1,0:T(8,128)(2,1)S(1)} %copy-done.4, bf16[32,2,64,128]{3,2,1,0:T(8,128)(2,1)S(1)} %get-tuple-element.89.upstream), custom_call_target="tpu_custom_call" | custom-call | flops 1207959552 | bytes 4194304 | tf_op jit(solution)/shard_map/pallas_call | solution.py:628
  16.9 2.9 %collective-permute-start.3 = (bf16[160,128]{1,0:T(8,128)(2,1)S(1)}, bf16[160,128]{1,0:T(8,128)(2,1)S(1)}, u32[]{:S(2)}, u32[]{:S(2)}) collective-permute-start(bf16[160,128]{1,0:T(8,128)(2,1)S(1)} %get-tuple-element.103), channel_id=1, source_target_pairs={{0,255},{1,2},{2,1},{3,4},{4,3},{5,6},{6,5},{7,8},{8,7},{9,10},{10... | collective-permute-start | bytes 122888 | tf_op jit(solution)/shard_map/ppermute | solution.py:548
  19.8 2.6 %shard_map.96 = (bf16[1536,256]{1,0:T(8,128)(2,1)S(1)}, bf16[3,33,2,64,128]{4,3,2,1,0:T(8,128)(2,1)S(1)}, f32[32,2,64,128]{3,2,1,0:T(8,128)S(1)}) custom-call(s32[1]{0:T(128)} %bitcast.refs_0_.token.me, bf16[3,3,128,128]{3,2,1,0:T(8,128)(2,1)S(1)} %copy-done.3, bf16[32,2,64,128]{3,2,1,0:T(8,128)(2,1)S(1)} %bitcast.15), custom_call_target="tpu_custom_call" | custom-call | flops 1207959552 | bytes 4194304 | tf_op jit(solution)/shard_map/pallas_call | solution.py:643
  22.5 2.6 %shard_map.97 = (bf16[32,2,64,128]{3,2,1,0:T(8,128)(2,1)S(1)}, bf16[32,2,64,128]{3,2,1,0:T(8,128)(2,1)S(1)}, bf16[160,128]{1,0:T(8,128)(2,1)S(1)}, bf16[160,128]...) custom-call(s32[1]{0:T(128)} %bitcast.refs_0_.token.me, ...), custom_call_target="tpu_custom_call" | custom-call | flops 1207959552 | bytes 4194304 | tf_op jit(solution)/shard_map/pallas_call | solution.py:646
  25.1 3.6 %shard_map.98 = f32[1152,128]{1,0:T(8,128)S(1)} custom-call(s32[1]{0:T(128)} %bitcast.refs_0_.token.me, s32[2,4,128]{2,1,0:T(4,128)S(1)} %bitcast.18, s32[2,4,128]{2,1,0:T(4,128)S(1)} %bitcast.23, bf16[160,128]{1,0:T(8,128)(2,1)S(1)} %get-tuple-element.98.refs_3_.refs_2_, bf16[160,128]{1,0:T(8,128)(2,1)S(1)} %get-tuple-element.99.refs_4_.refs_3_, ...), custom_call_target="tpu_custom_call" | custom-call | flops 1207959552 | bytes 4194304 | tf_op jit(solution)/shard_map/pallas_call | solution.py:657
  28.7 5.3 %collective-permute-start.4 = (f32[1152,128]{1,0:T(8,128)S(1)}, f32[1152,128]{1,0:T(8,128)S(1)}, u32[]{:S(2)}, u32[]{:S(2)}) collective-permute-start(f32[1152,128]{1,0:T(8,128)S(1)} %shard_map.98), channel_id=1, source_target_pairs={{0,2},{1,3},{2,0},{3,1},{4,6},{5,7},{6,4},{7,5},{8,10},{9,11},{10,... | collective-permute-start | bytes 1769480 | tf_op jit(solution)/shard_map/ppermute | solution.py:539
  34.0 3.3 %collective-permute-start.6 = (bf16[160,128]{1,0:T(8,128)(2,1)S(1)}, bf16[160,128]{1,0:T(8,128)(2,1)S(1)}, u32[]{:S(2)}, u32[]{:S(2)}) collective-permute-start(bf16[160,128]{1,0:T(8,128)(2,1)S(1)} %get-tuple-element.129), channel_id=1, source_target_pairs={{0,224},{1,225},{2,226},{3,227},{4,228},{5,229},{6,230},{7,231},{8... | collective-permute-start | bytes 122888 | tf_op jit(solution)/shard_map/ppermute | solution.py:548
  37.4 3.6 %shard_map.99 = f32[1152,128]{1,0:T(8,128)S(1)} custom-call(s32[1]{0:T(128)} %bitcast.refs_0_.token.me, s32[2,4,128]{2,1,0:T(4,128)S(1)} %bitcast.19, s32[2,4,128]{2,1,0:T(4,128)S(1)} %bitcast.24, bf16[160,128]{1,0:T(8,128)(2,1)S(1)} %get-tuple-element.98.refs_3_.refs_2_, bf16[160,128]{1,0:T(8,128)(2,1)S(1)} %get-tuple-element.99.refs_4_.refs_3_, ...), custom_call_target="tpu_custom_call" | custom-call | flops 1207959552 | bytes 4194304 | tf_op jit(solution)/shard_map/pallas_call | solution.py:657
  41.8 4.2 %all-to-all-start = ((bf16[16,72,128]{2,1,0:T(8,128)(2,1)}), bf16[16,72,128]{2,1,0:T(8,128)(2,1)S(1)}, u32[]{:S(2)}, u32[]{:S(2)}) async-start(bf16[16,72,128]{2,1,0:T(8,128)(2,1)} %bitcast.5), calls=%async_computation | async-start | bytes 589824 | tf_op jit(solution)/shard_map/all_to_all | solution.py:568
  46.1 1.4 %collective-permute-start.7 = (bf16[160,128]{1,0:T(8,128)(2,1)S(1)}, bf16[160,128]{1,0:T(8,128)(2,1)S(1)}, u32[]{:S(2)}, u32[]{:S(2)}) collective-permute-start(bf16[160,128]{1,0:T(8,128)(2,1)S(1)} %get-tuple-element.140), channel_id=1, source_target_pairs={{0,1},{1,0},{2,3},{3,2},{4,5},{5,4},{6,7},{7,6},{8,9},{9,8},{10,11... | collective-permute-start | bytes 122888 | tf_op jit(solution)/shard_map/ppermute | solution.py:548
  47.5 2.1 %collective-permute-start.8 = (bf16[160,128]{1,0:T(8,128)(2,1)S(1)}, bf16[160,128]{1,0:T(8,128)(2,1)S(1)}, u32[]{:S(2)}, u32[]{:S(2)}) collective-permute-start(bf16[160,128]{1,0:T(8,128)(2,1)S(1)} %get-tuple-element.141), channel_id=1, source_target_pairs={{0,255},{1,2},{2,1},{3,4},{4,3},{5,6},{6,5},{7,8},{8,7},{9,10},{10... | collective-permute-start | bytes 122888 | tf_op jit(solution)/shard_map/ppermute | solution.py:548
  49.6 4.4 %collective-permute-done.8.two = bf16[160,128]{1,0:T(8,128)(2,1)S(1)} collective-permute-done((bf16[160,128]{1,0:T(8,128)(2,1)S(1)}, bf16[160,128]{1,0:T(8,128)(2,1)S(1)}, u32[]{:S(2)}, u32[]{:S(2)}) %collective-permute-start.8) | collective-permute-done | bytes 40992 | tf_op jit(solution)/shard_map/ppermute | solution.py:548
  54.8 6.5 %all-to-all-start.1 = ((bf16[8,72,128]{2,1,0:T(8,128)(2,1)}), bf16[8,72,128]{2,1,0:T(8,128)(2,1)S(1)}, u32[]{:S(2)}, u32[]{:S(2)}) async-start(bf16[8,72,128]{2,1,0:T(8,128)(2,1)} %shard_map.101), calls=%async_computation.1 | async-start | bytes 294912 | tf_op jit(solution)/shard_map/all_to_all | solution.py:568
  61.6 4.7 %shard_map.104 = bf16[32,2,64,128]{3,2,1,0:T(8,128)(2,1)} custom-call(s32[1]{0:T(128)} %bitcast.refs_0_.token.me, s32[2,4,128]{2,1,0:T(4,128)S(1)} %bitcast.20, s32[2,4,128]{2,1,0:T(4,128)S(1)} %bitcast.25, bf16[160,128]{1,0:T(8,128)(2,1)S(1)} %get-tuple-element.150.refs_3_.vp, bf16[160,128]{1,0:T(8,128)(2,1)S(1)} %get-tuple-element.151.refs_4_.vm, ...), custom_call_target="tpu_custom_call" | custom-call | flops 1207959552 | bytes 4194304 | tf_op jit(solution)/shard_map/pallas_call | solution.py:685
  66.4 3.5 %shard_map.105 = bf16[32,2,64,128]{3,2,1,0:T(8,128)(2,1)} custom-call(bf16[32,2,64,128]{3,2,1,0:T(8,128)(2,1)S(1)} %get-tuple-element.116.refs_6_.hidden, bf16[160,128]{1,0:T(8,128)(2,1)S(1)} %get-tuple-element.150.refs_3_.vp, bf16[160,128]{1,0:T(8,128)(2,1)S(1)} %get-tuple-element.151.refs_4_.vm, bf16[160,128]{1,0:T(8,128)(2,1)S(1)} %get-tuple-element.155.refs_5_.hp, ...), custom_call_target="tpu_custom_call" | custom-call | flops 1207959552 | bytes 4194304 | tf_op jit(solution)/shard_map/pallas_call | solution.py:682
  69.9 13.6 %all_to_all.15 = bf16[16,72,128]{2,1,0:T(8,128)(2,1)S(1)} all-to-all(bf16[16,72,128]{2,1,0:T(8,128)(2,1)S(1)} %shard_map.106), channel_id=1, replica_groups={{0,128,64,192,32,160,96,224,1,129,65,193,33,161,97,225},{2,130,66,194,3..., dimensions={0} | all-to-all | bytes 589824 | tf_op jit(solution)/shard_map/all_to_all | solution.py:568
  83.5 2.2 %collective-permute-start.9 = (bf16[1152,128]{1,0:T(8,128)(2,1)S(1)}, bf16[1152,128]{1,0:T(8,128)(2,1)S(1)}, u32[]{:S(2)}, u32[]{:S(2)}) collective-permute-start(bf16[1152,128]{1,0:T(8,128)(2,1)S(1)} %bitcast.11), channel_id=1, source_target_pairs={{0,2},{1,3},{2,0},{3,1},{4,6},{5,7},{6,4},{7,5},{8,10},{9,11},{10,... | collective-permute-start | bytes 884744 | tf_op jit(solution)/shard_map/ppermute | solution.py:539
  85.7 1.2 %collective-permute-done.9.other = bf16[1152,128]{1,0:T(8,128)(2,1)S(1)} collective-permute-done((bf16[1152,128]{1,0:T(8,128)(2,1)S(1)}, bf16[1152,128]{1,0:T(8,128)(2,1)S(1)}, u32[]{:S(2)}, u32[]{:S(2)}) %collective-permute-start.9) | collective-permute-done | bytes 294944 | tf_op jit(solution)/shard_map/ppermute | solution.py:539
  86.9 1.1 %shard_map.107 = (f32[1152,128]{1,0:T(8,128)}, f32[1152,128]{1,0:T(8,128)}) custom-call(s32[1]{0:T(128)} %bitcast.refs_0_.token.me, bf16[1152,128]{1,0:T(8,128)(2,1)S(1)} %bitcast.12, bf16[1152,128]{1,0:T(8,128)(2,1)S(1)} %collective-permute-done.9.other), custom_call_target="tpu_custom_call" | custom-call | bytes 4194304 | tf_op jit(solution)/shard_map/pallas_call | solution.py:597
  (37 shorter events, 5.8 us)
Async XLA Ops:
  0.6 1.2 %copy-start = (bf16[1,1,64,64,128]{4,3,2,1,0:T(8,128)(2,1)S(1)}, bf16[1,1,64,64,128]{4,3,2,1,0:T(8,128)(2,1)}, u32[]{:S(2)}) copy-start(bf16[1,1,64,64,128]{4,3,2,1,0:T(8,128)(2,1)} %param.9) | copy-start | bytes 3145732
  1.9 1.2 %copy-start.1 = (bf16[1,1,64,64,128]{4,3,2,1,0:T(8,128)(2,1)S(1)}, bf16[1,1,64,64,128]{4,3,2,1,0:T(8,128)(2,1)}, u32[]{:S(2)}) copy-start(bf16[1,1,64,64,128]{4,3,2,1,0:T(8,128)(2,1)} %param.6) | copy-start | bytes 3145732
  3.1 0.7 copy-start.6
  3.8 0.7 copy-start.8
  4.5 15.4 %copy-start.2 = (bf16[1,1,64,64,128]{4,3,2,1,0:T(8,128)(2,1)S(1)}, bf16[1,1,64,64,128]{4,3,2,1,0:T(8,128)(2,1)}, u32[]{:S(2)}) copy-start(bf16[1,1,64,64,128]{4,3,2,1,0:T(8,128)(2,1)} %param.6) | copy-start | bytes 3145732
  4.5 15.4 %copy-start.3 = (bf16[3,3,128,128]{3,2,1,0:T(8,128)(2,1)S(1)}, bf16[3,3,128,128]{3,2,1,0:T(8,128)(2,1)}, u32[]{:S(2)}) copy-start(bf16[3,3,128,128]{3,2,1,0:T(8,128)(2,1)} %kernel_one.3) | copy-start | bytes 884740
  5.7 9.8 %collective-permute-start = (bf16[160,128]{1,0:T(8,128)(2,1)S(1)}, bf16[160,128]{1,0:T(8,128)(2,1)S(1)}, u32[]{:S(2)}, u32[]{:S(2)}) collective-permute-start(bf16[160,128]{1,0:T(8,128)(2,1)S(1)} %get-tuple-element.86), channel_id=1, source_target_pairs={{0,32},{1,33},{2,34},{3,35},{4,36},{5,37},{6,38},{7,39},{8,40},{9,... | collective-permute-start | bytes 122888 | tf_op jit(solution)/shard_map/ppermute | solution.py:548
  9.5 6.5 %collective-permute-start.1 = (bf16[160,128]{1,0:T(8,128)(2,1)S(1)}, bf16[160,128]{1,0:T(8,128)(2,1)S(1)}, u32[]{:S(2)}, u32[]{:S(2)}) collective-permute-start(bf16[160,128]{1,0:T(8,128)(2,1)S(1)} %get-tuple-element.87), channel_id=1, source_target_pairs={{0,224},{1,225},{2,226},{3,227},{4,228},{5,229},{6,230},{7,231},{8... | collective-permute-start | bytes 122888 | tf_op jit(solution)/shard_map/ppermute | solution.py:548
  11.8 1.0 %copy-start.4 = (bf16[3,3,128,128]{3,2,1,0:T(8,128)(2,1)S(1)}, bf16[3,3,128,128]{3,2,1,0:T(8,128)(2,1)}, u32[]{:S(2)}) copy-start(bf16[3,3,128,128]{3,2,1,0:T(8,128)(2,1)} %kernel_two.3) | copy-start | bytes 884740
  15.5 7.0 %copy-start.7 = (s32[128,2,4]{0,2,1:T(4,128)S(1)}, s32[128,2,4]{0,2,1:T(4,128)}, u32[]{:S(2)}) copy-start(s32[128,2,4]{0,2,1:T(4,128)} %param.10) | copy-start | bytes 12292
  15.5 7.0 %copy-start.9 = (s32[128,2,4]{0,2,1:T(4,128)S(1)}, s32[128,2,4]{0,2,1:T(4,128)}, u32[]{:S(2)}) copy-start(s32[128,2,4]{0,2,1:T(4,128)} %param.11) | copy-start | bytes 12292
  16.0 6.5 %collective-permute-start.2 = (bf16[160,128]{1,0:T(8,128)(2,1)S(1)}, bf16[160,128]{1,0:T(8,128)(2,1)S(1)}, u32[]{:S(2)}, u32[]{:S(2)}) collective-permute-start(bf16[160,128]{1,0:T(8,128)(2,1)S(1)} %get-tuple-element.102), channel_id=1, source_target_pairs={{0,1},{1,0},{2,3},{3,2},{4,5},{5,4},{6,7},{7,6},{8,9},{9,8},{10,11... | collective-permute-start | bytes 122888 | tf_op jit(solution)/shard_map/ppermute | solution.py:548
  16.9 5.6 %collective-permute-start.3 = (bf16[160,128]{1,0:T(8,128)(2,1)S(1)}, bf16[160,128]{1,0:T(8,128)(2,1)S(1)}, u32[]{:S(2)}, u32[]{:S(2)}) collective-permute-start(bf16[160,128]{1,0:T(8,128)(2,1)S(1)} %get-tuple-element.103), channel_id=1, source_target_pairs={{0,255},{1,2},{2,1},{3,4},{4,3},{5,6},{6,5},{7,8},{8,7},{9,10},{10... | collective-permute-start | bytes 122888 | tf_op jit(solution)/shard_map/ppermute | solution.py:548
  28.7 32.6 %copy-start.5 = (bf16[3,3,128,128]{3,2,1,0:T(8,128)(2,1)S(1)}, bf16[3,3,128,128]{3,2,1,0:T(8,128)(2,1)}, u32[]{:S(2)}) copy-start(bf16[3,3,128,128]{3,2,1,0:T(8,128)(2,1)} %kernel_two.3) | copy-start | bytes 884740
  28.7 12.3 %collective-permute-start.4 = (f32[1152,128]{1,0:T(8,128)S(1)}, f32[1152,128]{1,0:T(8,128)S(1)}, u32[]{:S(2)}, u32[]{:S(2)}) collective-permute-start(f32[1152,128]{1,0:T(8,128)S(1)} %shard_map.98), channel_id=1, source_target_pairs={{0,2},{1,3},{2,0},{3,1},{4,6},{5,7},{6,4},{7,5},{8,10},{9,11},{10,... | collective-permute-start | bytes 1769480 | tf_op jit(solution)/shard_map/ppermute | solution.py:539
  34.0 6.9 %collective-permute-start.5 = (bf16[160,128]{1,0:T(8,128)(2,1)S(1)}, bf16[160,128]{1,0:T(8,128)(2,1)S(1)}, u32[]{:S(2)}, u32[]{:S(2)}) collective-permute-start(bf16[160,128]{1,0:T(8,128)(2,1)S(1)} %get-tuple-element.128), channel_id=1, source_target_pairs={{0,32},{1,33},{2,34},{3,35},{4,36},{5,37},{6,38},{7,39},{8,40},{9,... | collective-permute-start | bytes 122888 | tf_op jit(solution)/shard_map/ppermute | solution.py:548
  34.0 6.9 %collective-permute-start.6 = (bf16[160,128]{1,0:T(8,128)(2,1)S(1)}, bf16[160,128]{1,0:T(8,128)(2,1)S(1)}, u32[]{:S(2)}, u32[]{:S(2)}) collective-permute-start(bf16[160,128]{1,0:T(8,128)(2,1)S(1)} %get-tuple-element.129), channel_id=1, source_target_pairs={{0,224},{1,225},{2,226},{3,227},{4,228},{5,229},{6,230},{7,231},{8... | collective-permute-start | bytes 122888 | tf_op jit(solution)/shard_map/ppermute | solution.py:548
  41.8 12.3 %all-to-all-start = ((bf16[16,72,128]{2,1,0:T(8,128)(2,1)}), bf16[16,72,128]{2,1,0:T(8,128)(2,1)S(1)}, u32[]{:S(2)}, u32[]{:S(2)}) async-start(bf16[16,72,128]{2,1,0:T(8,128)(2,1)} %bitcast.5), calls=%async_computation | async-start | bytes 589824 | tf_op jit(solution)/shard_map/all_to_all | solution.py:568
  46.1 3.5 %collective-permute-start.7 = (bf16[160,128]{1,0:T(8,128)(2,1)S(1)}, bf16[160,128]{1,0:T(8,128)(2,1)S(1)}, u32[]{:S(2)}, u32[]{:S(2)}) collective-permute-start(bf16[160,128]{1,0:T(8,128)(2,1)S(1)} %get-tuple-element.140), channel_id=1, source_target_pairs={{0,1},{1,0},{2,3},{3,2},{4,5},{5,4},{6,7},{7,6},{8,9},{9,8},{10,11... | collective-permute-start | bytes 122888 | tf_op jit(solution)/shard_map/ppermute | solution.py:548
  47.5 6.5 %collective-permute-start.8 = (bf16[160,128]{1,0:T(8,128)(2,1)S(1)}, bf16[160,128]{1,0:T(8,128)(2,1)S(1)}, u32[]{:S(2)}, u32[]{:S(2)}) collective-permute-start(bf16[160,128]{1,0:T(8,128)(2,1)S(1)} %get-tuple-element.141), channel_id=1, source_target_pairs={{0,255},{1,2},{2,1},{3,4},{4,3},{5,6},{6,5},{7,8},{8,7},{9,10},{10... | collective-permute-start | bytes 122888 | tf_op jit(solution)/shard_map/ppermute | solution.py:548
  54.8 15.0 %all-to-all-start.1 = ((bf16[8,72,128]{2,1,0:T(8,128)(2,1)}), bf16[8,72,128]{2,1,0:T(8,128)(2,1)S(1)}, u32[]{:S(2)}, u32[]{:S(2)}) async-start(bf16[8,72,128]{2,1,0:T(8,128)(2,1)} %shard_map.101), calls=%async_computation.1 | async-start | bytes 294912 | tf_op jit(solution)/shard_map/all_to_all | solution.py:568
  83.5 3.4 %collective-permute-start.9 = (bf16[1152,128]{1,0:T(8,128)(2,1)S(1)}, bf16[1152,128]{1,0:T(8,128)(2,1)S(1)}, u32[]{:S(2)}, u32[]{:S(2)}) collective-permute-start(bf16[1152,128]{1,0:T(8,128)(2,1)S(1)} %bitcast.11), channel_id=1, source_target_pairs={{0,2},{1,3},{2,0},{3,1},{4,6},{5,7},{6,4},{7,5},{8,10},{9,11},{10,... | collective-permute-start | bytes 884744 | tf_op jit(solution)/shard_map/ppermute | solution.py:539

commit v10 on v9

--- a/solution.py
+++ b/solution.py
@@ -667,14 +667,17 @@
         va, vb = both_ways(done["va"], done["vb"], width)
         return dict(keep=half(True, done["token"]), va=va, vb=vb)
 
+    late = {}
+
     def second_work(done):
         vp, vm, ha, hb = relay(done["token"], done["va"], done["vb"], hp2, hm2)
         ha, hb = both_ways(ha, hb, 1)
-        return dict(vp=vp, vm=vm, ha=ha, hb=hb)
+        late.update(ha=ha, hb=hb)
+        return dict(vp=vp, vm=vm)
 
     def third_work(done):
         hp, hm = call(name_kernel, 1, 2, (message, message), (), 0, 1 << 18)(
-            done["token"], done["ha"], done["hb"]
+            done["token"], late["ha"], late["hb"]
         )
         in_one, fwd_two = call(weights_kernel, 1, 2, (weights, weights))(
             done["token"], kernel_one, kernel_two

time: 88.4 us -> 86.9 us (0.983)
  blocking collectives: 13.6 us -> 10.7 us
  starting transfers between devices: 35 us -> 36.4 us
    all_to_all x2, waiting for transfers between devices: 0.13 us -> 4.55 us  [scatter(): lax.all_to_all(sent, AXES, 0, 0, axis_index_groups=groups, tiled=True)]
    ppermute x4, waiting for transfers between devices: 4.9 us -> 0.49 us  [both_ways(): lax.ppermute(two, AXES, pairs(1))]
    all_to_all x1, blocking collectives: 13.6 us -> 10.7 us  [scatter(): lax.all_to_all(sent, AXES, 0, 0, axis_index_groups=groups, tiled=True)]
    ppermute x2, starting transfers between devices: 7.48 us -> 8.92 us  [swap(): return lax.ppermute(x, AXES, [(i, i ^ bit) for i in range(size)])]
  transfers between devices with their start and end apart: 12 -> 12, of which waited for: 4 -> 3; matrix products, arithmetic and copies ran while one was open for 0% -> 0% of each run, Pallas kernels for 20% -> 21%
where the time goes in v10:
time: 86.9 us; the launch traced here: 86.5 us
  starting transfers between devices  36.4 us (42%)
  Pallas kernels  26.7 us (31%)
  blocking collectives  10.7 us (12%)
  waiting for transfers between devices  6.25 us (7%)
  local copies, waits for them, and re-layouts  4.8 us (6%)
    all_to_all x2, starting transfers between devices, scatter(): lax.all_to_all(sent, AXES, 0, 0, axis_index_groups=groups, tiled=True)  10.7 us
    all_to_all x1, blocking collectives, scatter(): lax.all_to_all(sent, AXES, 0, 0, axis_index_groups=groups, tiled=True)  10.7 us
    ppermute x4, starting transfers between devices, both_ways(): lax.ppermute(two, AXES, pairs(1))  10.6 us
    ppermute x2, starting transfers between devices, swap(): return lax.ppermute(x, AXES, [(i, i ^ bit) for i in range(size)])  8.92 us
    pallas_call x2, Pallas kernels, half(): call(lambda me, *refs: sums_kernel(count, width, scale, kept, me, *refs),...  7.16 us
    ppermute x4, starting transfers between devices, both_ways(): lax.ppermute(one, AXES, pairs(0))  6.17 us
    unnamed x20, local copies, waits for them, and re-layouts  4.8 us
    pallas_call x1, Pallas kernels, third_work(): call(lambda *refs: grads_kernel(count, width, *refs), 3, 6, (block,), [pl...  4.71 us
  transfers between devices with their start and end apart: 12, of which 3 were waited for; matrix products, arithmetic and copies ran while one was open for 0% of the time, Pallas kernels for 21%

profile of v10, /device:TPU:1, one launch (start us, length us, event | category | flops | bytes accessed | tf_op | source)
XLA Modules:
  0.0 86.5 jit_solution(9924190224473560503)
XLA Ops:
  0.6 1.2 %copy-done = bf16[1,1,64,64,128]{4,3,2,1,0:T(8,128)(2,1)S(1)} copy-done((bf16[1,1,64,64,128]{4,3,2,1,0:T(8,128)(2,1)S(1)}, bf16[1,1,64,64,128]{4,3,2,1,0:T(8,128)(2,1)}, u32[]{:S(2)}) %copy-start) | copy-done | bytes 1048600
  1.9 1.2 %copy-done.1 = bf16[1,1,64,64,128]{4,3,2,1,0:T(8,128)(2,1)S(1)} copy-done((bf16[1,1,64,64,128]{4,3,2,1,0:T(8,128)(2,1)S(1)}, bf16[1,1,64,64,128]{4,3,2,1,0:T(8,128)(2,1)}, u32[]{:S(2)}) %copy-start.1) | copy-done | bytes 1048600
  4.5 1.2 %shard_map.93 = (bf16[160,128]{1,0:T(8,128)(2,1)S(1)}, bf16[160,128]{1,0:T(8,128)(2,1)S(1)}, bf16[128,128]{1,0:T(8,128)(2,1)S(1)}, bf16[128,128]{1,0:T(8,128)(2,1)S(1)}, bf16[32,2,64,128]{3,2,1,0:T(8,128)(2,1)S(1)}) custom-call(s32[1]{0:T(128)} %bitcast.refs_0_.token.me, s32[2,4,128]{2,1,0:T(4,128)S(1)} %bitcast.16, s32[2,4,128]{2,1,0:T(4,128)S(1)} %bitcast.21, ...), custom_call_target="tpu_custom_call" | custom-call | bytes 4194304 | tf_op jit(solution)/shard_map/pallas_call | solution.py:622
  5.7 3.8 %collective-permute-start = (bf16[160,128]{1,0:T(8,128)(2,1)S(1)}, bf16[160,128]{1,0:T(8,128)(2,1)S(1)}, u32[]{:S(2)}, u32[]{:S(2)}) collective-permute-start(bf16[160,128]{1,0:T(8,128)(2,1)S(1)} %get-tuple-element.82), channel_id=1, source_target_pairs={{0,32},{1,33},{2,34},{3,35},{4,36},{5,37},{6,38},{7,39},{8,40},{9,... | collective-permute-start | bytes 122888 | tf_op jit(solution)/shard_map/ppermute | solution.py:548
  9.5 2.3 %collective-permute-start.1 = (bf16[160,128]{1,0:T(8,128)(2,1)S(1)}, bf16[160,128]{1,0:T(8,128)(2,1)S(1)}, u32[]{:S(2)}, u32[]{:S(2)}) collective-permute-start(bf16[160,128]{1,0:T(8,128)(2,1)S(1)} %get-tuple-element.83), channel_id=1, source_target_pairs={{0,224},{1,225},{2,226},{3,227},{4,228},{5,229},{6,230},{7,231},{8... | collective-permute-start | bytes 122888 | tf_op jit(solution)/shard_map/ppermute | solution.py:548
  12.8 2.7 %shard_map.94 = (bf16[1536,256]{1,0:T(8,128)(2,1)S(1)}, bf16[3,33,2,64,128]{4,3,2,1,0:T(8,128)(2,1)S(1)}, f32[32,2,64,128]{3,2,1,0:T(8,128)S(1)}) custom-call(s32[1]{0:T(128)} %bitcast.refs_0_.token.me, bf16[3,3,128,128]{3,2,1,0:T(8,128)(2,1)S(1)} %copy-done.4, bf16[32,2,64,128]{3,2,1,0:T(8,128)(2,1)S(1)} %get-tuple-element.85.upstream), custom_call_target="tpu_custom_call" | custom-call | flops 1207959552 | bytes 4194304 | tf_op jit(solution)/shard_map/pallas_call | solution.py:628
  16.9 2.9 %collective-permute-start.3 = (bf16[160,128]{1,0:T(8,128)(2,1)S(1)}, bf16[160,128]{1,0:T(8,128)(2,1)S(1)}, u32[]{:S(2)}, u32[]{:S(2)}) collective-permute-start(bf16[160,128]{1,0:T(8,128)(2,1)S(1)} %get-tuple-element.99), channel_id=1, source_target_pairs={{0,255},{1,2},{2,1},{3,4},{4,3},{5,6},{6,5},{7,8},{8,7},{9,10},{10... | collective-permute-start | bytes 122888 | tf_op jit(solution)/shard_map/ppermute | solution.py:548
  19.8 2.6 %shard_map.96 = (bf16[1536,256]{1,0:T(8,128)(2,1)S(1)}, bf16[3,33,2,64,128]{4,3,2,1,0:T(8,128)(2,1)S(1)}, f32[32,2,64,128]{3,2,1,0:T(8,128)S(1)}) custom-call(s32[1]{0:T(128)} %bitcast.refs_0_.token.me, bf16[3,3,128,128]{3,2,1,0:T(8,128)(2,1)S(1)} %copy-done.3, bf16[32,2,64,128]{3,2,1,0:T(8,128)(2,1)S(1)} %bitcast.15), custom_call_target="tpu_custom_call" | custom-call | flops 1207959552 | bytes 4194304 | tf_op jit(solution)/shard_map/pallas_call | solution.py:643
  22.5 2.6 %shard_map.97 = (bf16[32,2,64,128]{3,2,1,0:T(8,128)(2,1)S(1)}, bf16[32,2,64,128]{3,2,1,0:T(8,128)(2,1)S(1)}, bf16[160,128]{1,0:T(8,128)(2,1)S(1)}, bf16[160,128]...) custom-call(s32[1]{0:T(128)} %bitcast.refs_0_.token.me, ...), custom_call_target="tpu_custom_call" | custom-call | flops 1207959552 | bytes 4194304 | tf_op jit(solution)/shard_map/pallas_call | solution.py:646
  25.1 3.6 %shard_map.98 = f32[1152,128]{1,0:T(8,128)S(1)} custom-call(s32[1]{0:T(128)} %bitcast.refs_0_.token.me, s32[2,4,128]{2,1,0:T(4,128)S(1)} %bitcast.18, s32[2,4,128]{2,1,0:T(4,128)S(1)} %bitcast.23, bf16[160,128]{1,0:T(8,128)(2,1)S(1)} %get-tuple-element.94.refs_3_.refs_2_, bf16[160,128]{1,0:T(8,128)(2,1)S(1)} %get-tuple-element.95.refs_4_.refs_3_, ...), custom_call_target="tpu_custom_call" | custom-call | flops 1207959552 | bytes 4194304 | tf_op jit(solution)/shard_map/pallas_call | solution.py:657
  28.7 5.3 %collective-permute-start.4 = (f32[1152,128]{1,0:T(8,128)S(1)}, f32[1152,128]{1,0:T(8,128)S(1)}, u32[]{:S(2)}, u32[]{:S(2)}) collective-permute-start(f32[1152,128]{1,0:T(8,128)S(1)} %shard_map.98), channel_id=1, source_target_pairs={{0,2},{1,3},{2,0},{3,1},{4,6},{5,7},{6,4},{7,5},{8,10},{9,11},{10,... | collective-permute-start | bytes 1769480 | tf_op jit(solution)/shard_map/ppermute | solution.py:539
  34.0 3.3 %collective-permute-start.6 = (bf16[160,128]{1,0:T(8,128)(2,1)S(1)}, bf16[160,128]{1,0:T(8,128)(2,1)S(1)}, u32[]{:S(2)}, u32[]{:S(2)}) collective-permute-start(bf16[160,128]{1,0:T(8,128)(2,1)S(1)} %get-tuple-element.125), channel_id=1, source_target_pairs={{0,224},{1,225},{2,226},{3,227},{4,228},{5,229},{6,230},{7,231},{8... | collective-permute-start | bytes 122888 | tf_op jit(solution)/shard_map/ppermute | solution.py:548
  37.4 3.6 %shard_map.99 = f32[1152,128]{1,0:T(8,128)S(1)} custom-call(s32[1]{0:T(128)} %bitcast.refs_0_.token.me, s32[2,4,128]{2,1,0:T(4,128)S(1)} %bitcast.19, s32[2,4,128]{2,1,0:T(4,128)S(1)} %bitcast.24, bf16[160,128]{1,0:T(8,128)(2,1)S(1)} %get-tuple-element.94.refs_3_.refs_2_, bf16[160,128]{1,0:T(8,128)(2,1)S(1)} %get-tuple-element.95.refs_4_.refs_3_, ...), custom_call_target="tpu_custom_call" | custom-call | flops 1207959552 | bytes 4194304 | tf_op jit(solution)/shard_map/pallas_call | solution.py:657
  41.8 4.2 %all-to-all-start = ((bf16[16,72,128]{2,1,0:T(8,128)(2,1)}), bf16[16,72,128]{2,1,0:T(8,128)(2,1)S(1)}, u32[]{:S(2)}, u32[]{:S(2)}) async-start(bf16[16,72,128]{2,1,0:T(8,128)(2,1)} %bitcast.5), calls=%async_computation | async-start | bytes 589824 | tf_op jit(solution)/shard_map/all_to_all | solution.py:568
  46.1 1.4 %collective-permute-start.7 = (bf16[160,128]{1,0:T(8,128)(2,1)S(1)}, bf16[160,128]{1,0:T(8,128)(2,1)S(1)}, u32[]{:S(2)}, u32[]{:S(2)}) collective-permute-start(bf16[160,128]{1,0:T(8,128)(2,1)S(1)} %get-tuple-element.145), channel_id=1, source_target_pairs={{0,1},{1,0},{2,3},{3,2},{4,5},{5,4},{6,7},{7,6},{8,9},{9,8},{10,11... | collective-permute-start | bytes 122888 | tf_op jit(solution)/shard_map/ppermute | solution.py:548
  47.5 2.1 %collective-permute-start.8 = (bf16[160,128]{1,0:T(8,128)(2,1)S(1)}, bf16[160,128]{1,0:T(8,128)(2,1)S(1)}, u32[]{:S(2)}, u32[]{:S(2)}) collective-permute-start(bf16[160,128]{1,0:T(8,128)(2,1)S(1)} %get-tuple-element.146), channel_id=1, source_target_pairs={{0,255},{1,2},{2,1},{3,4},{4,3},{5,6},{6,5},{7,8},{8,7},{9,10},{10... | collective-permute-start | bytes 122888 | tf_op jit(solution)/shard_map/ppermute | solution.py:548
  49.6 4.5 %all-to-all-done.parts = bf16[16,72,128]{2,1,0:T(8,128)(2,1)S(1)} async-done(((bf16[16,72,128]{2,1,0:T(8,128)(2,1)}), bf16[16,72,128]{2,1,0:T(8,128)(2,1)S(1)}, u32[]{:S(2)}, u32[]{:S(2)}) %all-to-all-start) | async-done | bytes 294944 | tf_op jit(solution)/shard_map/all_to_all | solution.py:568
  54.8 6.5 %all-to-all-start.1 = ((bf16[8,72,128]{2,1,0:T(8,128)(2,1)}), bf16[8,72,128]{2,1,0:T(8,128)(2,1)S(1)}, u32[]{:S(2)}, u32[]{:S(2)}) async-start(bf16[8,72,128]{2,1,0:T(8,128)(2,1)} %shard_map.101), calls=%async_computation.1 | async-start | bytes 294912 | tf_op jit(solution)/shard_map/all_to_all | solution.py:568
  61.7 4.7 %shard_map.104 = bf16[32,2,64,128]{3,2,1,0:T(8,128)(2,1)} custom-call(s32[1]{0:T(128)} %bitcast.refs_0_.token.me, s32[2,4,128]{2,1,0:T(4,128)S(1)} %bitcast.20, s32[2,4,128]{2,1,0:T(4,128)S(1)} %bitcast.25, bf16[160,128]{1,0:T(8,128)(2,1)S(1)} %get-tuple-element.142.refs_3_.vp, bf16[160,128]{1,0:T(8,128)(2,1)S(1)} %get-tuple-element.143.refs_4_.vm, ...), custom_call_target="tpu_custom_call" | custom-call | flops 1207959552 | bytes 4194304 | tf_op jit(solution)/shard_map/pallas_call | solution.py:688
  66.4 3.5 %shard_map.105 = bf16[32,2,64,128]{3,2,1,0:T(8,128)(2,1)} custom-call(bf16[32,2,64,128]{3,2,1,0:T(8,128)(2,1)S(1)} %get-tuple-element.112.refs_6_.hidden, bf16[160,128]{1,0:T(8,128)(2,1)S(1)} %get-tuple-element.142.refs_3_.vp, bf16[160,128]{1,0:T(8,128)(2,1)S(1)} %get-tuple-element.143.refs_4_.vm, bf16[160,128]{1,0:T(8,128)(2,1)S(1)} %get-tuple-element.147.refs_5_.hp, ...), custom_call_target="tpu_custom_call" | custom-call | flops 1207959552 | bytes 4194304 | tf_op jit(solution)/shard_map/pallas_call | solution.py:685
  69.9 10.7 %all_to_all.15 = bf16[16,72,128]{2,1,0:T(8,128)(2,1)S(1)} all-to-all(bf16[16,72,128]{2,1,0:T(8,128)(2,1)S(1)} %shard_map.106), channel_id=1, replica_groups={{0,128,64,192,32,160,96,224,1,129,65,193,33,161,97,225},{2,130,66,194,3..., dimensions={0} | all-to-all | bytes 589824 | tf_op jit(solution)/shard_map/all_to_all | solution.py:568
  80.6 3.6 %collective-permute-start.9 = (bf16[1152,128]{1,0:T(8,128)(2,1)S(1)}, bf16[1152,128]{1,0:T(8,128)(2,1)S(1)}, u32[]{:S(2)}, u32[]{:S(2)}) collective-permute-start(bf16[1152,128]{1,0:T(8,128)(2,1)S(1)} %bitcast.11), channel_id=1, source_target_pairs={{0,2},{1,3},{2,0},{3,1},{4,6},{5,7},{6,4},{7,5},{8,10},{9,11},{10,... | collective-permute-start | bytes 884744 | tf_op jit(solution)/shard_map/ppermute | solution.py:539
  84.2 1.2 %collective-permute-done.9.other = bf16[1152,128]{1,0:T(8,128)(2,1)S(1)} collective-permute-done((bf16[1152,128]{1,0:T(8,128)(2,1)S(1)}, bf16[1152,128]{1,0:T(8,128)(2,1)S(1)}, u32[]{:S(2)}, u32[]{:S(2)}) %collective-permute-start.9) | collective-permute-done | bytes 294944 | tf_op jit(solution)/shard_map/ppermute | solution.py:539
  85.4 1.1 %shard_map.107 = (f32[1152,128]{1,0:T(8,128)}, f32[1152,128]{1,0:T(8,128)}) custom-call(s32[1]{0:T(128)} %bitcast.refs_0_.token.me, bf16[1152,128]{1,0:T(8,128)(2,1)S(1)} %bitcast.12, bf16[1152,128]{1,0:T(8,128)(2,1)S(1)} %collective-permute-done.9.other), custom_call_target="tpu_custom_call" | custom-call | bytes 4194304 | tf_op jit(solution)/shard_map/pallas_call | solution.py:597
  (37 shorter events, 5.6 us)
Async XLA Ops:
  0.6 1.2 %copy-start = (bf16[1,1,64,64,128]{4,3,2,1,0:T(8,128)(2,1)S(1)}, bf16[1,1,64,64,128]{4,3,2,1,0:T(8,128)(2,1)}, u32[]{:S(2)}) copy-start(bf16[1,1,64,64,128]{4,3,2,1,0:T(8,128)(2,1)} %param.9) | copy-start | bytes 3145732
  1.9 1.2 %copy-start.1 = (bf16[1,1,64,64,128]{4,3,2,1,0:T(8,128)(2,1)S(1)}, bf16[1,1,64,64,128]{4,3,2,1,0:T(8,128)(2,1)}, u32[]{:S(2)}) copy-start(bf16[1,1,64,64,128]{4,3,2,1,0:T(8,128)(2,1)} %param.6) | copy-start | bytes 3145732
  3.1 0.7 copy-start.6
  3.8 0.7 copy-start.8
  4.5 15.4 %copy-start.2 = (bf16[1,1,64,64,128]{4,3,2,1,0:T(8,128)(2,1)S(1)}, bf16[1,1,64,64,128]{4,3,2,1,0:T(8,128)(2,1)}, u32[]{:S(2)}) copy-start(bf16[1,1,64,64,128]{4,3,2,1,0:T(8,128)(2,1)} %param.6) | copy-start | bytes 3145732
  4.5 15.4 %copy-start.3 = (bf16[3,3,128,128]{3,2,1,0:T(8,128)(2,1)S(1)}, bf16[3,3,128,128]{3,2,1,0:T(8,128)(2,1)}, u32[]{:S(2)}) copy-start(bf16[3,3,128,128]{3,2,1,0:T(8,128)(2,1)} %kernel_one.3) | copy-start | bytes 884740
  5.7 9.8 %collective-permute-start = (bf16[160,128]{1,0:T(8,128)(2,1)S(1)}, bf16[160,128]{1,0:T(8,128)(2,1)S(1)}, u32[]{:S(2)}, u32[]{:S(2)}) collective-permute-start(bf16[160,128]{1,0:T(8,128)(2,1)S(1)} %get-tuple-element.82), channel_id=1, source_target_pairs={{0,32},{1,33},{2,34},{3,35},{4,36},{5,37},{6,38},{7,39},{8,40},{9,... | collective-permute-start | bytes 122888 | tf_op jit(solution)/shard_map/ppermute | solution.py:548
  9.5 6.5 %collective-permute-start.1 = (bf16[160,128]{1,0:T(8,128)(2,1)S(1)}, bf16[160,128]{1,0:T(8,128)(2,1)S(1)}, u32[]{:S(2)}, u32[]{:S(2)}) collective-permute-start(bf16[160,128]{1,0:T(8,128)(2,1)S(1)} %get-tuple-element.83), channel_id=1, source_target_pairs={{0,224},{1,225},{2,226},{3,227},{4,228},{5,229},{6,230},{7,231},{8... | collective-permute-start | bytes 122888 | tf_op jit(solution)/shard_map/ppermute | solution.py:548
  11.8 1.0 %copy-start.4 = (bf16[3,3,128,128]{3,2,1,0:T(8,128)(2,1)S(1)}, bf16[3,3,128,128]{3,2,1,0:T(8,128)(2,1)}, u32[]{:S(2)}) copy-start(bf16[3,3,128,128]{3,2,1,0:T(8,128)(2,1)} %kernel_two.3) | copy-start | bytes 884740
  15.5 7.0 %copy-start.7 = (s32[128,2,4]{0,2,1:T(4,128)S(1)}, s32[128,2,4]{0,2,1:T(4,128)}, u32[]{:S(2)}) copy-start(s32[128,2,4]{0,2,1:T(4,128)} %param.10) | copy-start | bytes 12292
  15.5 7.0 %copy-start.9 = (s32[128,2,4]{0,2,1:T(4,128)S(1)}, s32[128,2,4]{0,2,1:T(4,128)}, u32[]{:S(2)}) copy-start(s32[128,2,4]{0,2,1:T(4,128)} %param.11) | copy-start | bytes 12292
  16.0 6.4 %collective-permute-start.2 = (bf16[160,128]{1,0:T(8,128)(2,1)S(1)}, bf16[160,128]{1,0:T(8,128)(2,1)S(1)}, u32[]{:S(2)}, u32[]{:S(2)}) collective-permute-start(bf16[160,128]{1,0:T(8,128)(2,1)S(1)} %get-tuple-element.98), channel_id=1, source_target_pairs={{0,1},{1,0},{2,3},{3,2},{4,5},{5,4},{6,7},{7,6},{8,9},{9,8},{10,11... | collective-permute-start | bytes 122888 | tf_op jit(solution)/shard_map/ppermute | solution.py:548
  16.9 5.6 %collective-permute-start.3 = (bf16[160,128]{1,0:T(8,128)(2,1)S(1)}, bf16[160,128]{1,0:T(8,128)(2,1)S(1)}, u32[]{:S(2)}, u32[]{:S(2)}) collective-permute-start(bf16[160,128]{1,0:T(8,128)(2,1)S(1)} %get-tuple-element.99), channel_id=1, source_target_pairs={{0,255},{1,2},{2,1},{3,4},{4,3},{5,6},{6,5},{7,8},{8,7},{9,10},{10... | collective-permute-start | bytes 122888 | tf_op jit(solution)/shard_map/ppermute | solution.py:548
  28.7 32.6 %copy-start.5 = (bf16[3,3,128,128]{3,2,1,0:T(8,128)(2,1)S(1)}, bf16[3,3,128,128]{3,2,1,0:T(8,128)(2,1)}, u32[]{:S(2)}) copy-start(bf16[3,3,128,128]{3,2,1,0:T(8,128)(2,1)} %kernel_two.3) | copy-start | bytes 884740
  28.7 12.3 %collective-permute-start.4 = (f32[1152,128]{1,0:T(8,128)S(1)}, f32[1152,128]{1,0:T(8,128)S(1)}, u32[]{:S(2)}, u32[]{:S(2)}) collective-permute-start(f32[1152,128]{1,0:T(8,128)S(1)} %shard_map.98), channel_id=1, source_target_pairs={{0,2},{1,3},{2,0},{3,1},{4,6},{5,7},{6,4},{7,5},{8,10},{9,11},{10,... | collective-permute-start | bytes 1769480 | tf_op jit(solution)/shard_map/ppermute | solution.py:539
  34.0 6.9 %collective-permute-start.5 = (bf16[160,128]{1,0:T(8,128)(2,1)S(1)}, bf16[160,128]{1,0:T(8,128)(2,1)S(1)}, u32[]{:S(2)}, u32[]{:S(2)}) collective-permute-start(bf16[160,128]{1,0:T(8,128)(2,1)S(1)} %get-tuple-element.124), channel_id=1, source_target_pairs={{0,32},{1,33},{2,34},{3,35},{4,36},{5,37},{6,38},{7,39},{8,40},{9,... | collective-permute-start | bytes 122888 | tf_op jit(solution)/shard_map/ppermute | solution.py:548
  34.0 6.9 %collective-permute-start.6 = (bf16[160,128]{1,0:T(8,128)(2,1)S(1)}, bf16[160,128]{1,0:T(8,128)(2,1)S(1)}, u32[]{:S(2)}, u32[]{:S(2)}) collective-permute-start(bf16[160,128]{1,0:T(8,128)(2,1)S(1)} %get-tuple-element.125), channel_id=1, source_target_pairs={{0,224},{1,225},{2,226},{3,227},{4,228},{5,229},{6,230},{7,231},{8... | collective-permute-start | bytes 122888 | tf_op jit(solution)/shard_map/ppermute | solution.py:548
  41.8 12.3 %all-to-all-start = ((bf16[16,72,128]{2,1,0:T(8,128)(2,1)}), bf16[16,72,128]{2,1,0:T(8,128)(2,1)S(1)}, u32[]{:S(2)}, u32[]{:S(2)}) async-start(bf16[16,72,128]{2,1,0:T(8,128)(2,1)} %bitcast.5), calls=%async_computation | async-start | bytes 589824 | tf_op jit(solution)/shard_map/all_to_all | solution.py:568
  46.1 15.6 %collective-permute-start.7 = (bf16[160,128]{1,0:T(8,128)(2,1)S(1)}, bf16[160,128]{1,0:T(8,128)(2,1)S(1)}, u32[]{:S(2)}, u32[]{:S(2)}) collective-permute-start(bf16[160,128]{1,0:T(8,128)(2,1)S(1)} %get-tuple-element.145), channel_id=1, source_target_pairs={{0,1},{1,0},{2,3},{3,2},{4,5},{5,4},{6,7},{7,6},{8,9},{9,8},{10,11... | collective-permute-start | bytes 122888 | tf_op jit(solution)/shard_map/ppermute | solution.py:548
  47.5 14.1 %collective-permute-start.8 = (bf16[160,128]{1,0:T(8,128)(2,1)S(1)}, bf16[160,128]{1,0:T(8,128)(2,1)S(1)}, u32[]{:S(2)}, u32[]{:S(2)}) collective-permute-start(bf16[160,128]{1,0:T(8,128)(2,1)S(1)} %get-tuple-element.146), channel_id=1, source_target_pairs={{0,255},{1,2},{2,1},{3,4},{4,3},{5,6},{6,5},{7,8},{8,7},{9,10},{10... | collective-permute-start | bytes 122888 | tf_op jit(solution)/shard_map/ppermute | solution.py:548
  54.8 15.0 %all-to-all-start.1 = ((bf16[8,72,128]{2,1,0:T(8,128)(2,1)}), bf16[8,72,128]{2,1,0:T(8,128)(2,1)S(1)}, u32[]{:S(2)}, u32[]{:S(2)}) async-start(bf16[8,72,128]{2,1,0:T(8,128)(2,1)} %shard_map.101), calls=%async_computation.1 | async-start | bytes 294912 | tf_op jit(solution)/shard_map/all_to_all | solution.py:568
  80.6 4.8 %collective-permute-start.9 = (bf16[1152,128]{1,0:T(8,128)(2,1)S(1)}, bf16[1152,128]{1,0:T(8,128)(2,1)S(1)}, u32[]{:S(2)}, u32[]{:S(2)}) collective-permute-start(bf16[1152,128]{1,0:T(8,128)(2,1)S(1)} %bitcast.11), channel_id=1, source_target_pairs={{0,2},{1,3},{2,0},{3,1},{4,6},{5,7},{6,4},{7,5},{8,10},{9,11},{10,... | collective-permute-start | bytes 884744 | tf_op jit(solution)/shard_map/ppermute | solution.py:539
